TPU v7x, 512 devices: a whole 4x4x16 slice. The times are simulated.
512 devices in a mesh: dp: 32 (over z_lo, x), tensor: 16 (over z_hi, y, core).
Axes of the slice: x: 4, y: 4, z: 16 (z_hi: 2, z_lo: 8; z = z_hi * 8 + z_lo), core: 2. Of those that a mesh axis runs over, the one named last changes fastest.
Arguments:
- tokens: bfloat16 [8192, 3072], P('dp', 'tensor'), may hold values from -6 to 6
- tangent: bfloat16 [8192, 3072], P('dp', 'tensor'), may hold values from -6 to 6
- cotangent: bfloat16 [8192, 3072], P('dp', 'tensor'), may hold values from -6 to 6
- gates: float32 [8192], P('dp'), may hold values from 0.1 to 1
- slot_tokens: int32 [8192], P('dp'), may hold values from -1 to 255, as said below
- gate_weight: bfloat16 [3072, 8192], P('dp', 'tensor'), may hold values from -0.109375 to 0.109375
- up_weight: bfloat16 [3072, 8192], P('dp', 'tensor'), may hold values from -0.109375 to 0.109375
- down_weight: bfloat16 [8192, 3072], P('tensor', 'dp'), may hold values from -0.0625 to 0.0625
Outputs:
- hvp: bfloat16 [8192, 3072], P('dp', 'tensor')
Inputs may be any that keep to these rules, and one draw needn't show every extreme that they name: `slot_tokens`: each group of 256 slots holds its live slots first, naming distinct tokens of that group in ascending order, and -1 in the rest; some group has all 256 slots live.
All inputs are finite; a program needn't handle non-finite values.
Results may differ from a plain program's by a relative error of at most 0.0049.
Values may be sent and summed in bfloat16 or wider, within the bound.
No kernel may reach another device: no remote copies, remote signals or barrier semaphores. Data moves between devices by JAX's collectives and lax.ppermute only.
A program may use at most 64 MiB of HBM per device.

v0:
```python
import jax
import jax.numpy as jnp
from jax import lax
from jax.sharding import PartitionSpec as P


def right_product(left, right):
    return lax.dot_general(
        left, right, (((1,), (1,)), ((), ())), preferred_element_type=jnp.float32
    )


def body(tokens, tangent, cotangent, gates, slot_tokens, gate_weight, up_weight, down_weight):
    tok_rows = tokens.shape[0]
    onehot = slot_tokens[:, None] == lax.broadcasted_iota(
        jnp.int32, (slot_tokens.shape[0], tok_rows), 1
    )
    picker = onehot.astype(jnp.bfloat16)

    def select(field):
        return jnp.dot(picker, field, preferred_element_type=jnp.float32).astype(jnp.bfloat16)

    slot_gate = jnp.sum(jnp.where(onehot, gates[None, :], 0.0), axis=1)
    inputs, tangents, cotangents = (
        lax.all_gather(select(tokens), "tensor", axis=1, tiled=True),
        lax.all_gather(select(tangent), "tensor", axis=1, tiled=True),
        lax.all_gather(select(cotangent), "tensor", axis=1, tiled=True),
    )
    gate_full, up_full = (
        lax.all_gather(gate_weight, "dp", axis=0, tiled=True),
        lax.all_gather(up_weight, "dp", axis=0, tiled=True),
    )
    down_full = lax.all_gather(down_weight, "dp", axis=1, tiled=True)
    gate_pre = jnp.dot(inputs, gate_full, preferred_element_type=jnp.float32)
    up_pre = jnp.dot(inputs, up_full, preferred_element_type=jnp.float32)
    gate_tan = jnp.dot(tangents, gate_full, preferred_element_type=jnp.float32)
    up_tan = jnp.dot(tangents, up_full, preferred_element_type=jnp.float32)
    back_sum = right_product(cotangents, down_full)
    back = slot_gate[:, None] * back_sum
    squash = jax.nn.sigmoid(gate_pre)
    first = squash * (1.0 + gate_pre * (1.0 - squash))
    second = squash * (1.0 - squash) * (2.0 + gate_pre * (1.0 - 2.0 * squash))
    gate_dir = (back * (up_tan * first + up_pre * second * gate_tan)).astype(jnp.bfloat16)
    up_dir = (back * first * gate_tan).astype(jnp.bfloat16)
    partial_rows = right_product(gate_dir, gate_full) + right_product(up_dir, up_full)
    shares = lax.psum_scatter(partial_rows, "tensor", scatter_dimension=1, tiled=True)
    placed = jnp.dot(onehot.astype(jnp.float32).T, shares, precision=lax.Precision.HIGHEST)
    return placed.astype(jnp.bfloat16)


def solution(mesh):
    in_specs = (
        P("dp", "tensor"),
        P("dp", "tensor"),
        P("dp", "tensor"),
        P("dp"),
        P("dp"),
        P("dp", "tensor"),
        P("dp", "tensor"),
        P("tensor", "dp"),
    )
    out_specs = P("dp", "tensor")
    return jax.shard_map(body, mesh=mesh, in_specs=in_specs, out_specs=out_specs, check_vma=False)
```

profile of v0, /device:TPU:2, one launch (start us, length us, event | category | flops | bytes accessed | tf_op | source)
XLA Modules:
  0.0 1091.3 jit_solution(6250569064489598813)
XLA Ops:
  6.5 0.0 copy-start
  6.5 0.0 all-gather.15.cloned.1.call-start
  6.5 0.9 copy-done
  7.4 1.6 convolution_convert_fusion.1
  9.0 0.0 all-gather.15.cloned.1.call-update
  9.1 0.0 all-gather.17.cloned.1.call-start
  9.1 0.7 all-gather.17.cloned.1.call-update
  9.8 0.0 all-gather.11.cloned.1.call-start
  9.9 1.8 convolution_convert_fusion.2
  11.7 0.0 all-gather.11.cloned.1.call-update
  11.7 0.0 all-gather.13.cloned.1.call-start
  11.8 0.5 all-gather.13.cloned.1.call-update
  12.3 0.0 all-gather.7.cloned.1.call-start
  12.3 1.8 convolution_convert_fusion.3
  14.2 0.0 all-gather.7.cloned.1.call-update
  14.2 0.0 all-gather.9.cloned.1.call-start
  14.3 0.5 all-gather.9.cloned.1.call-update
  14.8 0.0 reduce-scatter.4.cloned.1.call-start
  14.8 0.9 select_reduce_fusion
  15.7 84.5 %all-gather.15.cloned.1.call-done = bf16[256,3072]{0,1:T(8,128)(2,1)} async-done(((bf16[256,192]{0,1:T(8,128)(2,1)}), bf16[256,3072]{0,1:T(8,128)(2,1)}) %all-gather.15.cloned.1.call-update) | async-done | bytes 1572880 | tf_op jit(solution)/shard_map/all_gather | solution.py:25
  100.2 219.0 %all-gather.17.cloned.1.call-done = bf16[3072,512]{1,0:T(8,128)(2,1)} async-done(((bf16[96,512]{1,0:T(8,128)(2,1)}), bf16[3072,512]{1,0:T(8,128)(2,1)}) %all-gather.17.cloned.1.call-update) | async-done | bytes 3145744 | tf_op jit(solution)/shard_map/all_gather | solution.py:30
  319.2 3.4 fusion.24
  322.6 0.0 copy-start.2
  322.6 83.2 %all-gather.11.cloned.1.call-done = bf16[256,3072]{0,1:T(8,128)(2,1)} async-done(((bf16[256,192]{0,1:T(8,128)(2,1)}), bf16[256,3072]{0,1:T(8,128)(2,1)}) %all-gather.11.cloned.1.call-update) | async-done | bytes 1572880 | tf_op jit(solution)/shard_map/all_gather | solution.py:26
  405.8 0.0 copy-start.4
  405.8 4.3 fusion.25
  410.1 214.6 %all-gather.13.cloned.1.call-done = bf16[3072,512]{1,0:T(8,128)(2,1)} async-done(((bf16[96,512]{1,0:T(8,128)(2,1)}), bf16[3072,512]{1,0:T(8,128)(2,1)}) %all-gather.13.cloned.1.call-update) | async-done | bytes 3145744 | tf_op jit(solution)/shard_map/all_gather | solution.py:31
  624.7 0.0 copy-done.2
  624.7 0.0 copy-done.4
  624.7 3.8 convolution_multiply_fusion.1
  628.4 0.0 copy-start.1
  628.4 82.7 %all-gather.7.cloned.1.call-done = bf16[256,3072]{0,1:T(8,128)(2,1)} async-done(((bf16[256,192]{0,1:T(8,128)(2,1)}), bf16[256,3072]{0,1:T(8,128)(2,1)}) %all-gather.7.cloned.1.call-update) | async-done | bytes 1572880 | tf_op jit(solution)/shard_map/all_gather | solution.py:27
  711.1 218.8 %all-gather.9.cloned.1.call-done = bf16[512,3072]{0,1:T(8,128)(2,1)} async-done(((bf16[512,96]{0,1:T(8,128)(2,1)}), bf16[512,3072]{0,1:T(8,128)(2,1)}) %all-gather.9.cloned.1.call-update) | async-done | bytes 3145744 | tf_op jit(solution)/shard_map/all_gather | solution.py:33
  930.0 4.2 convolution_multiply_fusion.2
  934.2 0.0 copy-done.1
  934.2 6.8 fusion.5
  941.0 5.2 fusion
  946.2 0.0 copy-start.3
  946.2 0.0 reduce-scatter.4.cloned.1.call-update
  946.2 136.3 %reduce-scatter.4.cloned.1.call-done = f32[192,256]{1,0:T(8,128)} async-done(((f32[3072,256]{1,0:T(8,128)}), f32[192,256]{1,0:T(8,128)}) %reduce-scatter.4.cloned.1.call-update) | async-done | bytes 196624
  1082.5 0.0 copy-done.3
  1082.5 1.9 convolution_convert_fusion
Async XLA Ops:
  6.5 0.9 copy-start
  6.5 93.7 %all-gather.15.cloned.1.call-start = ((), (), s32[]{:S(2)}) async-start(), calls=%async_computation.5 | async-start | bytes 1671168 | tf_op jit(solution)/shard_map/all_gather | solution.py:25
  9.1 310.1 %all-gather.17.cloned.1.call-start = ((), (), s32[]{:S(2)}) async-start(), calls=%async_computation.6 | async-start | bytes 3244032 | tf_op jit(solution)/shard_map/all_gather | solution.py:30
  9.8 396.0 %all-gather.11.cloned.1.call-start = ((), (), s32[]{:S(2)}) async-start(), calls=%async_computation.3 | async-start | bytes 1671168 | tf_op jit(solution)/shard_map/all_gather | solution.py:26
  11.7 612.9 %all-gather.13.cloned.1.call-start = ((), (), s32[]{:S(2)}) async-start(), calls=%async_computation.4 | async-start | bytes 3244032 | tf_op jit(solution)/shard_map/all_gather | solution.py:31
  12.3 698.8 %all-gather.7.cloned.1.call-start = ((), (), s32[]{:S(2)}) async-start(), calls=%async_computation.1 | async-start | bytes 1671168 | tf_op jit(solution)/shard_map/all_gather | solution.py:27
  14.2 915.7 %all-gather.9.cloned.1.call-start = ((), (), s32[]{:S(2)}) async-start(), calls=%async_computation.2 | async-start | bytes 3244032 | tf_op jit(solution)/shard_map/all_gather | solution.py:33
  14.8 1067.7 %reduce-scatter.4.cloned.1.call-start = ((), (), s32[]{:S(2)}) async-start(), calls=%async_computation.7 | async-start | bytes 3342336
  322.6 302.1 %copy-start.2 = (f32[256,512]{1,0:T(8,128)}, f32[256,512]{1,0:T(8,128)S(1)}, u32[]{:S(2)}) copy-start(f32[256,512]{1,0:T(8,128)S(1)} %fusion.24) | copy-start | bytes 1572868
  405.8 218.8 %copy-start.4 = (bf16[256,3072]{0,1:T(8,128)(2,1)S(1)}, bf16[256,3072]{0,1:T(8,128)(2,1)}, u32[]{:S(2)}) copy-start(bf16[256,3072]{0,1:T(8,128)(2,1)} %all-gather.11.cloned.1.call-done) | copy-start | bytes 4718596
  628.4 305.7 %copy-start.1 = (bf16[3072,512]{1,0:T(8,128)(2,1)S(1)}, bf16[3072,512]{1,0:T(8,128)(2,1)}, u32[]{:S(2)}) copy-start(bf16[3072,512]{1,0:T(8,128)(2,1)} %all-gather.13.cloned.1.call-done) | copy-start | bytes 9437188
  946.2 136.3 %copy-start.3 = (s32[256]{0:T(256)S(1)}, s32[256]{0:T(256)}, u32[]{:S(2)}) copy-start(s32[256]{0:T(256)} %param.12) | copy-start | bytes 3076
Sparse Core Ops, SparseCore 0:
  10.7 89.5 all-gather.14
  102.3 216.8 all-gather.16
  322.5 83.2 all-gather.10
  407.8 216.8 all-gather.12
  627.8 83.2 all-gather.6
  713.0 216.8 all-gather.8
  946.3 136.1 reduce-scatter.3
where the time goes:
time: 1090 us
  waiting for transfers between devices  1040 us (95%)
  matrix products  34.8 us (3%)
  between operations  13.5 us (1%)
    all_gather x1, waiting for transfers between devices, body(): lax.all_gather(gate_weight, 'dp', axis=0, tiled=True)  219 us
    all_gather x1, waiting for transfers between devices, body(): down_full = lax.all_gather(down_weight, 'dp', axis=1, tiled=True)  219 us
    all_gather x1, waiting for transfers between devices, body(): lax.all_gather(up_weight, 'dp', axis=0, tiled=True)  215 us
    unnamed x8, waiting for transfers between devices  138 us
    all_gather x1, waiting for transfers between devices, body(): lax.all_gather(select(tokens), 'tensor', axis=1, tiled=True)  84.5 us
    all_gather x1, waiting for transfers between devices, body(): lax.all_gather(select(tangent), 'tensor', axis=1, tiled=True)  83.2 us
    all_gather x1, waiting for transfers between devices, body(): lax.all_gather(select(cotangent), 'tensor', axis=1, tiled=True)  82.7 us
  transfers between devices with their start and end apart: 7, of which 7 were waited for; matrix products, arithmetic and copies ran while one was open for 1% of the time, Pallas kernels for 0%

commit v1 on v0

v1 whole, which is shorter than its diff:
```python
import jax
import jax.numpy as jnp
import numpy as np
from jax import lax
from jax.sharding import Mesh
from jax.sharding import PartitionSpec as P

BF = jnp.bfloat16
F32 = jnp.float32
NZ, NX, NH, NY, NC = 8, 4, 2, 4, 2
RING = (0, 2, 4, 6, 7, 5, 3, 1)


def shift(axis, order, step):
    n = len(order)
    pairs = [(order[i], order[(i + step) % n]) for i in range(n)]
    return lambda v: lax.ppermute(v, axis, pairs)


ring_up, ring_down = shift("zl", RING, 1), shift("zl", RING, -1)
x_up, x_down, x_far = (shift("x", range(NX), s) for s in (1, -1, 2))
y_up, y_down, y_far = (shift("y", range(NY), s) for s in (1, -1, 2))
other_half = shift("zh", range(NH), 1)
other_core = shift("c", range(NC), 1)


def take(v, i, axis=0):
    return lax.dynamic_index_in_dim(v, i, axis, keepdims=False)


def body(tokens, tangent, cotangent, gates, slot_tokens, gate_weight, up_weight, down_weight):
    zl, x, zh, y, c = (lax.axis_index(a) for a in ("zl", "x", "zh", "y", "c"))
    place = take(jnp.asarray(np.argsort(RING), jnp.int32), zl)
    ring = jnp.asarray(RING, jnp.int32)

    own = jnp.concatenate([gate_weight, up_weight, down_weight.T], axis=1)
    rows, width = own.shape
    half = rows // 2
    blocks = [(own[None], 0)]
    ups, downs = own, own
    rounds = [[(own, zl)]]
    for k in (1, 2, 3):
        ups, downs = ring_up(ups), ring_down(downs)
        rounds.append([(ups, take(ring, (place - k) % NZ)), (downs, take(ring, (place + k) % NZ))])
    last = jnp.concatenate([ring_up(ups[:half]), ring_down(downs[half:])], axis=0)
    rounds.append([(last, take(ring, (place + 4) % NZ))])

    fields = jnp.concatenate([tokens.T, tangent.T, cotangent.T], axis=1)
    feat, cols = fields.shape
    pair = jnp.stack([fields, other_half(fields)])
    pair = jnp.stack([take(pair, zh), take(pair, 1 - zh)])
    quad = jnp.zeros((NH, NY, feat, cols), BF)
    for part, src in ((pair, y), (y_up(pair), y - 1), (y_down(pair), y + 1), (y_far(pair), y + 2)):
        quad = lax.dynamic_update_slice(quad, part[:, None], (0, src % NY, 0, 0))
    across = other_core(quad)
    fields = jnp.zeros((NH, NY, NC, feat, cols), BF)
    fields = lax.dynamic_update_slice(fields, quad[:, :, None], (0, 0, c, 0, 0))
    fields = lax.dynamic_update_slice(fields, across[:, :, None], (0, 0, 1 - c, 0, 0))
    fields = fields.reshape(NH * NY * NC * feat, cols)

    full = jnp.zeros((NZ, NX, rows, width), BF)
    for group in rounds:
        for block, src in group:
            for part, at in ((block, x), (x_up(block), x - 1), (x_down(block), x + 1), (x_far(block), x + 2)):
                full = lax.dynamic_update_slice(full, part[None, None], (src, at % NX, 0, 0))
    full = full.reshape(NZ * NX * rows, width)

    n_tok = tokens.shape[0]
    ff = gate_weight.shape[1]
    both = full[:, : 2 * ff]
    pre = lax.dot_general(
        fields[:, : 2 * n_tok], both, (((0,), (0,)), ((), ())), preferred_element_type=F32
    )
    back = lax.dot_general(
        fields[:, 2 * n_tok :], full[:, 2 * ff :], (((0,), (0,)), ((), ())), preferred_element_type=F32
    )
    gate_pre, up_pre = pre[:n_tok, :ff], pre[:n_tok, ff:]
    gate_tan, up_tan = pre[n_tok:, :ff], pre[n_tok:, ff:]
    held = slot_tokens[:, None] == lax.broadcasted_iota(jnp.int32, (slot_tokens.shape[0], n_tok), 1)
    gate = jnp.where(jnp.any(held, axis=0), gates, 0.0)
    back = gate[:, None] * back
    squash = jax.nn.sigmoid(gate_pre)
    first = squash * (1.0 + gate_pre * (1.0 - squash))
    second = squash * (1.0 - squash) * (2.0 + gate_pre * (1.0 - 2.0 * squash))
    gate_dir = (back * (up_tan * first + up_pre * second * gate_tan)).astype(BF)
    up_dir = (back * first * gate_tan).astype(BF)
    dirs = jnp.concatenate([gate_dir, up_dir], axis=1)
    sums = lax.dot_general(both, dirs, (((1,), (1,)), ((), ())), preferred_element_type=F32)

    sums = sums.reshape(NH, NY, NC, feat, n_tok)
    sums = take(sums, c, 2) + other_core(take(sums, 1 - c, 2))

    def to(step):
        return take(sums, (y + step) % NY, 1)

    kept = to(0) + y_up(to(1).astype(BF)).astype(F32) + y_down(to(-1).astype(BF)).astype(F32)
    kept = kept + y_far(to(2).astype(BF)).astype(F32)
    out = take(kept, zh) + other_half(take(kept, 1 - zh).astype(BF)).astype(F32)
    return out.T.astype(BF)


def solution(mesh):
    fine = Mesh(mesh.devices.reshape(NZ, NX, NH, NY, NC), ("zl", "x", "zh", "y", "c"))
    dp, tensor = ("zl", "x"), ("zh", "y", "c")
    tok = P(dp, tensor)
    in_specs = (tok, tok, tok, P(dp), P(dp), tok, tok, P(tensor, dp))
    return jax.shard_map(body, mesh=fine, in_specs=in_specs, out_specs=tok, check_vma=False)
```

time: 1090 us -> 294 us (0.27)
  the two profiles are of different devices: /device:TPU:2 before, /device:TPU:38 now
where the time goes in v1:
time: 294 us; the launch traced here: 292 us
  starting transfers between devices  167 us (57%)
  waiting for transfers between devices  58.8 us (20%)
  local copies, waits for them, and re-layouts  30.9 us (11%)
  between operations  18.5 us (6%)
  matrix products  13.3 us (5%)
  other arithmetic  4.33 us (1%)
    ppermute x42, starting transfers between devices, shift(): return lambda v: lax.ppermute(v, axis, pairs)  167 us
    ppermute x42, waiting for transfers between devices, shift(): return lambda v: lax.ppermute(v, axis, pairs)  58.8 us
    dynamic_update_slice x31, local copies, waits for them, and re-layouts, body(): lax.dynamic_update_slice(full, part[None, None], (src, at % NX, 0, 0))  23 us
  transfers between devices with their start and end apart: 42, of which 17 were waited for; matrix products, arithmetic and copies ran while one was open for 11% of the time, Pallas kernels for 0%

profile of v1, /device:TPU:38, one launch (start us, length us, event | category | flops | bytes accessed | tf_op | source)
XLA Modules:
  0.0 292.5 jit_solution(960520104600108759)
XLA Ops:
  1.2 2.4 collective-permute-start
  3.5 3.5 %collective-permute-start.1 = (bf16[96,1536]{1,0:T(8,128)(2,1)S(1)}, bf16[96,1536]{1,0:T(8,128)(2,1)S(1)}, u32[]{:S(2)}, u32[]{:S(2)}) collective-permute-start(bf16[96,1536]{1,0:T(8,128)(2,1)S(1)} %pad_maximum_fusion.1), channel_id=1, source_target_pairs={{0,48},{16,0},{32,16},{48,32},{1,49},{17,1},{33,17},{49,33},{2,50}... | collective-permute-start | bytes 884744 | tf_op jit(solution)/shard_map/ppermute | solution.py:17
  7.0 3.3 %collective-permute-start.2 = (bf16[96,1536]{1,0:T(8,128)(2,1)S(1)}, bf16[96,1536]{1,0:T(8,128)(2,1)S(1)}, u32[]{:S(2)}, u32[]{:S(2)}) collective-permute-start(bf16[96,1536]{1,0:T(8,128)(2,1)S(1)} %pad_maximum_fusion.1), channel_id=1, source_target_pairs={{0,32},{16,48},{32,0},{48,16},{1,33},{17,49},{33,1},{49,17},{2,34}... | collective-permute-start | bytes 884744 | tf_op jit(solution)/shard_map/ppermute | solution.py:17
  10.3 5.9 %collective-permute-start.3 = (bf16[96,1536]{1,0:T(8,128)(2,1)S(1)}, bf16[96,1536]{1,0:T(8,128)(2,1)S(1)}, u32[]{:S(2)}, u32[]{:S(2)}) collective-permute-start(bf16[96,1536]{1,0:T(8,128)(2,1)S(1)} %pad_maximum_fusion.1), channel_id=1, source_target_pairs={{0,128},{128,256},{256,384},{384,448},{448,320},{320,192},{192,64}... | collective-permute-start | bytes 884744 | tf_op jit(solution)/shard_map/ppermute | solution.py:17
  17.3 11.9 %collective-permute-start.32 = (bf16[192,768]{1,0:T(8,128)(2,1)S(1)}, bf16[192,768]{1,0:T(8,128)(2,1)S(1)}, u32[]{:S(2)}, u32[]{:S(2)}) collective-permute-start(bf16[192,768]{1,0:T(8,128)(2,1)S(1)} %get-tuple-element.14), channel_id=1, source_target_pairs={{0,8},{8,0},{1,9},{9,1},{2,10},{10,2},{3,11},{11,3},{4,12},{12,4},... | collective-permute-start | bytes 884744 | tf_op jit(solution)/shard_map/ppermute | solution.py:17
  29.1 4.7 %broadcast_in_dim.129 = bf16[8,4,96,1536]{3,2,1,0:T(8,128)(2,1)} broadcast(bf16[]{:T(256)} %constant.225.clone.1), dimensions={} | broadcast | bytes 9437186 | tf_op jit(solution)/shard_map/broadcast_in_dim | solution.py:61
  53.9 3.8 %collective-permute-start.7 = (bf16[96,1536]{1,0:T(8,128)(2,1)S(1)}, bf16[96,1536]{1,0:T(8,128)(2,1)S(1)}, u32[]{:S(2)}, u32[]{:S(2)}) collective-permute-start(bf16[96,1536]{1,0:T(8,128)(2,1)S(1)} %pad_maximum_fusion.1), channel_id=1, source_target_pairs={{0,64},{128,0},{256,128},{384,256},{448,384},{320,448},{192,320},{... | collective-permute-start | bytes 884744 | tf_op jit(solution)/shard_map/ppermute | solution.py:17
  58.0 3.5 %collective-permute-start.33 = (bf16[2,192,768]{2,1,0:T(8,128)(2,1)S(1)}, bf16[2,192,768]{2,1,0:T(8,128)(2,1)S(1)}, u32[]{:S(2)}, u32[]{:S(2)}) collective-permute-start(bf16[2,192,768]{2,1,0:T(8,128)(2,1)S(1)} %pad_maximum_fusion), channel_id=1, source_target_pairs={{0,2},{2,4},{4,6},{6,0},{1,3},{3,5},{5,7},{7,1},{8,10},{10,12},{12... | collective-permute-start | bytes 1769480 | tf_op jit(solution)/shard_map/ppermute | solution.py:17
  62.2 3.6 %collective-permute-start.34 = (bf16[2,192,768]{2,1,0:T(8,128)(2,1)S(1)}, bf16[2,192,768]{2,1,0:T(8,128)(2,1)S(1)}, u32[]{:S(2)}, u32[]{:S(2)}) collective-permute-start(bf16[2,192,768]{2,1,0:T(8,128)(2,1)S(1)} %pad_maximum_fusion), channel_id=1, source_target_pairs={{0,6},{2,0},{4,2},{6,4},{1,7},{3,1},{5,3},{7,5},{8,14},{10,8},{12,... | collective-permute-start | bytes 1769480 | tf_op jit(solution)/shard_map/ppermute | solution.py:17
  66.6 3.9 %collective-permute-start.35 = (bf16[2,192,768]{2,1,0:T(8,128)(2,1)S(1)}, bf16[2,192,768]{2,1,0:T(8,128)(2,1)S(1)}, u32[]{:S(2)}, u32[]{:S(2)}) collective-permute-start(bf16[2,192,768]{2,1,0:T(8,128)(2,1)S(1)} %pad_maximum_fusion), channel_id=1, source_target_pairs={{0,4},{2,6},{4,0},{6,2},{1,5},{3,7},{5,1},{7,3},{8,12},{10,14},{12... | collective-permute-start | bytes 1769480 | tf_op jit(solution)/shard_map/ppermute | solution.py:17
  70.5 4.0 %collective-permute-start.4 = (bf16[96,1536]{1,0:T(8,128)(2,1)S(1)}, bf16[96,1536]{1,0:T(8,128)(2,1)S(1)}, u32[]{:S(2)}, u32[]{:S(2)}) collective-permute-start(bf16[96,1536]{1,0:T(8,128)(2,1)S(1)} %collective-permute-done.3), channel_id=1, source_target_pairs={{0,16},{16,32},{32,48},{48,0},{1,17},{17,33},{33,49},{49,1},{2,18}... | collective-permute-start | bytes 884744 | tf_op jit(solution)/shard_map/ppermute | solution.py:17
  76.2 2.9 collective-permute-done.4
  79.1 3.1 %collective-permute-start.5 = (bf16[96,1536]{1,0:T(8,128)(2,1)S(1)}, bf16[96,1536]{1,0:T(8,128)(2,1)S(1)}, u32[]{:S(2)}, u32[]{:S(2)}) collective-permute-start(bf16[96,1536]{1,0:T(8,128)(2,1)S(1)} %collective-permute-done.3), channel_id=1, source_target_pairs={{0,48},{16,0},{32,16},{48,32},{1,49},{17,1},{33,17},{49,33},{2,50}... | collective-permute-start | bytes 884744 | tf_op jit(solution)/shard_map/ppermute | solution.py:17
  82.9 5.5 %collective-permute-start.6 = (bf16[96,1536]{1,0:T(8,128)(2,1)S(1)}, bf16[96,1536]{1,0:T(8,128)(2,1)S(1)}, u32[]{:S(2)}, u32[]{:S(2)}) collective-permute-start(bf16[96,1536]{1,0:T(8,128)(2,1)S(1)} %collective-permute-done.3), channel_id=1, source_target_pairs={{0,32},{16,48},{32,0},{48,16},{1,33},{17,49},{33,1},{49,17},{2,34}... | collective-permute-start | bytes 884744 | tf_op jit(solution)/shard_map/ppermute | solution.py:17
  88.5 3.5 %collective-permute-done.5 = bf16[96,1536]{1,0:T(8,128)(2,1)S(1)} collective-permute-done((bf16[96,1536]{1,0:T(8,128)(2,1)S(1)}, bf16[96,1536]{1,0:T(8,128)(2,1)S(1)}, u32[]{:S(2)}, u32[]{:S(2)}) %collective-permute-start.5) | collective-permute-done | bytes 294944 | tf_op jit(solution)/shard_map/ppermute | solution.py:17
  92.0 2.5 collective-permute-start.8
  95.2 3.3 %collective-permute-start.9 = (bf16[96,1536]{1,0:T(8,128)(2,1)S(1)}, bf16[96,1536]{1,0:T(8,128)(2,1)S(1)}, u32[]{:S(2)}, u32[]{:S(2)}) collective-permute-start(bf16[96,1536]{1,0:T(8,128)(2,1)S(1)} %collective-permute-done.7), channel_id=1, source_target_pairs={{0,48},{16,0},{32,16},{48,32},{1,49},{17,1},{33,17},{49,33},{2,50}... | collective-permute-start | bytes 884744 | tf_op jit(solution)/shard_map/ppermute | solution.py:17
  100.6 4.3 %collective-permute-start.10 = (bf16[96,1536]{1,0:T(8,128)(2,1)S(1)}, bf16[96,1536]{1,0:T(8,128)(2,1)S(1)}, u32[]{:S(2)}, u32[]{:S(2)}) collective-permute-start(bf16[96,1536]{1,0:T(8,128)(2,1)S(1)} %collective-permute-done.7), channel_id=1, source_target_pairs={{0,32},{16,48},{32,0},{48,16},{1,33},{17,49},{33,1},{49,17},{2,34}... | collective-permute-start | bytes 884744 | tf_op jit(solution)/shard_map/ppermute | solution.py:17
  110.7 4.8 %collective-permute-start.15 = (bf16[96,1536]{1,0:T(8,128)(2,1)S(1)}, bf16[96,1536]{1,0:T(8,128)(2,1)S(1)}, u32[]{:S(2)}, u32[]{:S(2)}) collective-permute-start(bf16[96,1536]{1,0:T(8,128)(2,1)S(1)} %collective-permute-done.7), channel_id=1, source_target_pairs={{0,64},{128,0},{256,128},{384,256},{448,384},{320,448},{192,320},{... | collective-permute-start | bytes 884744 | tf_op jit(solution)/shard_map/ppermute | solution.py:17
  115.5 4.8 %collective-permute-done.11 = bf16[96,1536]{1,0:T(8,128)(2,1)S(1)} collective-permute-done((bf16[96,1536]{1,0:T(8,128)(2,1)S(1)}, bf16[96,1536]{1,0:T(8,128)(2,1)S(1)}, u32[]{:S(2)}, u32[]{:S(2)}) %collective-permute-start.11) | collective-permute-done | bytes 294944 | tf_op jit(solution)/shard_map/ppermute | solution.py:17
  123.7 5.2 %collective-permute-done.12 = bf16[96,1536]{1,0:T(8,128)(2,1)S(1)} collective-permute-done((bf16[96,1536]{1,0:T(8,128)(2,1)S(1)}, bf16[96,1536]{1,0:T(8,128)(2,1)S(1)}, u32[]{:S(2)}, u32[]{:S(2)}) %collective-permute-start.12) | collective-permute-done | bytes 294944 | tf_op jit(solution)/shard_map/ppermute | solution.py:17
  128.9 3.9 %collective-permute-start.13 = (bf16[96,1536]{1,0:T(8,128)(2,1)S(1)}, bf16[96,1536]{1,0:T(8,128)(2,1)S(1)}, u32[]{:S(2)}, u32[]{:S(2)}) collective-permute-start(bf16[96,1536]{1,0:T(8,128)(2,1)S(1)} %collective-permute-done.11), channel_id=1, source_target_pairs={{0,48},{16,0},{32,16},{48,32},{1,49},{17,1},{33,17},{49,33},{2,50}... | collective-permute-start | bytes 884744 | tf_op jit(solution)/shard_map/ppermute | solution.py:17
  133.6 5.8 %collective-permute-done.13 = bf16[96,1536]{1,0:T(8,128)(2,1)S(1)} collective-permute-done((bf16[96,1536]{1,0:T(8,128)(2,1)S(1)}, bf16[96,1536]{1,0:T(8,128)(2,1)S(1)}, u32[]{:S(2)}, u32[]{:S(2)}) %collective-permute-start.13) | collective-permute-done | bytes 294944 | tf_op jit(solution)/shard_map/ppermute | solution.py:17
  139.4 5.0 %collective-permute-start.14 = (bf16[96,1536]{1,0:T(8,128)(2,1)S(1)}, bf16[96,1536]{1,0:T(8,128)(2,1)S(1)}, u32[]{:S(2)}, u32[]{:S(2)}) collective-permute-start(bf16[96,1536]{1,0:T(8,128)(2,1)S(1)} %collective-permute-done.11), channel_id=1, source_target_pairs={{0,32},{16,48},{32,0},{48,16},{1,33},{17,49},{33,1},{49,17},{2,34}... | collective-permute-start | bytes 884744 | tf_op jit(solution)/shard_map/ppermute | solution.py:17
  147.0 2.4 collective-permute-done.14
  149.5 2.7 collective-permute-start.16
  153.6 13.7 %collective-permute-start.23 = (bf16[96,1536]{1,0:T(8,128)(2,1)S(1)}, bf16[96,1536]{1,0:T(8,128)(2,1)S(1)}, u32[]{:S(2)}, u32[]{:S(2)}) collective-permute-start(bf16[96,1536]{1,0:T(8,128)(2,1)S(1)} %collective-permute-done.15), channel_id=1, source_target_pairs={{0,64},{128,0},{256,128},{384,256},{448,384},{320,448},{192,320},{... | collective-permute-start | bytes 884744 | tf_op jit(solution)/shard_map/ppermute | solution.py:17
  167.4 2.6 collective-permute-start.17
  170.1 3.8 %collective-permute-start.18 = (bf16[96,1536]{1,0:T(8,128)(2,1)S(1)}, bf16[96,1536]{1,0:T(8,128)(2,1)S(1)}, u32[]{:S(2)}, u32[]{:S(2)}) collective-permute-start(bf16[96,1536]{1,0:T(8,128)(2,1)S(1)} %collective-permute-done.15), channel_id=1, source_target_pairs={{0,32},{16,48},{32,0},{48,16},{1,33},{17,49},{33,1},{49,17},{2,34}... | collective-permute-start | bytes 884744 | tf_op jit(solution)/shard_map/ppermute | solution.py:17
  175.9 4.8 %collective-permute-start.28 = (bf16[48,1536]{1,0:T(8,128)(2,1)S(1)}, bf16[48,1536]{1,0:T(8,128)(2,1)S(1)}, u32[]{:S(2)}, u32[]{:S(2)}) collective-permute-start(bf16[48,1536]{1,0:T(8,128)(2,1)S(1)} %slice.41), channel_id=1, source_target_pairs={{0,64},{128,0},{256,128},{384,256},{448,384},{320,448},{192,320},{... | collective-permute-start | bytes 442376 | tf_op jit(solution)/shard_map/ppermute | solution.py:17
  186.4 3.7 %collective-permute-start.20 = (bf16[96,1536]{1,0:T(8,128)(2,1)S(1)}, bf16[96,1536]{1,0:T(8,128)(2,1)S(1)}, u32[]{:S(2)}, u32[]{:S(2)}) collective-permute-start(bf16[96,1536]{1,0:T(8,128)(2,1)S(1)} %collective-permute-done.19), channel_id=1, source_target_pairs={{0,16},{16,32},{32,48},{48,0},{1,17},{17,33},{33,49},{49,1},{2,18}... | collective-permute-start | bytes 884744 | tf_op jit(solution)/shard_map/ppermute | solution.py:17
  190.0 2.2 collective-permute-start.21
  192.2 3.5 %collective-permute-start.22 = (bf16[96,1536]{1,0:T(8,128)(2,1)S(1)}, bf16[96,1536]{1,0:T(8,128)(2,1)S(1)}, u32[]{:S(2)}, u32[]{:S(2)}) collective-permute-start(bf16[96,1536]{1,0:T(8,128)(2,1)S(1)} %collective-permute-done.19), channel_id=1, source_target_pairs={{0,32},{16,48},{32,0},{48,16},{1,33},{17,49},{33,1},{49,17},{2,34}... | collective-permute-start | bytes 884744 | tf_op jit(solution)/shard_map/ppermute | solution.py:17
  195.8 4.5 %collective-permute-start.24 = (bf16[96,1536]{1,0:T(8,128)(2,1)S(1)}, bf16[96,1536]{1,0:T(8,128)(2,1)S(1)}, u32[]{:S(2)}, u32[]{:S(2)}) collective-permute-start(bf16[96,1536]{1,0:T(8,128)(2,1)S(1)} %collective-permute-done.23), channel_id=1, source_target_pairs={{0,16},{16,32},{32,48},{48,0},{1,17},{17,33},{33,49},{49,1},{2,18}... | collective-permute-start | bytes 884744 | tf_op jit(solution)/shard_map/ppermute | solution.py:17
  203.0 6.3 %collective-permute-done.21 = bf16[96,1536]{1,0:T(8,128)(2,1)S(1)} collective-permute-done((bf16[96,1536]{1,0:T(8,128)(2,1)S(1)}, bf16[96,1536]{1,0:T(8,128)(2,1)S(1)}, u32[]{:S(2)}, u32[]{:S(2)}) %collective-permute-start.21) | collective-permute-done | bytes 294944 | tf_op jit(solution)/shard_map/ppermute | solution.py:17
  215.4 3.9 %collective-permute-start.30 = (bf16[96,1536]{1,0:T(8,128)(2,1)S(1)}, bf16[96,1536]{1,0:T(8,128)(2,1)S(1)}, u32[]{:S(2)}, u32[]{:S(2)}) collective-permute-start(bf16[96,1536]{1,0:T(8,128)(2,1)S(1)} %constant_dynamic-update-slice_fusion), channel_id=1, source_target_pairs={{0,48},{16,0},{32,16},{48,32},{1,49},{17,1},{33,17},{49,33},{2,50}... | collective-permute-start | bytes 884744 | tf_op jit(solution)/shard_map/ppermute | solution.py:17
  221.9 3.7 %collective-permute-start.31 = (bf16[96,1536]{1,0:T(8,128)(2,1)S(1)}, bf16[96,1536]{1,0:T(8,128)(2,1)S(1)}, u32[]{:S(2)}, u32[]{:S(2)}) collective-permute-start(bf16[96,1536]{1,0:T(8,128)(2,1)S(1)} %constant_dynamic-update-slice_fusion), channel_id=1, source_target_pairs={{0,32},{16,48},{32,0},{48,16},{1,33},{17,49},{33,1},{49,17},{2,34}... | collective-permute-start | bytes 884744 | tf_op jit(solution)/shard_map/ppermute | solution.py:17
  229.4 4.6 %collective-permute-done.31 = bf16[96,1536]{1,0:T(8,128)(2,1)S(1)} collective-permute-done((bf16[96,1536]{1,0:T(8,128)(2,1)S(1)}, bf16[96,1536]{1,0:T(8,128)(2,1)S(1)}, u32[]{:S(2)}, u32[]{:S(2)}) %collective-permute-start.31) | collective-permute-done | bytes 294944 | tf_op jit(solution)/shard_map/ppermute | solution.py:17
  235.0 5.6 %fusion.2 = f32[512,1024]{1,0:T(8,128)S(1)} fusion(bf16[3072,1536]{1,0:T(8,128)(2,1)} %bitcast.47, bf16[3072,768]{1,0:T(8,128)(2,1)S(1)} %bitcast.135), kind=kOutput, calls=%fused_computation.2 | convolution fusion | flops 3221225472 | bytes 11534336 | tf_op jit(solution)/shard_map/dot_general | solution.py:71
  240.6 3.2 %fusion.20 = (bf16[256,512]{1,0:T(8,128)(2,1)S(1)}, bf16[256,512]{1,0:T(8,128)(2,1)S(1)}) fusion(f32[512,1024]{1,0:T(8,128)S(1)} %fusion.2, bf16[3072,1536]{1,0:T(8,128)(2,1)} %bitcast.47, bf16[3072,768]{1,0:T(8,128)(2,1)S(1)} %bitcast.136, f32[256]{0:T(256)S(1)} %broadcast_select_fusion), kind=kOutput, calls=%fused_computation.31 | convolution fusion | flops 808321024 | bytes 7341056 | tf_op jit(solution)/shard_map/dot_general | solution.py:74
  243.8 4.6 %fusion = f32[3072,256]{1,0:T(8,128)S(1)} fusion(bf16[3072,1536]{1,0:T(8,128)(2,1)} %bitcast.47, bf16[256,512]{1,0:T(8,128)(2,1)S(1)} %get-tuple-element.8, bf16[256,512]{1,0:T(8,128)(2,1)S(1)} %get-tuple-element.7), kind=kOutput, calls=%fused_computation | convolution fusion | flops 1611661312 | bytes 9961472 | tf_op jit(solution)/shard_map/dot_general | solution.py:88
  250.8 3.4 %collective-permute-done.37 = f32[2,4,192,256]{3,2,0,1:T(8,128)S(1)} collective-permute-done((f32[2,4,192,256]{3,2,0,1:T(8,128)S(1)}, f32[2,4,192,256]{3,2,0,1:T(8,128)S(1)}, u32[]{:S(2)}, u32[]{:S(2)}) %collective-permute-start.37) | collective-permute-done | bytes 1572896 | tf_op jit(solution)/shard_map/ppermute | solution.py:17
  254.5 2.9 %collective-permute-start.38 = (bf16[2,192,256]{2,1,0:T(8,128)(2,1)S(1)}, bf16[2,192,256]{2,1,0:T(8,128)(2,1)S(1)}, u32[]{:S(2)}, u32[]{:S(2)}) collective-permute-start(bf16[2,192,256]{2,1,0:T(8,128)(2,1)S(1)} %get-tuple-element.9), channel_id=1, source_target_pairs={{0,2},{2,4},{4,6},{6,0},{1,3},{3,5},{5,7},{7,1},{8,10},{10,12},{12... | collective-permute-start | bytes 589832 | tf_op jit(solution)/shard_map/ppermute | solution.py:17
  257.4 4.1 %collective-permute-start.39 = (bf16[2,192,256]{2,1,0:T(8,128)(2,1)S(1)}, bf16[2,192,256]{2,1,0:T(8,128)(2,1)S(1)}, u32[]{:S(2)}, u32[]{:S(2)}) collective-permute-start(bf16[2,192,256]{2,1,0:T(8,128)(2,1)S(1)} %get-tuple-element.11), channel_id=1, source_target_pairs={{0,6},{2,0},{4,2},{6,4},{1,7},{3,1},{5,3},{7,5},{8,14},{10,8},{12,... | collective-permute-start | bytes 589832 | tf_op jit(solution)/shard_map/ppermute | solution.py:17
  261.5 2.7 collective-permute-start.40
  264.5 5.4 %collective-permute-done.39 = bf16[2,192,256]{2,1,0:T(8,128)(2,1)S(1)} collective-permute-done((bf16[2,192,256]{2,1,0:T(8,128)(2,1)S(1)}, bf16[2,192,256]{2,1,0:T(8,128)(2,1)S(1)}, u32[]{:S(2)}, u32[]{:S(2)}) %collective-permute-start.39) | collective-permute-done | bytes 196640 | tf_op jit(solution)/shard_map/ppermute | solution.py:17
  271.5 12.3 %collective-permute-start.41 = (bf16[192,256]{1,0:T(8,128)(2,1)S(1)}, bf16[192,256]{1,0:T(8,128)(2,1)S(1)}, u32[]{:S(2)}, u32[]{:S(2)}) collective-permute-start(bf16[192,256]{1,0:T(8,128)(2,1)S(1)} %fusion.33), channel_id=1, source_target_pairs={{0,8},{8,0},{1,9},{9,1},{2,10},{10,2},{3,11},{11,3},{4,12},{12,4},... | collective-permute-start | bytes 294920 | tf_op jit(solution)/shard_map/ppermute | solution.py:17
  283.8 8.0 %collective-permute-done.41 = bf16[192,256]{1,0:T(8,128)(2,1)S(1)} collective-permute-done((bf16[192,256]{1,0:T(8,128)(2,1)S(1)}, bf16[192,256]{1,0:T(8,128)(2,1)S(1)}, u32[]{:S(2)}, u32[]{:S(2)}) %collective-permute-start.41) | collective-permute-done | bytes 98336 | tf_op jit(solution)/shard_map/ppermute | solution.py:17
  (113 shorter events, 54.3 us)
Async XLA Ops:
  0.0 34.8 %copy-start.6 = (s32[8]{0:T(128)S(1)}, s32[8]{0:T(128)}, u32[]{:S(2)}) copy-start(s32[8]{0:T(128)} %constant.250.clone) | copy-start | bytes 100
  0.0 40.1 %copy-start.3 = (s32[8]{0:T(128)S(1)}, s32[8]{0:T(128)}, u32[]{:S(2)}) copy-start(s32[8]{0:T(128)} %constant.251.clone) | copy-start | bytes 100
  0.0 33.9 %copy-start = (bf16[512,96]{0,1:T(8,128)(2,1)S(1)}, bf16[512,96]{0,1:T(8,128)(2,1)}, u32[]{:S(2)}) copy-start(bf16[512,96]{0,1:T(8,128)(2,1)} %param.17) | copy-start | bytes 294916
  0.0 33.9 %copy-start.2 = (bf16[96,512]{1,0:T(8,128)(2,1)S(1)}, bf16[96,512]{1,0:T(8,128)(2,1)}, u32[]{:S(2)}) copy-start(bf16[96,512]{1,0:T(8,128)(2,1)} %param.15) | copy-start | bytes 294916
  0.0 34.6 %copy-start.5 = (s32[256]{0:T(256)S(1)}, s32[256]{0:T(256)}, u32[]{:S(2)}) copy-start(s32[256]{0:T(256)} %param.14) | copy-start | bytes 3076
  0.0 34.7 %copy-start.4 = (f32[256]{0:T(256)S(1)}, f32[256]{0:T(256)}, u32[]{:S(2)}) copy-start(f32[256]{0:T(256)} %param.13) | copy-start | bytes 3076
  1.2 56.8 %collective-permute-start = (bf16[96,1536]{1,0:T(8,128)(2,1)S(1)}, bf16[96,1536]{1,0:T(8,128)(2,1)S(1)}, u32[]{:S(2)}, u32[]{:S(2)}) collective-permute-start(bf16[96,1536]{1,0:T(8,128)(2,1)S(1)} %pad_maximum_fusion.1), channel_id=1, source_target_pairs={{0,16},{16,32},{32,48},{48,0},{1,17},{17,33},{33,49},{49,1},{2,18}... | collective-permute-start | bytes 884744 | tf_op jit(solution)/shard_map/ppermute | solution.py:17
  3.5 58.7 %collective-permute-start.1 = (bf16[96,1536]{1,0:T(8,128)(2,1)S(1)}, bf16[96,1536]{1,0:T(8,128)(2,1)S(1)}, u32[]{:S(2)}, u32[]{:S(2)}) collective-permute-start(bf16[96,1536]{1,0:T(8,128)(2,1)S(1)} %pad_maximum_fusion.1), channel_id=1, source_target_pairs={{0,48},{16,0},{32,16},{48,32},{1,49},{17,1},{33,17},{49,33},{2,50}... | collective-permute-start | bytes 884744 | tf_op jit(solution)/shard_map/ppermute | solution.py:17
  7.0 59.6 %collective-permute-start.2 = (bf16[96,1536]{1,0:T(8,128)(2,1)S(1)}, bf16[96,1536]{1,0:T(8,128)(2,1)S(1)}, u32[]{:S(2)}, u32[]{:S(2)}) collective-permute-start(bf16[96,1536]{1,0:T(8,128)(2,1)S(1)} %pad_maximum_fusion.1), channel_id=1, source_target_pairs={{0,32},{16,48},{32,0},{48,16},{1,33},{17,49},{33,1},{49,17},{2,34}... | collective-permute-start | bytes 884744 | tf_op jit(solution)/shard_map/ppermute | solution.py:17
  10.3 60.1 %collective-permute-start.3 = (bf16[96,1536]{1,0:T(8,128)(2,1)S(1)}, bf16[96,1536]{1,0:T(8,128)(2,1)S(1)}, u32[]{:S(2)}, u32[]{:S(2)}) collective-permute-start(bf16[96,1536]{1,0:T(8,128)(2,1)S(1)} %pad_maximum_fusion.1), channel_id=1, source_target_pairs={{0,128},{128,256},{256,384},{384,448},{448,320},{320,192},{192,64}... | collective-permute-start | bytes 884744 | tf_op jit(solution)/shard_map/ppermute | solution.py:17
  17.3 36.6 %collective-permute-start.32 = (bf16[192,768]{1,0:T(8,128)(2,1)S(1)}, bf16[192,768]{1,0:T(8,128)(2,1)S(1)}, u32[]{:S(2)}, u32[]{:S(2)}) collective-permute-start(bf16[192,768]{1,0:T(8,128)(2,1)S(1)} %get-tuple-element.14), channel_id=1, source_target_pairs={{0,8},{8,0},{1,9},{9,1},{2,10},{10,2},{3,11},{11,3},{4,12},{12,4},... | collective-permute-start | bytes 884744 | tf_op jit(solution)/shard_map/ppermute | solution.py:17
  53.9 29.0 %collective-permute-start.7 = (bf16[96,1536]{1,0:T(8,128)(2,1)S(1)}, bf16[96,1536]{1,0:T(8,128)(2,1)S(1)}, u32[]{:S(2)}, u32[]{:S(2)}) collective-permute-start(bf16[96,1536]{1,0:T(8,128)(2,1)S(1)} %pad_maximum_fusion.1), channel_id=1, source_target_pairs={{0,64},{128,0},{256,128},{384,256},{448,384},{320,448},{192,320},{... | collective-permute-start | bytes 884744 | tf_op jit(solution)/shard_map/ppermute | solution.py:17
  58.0 95.6 %collective-permute-start.33 = (bf16[2,192,768]{2,1,0:T(8,128)(2,1)S(1)}, bf16[2,192,768]{2,1,0:T(8,128)(2,1)S(1)}, u32[]{:S(2)}, u32[]{:S(2)}) collective-permute-start(bf16[2,192,768]{2,1,0:T(8,128)(2,1)S(1)} %pad_maximum_fusion), channel_id=1, source_target_pairs={{0,2},{2,4},{4,6},{6,0},{1,3},{3,5},{5,7},{7,1},{8,10},{10,12},{12... | collective-permute-start | bytes 1769480 | tf_op jit(solution)/shard_map/ppermute | solution.py:17
  62.2 105.2 %collective-permute-start.34 = (bf16[2,192,768]{2,1,0:T(8,128)(2,1)S(1)}, bf16[2,192,768]{2,1,0:T(8,128)(2,1)S(1)}, u32[]{:S(2)}, u32[]{:S(2)}) collective-permute-start(bf16[2,192,768]{2,1,0:T(8,128)(2,1)S(1)} %pad_maximum_fusion), channel_id=1, source_target_pairs={{0,6},{2,0},{4,2},{6,4},{1,7},{3,1},{5,3},{7,5},{8,14},{10,8},{12,... | collective-permute-start | bytes 1769480 | tf_op jit(solution)/shard_map/ppermute | solution.py:17
  66.6 109.3 %collective-permute-start.35 = (bf16[2,192,768]{2,1,0:T(8,128)(2,1)S(1)}, bf16[2,192,768]{2,1,0:T(8,128)(2,1)S(1)}, u32[]{:S(2)}, u32[]{:S(2)}) collective-permute-start(bf16[2,192,768]{2,1,0:T(8,128)(2,1)S(1)} %pad_maximum_fusion), channel_id=1, source_target_pairs={{0,4},{2,6},{4,0},{6,2},{1,5},{3,7},{5,1},{7,3},{8,12},{10,14},{12... | collective-permute-start | bytes 1769480 | tf_op jit(solution)/shard_map/ppermute | solution.py:17
  70.5 8.6 %collective-permute-start.4 = (bf16[96,1536]{1,0:T(8,128)(2,1)S(1)}, bf16[96,1536]{1,0:T(8,128)(2,1)S(1)}, u32[]{:S(2)}, u32[]{:S(2)}) collective-permute-start(bf16[96,1536]{1,0:T(8,128)(2,1)S(1)} %collective-permute-done.3), channel_id=1, source_target_pairs={{0,16},{16,32},{32,48},{48,0},{1,17},{17,33},{33,49},{49,1},{2,18}... | collective-permute-start | bytes 884744 | tf_op jit(solution)/shard_map/ppermute | solution.py:17
  79.1 12.9 %collective-permute-start.5 = (bf16[96,1536]{1,0:T(8,128)(2,1)S(1)}, bf16[96,1536]{1,0:T(8,128)(2,1)S(1)}, u32[]{:S(2)}, u32[]{:S(2)}) collective-permute-start(bf16[96,1536]{1,0:T(8,128)(2,1)S(1)} %collective-permute-done.3), channel_id=1, source_target_pairs={{0,48},{16,0},{32,16},{48,32},{1,49},{17,1},{33,17},{49,33},{2,50}... | collective-permute-start | bytes 884744 | tf_op jit(solution)/shard_map/ppermute | solution.py:17
  82.9 12.3 %collective-permute-start.6 = (bf16[96,1536]{1,0:T(8,128)(2,1)S(1)}, bf16[96,1536]{1,0:T(8,128)(2,1)S(1)}, u32[]{:S(2)}, u32[]{:S(2)}) collective-permute-start(bf16[96,1536]{1,0:T(8,128)(2,1)S(1)} %collective-permute-done.3), channel_id=1, source_target_pairs={{0,32},{16,48},{32,0},{48,16},{1,33},{17,49},{33,1},{49,17},{2,34}... | collective-permute-start | bytes 884744 | tf_op jit(solution)/shard_map/ppermute | solution.py:17
  92.0 8.6 %collective-permute-start.8 = (bf16[96,1536]{1,0:T(8,128)(2,1)S(1)}, bf16[96,1536]{1,0:T(8,128)(2,1)S(1)}, u32[]{:S(2)}, u32[]{:S(2)}) collective-permute-start(bf16[96,1536]{1,0:T(8,128)(2,1)S(1)} %collective-permute-done.7), channel_id=1, source_target_pairs={{0,16},{16,32},{32,48},{48,0},{1,17},{17,33},{33,49},{49,1},{2,18}... | collective-permute-start | bytes 884744 | tf_op jit(solution)/shard_map/ppermute | solution.py:17
  95.2 12.3 %collective-permute-start.9 = (bf16[96,1536]{1,0:T(8,128)(2,1)S(1)}, bf16[96,1536]{1,0:T(8,128)(2,1)S(1)}, u32[]{:S(2)}, u32[]{:S(2)}) collective-permute-start(bf16[96,1536]{1,0:T(8,128)(2,1)S(1)} %collective-permute-done.7), channel_id=1, source_target_pairs={{0,48},{16,0},{32,16},{48,32},{1,49},{17,1},{33,17},{49,33},{2,50}... | collective-permute-start | bytes 884744 | tf_op jit(solution)/shard_map/ppermute | solution.py:17
  100.6 10.1 %collective-permute-start.10 = (bf16[96,1536]{1,0:T(8,128)(2,1)S(1)}, bf16[96,1536]{1,0:T(8,128)(2,1)S(1)}, u32[]{:S(2)}, u32[]{:S(2)}) collective-permute-start(bf16[96,1536]{1,0:T(8,128)(2,1)S(1)} %collective-permute-done.7), channel_id=1, source_target_pairs={{0,32},{16,48},{32,0},{48,16},{1,33},{17,49},{33,1},{49,17},{2,34}... | collective-permute-start | bytes 884744 | tf_op jit(solution)/shard_map/ppermute | solution.py:17
  107.6 12.8 %collective-permute-start.11 = (bf16[96,1536]{1,0:T(8,128)(2,1)S(1)}, bf16[96,1536]{1,0:T(8,128)(2,1)S(1)}, u32[]{:S(2)}, u32[]{:S(2)}) collective-permute-start(bf16[96,1536]{1,0:T(8,128)(2,1)S(1)} %collective-permute-done.3), channel_id=1, source_target_pairs={{0,128},{128,256},{256,384},{384,448},{448,320},{320,192},{192,64}... | collective-permute-start | bytes 884744 | tf_op jit(solution)/shard_map/ppermute | solution.py:17
  110.7 34.4 %collective-permute-start.15 = (bf16[96,1536]{1,0:T(8,128)(2,1)S(1)}, bf16[96,1536]{1,0:T(8,128)(2,1)S(1)}, u32[]{:S(2)}, u32[]{:S(2)}) collective-permute-start(bf16[96,1536]{1,0:T(8,128)(2,1)S(1)} %collective-permute-done.7), channel_id=1, source_target_pairs={{0,64},{128,0},{256,128},{384,256},{448,384},{320,448},{192,320},{... | collective-permute-start | bytes 884744 | tf_op jit(solution)/shard_map/ppermute | solution.py:17
  120.3 8.6 %collective-permute-start.12 = (bf16[96,1536]{1,0:T(8,128)(2,1)S(1)}, bf16[96,1536]{1,0:T(8,128)(2,1)S(1)}, u32[]{:S(2)}, u32[]{:S(2)}) collective-permute-start(bf16[96,1536]{1,0:T(8,128)(2,1)S(1)} %collective-permute-done.11), channel_id=1, source_target_pairs={{0,16},{16,32},{32,48},{48,0},{1,17},{17,33},{33,49},{49,1},{2,18}... | collective-permute-start | bytes 884744 | tf_op jit(solution)/shard_map/ppermute | solution.py:17
  128.9 10.4 %collective-permute-start.13 = (bf16[96,1536]{1,0:T(8,128)(2,1)S(1)}, bf16[96,1536]{1,0:T(8,128)(2,1)S(1)}, u32[]{:S(2)}, u32[]{:S(2)}) collective-permute-start(bf16[96,1536]{1,0:T(8,128)(2,1)S(1)} %collective-permute-done.11), channel_id=1, source_target_pairs={{0,48},{16,0},{32,16},{48,32},{1,49},{17,1},{33,17},{49,33},{2,50}... | collective-permute-start | bytes 884744 | tf_op jit(solution)/shard_map/ppermute | solution.py:17
  139.4 10.1 %collective-permute-start.14 = (bf16[96,1536]{1,0:T(8,128)(2,1)S(1)}, bf16[96,1536]{1,0:T(8,128)(2,1)S(1)}, u32[]{:S(2)}, u32[]{:S(2)}) collective-permute-start(bf16[96,1536]{1,0:T(8,128)(2,1)S(1)} %collective-permute-done.11), channel_id=1, source_target_pairs={{0,32},{16,48},{32,0},{48,16},{1,33},{17,49},{33,1},{49,17},{2,34}... | collective-permute-start | bytes 884744 | tf_op jit(solution)/shard_map/ppermute | solution.py:17
  145.1 24.9 %collective-permute-start.19 = (bf16[96,1536]{1,0:T(8,128)(2,1)S(1)}, bf16[96,1536]{1,0:T(8,128)(2,1)S(1)}, u32[]{:S(2)}, u32[]{:S(2)}) collective-permute-start(bf16[96,1536]{1,0:T(8,128)(2,1)S(1)} %collective-permute-done.11), channel_id=1, source_target_pairs={{0,128},{128,256},{256,384},{384,448},{448,320},{320,192},{192,64}... | collective-permute-start | bytes 884744 | tf_op jit(solution)/shard_map/ppermute | solution.py:17
  149.5 31.3 %collective-permute-start.16 = (bf16[96,1536]{1,0:T(8,128)(2,1)S(1)}, bf16[96,1536]{1,0:T(8,128)(2,1)S(1)}, u32[]{:S(2)}, u32[]{:S(2)}) collective-permute-start(bf16[96,1536]{1,0:T(8,128)(2,1)S(1)} %collective-permute-done.15), channel_id=1, source_target_pairs={{0,16},{16,32},{32,48},{48,0},{1,17},{17,33},{33,49},{49,1},{2,18}... | collective-permute-start | bytes 884744 | tf_op jit(solution)/shard_map/ppermute | solution.py:17
  153.6 20.3 %collective-permute-start.23 = (bf16[96,1536]{1,0:T(8,128)(2,1)S(1)}, bf16[96,1536]{1,0:T(8,128)(2,1)S(1)}, u32[]{:S(2)}, u32[]{:S(2)}) collective-permute-start(bf16[96,1536]{1,0:T(8,128)(2,1)S(1)} %collective-permute-done.15), channel_id=1, source_target_pairs={{0,64},{128,0},{256,128},{384,256},{448,384},{320,448},{192,320},{... | collective-permute-start | bytes 884744 | tf_op jit(solution)/shard_map/ppermute | solution.py:17
  167.4 16.0 %collective-permute-start.17 = (bf16[96,1536]{1,0:T(8,128)(2,1)S(1)}, bf16[96,1536]{1,0:T(8,128)(2,1)S(1)}, u32[]{:S(2)}, u32[]{:S(2)}) collective-permute-start(bf16[96,1536]{1,0:T(8,128)(2,1)S(1)} %collective-permute-done.15), channel_id=1, source_target_pairs={{0,48},{16,0},{32,16},{48,32},{1,49},{17,1},{33,17},{49,33},{2,50}... | collective-permute-start | bytes 884744 | tf_op jit(solution)/shard_map/ppermute | solution.py:17
  170.1 14.1 %collective-permute-start.18 = (bf16[96,1536]{1,0:T(8,128)(2,1)S(1)}, bf16[96,1536]{1,0:T(8,128)(2,1)S(1)}, u32[]{:S(2)}, u32[]{:S(2)}) collective-permute-start(bf16[96,1536]{1,0:T(8,128)(2,1)S(1)} %collective-permute-done.15), channel_id=1, source_target_pairs={{0,32},{16,48},{32,0},{48,16},{1,33},{17,49},{33,1},{49,17},{2,34}... | collective-permute-start | bytes 884744 | tf_op jit(solution)/shard_map/ppermute | solution.py:17
  173.9 18.3 %collective-permute-start.27 = (bf16[48,1536]{1,0:T(8,128)(2,1)S(1)}, bf16[48,1536]{1,0:T(8,128)(2,1)S(1)}, u32[]{:S(2)}, u32[]{:S(2)}) collective-permute-start(bf16[48,1536]{1,0:T(8,128)(2,1)S(1)} %slice.40), channel_id=1, source_target_pairs={{0,128},{128,256},{256,384},{384,448},{448,320},{320,192},{192,64}... | collective-permute-start | bytes 442376 | tf_op jit(solution)/shard_map/ppermute | solution.py:17
  175.9 19.9 %collective-permute-start.28 = (bf16[48,1536]{1,0:T(8,128)(2,1)S(1)}, bf16[48,1536]{1,0:T(8,128)(2,1)S(1)}, u32[]{:S(2)}, u32[]{:S(2)}) collective-permute-start(bf16[48,1536]{1,0:T(8,128)(2,1)S(1)} %slice.41), channel_id=1, source_target_pairs={{0,64},{128,0},{256,128},{384,256},{448,384},{320,448},{192,320},{... | collective-permute-start | bytes 442376 | tf_op jit(solution)/shard_map/ppermute | solution.py:17
  180.8 54.0 %collective-permute-start.36 = (bf16[2,4,192,768]{3,2,1,0:T(8,128)(2,1)S(1)}, bf16[2,4,192,768]{3,2,1,0:T(8,128)(2,1)S(1)}, u32[]{:S(2)}, u32[]{:S(2)}) collective-permute-start(bf16[2,4,192,768]{3,2,1,0:T(8,128)(2,1)S(1)} %bitcast_dynamic-update-slice_fusion.5), channel_id=1, source_target_pairs={{0,1},{1,0},{2,3},{3,2},{4,5},{5,4},{6,7},{7,6},{8,9},{9,8},{10,11... | collective-permute-start | bytes 7077896 | tf_op jit(solution)/shard_map/ppermute | solution.py:17
  186.4 13.9 %collective-permute-start.20 = (bf16[96,1536]{1,0:T(8,128)(2,1)S(1)}, bf16[96,1536]{1,0:T(8,128)(2,1)S(1)}, u32[]{:S(2)}, u32[]{:S(2)}) collective-permute-start(bf16[96,1536]{1,0:T(8,128)(2,1)S(1)} %collective-permute-done.19), channel_id=1, source_target_pairs={{0,16},{16,32},{32,48},{48,0},{1,17},{17,33},{33,49},{49,1},{2,18}... | collective-permute-start | bytes 884744 | tf_op jit(solution)/shard_map/ppermute | solution.py:17
  190.0 19.3 %collective-permute-start.21 = (bf16[96,1536]{1,0:T(8,128)(2,1)S(1)}, bf16[96,1536]{1,0:T(8,128)(2,1)S(1)}, u32[]{:S(2)}, u32[]{:S(2)}) collective-permute-start(bf16[96,1536]{1,0:T(8,128)(2,1)S(1)} %collective-permute-done.19), channel_id=1, source_target_pairs={{0,48},{16,0},{32,16},{48,32},{1,49},{17,1},{33,17},{49,33},{2,50}... | collective-permute-start | bytes 884744 | tf_op jit(solution)/shard_map/ppermute | solution.py:17
  192.2 19.8 %collective-permute-start.22 = (bf16[96,1536]{1,0:T(8,128)(2,1)S(1)}, bf16[96,1536]{1,0:T(8,128)(2,1)S(1)}, u32[]{:S(2)}, u32[]{:S(2)}) collective-permute-start(bf16[96,1536]{1,0:T(8,128)(2,1)S(1)} %collective-permute-done.19), channel_id=1, source_target_pairs={{0,32},{16,48},{32,0},{48,16},{1,33},{17,49},{33,1},{49,17},{2,34}... | collective-permute-start | bytes 884744 | tf_op jit(solution)/shard_map/ppermute | solution.py:17
  195.8 19.6 %collective-permute-start.24 = (bf16[96,1536]{1,0:T(8,128)(2,1)S(1)}, bf16[96,1536]{1,0:T(8,128)(2,1)S(1)}, u32[]{:S(2)}, u32[]{:S(2)}) collective-permute-start(bf16[96,1536]{1,0:T(8,128)(2,1)S(1)} %collective-permute-done.23), channel_id=1, source_target_pairs={{0,16},{16,32},{32,48},{48,0},{1,17},{17,33},{33,49},{49,1},{2,18}... | collective-permute-start | bytes 884744 | tf_op jit(solution)/shard_map/ppermute | solution.py:17
  200.3 21.6 %collective-permute-start.25 = (bf16[96,1536]{1,0:T(8,128)(2,1)S(1)}, bf16[96,1536]{1,0:T(8,128)(2,1)S(1)}, u32[]{:S(2)}, u32[]{:S(2)}) collective-permute-start(bf16[96,1536]{1,0:T(8,128)(2,1)S(1)} %collective-permute-done.23), channel_id=1, source_target_pairs={{0,48},{16,0},{32,16},{48,32},{1,49},{17,1},{33,17},{49,33},{2,50}... | collective-permute-start | bytes 884744 | tf_op jit(solution)/shard_map/ppermute | solution.py:17
  209.3 17.1 %collective-permute-start.26 = (bf16[96,1536]{1,0:T(8,128)(2,1)S(1)}, bf16[96,1536]{1,0:T(8,128)(2,1)S(1)}, u32[]{:S(2)}, u32[]{:S(2)}) collective-permute-start(bf16[96,1536]{1,0:T(8,128)(2,1)S(1)} %collective-permute-done.23), channel_id=1, source_target_pairs={{0,32},{16,48},{32,0},{48,16},{1,33},{17,49},{33,1},{49,17},{2,34}... | collective-permute-start | bytes 884744 | tf_op jit(solution)/shard_map/ppermute | solution.py:17
  212.0 15.9 %collective-permute-start.29 = (bf16[96,1536]{1,0:T(8,128)(2,1)S(1)}, bf16[96,1536]{1,0:T(8,128)(2,1)S(1)}, u32[]{:S(2)}, u32[]{:S(2)}) collective-permute-start(bf16[96,1536]{1,0:T(8,128)(2,1)S(1)} %constant_dynamic-update-slice_fusion), channel_id=1, source_target_pairs={{0,16},{16,32},{32,48},{48,0},{1,17},{17,33},{33,49},{49,1},{2,18}... | collective-permute-start | bytes 884744 | tf_op jit(solution)/shard_map/ppermute | solution.py:17
  215.4 13.2 %collective-permute-start.30 = (bf16[96,1536]{1,0:T(8,128)(2,1)S(1)}, bf16[96,1536]{1,0:T(8,128)(2,1)S(1)}, u32[]{:S(2)}, u32[]{:S(2)}) collective-permute-start(bf16[96,1536]{1,0:T(8,128)(2,1)S(1)} %constant_dynamic-update-slice_fusion), channel_id=1, source_target_pairs={{0,48},{16,0},{32,16},{48,32},{1,49},{17,1},{33,17},{49,33},{2,50}... | collective-permute-start | bytes 884744 | tf_op jit(solution)/shard_map/ppermute | solution.py:17
  221.9 12.0 %collective-permute-start.31 = (bf16[96,1536]{1,0:T(8,128)(2,1)S(1)}, bf16[96,1536]{1,0:T(8,128)(2,1)S(1)}, u32[]{:S(2)}, u32[]{:S(2)}) collective-permute-start(bf16[96,1536]{1,0:T(8,128)(2,1)S(1)} %constant_dynamic-update-slice_fusion), channel_id=1, source_target_pairs={{0,32},{16,48},{32,0},{48,16},{1,33},{17,49},{33,1},{49,17},{2,34}... | collective-permute-start | bytes 884744 | tf_op jit(solution)/shard_map/ppermute | solution.py:17
  248.9 5.3 %collective-permute-start.37 = (f32[2,4,192,256]{3,2,0,1:T(8,128)S(1)}, f32[2,4,192,256]{3,2,0,1:T(8,128)S(1)}, u32[]{:S(2)}, u32[]{:S(2)}) collective-permute-start(f32[2,4,192,256]{3,2,0,1:T(8,128)S(1)} %bitcast.138), channel_id=1, source_target_pairs={{0,1},{1,0},{2,3},{3,2},{4,5},{5,4},{6,7},{7,6},{8,9},{9,8},{10,11... | collective-permute-start | bytes 4718600 | tf_op jit(solution)/shard_map/ppermute | solution.py:17
  254.5 10.0 %collective-permute-start.38 = (bf16[2,192,256]{2,1,0:T(8,128)(2,1)S(1)}, bf16[2,192,256]{2,1,0:T(8,128)(2,1)S(1)}, u32[]{:S(2)}, u32[]{:S(2)}) collective-permute-start(bf16[2,192,256]{2,1,0:T(8,128)(2,1)S(1)} %get-tuple-element.9), channel_id=1, source_target_pairs={{0,2},{2,4},{4,6},{6,0},{1,3},{3,5},{5,7},{7,1},{8,10},{10,12},{12... | collective-permute-start | bytes 589832 | tf_op jit(solution)/shard_map/ppermute | solution.py:17
  257.4 12.5 %collective-permute-start.39 = (bf16[2,192,256]{2,1,0:T(8,128)(2,1)S(1)}, bf16[2,192,256]{2,1,0:T(8,128)(2,1)S(1)}, u32[]{:S(2)}, u32[]{:S(2)}) collective-permute-start(bf16[2,192,256]{2,1,0:T(8,128)(2,1)S(1)} %get-tuple-element.11), channel_id=1, source_target_pairs={{0,6},{2,0},{4,2},{6,4},{1,7},{3,1},{5,3},{7,5},{8,14},{10,8},{12,... | collective-permute-start | bytes 589832 | tf_op jit(solution)/shard_map/ppermute | solution.py:17
  261.5 9.8 %collective-permute-start.40 = (bf16[2,192,256]{2,1,0:T(8,128)(2,1)S(1)}, bf16[2,192,256]{2,1,0:T(8,128)(2,1)S(1)}, u32[]{:S(2)}, u32[]{:S(2)}) collective-permute-start(bf16[2,192,256]{2,1,0:T(8,128)(2,1)S(1)} %get-tuple-element.10), channel_id=1, source_target_pairs={{0,4},{2,6},{4,0},{6,2},{1,5},{3,7},{5,1},{7,3},{8,12},{10,14},{12... | collective-permute-start | bytes 589832 | tf_op jit(solution)/shard_map/ppermute | solution.py:17
  271.5 20.3 %collective-permute-start.41 = (bf16[192,256]{1,0:T(8,128)(2,1)S(1)}, bf16[192,256]{1,0:T(8,128)(2,1)S(1)}, u32[]{:S(2)}, u32[]{:S(2)}) collective-permute-start(bf16[192,256]{1,0:T(8,128)(2,1)S(1)} %fusion.33), channel_id=1, source_target_pairs={{0,8},{8,0},{1,9},{9,1},{2,10},{10,2},{3,11},{11,3},{4,12},{12,4},... | collective-permute-start | bytes 294920 | tf_op jit(solution)/shard_map/ppermute | solution.py:17
  (1 other events, 33.9 us)

commit v2 on v1

--- a/solution.py
+++ b/solution.py
@@ -33,37 +33,28 @@
     place = take(jnp.asarray(np.argsort(RING), jnp.int32), zl)
     ring = jnp.asarray(RING, jnp.int32)
 
+    fields = jnp.concatenate([tokens.T, tangent.T, cotangent.T], axis=1)
+    feat = fields.shape[0]
+    for axis in ("zh", "y", "c"):
+        fields = lax.all_gather(fields, axis, axis=0, tiled=True)
+
     own = jnp.concatenate([gate_weight, up_weight, down_weight.T], axis=1)
     rows, width = own.shape
-    half = rows // 2
-    blocks = [(own[None], 0)]
     ups, downs = own, own
-    rounds = [[(own, zl)]]
+    groups = [([own], [zl])]
     for k in (1, 2, 3):
         ups, downs = ring_up(ups), ring_down(downs)
-        rounds.append([(ups, take(ring, (place - k) % NZ)), (downs, take(ring, (place + k) % NZ))])
-    last = jnp.concatenate([ring_up(ups[:half]), ring_down(downs[half:])], axis=0)
-    rounds.append([(last, take(ring, (place + 4) % NZ))])
+        groups.append(([ups, downs], [take(ring, (place - k) % NZ), take(ring, (place + k) % NZ)]))
+    groups.append(([ring_up(ups)], [take(ring, (place + 4) % NZ)]))
 
-    fields = jnp.concatenate([tokens.T, tangent.T, cotangent.T], axis=1)
-    feat, cols = fields.shape
-    pair = jnp.stack([fields, other_half(fields)])
-    pair = jnp.stack([take(pair, zh), take(pair, 1 - zh)])
-    quad = jnp.zeros((NH, NY, feat, cols), BF)
-    for part, src in ((pair, y), (y_up(pair), y - 1), (y_down(pair), y + 1), (y_far(pair), y + 2)):
-        quad = lax.dynamic_update_slice(quad, part[:, None], (0, src % NY, 0, 0))
-    across = other_core(quad)
-    fields = jnp.zeros((NH, NY, NC, feat, cols), BF)
-    fields = lax.dynamic_update_slice(fields, quad[:, :, None], (0, 0, c, 0, 0))
-    fields = lax.dynamic_update_slice(fields, across[:, :, None], (0, 0, 1 - c, 0, 0))
-    fields = fields.reshape(NH * NY * NC * feat, cols)
-
-    full = jnp.zeros((NZ, NX, rows, width), BF)
-    for group in rounds:
-        for block, src in group:
-            for part, at in ((block, x), (x_up(block), x - 1), (x_down(block), x + 1), (x_far(block), x + 2)):
-                full = lax.dynamic_update_slice(full, part[None, None], (src, at % NX, 0, 0))
-    full = full.reshape(NZ * NX * rows, width)
+    full = jnp.zeros((NZ * NX * rows, width), BF)
+    for blocks, sources in groups:
+        sent = jnp.stack(blocks)
+        for part, at in ((sent, x), (x_up(sent), x - 1), (x_down(sent), x + 1), (x_far(sent), x + 2)):
+            at = at % NX
+            for j, src in enumerate(sources):
+                first_row = ((((at // 2) * NY + src % NY) * NH + src // NY) * 2 + at % 2) * rows
+                full = lax.dynamic_update_slice(full, part[j], (first_row, 0))
 
     n_tok = tokens.shape[0]
     ff = gate_weight.shape[1]
@@ -87,11 +78,11 @@
     dirs = jnp.concatenate([gate_dir, up_dir], axis=1)
     sums = lax.dot_general(both, dirs, (((1,), (1,)), ((), ())), preferred_element_type=F32)
 
-    sums = sums.reshape(NH, NY, NC, feat, n_tok)
-    sums = take(sums, c, 2) + other_core(take(sums, 1 - c, 2))
+    sums = sums.reshape(NC, NY, NH, feat, n_tok)
+    sums = take(sums, c) + other_core(take(sums, 1 - c))
 
     def to(step):
-        return take(sums, (y + step) % NY, 1)
+        return take(sums, (y + step) % NY)
 
     kept = to(0) + y_up(to(1).astype(BF)).astype(F32) + y_down(to(-1).astype(BF)).astype(F32)
     kept = kept + y_far(to(2).astype(BF)).astype(F32)

time: 294 us -> 279 us (0.949)
  the two profiles are of different devices: /device:TPU:38 before, /device:TPU:135 now
where the time goes in v2:
time: 279 us; the launch traced here: 277 us
  starting transfers between devices  103 us (37%)
  waiting for transfers between devices  55.7 us (20%)
  between operations  36.9 us (13%)
  blocking collectives  32.4 us (12%)
  local copies, waits for them, and re-layouts  31.5 us (11%)
  matrix products  14.8 us (5%)
  other arithmetic  3.46 us (1%)
    ppermute x27, starting transfers between devices, shift(): return lambda v: lax.ppermute(v, axis, pairs)  103 us
    ppermute x27, waiting for transfers between devices, shift(): return lambda v: lax.ppermute(v, axis, pairs)  53.5 us
    all_gather x1, blocking collectives, body(): fields = lax.all_gather(fields, axis, axis=0, tiled=True)  32.4 us
    dynamic_update_slice x31, local copies, waits for them, and re-layouts, body(): full = lax.dynamic_update_slice(full, part[j], (first_row, 0))  24 us
    dot_general x1, matrix products, body(): lax.dot_general(fields[:, :2 * n_tok], both, (((0,), (0,)), ((), ())), pr...  6.52 us
  transfers between devices with their start and end apart: 29, of which 13 were waited for; matrix products, arithmetic and copies ran while one was open for 9% of the time, Pallas kernels for 0%

profile of v2, /device:TPU:135, one launch (start us, length us, event | category | flops | bytes accessed | tf_op | source)
XLA Modules:
  0.0 277.3 jit_solution(1825684777318492325)
XLA Ops:
  6.7 4.2 %broadcast_in_dim.9 = bf16[3072,1536]{1,0:T(8,128)(2,1)} broadcast(bf16[]{:T(256)} %constant.533.clone.1), dimensions={} | broadcast | bytes 9437186 | tf_op jit(solution)/shard_map/broadcast_in_dim | solution.py:50
  11.0 0.8 pad_maximum_fusion.3
  11.8 2.1 collective-permute-start
  13.9 3.2 %collective-permute-start.1 = (bf16[1,96,1536]{2,1,0:T(8,128)(2,1)S(1)}, bf16[1,96,1536]{2,1,0:T(8,128)(2,1)S(1)}, u32[]{:S(2)}, u32[]{:S(2)}) collective-permute-start(bf16[1,96,1536]{2,1,0:T(8,128)(2,1)S(1)} %get-tuple-element.12), channel_id=1, source_target_pairs={{0,48},{16,0},{32,16},{48,32},{1,49},{17,1},{33,17},{49,33},{2,50}... | collective-permute-start | bytes 884744 | tf_op jit(solution)/shard_map/ppermute | solution.py:17
  17.1 3.0 %collective-permute-start.2 = (bf16[1,96,1536]{2,1,0:T(8,128)(2,1)S(1)}, bf16[1,96,1536]{2,1,0:T(8,128)(2,1)S(1)}, u32[]{:S(2)}, u32[]{:S(2)}) collective-permute-start(bf16[1,96,1536]{2,1,0:T(8,128)(2,1)S(1)} %get-tuple-element.12), channel_id=1, source_target_pairs={{0,32},{16,48},{32,0},{48,16},{1,33},{17,49},{33,1},{49,17},{2,34}... | collective-permute-start | bytes 884744 | tf_op jit(solution)/shard_map/ppermute | solution.py:17
  20.1 4.9 %collective-permute-start.3 = (bf16[96,1536]{1,0:T(8,128)(2,1)S(1)}, bf16[96,1536]{1,0:T(8,128)(2,1)S(1)}, u32[]{:S(2)}, u32[]{:S(2)}) collective-permute-start(bf16[96,1536]{1,0:T(8,128)(2,1)S(1)} %get-tuple-element.10), channel_id=1, source_target_pairs={{0,128},{128,256},{256,384},{384,448},{448,320},{320,192},{192,64}... | collective-permute-start | bytes 884744 | tf_op jit(solution)/shard_map/ppermute | solution.py:17
  25.0 2.5 collective-permute-start.4
  27.5 32.4 %all_gather.9 = bf16[384,768]{1,0:T(8,128)(2,1)} all-gather(bf16[192,768]{1,0:T(8,128)(2,1)S(1)} %pad_maximum_fusion.4), channel_id=1, replica_groups=mesh['zl'=8,'x'=4,'zh'=2,'y'=4,'c'=2] {'zh'}, dimensions={0}, use_global_device_ids=true | all-gather | bytes 884736 | tf_op jit(solution)/shard_map/all_gather | solution.py:39
  84.4 4.2 %collective-permute-start.5 = (bf16[2,96,1536]{2,1,0:T(8,128)(2,1)S(1)}, bf16[2,96,1536]{2,1,0:T(8,128)(2,1)S(1)}, u32[]{:S(2)}, u32[]{:S(2)}) collective-permute-start(bf16[2,96,1536]{2,1,0:T(8,128)(2,1)S(1)} %pad_maximum_fusion), channel_id=1, source_target_pairs={{0,16},{16,32},{32,48},{48,0},{1,17},{17,33},{33,49},{49,1},{2,18}... | collective-permute-start | bytes 1769480 | tf_op jit(solution)/shard_map/ppermute | solution.py:17
  88.6 1.9 collective-permute-start.6
  90.5 3.1 %collective-permute-start.7 = (bf16[2,96,1536]{2,1,0:T(8,128)(2,1)S(1)}, bf16[2,96,1536]{2,1,0:T(8,128)(2,1)S(1)}, u32[]{:S(2)}, u32[]{:S(2)}) collective-permute-start(bf16[2,96,1536]{2,1,0:T(8,128)(2,1)S(1)} %pad_maximum_fusion), channel_id=1, source_target_pairs={{0,32},{16,48},{32,0},{48,16},{1,33},{17,49},{33,1},{49,17},{2,34}... | collective-permute-start | bytes 1769480 | tf_op jit(solution)/shard_map/ppermute | solution.py:17
  94.3 14.0 %collective-permute-start.8 = (bf16[96,1536]{1,0:T(8,128)(2,1)S(1)}, bf16[96,1536]{1,0:T(8,128)(2,1)S(1)}, u32[]{:S(2)}, u32[]{:S(2)}) collective-permute-start(bf16[96,1536]{1,0:T(8,128)(2,1)S(1)} %collective-permute-done.3), channel_id=1, source_target_pairs={{0,128},{128,256},{256,384},{384,448},{448,320},{320,192},{192,64}... | collective-permute-start | bytes 884744 | tf_op jit(solution)/shard_map/ppermute | solution.py:17
  109.1 1.9 collective-permute-start.9
  113.2 9.5 %collective-permute-done.9 = bf16[96,1536]{1,0:T(8,128)(2,1)S(1)} collective-permute-done((bf16[96,1536]{1,0:T(8,128)(2,1)S(1)}, bf16[96,1536]{1,0:T(8,128)(2,1)S(1)}, u32[]{:S(2)}, u32[]{:S(2)}) %collective-permute-start.9) | collective-permute-done | bytes 294944 | tf_op jit(solution)/shard_map/ppermute | solution.py:17
  122.8 3.3 %collective-permute-start.10 = (bf16[2,96,1536]{2,1,0:T(8,128)(2,1)S(1)}, bf16[2,96,1536]{2,1,0:T(8,128)(2,1)S(1)}, u32[]{:S(2)}, u32[]{:S(2)}) collective-permute-start(bf16[2,96,1536]{2,1,0:T(8,128)(2,1)S(1)} %pad_maximum_fusion.1), channel_id=1, source_target_pairs={{0,16},{16,32},{32,48},{48,0},{1,17},{17,33},{33,49},{49,1},{2,18}... | collective-permute-start | bytes 1769480 | tf_op jit(solution)/shard_map/ppermute | solution.py:17
  126.0 1.9 collective-permute-start.13
  128.0 5.5 %collective-permute-start.14 = (bf16[96,1536]{1,0:T(8,128)(2,1)S(1)}, bf16[96,1536]{1,0:T(8,128)(2,1)S(1)}, u32[]{:S(2)}, u32[]{:S(2)}) collective-permute-start(bf16[96,1536]{1,0:T(8,128)(2,1)S(1)} %collective-permute-done.9), channel_id=1, source_target_pairs={{0,64},{128,0},{256,128},{384,256},{448,384},{320,448},{192,320},{... | collective-permute-start | bytes 884744 | tf_op jit(solution)/shard_map/ppermute | solution.py:17
  134.2 3.6 %collective-permute-done.13 = bf16[96,1536]{1,0:T(8,128)(2,1)S(1)} collective-permute-done((bf16[96,1536]{1,0:T(8,128)(2,1)S(1)}, bf16[96,1536]{1,0:T(8,128)(2,1)S(1)}, u32[]{:S(2)}, u32[]{:S(2)}) %collective-permute-start.13) | collective-permute-done | bytes 294944 | tf_op jit(solution)/shard_map/ppermute | solution.py:17
  137.8 2.2 collective-permute-start.11
  140.2 4.0 %collective-permute-start.12 = (bf16[2,96,1536]{2,1,0:T(8,128)(2,1)S(1)}, bf16[2,96,1536]{2,1,0:T(8,128)(2,1)S(1)}, u32[]{:S(2)}, u32[]{:S(2)}) collective-permute-start(bf16[2,96,1536]{2,1,0:T(8,128)(2,1)S(1)} %pad_maximum_fusion.1), channel_id=1, source_target_pairs={{0,32},{16,48},{32,0},{48,16},{1,33},{17,49},{33,1},{49,17},{2,34}... | collective-permute-start | bytes 1769480 | tf_op jit(solution)/shard_map/ppermute | solution.py:17
  144.3 0.8 fusion.42
  145.1 3.1 %collective-permute-start.15 = (bf16[2,96,1536]{2,1,0:T(8,128)(2,1)S(1)}, bf16[2,96,1536]{2,1,0:T(8,128)(2,1)S(1)}, u32[]{:S(2)}, u32[]{:S(2)}) collective-permute-start(bf16[2,96,1536]{2,1,0:T(8,128)(2,1)S(1)} %pad_maximum_fusion.2), channel_id=1, source_target_pairs={{0,16},{16,32},{32,48},{48,0},{1,17},{17,33},{33,49},{49,1},{2,18}... | collective-permute-start | bytes 1769480 | tf_op jit(solution)/shard_map/ppermute | solution.py:17
  149.7 2.1 collective-permute-start.16
  154.8 4.8 %collective-permute-start.18 = (bf16[96,1536]{1,0:T(8,128)(2,1)S(1)}, bf16[96,1536]{1,0:T(8,128)(2,1)S(1)}, u32[]{:S(2)}, u32[]{:S(2)}) collective-permute-start(bf16[96,1536]{1,0:T(8,128)(2,1)S(1)} %collective-permute-done.13), channel_id=1, source_target_pairs={{0,128},{128,256},{256,384},{384,448},{448,320},{320,192},{192,64}... | collective-permute-start | bytes 884744 | tf_op jit(solution)/shard_map/ppermute | solution.py:17
  161.1 3.3 %collective-permute-start.17 = (bf16[2,96,1536]{2,1,0:T(8,128)(2,1)S(1)}, bf16[2,96,1536]{2,1,0:T(8,128)(2,1)S(1)}, u32[]{:S(2)}, u32[]{:S(2)}) collective-permute-start(bf16[2,96,1536]{2,1,0:T(8,128)(2,1)S(1)} %pad_maximum_fusion.2), channel_id=1, source_target_pairs={{0,32},{16,48},{32,0},{48,16},{1,33},{17,49},{33,1},{49,17},{2,34}... | collective-permute-start | bytes 1769480 | tf_op jit(solution)/shard_map/ppermute | solution.py:17
  164.7 4.1 %collective-permute-start.19 = (bf16[1,96,1536]{2,1,0:T(8,128)(2,1)S(1)}, bf16[1,96,1536]{2,1,0:T(8,128)(2,1)S(1)}, u32[]{:S(2)}, u32[]{:S(2)}) collective-permute-start(bf16[1,96,1536]{2,1,0:T(8,128)(2,1)S(1)} %bitcast.146), channel_id=1, source_target_pairs={{0,16},{16,32},{32,48},{48,0},{1,17},{17,33},{33,49},{49,1},{2,18}... | collective-permute-start | bytes 884744 | tf_op jit(solution)/shard_map/ppermute | solution.py:17
  170.3 1.9 collective-permute-start.20
  175.2 3.1 %collective-permute-start.21 = (bf16[1,96,1536]{2,1,0:T(8,128)(2,1)S(1)}, bf16[1,96,1536]{2,1,0:T(8,128)(2,1)S(1)}, u32[]{:S(2)}, u32[]{:S(2)}) collective-permute-start(bf16[1,96,1536]{2,1,0:T(8,128)(2,1)S(1)} %bitcast.148), channel_id=1, source_target_pairs={{0,32},{16,48},{32,0},{48,16},{1,33},{17,49},{33,1},{49,17},{2,34}... | collective-permute-start | bytes 884744 | tf_op jit(solution)/shard_map/ppermute | solution.py:17
  179.8 1.1 collective-permute-done.16
  182.4 8.1 %collective-permute-done.17 = bf16[2,96,1536]{2,1,0:T(8,128)(2,1)S(1)} collective-permute-done((bf16[2,96,1536]{2,1,0:T(8,128)(2,1)S(1)}, bf16[2,96,1536]{2,1,0:T(8,128)(2,1)S(1)}, u32[]{:S(2)}, u32[]{:S(2)}) %collective-permute-start.17) | collective-permute-done | bytes 589856 | tf_op jit(solution)/shard_map/ppermute | solution.py:17
  193.4 6.5 %collective-permute-done.20 = bf16[1,96,1536]{2,1,0:T(8,128)(2,1)} collective-permute-done((bf16[1,96,1536]{2,1,0:T(8,128)(2,1)S(1)}, bf16[1,96,1536]{2,1,0:T(8,128)(2,1)}, u32[]{:S(2)}, u32[]{:S(2)}) %collective-permute-start.20) | collective-permute-done | bytes 294944 | tf_op jit(solution)/shard_map/ppermute | solution.py:17
  199.9 1.8 bitcast_dynamic-update-slice_fusion.1
  201.7 1.4 collective-permute-done.21
  203.8 2.1 all-gather.5.cloned.1.call-done
  206.0 6.5 %fusion.2 = f32[512,1024]{1,0:T(8,128)S(1)} fusion(bf16[3072,1536]{1,0:T(8,128)(2,1)} %bitcast_dynamic-update-slice_fusion, bf16[3072,768]{1,0:T(8,128)(2,1)} %all-gather.5.cloned.1.call-done), kind=kOutput, calls=%fused_computation.2 | convolution fusion | flops 3221225472 | bytes 11534336 | tf_op jit(solution)/shard_map/dot_general | solution.py:62
  212.5 3.6 %fusion.20 = (bf16[256,512]{1,0:T(8,128)(2,1)S(1)}, bf16[256,512]{1,0:T(8,128)(2,1)S(1)}) fusion(f32[512,1024]{1,0:T(8,128)S(1)} %fusion.2, bf16[3072,1536]{1,0:T(8,128)(2,1)} %bitcast_dynamic-update-slice_fusion, bf16[3072,768]{1,0:T(8,128)(2,1)} %all-gather.5.cloned.1.call-done, f32[256]{0:T(256)S(1)} %broadcast_select_fusion), kind=kOutput, calls=%fused_computation.23 | convolution fusion | flops 808321024 | bytes 7341056 | tf_op jit(solution)/shard_map/dot_general | solution.py:65
  216.2 4.6 %fusion = f32[3072,256]{1,0:T(8,128)S(1)} fusion(bf16[3072,1536]{1,0:T(8,128)(2,1)} %bitcast_dynamic-update-slice_fusion, bf16[256,512]{1,0:T(8,128)(2,1)S(1)} %get-tuple-element.6, bf16[256,512]{1,0:T(8,128)(2,1)S(1)} %get-tuple-element.5), kind=kOutput, calls=%fused_computation | convolution fusion | flops 1611661312 | bytes 9961472 | tf_op jit(solution)/shard_map/dot_general | solution.py:79
  220.8 1.6 copy-done
  222.6 5.7 %collective-permute-start.22 = (f32[4,2,192,256]{3,2,1,0:T(8,128)S(1)}, f32[4,2,192,256]{3,2,1,0:T(8,128)S(1)}, u32[]{:S(2)}, u32[]{:S(2)}) collective-permute-start(f32[4,2,192,256]{3,2,1,0:T(8,128)S(1)} %dynamic-slice_bitcast_fusion), channel_id=1, source_target_pairs={{0,1},{1,0},{2,3},{3,2},{4,5},{5,4},{6,7},{7,6},{8,9},{9,8},{10,11... | collective-permute-start | bytes 4718600 | tf_op jit(solution)/shard_map/ppermute | solution.py:17
  228.4 3.0 %collective-permute-done.22 = f32[4,2,192,256]{3,2,1,0:T(8,128)S(1)} collective-permute-done((f32[4,2,192,256]{3,2,1,0:T(8,128)S(1)}, f32[4,2,192,256]{3,2,1,0:T(8,128)S(1)}, u32[]{:S(2)}, u32[]{:S(2)}) %collective-permute-start.22) | collective-permute-done | bytes 1572896 | tf_op jit(solution)/shard_map/ppermute | solution.py:17
  231.3 1.6 bitcast_add_fusion
  233.0 4.8 %collective-permute-start.25 = (bf16[2,192,256]{2,1,0:T(8,128)(2,1)S(1)}, bf16[2,192,256]{2,1,0:T(8,128)(2,1)S(1)}, u32[]{:S(2)}, u32[]{:S(2)}) collective-permute-start(bf16[2,192,256]{2,1,0:T(8,128)(2,1)S(1)} %get-tuple-element.8), channel_id=1, source_target_pairs={{0,4},{2,6},{4,0},{6,2},{1,5},{3,7},{5,1},{7,3},{8,12},{10,14},{12... | collective-permute-start | bytes 589832 | tf_op jit(solution)/shard_map/ppermute | solution.py:17
  237.9 2.7 collective-permute-start.24
  240.5 2.6 collective-permute-start.23
  243.2 3.9 %collective-permute-done.24 = bf16[2,192,256]{2,1,0:T(8,128)(2,1)S(1)} collective-permute-done((bf16[2,192,256]{2,1,0:T(8,128)(2,1)S(1)}, bf16[2,192,256]{2,1,0:T(8,128)(2,1)S(1)}, u32[]{:S(2)}, u32[]{:S(2)}) %collective-permute-start.24) | collective-permute-done | bytes 196640 | tf_op jit(solution)/shard_map/ppermute | solution.py:17
  247.1 2.0 collective-permute-done.23
  249.2 6.7 %collective-permute-start.26 = (bf16[192,256]{1,0:T(8,128)(2,1)S(1)}, bf16[192,256]{1,0:T(8,128)(2,1)S(1)}, u32[]{:S(2)}, u32[]{:S(2)}) collective-permute-start(bf16[192,256]{1,0:T(8,128)(2,1)S(1)} %fusion.49), channel_id=1, source_target_pairs={{0,8},{8,0},{1,9},{9,1},{2,10},{10,2},{3,11},{11,3},{4,12},{12,4},... | collective-permute-start | bytes 294920 | tf_op jit(solution)/shard_map/ppermute | solution.py:17
  255.9 13.8 %collective-permute-done.26 = bf16[192,256]{1,0:T(8,128)(2,1)S(1)} collective-permute-done((bf16[192,256]{1,0:T(8,128)(2,1)S(1)}, bf16[192,256]{1,0:T(8,128)(2,1)S(1)}, u32[]{:S(2)}, u32[]{:S(2)}) %collective-permute-start.26) | collective-permute-done | bytes 98336 | tf_op jit(solution)/shard_map/ppermute | solution.py:17
  (85 shorter events, 24.8 us)
Async XLA Ops:
  6.5 53.7 %copy-start.10 = (s32[8]{0:T(128)S(1)}, s32[8]{0:T(128)}, u32[]{:S(2)}) copy-start(s32[8]{0:T(128)} %constant.560.clone) | copy-start | bytes 100
  6.5 59.0 %copy-start.7 = (s32[8]{0:T(128)S(1)}, s32[8]{0:T(128)}, u32[]{:S(2)}) copy-start(s32[8]{0:T(128)} %constant.561.clone) | copy-start | bytes 100
  6.5 4.4 %copy-start.1 = (bf16[512,96]{0,1:T(8,128)(2,1)S(1)}, bf16[512,96]{0,1:T(8,128)(2,1)}, u32[]{:S(2)}) copy-start(bf16[512,96]{0,1:T(8,128)(2,1)} %param.17) | copy-start | bytes 294916
  6.5 4.4 %copy-start.2 = (bf16[96,512]{1,0:T(8,128)(2,1)S(1)}, bf16[96,512]{1,0:T(8,128)(2,1)}, u32[]{:S(2)}) copy-start(bf16[96,512]{1,0:T(8,128)(2,1)} %param.16) | copy-start | bytes 294916
  6.5 4.4 %copy-start.3 = (bf16[96,512]{1,0:T(8,128)(2,1)S(1)}, bf16[96,512]{1,0:T(8,128)(2,1)}, u32[]{:S(2)}) copy-start(bf16[96,512]{1,0:T(8,128)(2,1)} %param.15) | copy-start | bytes 294916
  6.5 20.9 %copy-start.4 = (bf16[256,192]{0,1:T(8,128)(2,1)S(1)}, bf16[256,192]{0,1:T(8,128)(2,1)}, u32[]{:S(2)}) copy-start(bf16[256,192]{0,1:T(8,128)(2,1)} %param.12) | copy-start | bytes 294916
  6.6 20.9 %copy-start.5 = (bf16[256,192]{0,1:T(8,128)(2,1)S(1)}, bf16[256,192]{0,1:T(8,128)(2,1)}, u32[]{:S(2)}) copy-start(bf16[256,192]{0,1:T(8,128)(2,1)} %param.11) | copy-start | bytes 294916
  6.6 20.9 %copy-start.6 = (bf16[256,192]{0,1:T(8,128)(2,1)S(1)}, bf16[256,192]{0,1:T(8,128)(2,1)}, u32[]{:S(2)}) copy-start(bf16[256,192]{0,1:T(8,128)(2,1)} %param.10) | copy-start | bytes 294916
  6.6 53.4 %copy-start.9 = (s32[256]{0:T(256)S(1)}, s32[256]{0:T(256)}, u32[]{:S(2)}) copy-start(s32[256]{0:T(256)} %param.14) | copy-start | bytes 3076
  6.6 53.5 %copy-start.8 = (f32[256]{0:T(256)S(1)}, f32[256]{0:T(256)}, u32[]{:S(2)}) copy-start(f32[256]{0:T(256)} %param.13) | copy-start | bytes 3076
  6.6 167.1 %all-gather.3.cloned.1.call-start = ((), (), s32[]{:S(2)}) async-start(), calls=%async_computation | async-start | bytes 2949120 | tf_op jit(solution)/shard_map/all_gather | solution.py:39
  11.8 78.7 %collective-permute-start = (bf16[1,96,1536]{2,1,0:T(8,128)(2,1)S(1)}, bf16[1,96,1536]{2,1,0:T(8,128)(2,1)S(1)}, u32[]{:S(2)}, u32[]{:S(2)}) collective-permute-start(bf16[1,96,1536]{2,1,0:T(8,128)(2,1)S(1)} %get-tuple-element.12), channel_id=1, source_target_pairs={{0,16},{16,32},{32,48},{48,0},{1,17},{17,33},{33,49},{49,1},{2,18}... | collective-permute-start | bytes 884744 | tf_op jit(solution)/shard_map/ppermute | solution.py:17
  13.9 80.5 %collective-permute-start.1 = (bf16[1,96,1536]{2,1,0:T(8,128)(2,1)S(1)}, bf16[1,96,1536]{2,1,0:T(8,128)(2,1)S(1)}, u32[]{:S(2)}, u32[]{:S(2)}) collective-permute-start(bf16[1,96,1536]{2,1,0:T(8,128)(2,1)S(1)} %get-tuple-element.12), channel_id=1, source_target_pairs={{0,48},{16,0},{32,16},{48,32},{1,49},{17,1},{33,17},{49,33},{2,50}... | collective-permute-start | bytes 884744 | tf_op jit(solution)/shard_map/ppermute | solution.py:17
  17.1 92.0 %collective-permute-start.2 = (bf16[1,96,1536]{2,1,0:T(8,128)(2,1)S(1)}, bf16[1,96,1536]{2,1,0:T(8,128)(2,1)S(1)}, u32[]{:S(2)}, u32[]{:S(2)}) collective-permute-start(bf16[1,96,1536]{2,1,0:T(8,128)(2,1)S(1)} %get-tuple-element.12), channel_id=1, source_target_pairs={{0,32},{16,48},{32,0},{48,16},{1,33},{17,49},{33,1},{49,17},{2,34}... | collective-permute-start | bytes 884744 | tf_op jit(solution)/shard_map/ppermute | solution.py:17
  20.1 64.2 %collective-permute-start.3 = (bf16[96,1536]{1,0:T(8,128)(2,1)S(1)}, bf16[96,1536]{1,0:T(8,128)(2,1)S(1)}, u32[]{:S(2)}, u32[]{:S(2)}) collective-permute-start(bf16[96,1536]{1,0:T(8,128)(2,1)S(1)} %get-tuple-element.10), channel_id=1, source_target_pairs={{0,128},{128,256},{256,384},{384,448},{448,320},{320,192},{192,64}... | collective-permute-start | bytes 884744 | tf_op jit(solution)/shard_map/ppermute | solution.py:17
  25.0 59.3 %collective-permute-start.4 = (bf16[96,1536]{1,0:T(8,128)(2,1)S(1)}, bf16[96,1536]{1,0:T(8,128)(2,1)S(1)}, u32[]{:S(2)}, u32[]{:S(2)}) collective-permute-start(bf16[96,1536]{1,0:T(8,128)(2,1)S(1)} %get-tuple-element.10), channel_id=1, source_target_pairs={{0,64},{128,0},{256,128},{384,256},{448,384},{320,448},{192,320},{... | collective-permute-start | bytes 884744 | tf_op jit(solution)/shard_map/ppermute | solution.py:17
  59.9 146.1 %all-gather.5.cloned.1.call-start = ((), (), s32[]{:S(2)}) async-start(), calls=%async_computation.1 | async-start | bytes 7077888 | tf_op jit(solution)/shard_map/all_gather | solution.py:39
  84.4 43.6 %collective-permute-start.5 = (bf16[2,96,1536]{2,1,0:T(8,128)(2,1)S(1)}, bf16[2,96,1536]{2,1,0:T(8,128)(2,1)S(1)}, u32[]{:S(2)}, u32[]{:S(2)}) collective-permute-start(bf16[2,96,1536]{2,1,0:T(8,128)(2,1)S(1)} %pad_maximum_fusion), channel_id=1, source_target_pairs={{0,16},{16,32},{32,48},{48,0},{1,17},{17,33},{33,49},{49,1},{2,18}... | collective-permute-start | bytes 1769480 | tf_op jit(solution)/shard_map/ppermute | solution.py:17
  88.6 56.5 %collective-permute-start.6 = (bf16[2,96,1536]{2,1,0:T(8,128)(2,1)S(1)}, bf16[2,96,1536]{2,1,0:T(8,128)(2,1)S(1)}, u32[]{:S(2)}, u32[]{:S(2)}) collective-permute-start(bf16[2,96,1536]{2,1,0:T(8,128)(2,1)S(1)} %pad_maximum_fusion), channel_id=1, source_target_pairs={{0,48},{16,0},{32,16},{48,32},{1,49},{17,1},{33,17},{49,33},{2,50}... | collective-permute-start | bytes 1769480 | tf_op jit(solution)/shard_map/ppermute | solution.py:17
  90.5 59.2 %collective-permute-start.7 = (bf16[2,96,1536]{2,1,0:T(8,128)(2,1)S(1)}, bf16[2,96,1536]{2,1,0:T(8,128)(2,1)S(1)}, u32[]{:S(2)}, u32[]{:S(2)}) collective-permute-start(bf16[2,96,1536]{2,1,0:T(8,128)(2,1)S(1)} %pad_maximum_fusion), channel_id=1, source_target_pairs={{0,32},{16,48},{32,0},{48,16},{1,33},{17,49},{33,1},{49,17},{2,34}... | collective-permute-start | bytes 1769480 | tf_op jit(solution)/shard_map/ppermute | solution.py:17
  94.3 18.9 %collective-permute-start.8 = (bf16[96,1536]{1,0:T(8,128)(2,1)S(1)}, bf16[96,1536]{1,0:T(8,128)(2,1)S(1)}, u32[]{:S(2)}, u32[]{:S(2)}) collective-permute-start(bf16[96,1536]{1,0:T(8,128)(2,1)S(1)} %collective-permute-done.3), channel_id=1, source_target_pairs={{0,128},{128,256},{256,384},{384,448},{448,320},{320,192},{192,64}... | collective-permute-start | bytes 884744 | tf_op jit(solution)/shard_map/ppermute | solution.py:17
  109.1 13.6 %collective-permute-start.9 = (bf16[96,1536]{1,0:T(8,128)(2,1)S(1)}, bf16[96,1536]{1,0:T(8,128)(2,1)S(1)}, u32[]{:S(2)}, u32[]{:S(2)}) collective-permute-start(bf16[96,1536]{1,0:T(8,128)(2,1)S(1)} %collective-permute-done.4), channel_id=1, source_target_pairs={{0,64},{128,0},{256,128},{384,256},{448,384},{320,448},{192,320},{... | collective-permute-start | bytes 884744 | tf_op jit(solution)/shard_map/ppermute | solution.py:17
  122.8 32.1 %collective-permute-start.10 = (bf16[2,96,1536]{2,1,0:T(8,128)(2,1)S(1)}, bf16[2,96,1536]{2,1,0:T(8,128)(2,1)S(1)}, u32[]{:S(2)}, u32[]{:S(2)}) collective-permute-start(bf16[2,96,1536]{2,1,0:T(8,128)(2,1)S(1)} %pad_maximum_fusion.1), channel_id=1, source_target_pairs={{0,16},{16,32},{32,48},{48,0},{1,17},{17,33},{33,49},{49,1},{2,18}... | collective-permute-start | bytes 1769480 | tf_op jit(solution)/shard_map/ppermute | solution.py:17
  126.0 11.8 %collective-permute-start.13 = (bf16[96,1536]{1,0:T(8,128)(2,1)S(1)}, bf16[96,1536]{1,0:T(8,128)(2,1)S(1)}, u32[]{:S(2)}, u32[]{:S(2)}) collective-permute-start(bf16[96,1536]{1,0:T(8,128)(2,1)S(1)} %collective-permute-done.8), channel_id=1, source_target_pairs={{0,128},{128,256},{256,384},{384,448},{448,320},{320,192},{192,64}... | collective-permute-start | bytes 884744 | tf_op jit(solution)/shard_map/ppermute | solution.py:17
  128.0 12.2 %collective-permute-start.14 = (bf16[96,1536]{1,0:T(8,128)(2,1)S(1)}, bf16[96,1536]{1,0:T(8,128)(2,1)S(1)}, u32[]{:S(2)}, u32[]{:S(2)}) collective-permute-start(bf16[96,1536]{1,0:T(8,128)(2,1)S(1)} %collective-permute-done.9), channel_id=1, source_target_pairs={{0,64},{128,0},{256,128},{384,256},{448,384},{320,448},{192,320},{... | collective-permute-start | bytes 884744 | tf_op jit(solution)/shard_map/ppermute | solution.py:17
  137.8 23.3 %collective-permute-start.11 = (bf16[2,96,1536]{2,1,0:T(8,128)(2,1)S(1)}, bf16[2,96,1536]{2,1,0:T(8,128)(2,1)S(1)}, u32[]{:S(2)}, u32[]{:S(2)}) collective-permute-start(bf16[2,96,1536]{2,1,0:T(8,128)(2,1)S(1)} %pad_maximum_fusion.1), channel_id=1, source_target_pairs={{0,48},{16,0},{32,16},{48,32},{1,49},{17,1},{33,17},{49,33},{2,50}... | collective-permute-start | bytes 1769480 | tf_op jit(solution)/shard_map/ppermute | solution.py:17
  140.2 30.1 %collective-permute-start.12 = (bf16[2,96,1536]{2,1,0:T(8,128)(2,1)S(1)}, bf16[2,96,1536]{2,1,0:T(8,128)(2,1)S(1)}, u32[]{:S(2)}, u32[]{:S(2)}) collective-permute-start(bf16[2,96,1536]{2,1,0:T(8,128)(2,1)S(1)} %pad_maximum_fusion.1), channel_id=1, source_target_pairs={{0,32},{16,48},{32,0},{48,16},{1,33},{17,49},{33,1},{49,17},{2,34}... | collective-permute-start | bytes 1769480 | tf_op jit(solution)/shard_map/ppermute | solution.py:17
  145.1 30.1 %collective-permute-start.15 = (bf16[2,96,1536]{2,1,0:T(8,128)(2,1)S(1)}, bf16[2,96,1536]{2,1,0:T(8,128)(2,1)S(1)}, u32[]{:S(2)}, u32[]{:S(2)}) collective-permute-start(bf16[2,96,1536]{2,1,0:T(8,128)(2,1)S(1)} %pad_maximum_fusion.2), channel_id=1, source_target_pairs={{0,16},{16,32},{32,48},{48,0},{1,17},{17,33},{33,49},{49,1},{2,18}... | collective-permute-start | bytes 1769480 | tf_op jit(solution)/shard_map/ppermute | solution.py:17
  149.7 31.2 %collective-permute-start.16 = (bf16[2,96,1536]{2,1,0:T(8,128)(2,1)S(1)}, bf16[2,96,1536]{2,1,0:T(8,128)(2,1)S(1)}, u32[]{:S(2)}, u32[]{:S(2)}) collective-permute-start(bf16[2,96,1536]{2,1,0:T(8,128)(2,1)S(1)} %pad_maximum_fusion.2), channel_id=1, source_target_pairs={{0,48},{16,0},{32,16},{48,32},{1,49},{17,1},{33,17},{49,33},{2,50}... | collective-permute-start | bytes 1769480 | tf_op jit(solution)/shard_map/ppermute | solution.py:17
  154.8 9.9 %collective-permute-start.18 = (bf16[96,1536]{1,0:T(8,128)(2,1)S(1)}, bf16[96,1536]{1,0:T(8,128)(2,1)S(1)}, u32[]{:S(2)}, u32[]{:S(2)}) collective-permute-start(bf16[96,1536]{1,0:T(8,128)(2,1)S(1)} %collective-permute-done.13), channel_id=1, source_target_pairs={{0,128},{128,256},{256,384},{384,448},{448,320},{320,192},{192,64}... | collective-permute-start | bytes 884744 | tf_op jit(solution)/shard_map/ppermute | solution.py:17
  161.1 29.4 %collective-permute-start.17 = (bf16[2,96,1536]{2,1,0:T(8,128)(2,1)S(1)}, bf16[2,96,1536]{2,1,0:T(8,128)(2,1)S(1)}, u32[]{:S(2)}, u32[]{:S(2)}) collective-permute-start(bf16[2,96,1536]{2,1,0:T(8,128)(2,1)S(1)} %pad_maximum_fusion.2), channel_id=1, source_target_pairs={{0,32},{16,48},{32,0},{48,16},{1,33},{17,49},{33,1},{49,17},{2,34}... | collective-permute-start | bytes 1769480 | tf_op jit(solution)/shard_map/ppermute | solution.py:17
  164.7 28.0 %collective-permute-start.19 = (bf16[1,96,1536]{2,1,0:T(8,128)(2,1)S(1)}, bf16[1,96,1536]{2,1,0:T(8,128)(2,1)S(1)}, u32[]{:S(2)}, u32[]{:S(2)}) collective-permute-start(bf16[1,96,1536]{2,1,0:T(8,128)(2,1)S(1)} %bitcast.146), channel_id=1, source_target_pairs={{0,16},{16,32},{32,48},{48,0},{1,17},{17,33},{33,49},{49,1},{2,18}... | collective-permute-start | bytes 884744 | tf_op jit(solution)/shard_map/ppermute | solution.py:17
  170.3 29.7 %collective-permute-start.20 = (bf16[1,96,1536]{2,1,0:T(8,128)(2,1)S(1)}, bf16[1,96,1536]{2,1,0:T(8,128)(2,1)}, u32[]{:S(2)}, u32[]{:S(2)}) collective-permute-start(bf16[1,96,1536]{2,1,0:T(8,128)(2,1)S(1)} %bitcast.147), channel_id=1, source_target_pairs={{0,48},{16,0},{32,16},{48,32},{1,49},{17,1},{33,17},{49,33},{2,50}... | collective-permute-start | bytes 884744 | tf_op jit(solution)/shard_map/ppermute | solution.py:17
  175.2 27.9 %collective-permute-start.21 = (bf16[1,96,1536]{2,1,0:T(8,128)(2,1)S(1)}, bf16[1,96,1536]{2,1,0:T(8,128)(2,1)S(1)}, u32[]{:S(2)}, u32[]{:S(2)}) collective-permute-start(bf16[1,96,1536]{2,1,0:T(8,128)(2,1)S(1)} %bitcast.148), channel_id=1, source_target_pairs={{0,32},{16,48},{32,0},{48,16},{1,33},{17,49},{33,1},{49,17},{2,34}... | collective-permute-start | bytes 884744 | tf_op jit(solution)/shard_map/ppermute | solution.py:17
  220.8 1.7 copy-start
  222.6 8.7 %collective-permute-start.22 = (f32[4,2,192,256]{3,2,1,0:T(8,128)S(1)}, f32[4,2,192,256]{3,2,1,0:T(8,128)S(1)}, u32[]{:S(2)}, u32[]{:S(2)}) collective-permute-start(f32[4,2,192,256]{3,2,1,0:T(8,128)S(1)} %dynamic-slice_bitcast_fusion), channel_id=1, source_target_pairs={{0,1},{1,0},{2,3},{3,2},{4,5},{5,4},{6,7},{7,6},{8,9},{9,8},{10,11... | collective-permute-start | bytes 4718600 | tf_op jit(solution)/shard_map/ppermute | solution.py:17
  233.0 10.2 %collective-permute-start.25 = (bf16[2,192,256]{2,1,0:T(8,128)(2,1)S(1)}, bf16[2,192,256]{2,1,0:T(8,128)(2,1)S(1)}, u32[]{:S(2)}, u32[]{:S(2)}) collective-permute-start(bf16[2,192,256]{2,1,0:T(8,128)(2,1)S(1)} %get-tuple-element.8), channel_id=1, source_target_pairs={{0,4},{2,6},{4,0},{6,2},{1,5},{3,7},{5,1},{7,3},{8,12},{10,14},{12... | collective-permute-start | bytes 589832 | tf_op jit(solution)/shard_map/ppermute | solution.py:17
  237.9 9.2 %collective-permute-start.24 = (bf16[2,192,256]{2,1,0:T(8,128)(2,1)S(1)}, bf16[2,192,256]{2,1,0:T(8,128)(2,1)S(1)}, u32[]{:S(2)}, u32[]{:S(2)}) collective-permute-start(bf16[2,192,256]{2,1,0:T(8,128)(2,1)S(1)} %get-tuple-element.9), channel_id=1, source_target_pairs={{0,6},{2,0},{4,2},{6,4},{1,7},{3,1},{5,3},{7,5},{8,14},{10,8},{12,... | collective-permute-start | bytes 589832 | tf_op jit(solution)/shard_map/ppermute | solution.py:17
  240.5 8.6 %collective-permute-start.23 = (bf16[2,192,256]{2,1,0:T(8,128)(2,1)S(1)}, bf16[2,192,256]{2,1,0:T(8,128)(2,1)S(1)}, u32[]{:S(2)}, u32[]{:S(2)}) collective-permute-start(bf16[2,192,256]{2,1,0:T(8,128)(2,1)S(1)} %get-tuple-element.7), channel_id=1, source_target_pairs={{0,2},{2,4},{4,6},{6,0},{1,3},{3,5},{5,7},{7,1},{8,10},{10,12},{12... | collective-permute-start | bytes 589832 | tf_op jit(solution)/shard_map/ppermute | solution.py:17
  249.2 20.5 %collective-permute-start.26 = (bf16[192,256]{1,0:T(8,128)(2,1)S(1)}, bf16[192,256]{1,0:T(8,128)(2,1)S(1)}, u32[]{:S(2)}, u32[]{:S(2)}) collective-permute-start(bf16[192,256]{1,0:T(8,128)(2,1)S(1)} %fusion.49), channel_id=1, source_target_pairs={{0,8},{8,0},{1,9},{9,1},{2,10},{10,2},{3,11},{11,3},{4,12},{12,4},... | collective-permute-start | bytes 294920 | tf_op jit(solution)/shard_map/ppermute | solution.py:17
Sparse Core Ops, SparseCore 0:
  60.0 49.9 all-gather.2
  173.8 32.1 all-gather.4

commit v3 on v2

--- a/solution.py
+++ b/solution.py
@@ -19,7 +19,13 @@
 
 ring_up, ring_down = shift("zl", RING, 1), shift("zl", RING, -1)
 x_up, x_down, x_far = (shift("x", range(NX), s) for s in (1, -1, 2))
-y_up, y_down, y_far = (shift("y", range(NY), s) for s in (1, -1, 2))
+
+
+def flip(axis, n, bit):
+    return lambda v: lax.ppermute(v, axis, [(i, i ^ bit) for i in range(n)])
+
+
+y_near, y_far = flip("y", NY, 1), flip("y", NY, 2)
 other_half = shift("zh", range(NH), 1)
 other_core = shift("c", range(NC), 1)
 
@@ -33,11 +39,6 @@
     place = take(jnp.asarray(np.argsort(RING), jnp.int32), zl)
     ring = jnp.asarray(RING, jnp.int32)
 
-    fields = jnp.concatenate([tokens.T, tangent.T, cotangent.T], axis=1)
-    feat = fields.shape[0]
-    for axis in ("zh", "y", "c"):
-        fields = lax.all_gather(fields, axis, axis=0, tiled=True)
-
     own = jnp.concatenate([gate_weight, up_weight, down_weight.T], axis=1)
     rows, width = own.shape
     ups, downs = own, own
@@ -47,10 +48,25 @@
         groups.append(([ups, downs], [take(ring, (place - k) % NZ), take(ring, (place + k) % NZ)]))
     groups.append(([ring_up(ups)], [take(ring, (place + 4) % NZ)]))
 
+    fields = jnp.concatenate([tokens.T, tangent.T, cotangent.T], axis=1)
+    feat = fields.shape[0]
+
+    def join(v, send, bit):
+        got = send(v)
+        return jnp.concatenate([jnp.where(bit == 0, v, got), jnp.where(bit == 0, got, v)])
+
+    fields = join(fields, other_half, zh)
+    fields = join(fields, y_near, y % 2)
+    fields = join(fields, y_far, y // 2)
+    fields = join(fields, other_core, c)
+
     full = jnp.zeros((NZ * NX * rows, width), BF)
     for blocks, sources in groups:
         sent = jnp.stack(blocks)
-        for part, at in ((sent, x), (x_up(sent), x - 1), (x_down(sent), x + 1), (x_far(sent), x + 2)):
+        late = sent
+        if blocks[0] is own:
+            late, _ = lax.optimization_barrier((sent, groups[1][0]))
+        for part, at in ((sent, x), (x_up(sent), x - 1), (x_down(sent), x + 1), (x_far(late), x + 2)):
             at = at % NX
             for j, src in enumerate(sources):
                 first_row = ((((at // 2) * NY + src % NY) * NH + src // NY) * 2 + at % 2) * rows
@@ -81,11 +97,8 @@
     sums = sums.reshape(NC, NY, NH, feat, n_tok)
     sums = take(sums, c) + other_core(take(sums, 1 - c))
 
-    def to(step):
-        return take(sums, (y + step) % NY)
-
-    kept = to(0) + y_up(to(1).astype(BF)).astype(F32) + y_down(to(-1).astype(BF)).astype(F32)
-    kept = kept + y_far(to(2).astype(BF)).astype(F32)
+    shares = lax.all_to_all(sums.astype(BF), "y", 0, 0, tiled=True).astype(F32)
+    kept = jnp.sum(shares, axis=0)
     out = take(kept, zh) + other_half(take(kept, 1 - zh).astype(BF)).astype(F32)
     return out.T.astype(BF)
 

time: 279 us -> 237 us (0.85)
  the two profiles are of different devices: /device:TPU:135 before, /device:TPU:98 now
where the time goes in v3:
time: 237 us; the launch traced here: 236 us
  starting transfers between devices  112 us (47%)
  waiting for transfers between devices  49.9 us (21%)
  local copies, waits for them, and re-layouts  29.9 us (13%)
  between operations  23.9 us (10%)
  matrix products  13.3 us (6%)
  other arithmetic  6.38 us (3%)
    ppermute x26, starting transfers between devices, shift(): return lambda v: lax.ppermute(v, axis, pairs)  99.8 us
    ppermute x26, waiting for transfers between devices, shift(): return lambda v: lax.ppermute(v, axis, pairs)  37.1 us
    dynamic_update_slice x31, local copies, waits for them, and re-layouts, body(): full = lax.dynamic_update_slice(full, part[j], (first_row, 0))  23 us
    all_to_all x1, waiting for transfers between devices, body(): shares = lax.all_to_all(sums.astype(BF), 'y', 0, 0, tiled=True).astype(F32)  12.8 us
    ppermute x2, starting transfers between devices, flip(): return lambda v: lax.ppermute(v, axis, [(i, i ^ bit) for i in range(n)])  8.28 us
    dot_general x1, matrix products, body(): lax.dot_general(fields[:, :2 * n_tok], both, (((0,), (0,)), ((), ())), pr...  5.56 us
  transfers between devices with their start and end apart: 29, of which 6 were waited for; matrix products, arithmetic and copies ran while one was open for 11% of the time, Pallas kernels for 0%

profile of v3, /device:TPU:98, one launch (start us, length us, event | category | flops | bytes accessed | tf_op | source)
XLA Modules:
  0.0 235.7 jit_solution(14497549998119468719)
XLA Ops:
  0.1 4.2 %broadcast_in_dim.9 = bf16[3072,1536]{1,0:T(8,128)(2,1)} broadcast(bf16[]{:T(256)} %constant.517.clone.1), dimensions={} | broadcast | bytes 9437186 | tf_op jit(solution)/shard_map/broadcast_in_dim | solution.py:63
  4.4 0.8 pad_maximum_fusion.8
  5.2 3.4 %collective-permute-start = (bf16[1,96,1536]{2,1,0:T(8,128)(2,1)S(1)}, bf16[1,96,1536]{2,1,0:T(8,128)(2,1)S(1)}, u32[]{:S(2)}, u32[]{:S(2)}) collective-permute-start(bf16[1,96,1536]{2,1,0:T(8,128)(2,1)S(1)} %get-tuple-element.6), channel_id=1, source_target_pairs={{0,16},{16,32},{32,48},{48,0},{1,17},{17,33},{33,49},{49,1},{2,18}... | collective-permute-start | bytes 884744 | tf_op jit(solution)/shard_map/ppermute | solution.py:17
  8.6 2.4 %collective-permute-start.1 = (bf16[1,96,1536]{2,1,0:T(8,128)(2,1)S(1)}, bf16[1,96,1536]{2,1,0:T(8,128)(2,1)S(1)}, u32[]{:S(2)}, u32[]{:S(2)}) collective-permute-start(bf16[1,96,1536]{2,1,0:T(8,128)(2,1)S(1)} %get-tuple-element.6), channel_id=1, source_target_pairs={{0,48},{16,0},{32,16},{48,32},{1,49},{17,1},{33,17},{49,33},{2,50}... | collective-permute-start | bytes 884744 | tf_op jit(solution)/shard_map/ppermute | solution.py:17
  11.1 1.9 collective-permute-start.2
  13.0 6.4 %collective-permute-start.3 = (bf16[96,1536]{1,0:T(8,128)(2,1)S(1)}, bf16[96,1536]{1,0:T(8,128)(2,1)S(1)}, u32[]{:S(2)}, u32[]{:S(2)}) collective-permute-start(bf16[96,1536]{1,0:T(8,128)(2,1)S(1)} %get-tuple-element.17), channel_id=1, source_target_pairs={{0,64},{128,0},{256,128},{384,256},{448,384},{320,448},{192,320},{... | collective-permute-start | bytes 884744 | tf_op jit(solution)/shard_map/ppermute | solution.py:17
  19.4 12.7 %collective-permute-start.22 = (bf16[192,768]{1,0:T(8,128)(2,1)S(1)}, bf16[192,768]{1,0:T(8,128)(2,1)S(1)}, u32[]{:S(2)}, u32[]{:S(2)}) collective-permute-start(bf16[192,768]{1,0:T(8,128)(2,1)S(1)} %pad_maximum_fusion.9), channel_id=1, source_target_pairs={{0,8},{8,0},{1,9},{9,1},{2,10},{10,2},{3,11},{11,3},{4,12},{12,4},... | collective-permute-start | bytes 884744 | tf_op jit(solution)/shard_map/ppermute | solution.py:17
  56.9 3.4 %collective-permute-start.5 = (bf16[2,96,1536]{2,1,0:T(8,128)(2,1)S(1)}, bf16[2,96,1536]{2,1,0:T(8,128)(2,1)S(1)}, u32[]{:S(2)}, u32[]{:S(2)}) collective-permute-start(bf16[2,96,1536]{2,1,0:T(8,128)(2,1)S(1)} %pad_maximum_fusion.4), channel_id=1, source_target_pairs={{0,16},{16,32},{32,48},{48,0},{1,17},{17,33},{33,49},{49,1},{2,18}... | collective-permute-start | bytes 1769480 | tf_op jit(solution)/shard_map/ppermute | solution.py:17
  60.4 2.4 %collective-permute-start.6 = (bf16[2,96,1536]{2,1,0:T(8,128)(2,1)S(1)}, bf16[2,96,1536]{2,1,0:T(8,128)(2,1)S(1)}, u32[]{:S(2)}, u32[]{:S(2)}) collective-permute-start(bf16[2,96,1536]{2,1,0:T(8,128)(2,1)S(1)} %pad_maximum_fusion.4), channel_id=1, source_target_pairs={{0,48},{16,0},{32,16},{48,32},{1,49},{17,1},{33,17},{49,33},{2,50}... | collective-permute-start | bytes 1769480 | tf_op jit(solution)/shard_map/ppermute | solution.py:17
  62.8 4.0 %collective-permute-start.4 = (bf16[1,96,1536]{2,1,0:T(8,128)(2,1)S(1)}, bf16[1,96,1536]{2,1,0:T(8,128)(2,1)S(1)}, u32[]{:S(2)}, u32[]{:S(2)}) collective-permute-start(bf16[1,96,1536]{2,1,0:T(8,128)(2,1)S(1)} %get-tuple-element.6), channel_id=1, source_target_pairs={{0,32},{16,48},{32,0},{48,16},{1,33},{17,49},{33,1},{49,17},{2,34}... | collective-permute-start | bytes 884744 | tf_op jit(solution)/shard_map/ppermute | solution.py:17
  67.6 2.1 collective-permute-start.8
  69.7 0.8 bitcast_dynamic-update-slice_fusion.4
  70.5 5.8 %collective-permute-start.9 = (bf16[96,1536]{1,0:T(8,128)(2,1)S(1)}, bf16[96,1536]{1,0:T(8,128)(2,1)S(1)}, u32[]{:S(2)}, u32[]{:S(2)}) collective-permute-start(bf16[96,1536]{1,0:T(8,128)(2,1)S(1)} %collective-permute-done.3), channel_id=1, source_target_pairs={{0,64},{128,0},{256,128},{384,256},{448,384},{320,448},{192,320},{... | collective-permute-start | bytes 884744 | tf_op jit(solution)/shard_map/ppermute | solution.py:17
  76.5 8.1 %collective-permute-done.8 = bf16[96,1536]{1,0:T(8,128)(2,1)S(1)} collective-permute-done((bf16[96,1536]{1,0:T(8,128)(2,1)S(1)}, bf16[96,1536]{1,0:T(8,128)(2,1)S(1)}, u32[]{:S(2)}, u32[]{:S(2)}) %collective-permute-start.8) | collective-permute-done | bytes 294944 | tf_op jit(solution)/shard_map/ppermute | solution.py:17
  84.5 3.3 %collective-permute-start.7 = (bf16[2,96,1536]{2,1,0:T(8,128)(2,1)S(1)}, bf16[2,96,1536]{2,1,0:T(8,128)(2,1)S(1)}, u32[]{:S(2)}, u32[]{:S(2)}) collective-permute-start(bf16[2,96,1536]{2,1,0:T(8,128)(2,1)S(1)} %pad_maximum_fusion.4), channel_id=1, source_target_pairs={{0,32},{16,48},{32,0},{48,16},{1,33},{17,49},{33,1},{49,17},{2,34}... | collective-permute-start | bytes 1769480 | tf_op jit(solution)/shard_map/ppermute | solution.py:17
  87.9 3.5 %collective-permute-start.23 = (bf16[384,768]{1,0:T(8,128)(2,1)S(1)}, bf16[384,768]{1,0:T(8,128)(2,1)S(1)}, u32[]{:S(2)}, u32[]{:S(2)}) collective-permute-start(bf16[384,768]{1,0:T(8,128)(2,1)S(1)} %pad_maximum_fusion.7), channel_id=1, source_target_pairs={{0,2},{2,0},{4,6},{6,4},{1,3},{3,1},{5,7},{7,5},{8,10},{10,8},{12,... | collective-permute-start | bytes 1769480 | tf_op jit(solution)/shard_map/ppermute | solution.py:25
  91.4 3.4 %collective-permute-start.10 = (bf16[2,96,1536]{2,1,0:T(8,128)(2,1)S(1)}, bf16[2,96,1536]{2,1,0:T(8,128)(2,1)S(1)}, u32[]{:S(2)}, u32[]{:S(2)}) collective-permute-start(bf16[2,96,1536]{2,1,0:T(8,128)(2,1)S(1)} %pad_maximum_fusion.5), channel_id=1, source_target_pairs={{0,16},{16,32},{32,48},{48,0},{1,17},{17,33},{33,49},{49,1},{2,18}... | collective-permute-start | bytes 1769480 | tf_op jit(solution)/shard_map/ppermute | solution.py:17
  94.9 0.8 bitcast_dynamic-update-slice_fusion.3
  97.1 1.9 collective-permute-start.13
  100.5 6.0 %collective-permute-start.14 = (bf16[96,1536]{1,0:T(8,128)(2,1)S(1)}, bf16[96,1536]{1,0:T(8,128)(2,1)S(1)}, u32[]{:S(2)}, u32[]{:S(2)}) collective-permute-start(bf16[96,1536]{1,0:T(8,128)(2,1)S(1)} %collective-permute-done.9), channel_id=1, source_target_pairs={{0,64},{128,0},{256,128},{384,256},{448,384},{320,448},{192,320},{... | collective-permute-start | bytes 884744 | tf_op jit(solution)/shard_map/ppermute | solution.py:17
  107.3 5.8 %collective-permute-done.13 = bf16[96,1536]{1,0:T(8,128)(2,1)S(1)} collective-permute-done((bf16[96,1536]{1,0:T(8,128)(2,1)S(1)}, bf16[96,1536]{1,0:T(8,128)(2,1)S(1)}, u32[]{:S(2)}, u32[]{:S(2)}) %collective-permute-start.13) | collective-permute-done | bytes 294944 | tf_op jit(solution)/shard_map/ppermute | solution.py:17
  113.1 1.9 collective-permute-start.11
  115.0 3.9 %collective-permute-start.12 = (bf16[2,96,1536]{2,1,0:T(8,128)(2,1)S(1)}, bf16[2,96,1536]{2,1,0:T(8,128)(2,1)S(1)}, u32[]{:S(2)}, u32[]{:S(2)}) collective-permute-start(bf16[2,96,1536]{2,1,0:T(8,128)(2,1)S(1)} %pad_maximum_fusion.5), channel_id=1, source_target_pairs={{0,32},{16,48},{32,0},{48,16},{1,33},{17,49},{33,1},{49,17},{2,34}... | collective-permute-start | bytes 1769480 | tf_op jit(solution)/shard_map/ppermute | solution.py:17
  119.8 4.0 %collective-permute-start.15 = (bf16[2,96,1536]{2,1,0:T(8,128)(2,1)S(1)}, bf16[2,96,1536]{2,1,0:T(8,128)(2,1)S(1)}, u32[]{:S(2)}, u32[]{:S(2)}) collective-permute-start(bf16[2,96,1536]{2,1,0:T(8,128)(2,1)S(1)} %pad_maximum_fusion.6), channel_id=1, source_target_pairs={{0,16},{16,32},{32,48},{48,0},{1,17},{17,33},{33,49},{49,1},{2,18}... | collective-permute-start | bytes 1769480 | tf_op jit(solution)/shard_map/ppermute | solution.py:17
  125.2 1.9 collective-permute-start.16
  128.9 4.0 %collective-permute-start.17 = (bf16[2,96,1536]{2,1,0:T(8,128)(2,1)S(1)}, bf16[2,96,1536]{2,1,0:T(8,128)(2,1)S(1)}, u32[]{:S(2)}, u32[]{:S(2)}) collective-permute-start(bf16[2,96,1536]{2,1,0:T(8,128)(2,1)S(1)} %pad_maximum_fusion.6), channel_id=1, source_target_pairs={{0,32},{16,48},{32,0},{48,16},{1,33},{17,49},{33,1},{49,17},{2,34}... | collective-permute-start | bytes 1769480 | tf_op jit(solution)/shard_map/ppermute | solution.py:17
  132.9 0.8 fusion.38
  134.4 1.9 collective-permute-start.18
  137.8 5.1 %collective-permute-done.12 = bf16[2,96,1536]{2,1,0:T(8,128)(2,1)S(1)} collective-permute-done((bf16[2,96,1536]{2,1,0:T(8,128)(2,1)S(1)}, bf16[2,96,1536]{2,1,0:T(8,128)(2,1)S(1)}, u32[]{:S(2)}, u32[]{:S(2)}) %collective-permute-start.12) | collective-permute-done | bytes 589856 | tf_op jit(solution)/shard_map/ppermute | solution.py:17
  142.9 4.8 %collective-permute-start.24 = (bf16[768,768]{1,0:T(8,128)(2,1)S(1)}, bf16[768,768]{1,0:T(8,128)(2,1)S(1)}, u32[]{:S(2)}, u32[]{:S(2)}) collective-permute-start(bf16[768,768]{1,0:T(8,128)(2,1)S(1)} %pad_maximum_fusion.3), channel_id=1, source_target_pairs={{0,4},{2,6},{4,0},{6,2},{1,5},{3,7},{5,1},{7,3},{8,12},{10,14},{12... | collective-permute-start | bytes 3538952 | tf_op jit(solution)/shard_map/ppermute | solution.py:25
  147.7 1.9 collective-permute-start.19
  152.6 3.9 %collective-permute-start.20 = (bf16[1,96,1536]{2,1,0:T(8,128)(2,1)S(1)}, bf16[1,96,1536]{2,1,0:T(8,128)(2,1)S(1)}, u32[]{:S(2)}, u32[]{:S(2)}) collective-permute-start(bf16[1,96,1536]{2,1,0:T(8,128)(2,1)S(1)} %bitcast.143), channel_id=1, source_target_pairs={{0,48},{16,0},{32,16},{48,32},{1,49},{17,1},{33,17},{49,33},{2,50}... | collective-permute-start | bytes 884744 | tf_op jit(solution)/shard_map/ppermute | solution.py:17
  158.0 10.6 %collective-permute-start.21 = (bf16[1,96,1536]{2,1,0:T(8,128)(2,1)S(1)}, bf16[1,96,1536]{2,1,0:T(8,128)(2,1)S(1)}, u32[]{:S(2)}, u32[]{:S(2)}) collective-permute-start(bf16[1,96,1536]{2,1,0:T(8,128)(2,1)S(1)} %bitcast.144), channel_id=1, source_target_pairs={{0,32},{16,48},{32,0},{48,16},{1,33},{17,49},{33,1},{49,17},{2,34}... | collective-permute-start | bytes 884744 | tf_op jit(solution)/shard_map/ppermute | solution.py:17
  168.6 0.8 fusion.30
  170.8 2.1 collective-permute-start.25
  175.1 0.8 bitcast_dynamic-update-slice_fusion.2
  177.3 1.0 broadcast_select_fusion.1
  178.3 5.6 %fusion.2 = f32[512,1024]{1,0:T(8,128)S(1)} fusion(bf16[3072,1536]{1,0:T(8,128)(2,1)} %bitcast_dynamic-update-slice_fusion, bf16[1536,768]{1,0:T(8,128)(2,1)S(1)} %get-tuple-element.8, bf16[1536,768]{1,0:T(8,128)(2,1)S(1)} %get-tuple-element.7), kind=kOutput, calls=%fused_computation.2 | convolution fusion | flops 3227516928 | bytes 13107200 | tf_op jit(solution)/shard_map/dot_general | solution.py:78
  183.9 3.2 %fusion.23 = (bf16[256,512]{1,0:T(8,128)(2,1)S(1)}, bf16[256,512]{1,0:T(8,128)(2,1)S(1)}) fusion(f32[512,1024]{1,0:T(8,128)S(1)} %fusion.2, bf16[3072,1536]{1,0:T(8,128)(2,1)} %bitcast_dynamic-update-slice_fusion, bf16[1536,768]{1,0:T(8,128)(2,1)S(1)} %get-tuple-element.8, bf16[1536,768]{1,0:T(8,128)(2,1)S(1)} %get-tuple-element.7, ...), kind=kOutput, calls=%fused_computation.37 | convolution fusion | flops 811466752 | bytes 10486784 | tf_op jit(solution)/shard_map/dot_general | solution.py:81
  187.0 4.6 %fusion = f32[3072,256]{1,0:T(8,128)S(1)} fusion(bf16[3072,1536]{1,0:T(8,128)(2,1)} %bitcast_dynamic-update-slice_fusion, bf16[256,512]{1,0:T(8,128)(2,1)S(1)} %get-tuple-element.10, bf16[256,512]{1,0:T(8,128)(2,1)S(1)} %get-tuple-element.9), kind=kOutput, calls=%fused_computation | convolution fusion | flops 1611661312 | bytes 9961472 | tf_op jit(solution)/shard_map/dot_general | solution.py:95
  191.7 1.3 dynamic-slice_bitcast_fusion
  193.0 2.4 %collective-permute-start.26 = (f32[4,2,192,256]{3,2,1,0:T(8,128)}, f32[4,2,192,256]{3,2,1,0:T(8,128)}, u32[]{:S(2)}, u32[]{:S(2)}) collective-permute-start(f32[4,2,192,256]{3,2,1,0:T(8,128)} %dynamic-slice_bitcast_fusion), channel_id=1, source_target_pairs={{0,1},{1,0},{2,3},{3,2},{4,5},{5,4},{6,7},{7,6},{8,9},{9,8},{10,11... | collective-permute-start | bytes 4718600 | tf_op jit(solution)/shard_map/ppermute | solution.py:17
  195.4 3.4 %collective-permute-done.26 = f32[4,2,192,256]{3,2,1,0:T(8,128)} collective-permute-done((f32[4,2,192,256]{3,2,1,0:T(8,128)}, f32[4,2,192,256]{3,2,1,0:T(8,128)}, u32[]{:S(2)}, u32[]{:S(2)}) %collective-permute-start.26) | collective-permute-done | bytes 1572896 | tf_op jit(solution)/shard_map/ppermute | solution.py:17
  198.8 2.5 %fusion.10 = bf16[4,2,192,256]{3,2,1,0:T(8,128)(2,1)} fusion(f32[4,2,192,256]{3,2,1,0:T(8,128)} %collective-permute-done.26, f32[2,4,2,192,256]{4,3,2,1,0:T(8,128)S(1)} %bitcast.129, s32[]{:T(128)S(6)} %select_n.604), kind=kLoop, calls=%fused_computation.15 | loop fusion | flops 786432 | bytes 3932164 | tf_op jit(solution)/shard_map/convert_element_type | solution.py:100
  201.2 4.2 %all-to-all-start = ((bf16[4,2,192,256]{3,2,1,0:T(8,128)(2,1)}), bf16[4,2,192,256]{3,2,1,0:T(8,128)(2,1)S(1)}, u32[]{:S(2)}, u32[]{:S(2)}) async-start(bf16[4,2,192,256]{3,2,1,0:T(8,128)(2,1)} %fusion.10), calls=%async_computation | async-start | bytes 1572864 | tf_op jit(solution)/shard_map/all_to_all | solution.py:100
  205.4 12.8 %all-to-all-done = bf16[4,2,192,256]{3,2,1,0:T(8,128)(2,1)S(1)} async-done(((bf16[4,2,192,256]{3,2,1,0:T(8,128)(2,1)}), bf16[4,2,192,256]{3,2,1,0:T(8,128)(2,1)S(1)}, u32[]{:S(2)}, u32[]{:S(2)}) %all-to-all-start) | async-done | bytes 786464 | tf_op jit(solution)/shard_map/all_to_all | solution.py:100
  218.4 1.9 collective-permute-start.27
  220.3 14.7 %collective-permute-done.27 = bf16[192,256]{1,0:T(8,128)(2,1)S(1)} collective-permute-done((bf16[192,256]{1,0:T(8,128)(2,1)S(1)}, bf16[192,256]{1,0:T(8,128)(2,1)S(1)}, u32[]{:S(2)}, u32[]{:S(2)}) %collective-permute-start.27) | collective-permute-done | bytes 98336 | tf_op jit(solution)/shard_map/ppermute | solution.py:17
  (86 shorter events, 22.7 us)
Async XLA Ops:
  0.0 32.4 %copy-start.9 = (s32[8]{0:T(128)S(1)}, s32[8]{0:T(128)}, u32[]{:S(2)}) copy-start(s32[8]{0:T(128)} %constant.544.clone) | copy-start | bytes 100
  0.0 37.7 %copy-start.6 = (s32[8]{0:T(128)S(1)}, s32[8]{0:T(128)}, u32[]{:S(2)}) copy-start(s32[8]{0:T(128)} %constant.545.clone) | copy-start | bytes 100
  0.0 4.4 %copy-start.3 = (bf16[512,96]{0,1:T(8,128)(2,1)S(1)}, bf16[512,96]{0,1:T(8,128)(2,1)}, u32[]{:S(2)}) copy-start(bf16[512,96]{0,1:T(8,128)(2,1)} %param.17) | copy-start | bytes 294916
  0.0 4.4 %copy-start.4 = (bf16[96,512]{1,0:T(8,128)(2,1)S(1)}, bf16[96,512]{1,0:T(8,128)(2,1)}, u32[]{:S(2)}) copy-start(bf16[96,512]{1,0:T(8,128)(2,1)} %param.16) | copy-start | bytes 294916
  0.0 4.4 %copy-start.5 = (bf16[96,512]{1,0:T(8,128)(2,1)S(1)}, bf16[96,512]{1,0:T(8,128)(2,1)}, u32[]{:S(2)}) copy-start(bf16[96,512]{1,0:T(8,128)(2,1)} %param.15) | copy-start | bytes 294916
  0.0 19.3 %copy-start = (bf16[256,192]{0,1:T(8,128)(2,1)S(1)}, bf16[256,192]{0,1:T(8,128)(2,1)}, u32[]{:S(2)}) copy-start(bf16[256,192]{0,1:T(8,128)(2,1)} %param.12) | copy-start | bytes 294916
  0.0 19.3 %copy-start.1 = (bf16[256,192]{0,1:T(8,128)(2,1)S(1)}, bf16[256,192]{0,1:T(8,128)(2,1)}, u32[]{:S(2)}) copy-start(bf16[256,192]{0,1:T(8,128)(2,1)} %param.11) | copy-start | bytes 294916
  0.0 19.3 %copy-start.2 = (bf16[256,192]{0,1:T(8,128)(2,1)S(1)}, bf16[256,192]{0,1:T(8,128)(2,1)}, u32[]{:S(2)}) copy-start(bf16[256,192]{0,1:T(8,128)(2,1)} %param.10) | copy-start | bytes 294916
  0.1 32.1 %copy-start.8 = (s32[256]{0:T(256)S(1)}, s32[256]{0:T(256)}, u32[]{:S(2)}) copy-start(s32[256]{0:T(256)} %param.14) | copy-start | bytes 3076
  0.1 32.2 %copy-start.7 = (f32[256]{0:T(256)S(1)}, f32[256]{0:T(256)}, u32[]{:S(2)}) copy-start(f32[256]{0:T(256)} %param.13) | copy-start | bytes 3076
  5.2 57.6 %collective-permute-start = (bf16[1,96,1536]{2,1,0:T(8,128)(2,1)S(1)}, bf16[1,96,1536]{2,1,0:T(8,128)(2,1)S(1)}, u32[]{:S(2)}, u32[]{:S(2)}) collective-permute-start(bf16[1,96,1536]{2,1,0:T(8,128)(2,1)S(1)} %get-tuple-element.6), channel_id=1, source_target_pairs={{0,16},{16,32},{32,48},{48,0},{1,17},{17,33},{33,49},{49,1},{2,18}... | collective-permute-start | bytes 884744 | tf_op jit(solution)/shard_map/ppermute | solution.py:17
  8.6 59.0 %collective-permute-start.1 = (bf16[1,96,1536]{2,1,0:T(8,128)(2,1)S(1)}, bf16[1,96,1536]{2,1,0:T(8,128)(2,1)S(1)}, u32[]{:S(2)}, u32[]{:S(2)}) collective-permute-start(bf16[1,96,1536]{2,1,0:T(8,128)(2,1)S(1)} %get-tuple-element.6), channel_id=1, source_target_pairs={{0,48},{16,0},{32,16},{48,32},{1,49},{17,1},{33,17},{49,33},{2,50}... | collective-permute-start | bytes 884744 | tf_op jit(solution)/shard_map/ppermute | solution.py:17
  11.1 45.8 %collective-permute-start.2 = (bf16[96,1536]{1,0:T(8,128)(2,1)S(1)}, bf16[96,1536]{1,0:T(8,128)(2,1)S(1)}, u32[]{:S(2)}, u32[]{:S(2)}) collective-permute-start(bf16[96,1536]{1,0:T(8,128)(2,1)S(1)} %get-tuple-element.17), channel_id=1, source_target_pairs={{0,128},{128,256},{256,384},{384,448},{448,320},{320,192},{192,64}... | collective-permute-start | bytes 884744 | tf_op jit(solution)/shard_map/ppermute | solution.py:17
  13.0 43.9 %collective-permute-start.3 = (bf16[96,1536]{1,0:T(8,128)(2,1)S(1)}, bf16[96,1536]{1,0:T(8,128)(2,1)S(1)}, u32[]{:S(2)}, u32[]{:S(2)}) collective-permute-start(bf16[96,1536]{1,0:T(8,128)(2,1)S(1)} %get-tuple-element.17), channel_id=1, source_target_pairs={{0,64},{128,0},{256,128},{384,256},{448,384},{320,448},{192,320},{... | collective-permute-start | bytes 884744 | tf_op jit(solution)/shard_map/ppermute | solution.py:17
  19.4 51.1 %collective-permute-start.22 = (bf16[192,768]{1,0:T(8,128)(2,1)S(1)}, bf16[192,768]{1,0:T(8,128)(2,1)S(1)}, u32[]{:S(2)}, u32[]{:S(2)}) collective-permute-start(bf16[192,768]{1,0:T(8,128)(2,1)S(1)} %pad_maximum_fusion.9), channel_id=1, source_target_pairs={{0,8},{8,0},{1,9},{9,1},{2,10},{10,2},{3,11},{11,3},{4,12},{12,4},... | collective-permute-start | bytes 884744 | tf_op jit(solution)/shard_map/ppermute | solution.py:17
  56.9 40.2 %collective-permute-start.5 = (bf16[2,96,1536]{2,1,0:T(8,128)(2,1)S(1)}, bf16[2,96,1536]{2,1,0:T(8,128)(2,1)S(1)}, u32[]{:S(2)}, u32[]{:S(2)}) collective-permute-start(bf16[2,96,1536]{2,1,0:T(8,128)(2,1)S(1)} %pad_maximum_fusion.4), channel_id=1, source_target_pairs={{0,16},{16,32},{32,48},{48,0},{1,17},{17,33},{33,49},{49,1},{2,18}... | collective-permute-start | bytes 1769480 | tf_op jit(solution)/shard_map/ppermute | solution.py:17
  60.4 40.1 %collective-permute-start.6 = (bf16[2,96,1536]{2,1,0:T(8,128)(2,1)S(1)}, bf16[2,96,1536]{2,1,0:T(8,128)(2,1)S(1)}, u32[]{:S(2)}, u32[]{:S(2)}) collective-permute-start(bf16[2,96,1536]{2,1,0:T(8,128)(2,1)S(1)} %pad_maximum_fusion.4), channel_id=1, source_target_pairs={{0,48},{16,0},{32,16},{48,32},{1,49},{17,1},{33,17},{49,33},{2,50}... | collective-permute-start | bytes 1769480 | tf_op jit(solution)/shard_map/ppermute | solution.py:17
  62.8 28.6 %collective-permute-start.4 = (bf16[1,96,1536]{2,1,0:T(8,128)(2,1)S(1)}, bf16[1,96,1536]{2,1,0:T(8,128)(2,1)S(1)}, u32[]{:S(2)}, u32[]{:S(2)}) collective-permute-start(bf16[1,96,1536]{2,1,0:T(8,128)(2,1)S(1)} %get-tuple-element.6), channel_id=1, source_target_pairs={{0,32},{16,48},{32,0},{48,16},{1,33},{17,49},{33,1},{49,17},{2,34}... | collective-permute-start | bytes 884744 | tf_op jit(solution)/shard_map/ppermute | solution.py:17
  67.6 16.9 %collective-permute-start.8 = (bf16[96,1536]{1,0:T(8,128)(2,1)S(1)}, bf16[96,1536]{1,0:T(8,128)(2,1)S(1)}, u32[]{:S(2)}, u32[]{:S(2)}) collective-permute-start(bf16[96,1536]{1,0:T(8,128)(2,1)S(1)} %collective-permute-done.2), channel_id=1, source_target_pairs={{0,128},{128,256},{256,384},{384,448},{448,320},{320,192},{192,64}... | collective-permute-start | bytes 884744 | tf_op jit(solution)/shard_map/ppermute | solution.py:17
  70.5 17.4 %collective-permute-start.9 = (bf16[96,1536]{1,0:T(8,128)(2,1)S(1)}, bf16[96,1536]{1,0:T(8,128)(2,1)S(1)}, u32[]{:S(2)}, u32[]{:S(2)}) collective-permute-start(bf16[96,1536]{1,0:T(8,128)(2,1)S(1)} %collective-permute-done.3), channel_id=1, source_target_pairs={{0,64},{128,0},{256,128},{384,256},{448,384},{320,448},{192,320},{... | collective-permute-start | bytes 884744 | tf_op jit(solution)/shard_map/ppermute | solution.py:17
  84.5 35.2 %collective-permute-start.7 = (bf16[2,96,1536]{2,1,0:T(8,128)(2,1)S(1)}, bf16[2,96,1536]{2,1,0:T(8,128)(2,1)S(1)}, u32[]{:S(2)}, u32[]{:S(2)}) collective-permute-start(bf16[2,96,1536]{2,1,0:T(8,128)(2,1)S(1)} %pad_maximum_fusion.4), channel_id=1, source_target_pairs={{0,32},{16,48},{32,0},{48,16},{1,33},{17,49},{33,1},{49,17},{2,34}... | collective-permute-start | bytes 1769480 | tf_op jit(solution)/shard_map/ppermute | solution.py:17
  87.9 37.3 %collective-permute-start.23 = (bf16[384,768]{1,0:T(8,128)(2,1)S(1)}, bf16[384,768]{1,0:T(8,128)(2,1)S(1)}, u32[]{:S(2)}, u32[]{:S(2)}) collective-permute-start(bf16[384,768]{1,0:T(8,128)(2,1)S(1)} %pad_maximum_fusion.7), channel_id=1, source_target_pairs={{0,2},{2,0},{4,6},{6,4},{1,3},{3,1},{5,7},{7,5},{8,10},{10,8},{12,... | collective-permute-start | bytes 1769480 | tf_op jit(solution)/shard_map/ppermute | solution.py:25
  91.4 37.5 %collective-permute-start.10 = (bf16[2,96,1536]{2,1,0:T(8,128)(2,1)S(1)}, bf16[2,96,1536]{2,1,0:T(8,128)(2,1)S(1)}, u32[]{:S(2)}, u32[]{:S(2)}) collective-permute-start(bf16[2,96,1536]{2,1,0:T(8,128)(2,1)S(1)} %pad_maximum_fusion.5), channel_id=1, source_target_pairs={{0,16},{16,32},{32,48},{48,0},{1,17},{17,33},{33,49},{49,1},{2,18}... | collective-permute-start | bytes 1769480 | tf_op jit(solution)/shard_map/ppermute | solution.py:17
  97.1 16.0 %collective-permute-start.13 = (bf16[96,1536]{1,0:T(8,128)(2,1)S(1)}, bf16[96,1536]{1,0:T(8,128)(2,1)S(1)}, u32[]{:S(2)}, u32[]{:S(2)}) collective-permute-start(bf16[96,1536]{1,0:T(8,128)(2,1)S(1)} %collective-permute-done.8), channel_id=1, source_target_pairs={{0,128},{128,256},{256,384},{384,448},{448,320},{320,192},{192,64}... | collective-permute-start | bytes 884744 | tf_op jit(solution)/shard_map/ppermute | solution.py:17
  100.5 14.5 %collective-permute-start.14 = (bf16[96,1536]{1,0:T(8,128)(2,1)S(1)}, bf16[96,1536]{1,0:T(8,128)(2,1)S(1)}, u32[]{:S(2)}, u32[]{:S(2)}) collective-permute-start(bf16[96,1536]{1,0:T(8,128)(2,1)S(1)} %collective-permute-done.9), channel_id=1, source_target_pairs={{0,64},{128,0},{256,128},{384,256},{448,384},{320,448},{192,320},{... | collective-permute-start | bytes 884744 | tf_op jit(solution)/shard_map/ppermute | solution.py:17
  113.1 21.3 %collective-permute-start.11 = (bf16[2,96,1536]{2,1,0:T(8,128)(2,1)S(1)}, bf16[2,96,1536]{2,1,0:T(8,128)(2,1)S(1)}, u32[]{:S(2)}, u32[]{:S(2)}) collective-permute-start(bf16[2,96,1536]{2,1,0:T(8,128)(2,1)S(1)} %pad_maximum_fusion.5), channel_id=1, source_target_pairs={{0,48},{16,0},{32,16},{48,32},{1,49},{17,1},{33,17},{49,33},{2,50}... | collective-permute-start | bytes 1769480 | tf_op jit(solution)/shard_map/ppermute | solution.py:17
  115.0 27.9 %collective-permute-start.12 = (bf16[2,96,1536]{2,1,0:T(8,128)(2,1)S(1)}, bf16[2,96,1536]{2,1,0:T(8,128)(2,1)S(1)}, u32[]{:S(2)}, u32[]{:S(2)}) collective-permute-start(bf16[2,96,1536]{2,1,0:T(8,128)(2,1)S(1)} %pad_maximum_fusion.5), channel_id=1, source_target_pairs={{0,32},{16,48},{32,0},{48,16},{1,33},{17,49},{33,1},{49,17},{2,34}... | collective-permute-start | bytes 1769480 | tf_op jit(solution)/shard_map/ppermute | solution.py:17
  119.8 32.8 %collective-permute-start.15 = (bf16[2,96,1536]{2,1,0:T(8,128)(2,1)S(1)}, bf16[2,96,1536]{2,1,0:T(8,128)(2,1)S(1)}, u32[]{:S(2)}, u32[]{:S(2)}) collective-permute-start(bf16[2,96,1536]{2,1,0:T(8,128)(2,1)S(1)} %pad_maximum_fusion.6), channel_id=1, source_target_pairs={{0,16},{16,32},{32,48},{48,0},{1,17},{17,33},{33,49},{49,1},{2,18}... | collective-permute-start | bytes 1769480 | tf_op jit(solution)/shard_map/ppermute | solution.py:17
  125.2 32.8 %collective-permute-start.16 = (bf16[2,96,1536]{2,1,0:T(8,128)(2,1)S(1)}, bf16[2,96,1536]{2,1,0:T(8,128)(2,1)S(1)}, u32[]{:S(2)}, u32[]{:S(2)}) collective-permute-start(bf16[2,96,1536]{2,1,0:T(8,128)(2,1)S(1)} %pad_maximum_fusion.6), channel_id=1, source_target_pairs={{0,48},{16,0},{32,16},{48,32},{1,49},{17,1},{33,17},{49,33},{2,50}... | collective-permute-start | bytes 1769480 | tf_op jit(solution)/shard_map/ppermute | solution.py:17
  128.9 44.0 %collective-permute-start.17 = (bf16[2,96,1536]{2,1,0:T(8,128)(2,1)S(1)}, bf16[2,96,1536]{2,1,0:T(8,128)(2,1)S(1)}, u32[]{:S(2)}, u32[]{:S(2)}) collective-permute-start(bf16[2,96,1536]{2,1,0:T(8,128)(2,1)S(1)} %pad_maximum_fusion.6), channel_id=1, source_target_pairs={{0,32},{16,48},{32,0},{48,16},{1,33},{17,49},{33,1},{49,17},{2,34}... | collective-permute-start | bytes 1769480 | tf_op jit(solution)/shard_map/ppermute | solution.py:17
  134.4 13.3 %collective-permute-start.18 = (bf16[96,1536]{1,0:T(8,128)(2,1)S(1)}, bf16[96,1536]{1,0:T(8,128)(2,1)S(1)}, u32[]{:S(2)}, u32[]{:S(2)}) collective-permute-start(bf16[96,1536]{1,0:T(8,128)(2,1)S(1)} %collective-permute-done.13), channel_id=1, source_target_pairs={{0,128},{128,256},{256,384},{384,448},{448,320},{320,192},{192,64}... | collective-permute-start | bytes 884744 | tf_op jit(solution)/shard_map/ppermute | solution.py:17
  142.9 27.2 %collective-permute-start.24 = (bf16[768,768]{1,0:T(8,128)(2,1)S(1)}, bf16[768,768]{1,0:T(8,128)(2,1)S(1)}, u32[]{:S(2)}, u32[]{:S(2)}) collective-permute-start(bf16[768,768]{1,0:T(8,128)(2,1)S(1)} %pad_maximum_fusion.3), channel_id=1, source_target_pairs={{0,4},{2,6},{4,0},{6,2},{1,5},{3,7},{5,1},{7,3},{8,12},{10,14},{12... | collective-permute-start | bytes 3538952 | tf_op jit(solution)/shard_map/ppermute | solution.py:25
  147.7 27.4 %collective-permute-start.19 = (bf16[1,96,1536]{2,1,0:T(8,128)(2,1)S(1)}, bf16[1,96,1536]{2,1,0:T(8,128)(2,1)S(1)}, u32[]{:S(2)}, u32[]{:S(2)}) collective-permute-start(bf16[1,96,1536]{2,1,0:T(8,128)(2,1)S(1)} %bitcast.142), channel_id=1, source_target_pairs={{0,16},{16,32},{32,48},{48,0},{1,17},{17,33},{33,49},{49,1},{2,18}... | collective-permute-start | bytes 884744 | tf_op jit(solution)/shard_map/ppermute | solution.py:17
  152.6 23.3 %collective-permute-start.20 = (bf16[1,96,1536]{2,1,0:T(8,128)(2,1)S(1)}, bf16[1,96,1536]{2,1,0:T(8,128)(2,1)S(1)}, u32[]{:S(2)}, u32[]{:S(2)}) collective-permute-start(bf16[1,96,1536]{2,1,0:T(8,128)(2,1)S(1)} %bitcast.143), channel_id=1, source_target_pairs={{0,48},{16,0},{32,16},{48,32},{1,49},{17,1},{33,17},{49,33},{2,50}... | collective-permute-start | bytes 884744 | tf_op jit(solution)/shard_map/ppermute | solution.py:17
  158.0 18.6 %collective-permute-start.21 = (bf16[1,96,1536]{2,1,0:T(8,128)(2,1)S(1)}, bf16[1,96,1536]{2,1,0:T(8,128)(2,1)S(1)}, u32[]{:S(2)}, u32[]{:S(2)}) collective-permute-start(bf16[1,96,1536]{2,1,0:T(8,128)(2,1)S(1)} %bitcast.144), channel_id=1, source_target_pairs={{0,32},{16,48},{32,0},{48,16},{1,33},{17,49},{33,1},{49,17},{2,34}... | collective-permute-start | bytes 884744 | tf_op jit(solution)/shard_map/ppermute | solution.py:17
  170.8 6.6 %collective-permute-start.25 = (bf16[1536,768]{1,0:T(8,128)(2,1)S(1)}, bf16[1536,768]{1,0:T(8,128)(2,1)S(1)}, u32[]{:S(2)}, u32[]{:S(2)}) collective-permute-start(bf16[1536,768]{1,0:T(8,128)(2,1)S(1)} %pad_maximum_fusion.2), channel_id=1, source_target_pairs={{0,1},{1,0},{2,3},{3,2},{4,5},{5,4},{6,7},{7,6},{8,9},{9,8},{10,11... | collective-permute-start | bytes 7077896 | tf_op jit(solution)/shard_map/ppermute | solution.py:17
  193.0 5.8 %collective-permute-start.26 = (f32[4,2,192,256]{3,2,1,0:T(8,128)}, f32[4,2,192,256]{3,2,1,0:T(8,128)}, u32[]{:S(2)}, u32[]{:S(2)}) collective-permute-start(f32[4,2,192,256]{3,2,1,0:T(8,128)} %dynamic-slice_bitcast_fusion), channel_id=1, source_target_pairs={{0,1},{1,0},{2,3},{3,2},{4,5},{5,4},{6,7},{7,6},{8,9},{9,8},{10,11... | collective-permute-start | bytes 4718600 | tf_op jit(solution)/shard_map/ppermute | solution.py:17
  201.2 17.0 %all-to-all-start = ((bf16[4,2,192,256]{3,2,1,0:T(8,128)(2,1)}), bf16[4,2,192,256]{3,2,1,0:T(8,128)(2,1)S(1)}, u32[]{:S(2)}, u32[]{:S(2)}) async-start(bf16[4,2,192,256]{3,2,1,0:T(8,128)(2,1)} %fusion.10), calls=%async_computation | async-start | bytes 1572864 | tf_op jit(solution)/shard_map/all_to_all | solution.py:100
  218.4 16.7 %collective-permute-start.27 = (bf16[192,256]{1,0:T(8,128)(2,1)S(1)}, bf16[192,256]{1,0:T(8,128)(2,1)S(1)}, u32[]{:S(2)}, u32[]{:S(2)}) collective-permute-start(bf16[192,256]{1,0:T(8,128)(2,1)S(1)} %fusion.47), channel_id=1, source_target_pairs={{0,8},{8,0},{1,9},{9,1},{2,10},{10,2},{3,11},{11,3},{4,12},{12,4},... | collective-permute-start | bytes 294920 | tf_op jit(solution)/shard_map/ppermute | solution.py:17

commit v4 on v3

--- a/solution.py
+++ b/solution.py
@@ -9,6 +9,10 @@
 F32 = jnp.float32
 NZ, NX, NH, NY, NC = 8, 4, 2, 4, 2
 RING = (0, 2, 4, 6, 7, 5, 3, 1)
+STEPS = (0, -1, 1, -2, 2, -3, 3, -4)
+SOURCES = np.array(
+    [sum(RING[(RING.index(z) + s) % NZ] << 3 * j for j, s in enumerate(STEPS)) for z in range(NZ)], np.uint32
+)
 
 
 def shift(axis, order, step):
@@ -35,18 +39,17 @@
 
 
 def body(tokens, tangent, cotangent, gates, slot_tokens, gate_weight, up_weight, down_weight):
-    zl, x, zh, y, c = (lax.axis_index(a) for a in ("zl", "x", "zh", "y", "c"))
-    place = take(jnp.asarray(np.argsort(RING), jnp.int32), zl)
-    ring = jnp.asarray(RING, jnp.int32)
+    zl, x, zh, y, c = (lax.axis_index(a).astype(jnp.uint32) for a in ("zl", "x", "zh", "y", "c"))
+    packed = take(jnp.asarray(SOURCES), zl)
 
     own = jnp.concatenate([gate_weight, up_weight, down_weight.T], axis=1)
     rows, width = own.shape
     ups, downs = own, own
-    groups = [([own], [zl])]
-    for k in (1, 2, 3):
+    groups = [[own]]
+    for _ in range(3):
         ups, downs = ring_up(ups), ring_down(downs)
-        groups.append(([ups, downs], [take(ring, (place - k) % NZ), take(ring, (place + k) % NZ)]))
-    groups.append(([ring_up(ups)], [take(ring, (place + 4) % NZ)]))
+        groups.append([ups, downs])
+    groups.append([ring_up(ups)])
 
     fields = jnp.concatenate([tokens.T, tangent.T, cotangent.T], axis=1)
     feat = fields.shape[0]
@@ -56,21 +59,27 @@
         return jnp.concatenate([jnp.where(bit == 0, v, got), jnp.where(bit == 0, got, v)])
 
     fields = join(fields, other_half, zh)
-    fields = join(fields, y_near, y % 2)
-    fields = join(fields, y_far, y // 2)
+    fields = join(fields, y_near, y & 1)
+    fields = join(fields, y_far, y >> 1)
     fields = join(fields, other_core, c)
 
-    full = jnp.zeros((NZ * NX * rows, width), BF)
-    for blocks, sources in groups:
+    zero = groups[2][0][0, 0] * 0
+    full = jnp.broadcast_to(zero, (NC, NY, NH, 2, rows, width))
+    none = jnp.uint32(0)
+    sources = iter((((packed >> 3 * j) & 3, (packed >> 3 * j + 2) & 1) for j in range(NZ)))
+    for blocks in groups:
         sent = jnp.stack(blocks)
         late = sent
         if blocks[0] is own:
             late, _ = lax.optimization_barrier((sent, groups[1][0]))
-        for part, at in ((sent, x), (x_up(sent), x - 1), (x_down(sent), x + 1), (x_far(late), x + 2)):
-            at = at % NX
-            for j, src in enumerate(sources):
-                first_row = ((((at // 2) * NY + src % NY) * NH + src // NY) * 2 + at % 2) * rows
-                full = lax.dynamic_update_slice(full, part[j], (first_row, 0))
+        parts = (sent, x_down(sent), x_far(late), x_up(sent))
+        at = [next(sources) for _ in blocks]
+        for step, part in enumerate(parts):
+            col = x + step
+            for j, (row, far) in enumerate(at):
+                where = ((col >> 1) & 1, row, far, col & 1, none, none)
+                full = lax.dynamic_update_slice(full, part[j][None, None, None, None], where)
+    full = full.reshape(NZ * NX * rows, width)
 
     n_tok = tokens.shape[0]
     ff = gate_weight.shape[1]

time: 237 us -> 244 us (1.030)
  the two profiles are of different devices: /device:TPU:98 before, /device:TPU:96 now
where the time goes in v4:
time: 244 us; the launch traced here: 243 us
  waiting for transfers between devices  108 us (44%)
  starting transfers between devices  104 us (43%)
  between operations  11.8 us (5%)
  other arithmetic  8.72 us (4%)
  matrix products  6.51 us (3%)
  local copies, waits for them, and re-layouts  3.9 us (2%)
    ppermute x26, starting transfers between devices, shift(): return lambda v: lax.ppermute(v, axis, pairs)  91.3 us
    ppermute x26, waiting for transfers between devices, shift(): return lambda v: lax.ppermute(v, axis, pairs)  83.2 us
    all_to_all x1, waiting for transfers between devices, body(): shares = lax.all_to_all(sums.astype(BF), 'y', 0, 0, tiled=True).astype(F32)  12.6 us
    ppermute x2, waiting for transfers between devices, flip(): return lambda v: lax.ppermute(v, axis, [(i, i ^ bit) for i in range(n)])  12.5 us
    ppermute x2, starting transfers between devices, flip(): return lambda v: lax.ppermute(v, axis, [(i, i ^ bit) for i in range(n)])  8.27 us
  transfers between devices with their start and end apart: 29, of which 13 were waited for; matrix products, arithmetic and copies ran while one was open for 3% of the time, Pallas kernels for 0%

profile of v4, /device:TPU:96, one launch (start us, length us, event | category | flops | bytes accessed | tf_op | source)
XLA Modules:
  0.0 243.0 jit_solution(17252876097650964346)
XLA Ops:
  0.0 1.1 fusion.52
  1.1 4.7 %collective-permute-start.2 = (bf16[1,96,1536]{2,1,0:T(8,128)(2,1)S(1)}, bf16[1,96,1536]{2,1,0:T(8,128)(2,1)S(1)}, u32[]{:S(2)}, u32[]{:S(2)}) collective-permute-start(bf16[1,96,1536]{2,1,0:T(8,128)(2,1)S(1)} %get-tuple-element.6), channel_id=1, source_target_pairs={{0,48},{16,0},{32,16},{48,32},{1,49},{17,1},{33,17},{49,33},{2,50}... | collective-permute-start | bytes 884744 | tf_op jit(solution)/shard_map/ppermute | solution.py:21
  5.8 1.9 collective-permute-start.4
  7.7 1.9 collective-permute-start
  9.6 6.4 %collective-permute-start.5 = (bf16[96,1536]{1,0:T(8,128)(2,1)S(1)}, bf16[96,1536]{1,0:T(8,128)(2,1)S(1)}, u32[]{:S(2)}, u32[]{:S(2)}) collective-permute-start(bf16[96,1536]{1,0:T(8,128)(2,1)S(1)} %get-tuple-element.18), channel_id=1, source_target_pairs={{0,64},{128,0},{256,128},{384,256},{448,384},{320,448},{192,320},{... | collective-permute-start | bytes 884744 | tf_op jit(solution)/shard_map/ppermute | solution.py:21
  17.0 12.7 %collective-permute-start.22 = (bf16[192,768]{1,0:T(8,128)(2,1)S(1)}, bf16[192,768]{1,0:T(8,128)(2,1)S(1)}, u32[]{:S(2)}, u32[]{:S(2)}) collective-permute-start(bf16[192,768]{1,0:T(8,128)(2,1)S(1)} %pad_maximum_fusion.9), channel_id=1, source_target_pairs={{0,8},{8,0},{1,9},{9,1},{2,10},{10,2},{3,11},{11,3},{4,12},{12,4},... | collective-permute-start | bytes 884744 | tf_op jit(solution)/shard_map/ppermute | solution.py:21
  31.2 1.2 dynamic_slice.18
  42.9 5.1 %collective-permute-start.6 = (bf16[2,96,1536]{2,1,0:T(8,128)(2,1)S(1)}, bf16[2,96,1536]{2,1,0:T(8,128)(2,1)S(1)}, u32[]{:S(2)}, u32[]{:S(2)}) collective-permute-start(bf16[2,96,1536]{2,1,0:T(8,128)(2,1)S(1)} %pad_maximum_fusion.4), channel_id=1, source_target_pairs={{0,48},{16,0},{32,16},{48,32},{1,49},{17,1},{33,17},{49,33},{2,50}... | collective-permute-start | bytes 1769480 | tf_op jit(solution)/shard_map/ppermute | solution.py:21
  48.0 1.9 collective-permute-start.7
  50.0 2.3 collective-permute-done.22
  52.3 1.9 collective-permute-start.1
  54.2 1.1 broadcast_select_fusion.7
  55.4 16.5 %collective-permute-done.1 = bf16[96,1536]{1,0:T(8,128)(2,1)S(1)} collective-permute-done((bf16[96,1536]{1,0:T(8,128)(2,1)S(1)}, bf16[96,1536]{1,0:T(8,128)(2,1)S(1)}, u32[]{:S(2)}, u32[]{:S(2)}) %collective-permute-start.1) | collective-permute-done | bytes 294944 | tf_op jit(solution)/shard_map/ppermute | solution.py:21
  71.9 2.3 collective-permute-start.8
  76.5 5.8 %collective-permute-start.3 = (bf16[1,96,1536]{2,1,0:T(8,128)(2,1)S(1)}, bf16[1,96,1536]{2,1,0:T(8,128)(2,1)S(1)}, u32[]{:S(2)}, u32[]{:S(2)}) collective-permute-start(bf16[1,96,1536]{2,1,0:T(8,128)(2,1)S(1)} %get-tuple-element.6), channel_id=1, source_target_pairs={{0,32},{16,48},{32,0},{48,16},{1,33},{17,49},{33,1},{49,17},{2,34}... | collective-permute-start | bytes 884744 | tf_op jit(solution)/shard_map/ppermute | solution.py:21
  82.4 14.4 %collective-permute-done.3 = bf16[1,96,1536]{2,1,0:T(8,128)(2,1)S(1)} collective-permute-done((bf16[1,96,1536]{2,1,0:T(8,128)(2,1)S(1)}, bf16[1,96,1536]{2,1,0:T(8,128)(2,1)S(1)}, u32[]{:S(2)}, u32[]{:S(2)}) %collective-permute-start.3) | collective-permute-done | bytes 294944 | tf_op jit(solution)/shard_map/ppermute | solution.py:21
  96.8 4.2 %collective-permute-start.9 = (bf16[96,1536]{1,0:T(8,128)(2,1)S(1)}, bf16[96,1536]{1,0:T(8,128)(2,1)S(1)}, u32[]{:S(2)}, u32[]{:S(2)}) collective-permute-start(bf16[96,1536]{1,0:T(8,128)(2,1)S(1)} %collective-permute-done.5), channel_id=1, source_target_pairs={{0,64},{128,0},{256,128},{384,256},{448,384},{320,448},{192,320},{... | collective-permute-start | bytes 884744 | tf_op jit(solution)/shard_map/ppermute | solution.py:21
  101.0 5.7 %collective-permute-done.9 = bf16[96,1536]{1,0:T(8,128)(2,1)S(1)} collective-permute-done((bf16[96,1536]{1,0:T(8,128)(2,1)S(1)}, bf16[96,1536]{1,0:T(8,128)(2,1)S(1)}, u32[]{:S(2)}, u32[]{:S(2)}) %collective-permute-start.9) | collective-permute-done | bytes 294944 | tf_op jit(solution)/shard_map/ppermute | solution.py:21
  106.7 3.5 %collective-permute-start.23 = (bf16[384,768]{1,0:T(8,128)(2,1)S(1)}, bf16[384,768]{1,0:T(8,128)(2,1)S(1)}, u32[]{:S(2)}, u32[]{:S(2)}) collective-permute-start(bf16[384,768]{1,0:T(8,128)(2,1)S(1)} %pad_maximum_fusion.7), channel_id=1, source_target_pairs={{0,2},{2,0},{4,6},{6,4},{1,3},{3,1},{5,7},{7,5},{8,10},{10,8},{12,... | collective-permute-start | bytes 1769480 | tf_op jit(solution)/shard_map/ppermute | solution.py:29
  110.2 1.9 collective-permute-start.10
  112.3 1.9 collective-permute-start.13
  114.3 6.0 %collective-permute-start.14 = (bf16[96,1536]{1,0:T(8,128)(2,1)S(1)}, bf16[96,1536]{1,0:T(8,128)(2,1)S(1)}, u32[]{:S(2)}, u32[]{:S(2)}) collective-permute-start(bf16[96,1536]{1,0:T(8,128)(2,1)S(1)} %collective-permute-done.9), channel_id=1, source_target_pairs={{0,64},{128,0},{256,128},{384,256},{448,384},{320,448},{192,320},{... | collective-permute-start | bytes 884744 | tf_op jit(solution)/shard_map/ppermute | solution.py:21
  120.4 5.8 %collective-permute-done.13 = bf16[96,1536]{1,0:T(8,128)(2,1)S(1)} collective-permute-done((bf16[96,1536]{1,0:T(8,128)(2,1)S(1)}, bf16[96,1536]{1,0:T(8,128)(2,1)S(1)}, u32[]{:S(2)}, u32[]{:S(2)}) %collective-permute-start.13) | collective-permute-done | bytes 294944 | tf_op jit(solution)/shard_map/ppermute | solution.py:21
  126.2 1.9 collective-permute-start.11
  128.5 3.6 %collective-permute-start.12 = (bf16[2,96,1536]{2,1,0:T(8,128)(2,1)S(1)}, bf16[2,96,1536]{2,1,0:T(8,128)(2,1)S(1)}, u32[]{:S(2)}, u32[]{:S(2)}) collective-permute-start(bf16[2,96,1536]{2,1,0:T(8,128)(2,1)S(1)} %pad_maximum_fusion.5), channel_id=1, source_target_pairs={{0,16},{16,32},{32,48},{48,0},{1,17},{17,33},{33,49},{49,1},{2,18}... | collective-permute-start | bytes 1769480 | tf_op jit(solution)/shard_map/ppermute | solution.py:21
  132.3 4.5 %collective-permute-start.15 = (bf16[2,96,1536]{2,1,0:T(8,128)(2,1)S(1)}, bf16[2,96,1536]{2,1,0:T(8,128)(2,1)S(1)}, u32[]{:S(2)}, u32[]{:S(2)}) collective-permute-start(bf16[2,96,1536]{2,1,0:T(8,128)(2,1)S(1)} %pad_maximum_fusion.6), channel_id=1, source_target_pairs={{0,48},{16,0},{32,16},{48,32},{1,49},{17,1},{33,17},{49,33},{2,50}... | collective-permute-start | bytes 1769480 | tf_op jit(solution)/shard_map/ppermute | solution.py:21
  136.8 3.4 %collective-permute-start.16 = (bf16[2,96,1536]{2,1,0:T(8,128)(2,1)S(1)}, bf16[2,96,1536]{2,1,0:T(8,128)(2,1)S(1)}, u32[]{:S(2)}, u32[]{:S(2)}) collective-permute-start(bf16[2,96,1536]{2,1,0:T(8,128)(2,1)S(1)} %pad_maximum_fusion.6), channel_id=1, source_target_pairs={{0,32},{16,48},{32,0},{48,16},{1,33},{17,49},{33,1},{49,17},{2,34}... | collective-permute-start | bytes 1769480 | tf_op jit(solution)/shard_map/ppermute | solution.py:21
  140.6 3.3 %collective-permute-start.17 = (bf16[2,96,1536]{2,1,0:T(8,128)(2,1)S(1)}, bf16[2,96,1536]{2,1,0:T(8,128)(2,1)S(1)}, u32[]{:S(2)}, u32[]{:S(2)}) collective-permute-start(bf16[2,96,1536]{2,1,0:T(8,128)(2,1)S(1)} %pad_maximum_fusion.6), channel_id=1, source_target_pairs={{0,16},{16,32},{32,48},{48,0},{1,17},{17,33},{33,49},{49,1},{2,18}... | collective-permute-start | bytes 1769480 | tf_op jit(solution)/shard_map/ppermute | solution.py:21
  144.0 1.8 collective-permute-done.11
  145.8 1.9 collective-permute-start.18
  147.8 13.8 %collective-permute-done.12 = bf16[2,96,1536]{2,1,0:T(8,128)(2,1)S(1)} collective-permute-done((bf16[2,96,1536]{2,1,0:T(8,128)(2,1)S(1)}, bf16[2,96,1536]{2,1,0:T(8,128)(2,1)S(1)}, u32[]{:S(2)}, u32[]{:S(2)}) %collective-permute-start.12) | collective-permute-done | bytes 589856 | tf_op jit(solution)/shard_map/ppermute | solution.py:21
  161.6 4.8 %collective-permute-start.24 = (bf16[768,768]{1,0:T(8,128)(2,1)S(1)}, bf16[768,768]{1,0:T(8,128)(2,1)S(1)}, u32[]{:S(2)}, u32[]{:S(2)}) collective-permute-start(bf16[768,768]{1,0:T(8,128)(2,1)S(1)} %pad_maximum_fusion.3), channel_id=1, source_target_pairs={{0,4},{2,6},{4,0},{6,2},{1,5},{3,7},{5,1},{7,3},{8,12},{10,14},{12... | collective-permute-start | bytes 3538952 | tf_op jit(solution)/shard_map/ppermute | solution.py:29
  166.4 1.9 collective-permute-start.19
  168.5 2.7 %collective-permute-start.20 = (bf16[1,96,1536]{2,1,0:T(8,128)(2,1)S(1)}, bf16[1,96,1536]{2,1,0:T(8,128)(2,1)S(1)}, u32[]{:S(2)}, u32[]{:S(2)}) collective-permute-start(bf16[1,96,1536]{2,1,0:T(8,128)(2,1)S(1)} %bitcast.168), channel_id=1, source_target_pairs={{0,32},{16,48},{32,0},{48,16},{1,33},{17,49},{33,1},{49,17},{2,34}... | collective-permute-start | bytes 884744 | tf_op jit(solution)/shard_map/ppermute | solution.py:21
  171.3 3.3 %collective-permute-start.21 = (bf16[1,96,1536]{2,1,0:T(8,128)(2,1)S(1)}, bf16[1,96,1536]{2,1,0:T(8,128)(2,1)S(1)}, u32[]{:S(2)}, u32[]{:S(2)}) collective-permute-start(bf16[1,96,1536]{2,1,0:T(8,128)(2,1)S(1)} %bitcast.169), channel_id=1, source_target_pairs={{0,16},{16,32},{32,48},{48,0},{1,17},{17,33},{33,49},{49,1},{2,18}... | collective-permute-start | bytes 884744 | tf_op jit(solution)/shard_map/ppermute | solution.py:21
  174.7 12.5 %collective-permute-done.24 = bf16[768,768]{1,0:T(8,128)(2,1)S(1)} collective-permute-done((bf16[768,768]{1,0:T(8,128)(2,1)S(1)}, bf16[768,768]{1,0:T(8,128)(2,1)S(1)}, u32[]{:S(2)}, u32[]{:S(2)}) %collective-permute-start.24) | collective-permute-done | bytes 1179680 | tf_op jit(solution)/shard_map/ppermute | solution.py:29
  187.9 2.1 collective-permute-start.25
  190.2 4.1 %collective-permute-done.25 = bf16[1536,768]{1,0:T(8,128)(2,1)S(1)} collective-permute-done((bf16[1536,768]{1,0:T(8,128)(2,1)S(1)}, bf16[1536,768]{1,0:T(8,128)(2,1)S(1)}, u32[]{:S(2)}, u32[]{:S(2)}) %collective-permute-start.25) | collective-permute-done | bytes 2359328 | tf_op jit(solution)/shard_map/ppermute | solution.py:21
  195.3 3.4 %fusion.2 = f32[512,1024]{1,0:T(8,128)S(1)} fusion(bf16[3072,1536]{1,0:T(8,128)(2,1)S(1)} %bitcast.148, bf16[1536,768]{1,0:T(8,128)(2,1)S(1)} %get-tuple-element.8, bf16[1536,768]{1,0:T(8,128)(2,1)S(1)} %get-tuple-element.7), kind=kOutput, calls=%fused_computation.2 | convolution fusion | flops 3227516928 | bytes 13107200 | tf_op jit(solution)/shard_map/dot_general | solution.py:87
  198.7 1.3 fusion.23
  200.0 1.8 fusion
  202.0 2.0 collective-permute-start.26
  204.0 3.3 %collective-permute-done.26 = f32[4,2,192,256]{3,2,1,0:T(8,128)S(1)} collective-permute-done((f32[4,2,192,256]{3,2,1,0:T(8,128)S(1)}, f32[4,2,192,256]{3,2,1,0:T(8,128)S(1)}, u32[]{:S(2)}, u32[]{:S(2)}) %collective-permute-start.26) | collective-permute-done | bytes 1572896 | tf_op jit(solution)/shard_map/ppermute | solution.py:21
  207.3 1.1 fusion.10
  208.4 4.2 %all-to-all-start = ((bf16[4,2,192,256]{3,2,1,0:T(8,128)(2,1)}), bf16[4,2,192,256]{3,2,1,0:T(8,128)(2,1)S(1)}, u32[]{:S(2)}, u32[]{:S(2)}) async-start(bf16[4,2,192,256]{3,2,1,0:T(8,128)(2,1)} %fusion.10), calls=%async_computation | async-start | bytes 1572864 | tf_op jit(solution)/shard_map/all_to_all | solution.py:109
  212.6 12.6 %all-to-all-done = bf16[4,2,192,256]{3,2,1,0:T(8,128)(2,1)S(1)} async-done(((bf16[4,2,192,256]{3,2,1,0:T(8,128)(2,1)}), bf16[4,2,192,256]{3,2,1,0:T(8,128)(2,1)S(1)}, u32[]{:S(2)}, u32[]{:S(2)}) %all-to-all-start) | async-done | bytes 786464 | tf_op jit(solution)/shard_map/all_to_all | solution.py:109
  225.3 1.9 collective-permute-start.27
  227.3 15.1 %collective-permute-done.27 = bf16[192,256]{1,0:T(8,128)(2,1)S(1)} collective-permute-done((bf16[192,256]{1,0:T(8,128)(2,1)S(1)}, bf16[192,256]{1,0:T(8,128)(2,1)S(1)}, u32[]{:S(2)}, u32[]{:S(2)}) %collective-permute-start.27) | collective-permute-done | bytes 98336 | tf_op jit(solution)/shard_map/ppermute | solution.py:21
  (73 shorter events, 8.6 us)
Async XLA Ops:
  0.0 76.4 %copy-start = (bf16[512,96]{0,1:T(8,128)(2,1)S(1)}, bf16[512,96]{0,1:T(8,128)(2,1)}, u32[]{:S(2)}) copy-start(bf16[512,96]{0,1:T(8,128)(2,1)} %param.16) | copy-start | bytes 294916
  0.0 76.4 %copy-start.2 = (bf16[96,512]{1,0:T(8,128)(2,1)S(1)}, bf16[96,512]{1,0:T(8,128)(2,1)}, u32[]{:S(2)}) copy-start(bf16[96,512]{1,0:T(8,128)(2,1)} %param.14) | copy-start | bytes 294916
  0.0 76.4 %copy-start.1 = (bf16[96,512]{1,0:T(8,128)(2,1)S(1)}, bf16[96,512]{1,0:T(8,128)(2,1)}, u32[]{:S(2)}) copy-start(bf16[96,512]{1,0:T(8,128)(2,1)} %param.15) | copy-start | bytes 294916
  1.1 75.4 %collective-permute-start.2 = (bf16[1,96,1536]{2,1,0:T(8,128)(2,1)S(1)}, bf16[1,96,1536]{2,1,0:T(8,128)(2,1)S(1)}, u32[]{:S(2)}, u32[]{:S(2)}) collective-permute-start(bf16[1,96,1536]{2,1,0:T(8,128)(2,1)S(1)} %get-tuple-element.6), channel_id=1, source_target_pairs={{0,48},{16,0},{32,16},{48,32},{1,49},{17,1},{33,17},{49,33},{2,50}... | collective-permute-start | bytes 884744 | tf_op jit(solution)/shard_map/ppermute | solution.py:21
  5.8 104.5 %collective-permute-start.4 = (bf16[1,96,1536]{2,1,0:T(8,128)(2,1)S(1)}, bf16[1,96,1536]{2,1,0:T(8,128)(2,1)S(1)}, u32[]{:S(2)}, u32[]{:S(2)}) collective-permute-start(bf16[1,96,1536]{2,1,0:T(8,128)(2,1)S(1)} %get-tuple-element.6), channel_id=1, source_target_pairs={{0,16},{16,32},{32,48},{48,0},{1,17},{17,33},{33,49},{49,1},{2,18}... | collective-permute-start | bytes 884744 | tf_op jit(solution)/shard_map/ppermute | solution.py:21
  7.7 35.1 %collective-permute-start = (bf16[96,1536]{1,0:T(8,128)(2,1)S(1)}, bf16[96,1536]{1,0:T(8,128)(2,1)S(1)}, u32[]{:S(2)}, u32[]{:S(2)}) collective-permute-start(bf16[96,1536]{1,0:T(8,128)(2,1)S(1)} %get-tuple-element.18), channel_id=1, source_target_pairs={{0,128},{128,256},{256,384},{384,448},{448,320},{320,192},{192,64}... | collective-permute-start | bytes 884744 | tf_op jit(solution)/shard_map/ppermute | solution.py:21
  9.6 33.2 %collective-permute-start.5 = (bf16[96,1536]{1,0:T(8,128)(2,1)S(1)}, bf16[96,1536]{1,0:T(8,128)(2,1)S(1)}, u32[]{:S(2)}, u32[]{:S(2)}) collective-permute-start(bf16[96,1536]{1,0:T(8,128)(2,1)S(1)} %get-tuple-element.18), channel_id=1, source_target_pairs={{0,64},{128,0},{256,128},{384,256},{448,384},{320,448},{192,320},{... | collective-permute-start | bytes 884744 | tf_op jit(solution)/shard_map/ppermute | solution.py:21
  17.0 35.3 %collective-permute-start.22 = (bf16[192,768]{1,0:T(8,128)(2,1)S(1)}, bf16[192,768]{1,0:T(8,128)(2,1)S(1)}, u32[]{:S(2)}, u32[]{:S(2)}) collective-permute-start(bf16[192,768]{1,0:T(8,128)(2,1)S(1)} %pad_maximum_fusion.9), channel_id=1, source_target_pairs={{0,8},{8,0},{1,9},{9,1},{2,10},{10,2},{3,11},{11,3},{4,12},{12,4},... | collective-permute-start | bytes 884744 | tf_op jit(solution)/shard_map/ppermute | solution.py:21
  42.9 69.4 %collective-permute-start.6 = (bf16[2,96,1536]{2,1,0:T(8,128)(2,1)S(1)}, bf16[2,96,1536]{2,1,0:T(8,128)(2,1)S(1)}, u32[]{:S(2)}, u32[]{:S(2)}) collective-permute-start(bf16[2,96,1536]{2,1,0:T(8,128)(2,1)S(1)} %pad_maximum_fusion.4), channel_id=1, source_target_pairs={{0,48},{16,0},{32,16},{48,32},{1,49},{17,1},{33,17},{49,33},{2,50}... | collective-permute-start | bytes 1769480 | tf_op jit(solution)/shard_map/ppermute | solution.py:21
  48.0 66.3 %collective-permute-start.7 = (bf16[2,96,1536]{2,1,0:T(8,128)(2,1)S(1)}, bf16[2,96,1536]{2,1,0:T(8,128)(2,1)S(1)}, u32[]{:S(2)}, u32[]{:S(2)}) collective-permute-start(bf16[2,96,1536]{2,1,0:T(8,128)(2,1)S(1)} %pad_maximum_fusion.4), channel_id=1, source_target_pairs={{0,32},{16,48},{32,0},{48,16},{1,33},{17,49},{33,1},{49,17},{2,34}... | collective-permute-start | bytes 1769480 | tf_op jit(solution)/shard_map/ppermute | solution.py:21
  52.3 19.6 %collective-permute-start.1 = (bf16[96,1536]{1,0:T(8,128)(2,1)S(1)}, bf16[96,1536]{1,0:T(8,128)(2,1)S(1)}, u32[]{:S(2)}, u32[]{:S(2)}) collective-permute-start(bf16[96,1536]{1,0:T(8,128)(2,1)S(1)} %collective-permute-done), channel_id=1, source_target_pairs={{0,128},{128,256},{256,384},{384,448},{448,320},{320,192},{192,64}... | collective-permute-start | bytes 884744 | tf_op jit(solution)/shard_map/ppermute | solution.py:21
  71.9 60.3 %collective-permute-start.8 = (bf16[2,96,1536]{2,1,0:T(8,128)(2,1)S(1)}, bf16[2,96,1536]{2,1,0:T(8,128)(2,1)S(1)}, u32[]{:S(2)}, u32[]{:S(2)}) collective-permute-start(bf16[2,96,1536]{2,1,0:T(8,128)(2,1)S(1)} %pad_maximum_fusion.4), channel_id=1, source_target_pairs={{0,16},{16,32},{32,48},{48,0},{1,17},{17,33},{33,49},{49,1},{2,18}... | collective-permute-start | bytes 1769480 | tf_op jit(solution)/shard_map/ppermute | solution.py:21
  76.5 20.3 %collective-permute-start.3 = (bf16[1,96,1536]{2,1,0:T(8,128)(2,1)S(1)}, bf16[1,96,1536]{2,1,0:T(8,128)(2,1)S(1)}, u32[]{:S(2)}, u32[]{:S(2)}) collective-permute-start(bf16[1,96,1536]{2,1,0:T(8,128)(2,1)S(1)} %get-tuple-element.6), channel_id=1, source_target_pairs={{0,32},{16,48},{32,0},{48,16},{1,33},{17,49},{33,1},{49,17},{2,34}... | collective-permute-start | bytes 884744 | tf_op jit(solution)/shard_map/ppermute | solution.py:21
  96.8 9.9 %collective-permute-start.9 = (bf16[96,1536]{1,0:T(8,128)(2,1)S(1)}, bf16[96,1536]{1,0:T(8,128)(2,1)S(1)}, u32[]{:S(2)}, u32[]{:S(2)}) collective-permute-start(bf16[96,1536]{1,0:T(8,128)(2,1)S(1)} %collective-permute-done.5), channel_id=1, source_target_pairs={{0,64},{128,0},{256,128},{384,256},{448,384},{320,448},{192,320},{... | collective-permute-start | bytes 884744 | tf_op jit(solution)/shard_map/ppermute | solution.py:21
  106.7 30.1 %collective-permute-start.23 = (bf16[384,768]{1,0:T(8,128)(2,1)S(1)}, bf16[384,768]{1,0:T(8,128)(2,1)S(1)}, u32[]{:S(2)}, u32[]{:S(2)}) collective-permute-start(bf16[384,768]{1,0:T(8,128)(2,1)S(1)} %pad_maximum_fusion.7), channel_id=1, source_target_pairs={{0,2},{2,0},{4,6},{6,4},{1,3},{3,1},{5,7},{7,5},{8,10},{10,8},{12,... | collective-permute-start | bytes 1769480 | tf_op jit(solution)/shard_map/ppermute | solution.py:29
  110.2 30.3 %collective-permute-start.10 = (bf16[2,96,1536]{2,1,0:T(8,128)(2,1)S(1)}, bf16[2,96,1536]{2,1,0:T(8,128)(2,1)S(1)}, u32[]{:S(2)}, u32[]{:S(2)}) collective-permute-start(bf16[2,96,1536]{2,1,0:T(8,128)(2,1)S(1)} %pad_maximum_fusion.5), channel_id=1, source_target_pairs={{0,48},{16,0},{32,16},{48,32},{1,49},{17,1},{33,17},{49,33},{2,50}... | collective-permute-start | bytes 1769480 | tf_op jit(solution)/shard_map/ppermute | solution.py:21
  112.3 13.9 %collective-permute-start.13 = (bf16[96,1536]{1,0:T(8,128)(2,1)S(1)}, bf16[96,1536]{1,0:T(8,128)(2,1)S(1)}, u32[]{:S(2)}, u32[]{:S(2)}) collective-permute-start(bf16[96,1536]{1,0:T(8,128)(2,1)S(1)} %collective-permute-done.1), channel_id=1, source_target_pairs={{0,128},{128,256},{256,384},{384,448},{448,320},{320,192},{192,64}... | collective-permute-start | bytes 884744 | tf_op jit(solution)/shard_map/ppermute | solution.py:21
  114.3 14.2 %collective-permute-start.14 = (bf16[96,1536]{1,0:T(8,128)(2,1)S(1)}, bf16[96,1536]{1,0:T(8,128)(2,1)S(1)}, u32[]{:S(2)}, u32[]{:S(2)}) collective-permute-start(bf16[96,1536]{1,0:T(8,128)(2,1)S(1)} %collective-permute-done.9), channel_id=1, source_target_pairs={{0,64},{128,0},{256,128},{384,256},{448,384},{320,448},{192,320},{... | collective-permute-start | bytes 884744 | tf_op jit(solution)/shard_map/ppermute | solution.py:21
  126.2 19.6 %collective-permute-start.11 = (bf16[2,96,1536]{2,1,0:T(8,128)(2,1)S(1)}, bf16[2,96,1536]{2,1,0:T(8,128)(2,1)S(1)}, u32[]{:S(2)}, u32[]{:S(2)}) collective-permute-start(bf16[2,96,1536]{2,1,0:T(8,128)(2,1)S(1)} %pad_maximum_fusion.5), channel_id=1, source_target_pairs={{0,32},{16,48},{32,0},{48,16},{1,33},{17,49},{33,1},{49,17},{2,34}... | collective-permute-start | bytes 1769480 | tf_op jit(solution)/shard_map/ppermute | solution.py:21
  128.5 33.1 %collective-permute-start.12 = (bf16[2,96,1536]{2,1,0:T(8,128)(2,1)S(1)}, bf16[2,96,1536]{2,1,0:T(8,128)(2,1)S(1)}, u32[]{:S(2)}, u32[]{:S(2)}) collective-permute-start(bf16[2,96,1536]{2,1,0:T(8,128)(2,1)S(1)} %pad_maximum_fusion.5), channel_id=1, source_target_pairs={{0,16},{16,32},{32,48},{48,0},{1,17},{17,33},{33,49},{49,1},{2,18}... | collective-permute-start | bytes 1769480 | tf_op jit(solution)/shard_map/ppermute | solution.py:21
  132.3 36.2 %collective-permute-start.15 = (bf16[2,96,1536]{2,1,0:T(8,128)(2,1)S(1)}, bf16[2,96,1536]{2,1,0:T(8,128)(2,1)S(1)}, u32[]{:S(2)}, u32[]{:S(2)}) collective-permute-start(bf16[2,96,1536]{2,1,0:T(8,128)(2,1)S(1)} %pad_maximum_fusion.6), channel_id=1, source_target_pairs={{0,48},{16,0},{32,16},{48,32},{1,49},{17,1},{33,17},{49,33},{2,50}... | collective-permute-start | bytes 1769480 | tf_op jit(solution)/shard_map/ppermute | solution.py:21
  136.8 34.5 %collective-permute-start.16 = (bf16[2,96,1536]{2,1,0:T(8,128)(2,1)S(1)}, bf16[2,96,1536]{2,1,0:T(8,128)(2,1)S(1)}, u32[]{:S(2)}, u32[]{:S(2)}) collective-permute-start(bf16[2,96,1536]{2,1,0:T(8,128)(2,1)S(1)} %pad_maximum_fusion.6), channel_id=1, source_target_pairs={{0,32},{16,48},{32,0},{48,16},{1,33},{17,49},{33,1},{49,17},{2,34}... | collective-permute-start | bytes 1769480 | tf_op jit(solution)/shard_map/ppermute | solution.py:21
  140.6 49.4 %collective-permute-start.17 = (bf16[2,96,1536]{2,1,0:T(8,128)(2,1)S(1)}, bf16[2,96,1536]{2,1,0:T(8,128)(2,1)S(1)}, u32[]{:S(2)}, u32[]{:S(2)}) collective-permute-start(bf16[2,96,1536]{2,1,0:T(8,128)(2,1)S(1)} %pad_maximum_fusion.6), channel_id=1, source_target_pairs={{0,16},{16,32},{32,48},{48,0},{1,17},{17,33},{33,49},{49,1},{2,18}... | collective-permute-start | bytes 1769480 | tf_op jit(solution)/shard_map/ppermute | solution.py:21
  145.8 20.6 %collective-permute-start.18 = (bf16[96,1536]{1,0:T(8,128)(2,1)S(1)}, bf16[96,1536]{1,0:T(8,128)(2,1)S(1)}, u32[]{:S(2)}, u32[]{:S(2)}) collective-permute-start(bf16[96,1536]{1,0:T(8,128)(2,1)S(1)} %collective-permute-done.13), channel_id=1, source_target_pairs={{0,128},{128,256},{256,384},{384,448},{448,320},{320,192},{192,64}... | collective-permute-start | bytes 884744 | tf_op jit(solution)/shard_map/ppermute | solution.py:21
  161.6 25.6 %collective-permute-start.24 = (bf16[768,768]{1,0:T(8,128)(2,1)S(1)}, bf16[768,768]{1,0:T(8,128)(2,1)S(1)}, u32[]{:S(2)}, u32[]{:S(2)}) collective-permute-start(bf16[768,768]{1,0:T(8,128)(2,1)S(1)} %pad_maximum_fusion.3), channel_id=1, source_target_pairs={{0,4},{2,6},{4,0},{6,2},{1,5},{3,7},{5,1},{7,3},{8,12},{10,14},{12... | collective-permute-start | bytes 3538952 | tf_op jit(solution)/shard_map/ppermute | solution.py:29
  166.4 23.7 %collective-permute-start.19 = (bf16[1,96,1536]{2,1,0:T(8,128)(2,1)S(1)}, bf16[1,96,1536]{2,1,0:T(8,128)(2,1)S(1)}, u32[]{:S(2)}, u32[]{:S(2)}) collective-permute-start(bf16[1,96,1536]{2,1,0:T(8,128)(2,1)S(1)} %bitcast.167), channel_id=1, source_target_pairs={{0,48},{16,0},{32,16},{48,32},{1,49},{17,1},{33,17},{49,33},{2,50}... | collective-permute-start | bytes 884744 | tf_op jit(solution)/shard_map/ppermute | solution.py:21
  168.5 21.6 %collective-permute-start.20 = (bf16[1,96,1536]{2,1,0:T(8,128)(2,1)S(1)}, bf16[1,96,1536]{2,1,0:T(8,128)(2,1)S(1)}, u32[]{:S(2)}, u32[]{:S(2)}) collective-permute-start(bf16[1,96,1536]{2,1,0:T(8,128)(2,1)S(1)} %bitcast.168), channel_id=1, source_target_pairs={{0,32},{16,48},{32,0},{48,16},{1,33},{17,49},{33,1},{49,17},{2,34}... | collective-permute-start | bytes 884744 | tf_op jit(solution)/shard_map/ppermute | solution.py:21
  171.3 18.9 %collective-permute-start.21 = (bf16[1,96,1536]{2,1,0:T(8,128)(2,1)S(1)}, bf16[1,96,1536]{2,1,0:T(8,128)(2,1)S(1)}, u32[]{:S(2)}, u32[]{:S(2)}) collective-permute-start(bf16[1,96,1536]{2,1,0:T(8,128)(2,1)S(1)} %bitcast.169), channel_id=1, source_target_pairs={{0,16},{16,32},{32,48},{48,0},{1,17},{17,33},{33,49},{49,1},{2,18}... | collective-permute-start | bytes 884744 | tf_op jit(solution)/shard_map/ppermute | solution.py:21
  187.9 6.4 %collective-permute-start.25 = (bf16[1536,768]{1,0:T(8,128)(2,1)S(1)}, bf16[1536,768]{1,0:T(8,128)(2,1)S(1)}, u32[]{:S(2)}, u32[]{:S(2)}) collective-permute-start(bf16[1536,768]{1,0:T(8,128)(2,1)S(1)} %pad_maximum_fusion.2), channel_id=1, source_target_pairs={{0,1},{1,0},{2,3},{3,2},{4,5},{5,4},{6,7},{7,6},{8,9},{9,8},{10,11... | collective-permute-start | bytes 7077896 | tf_op jit(solution)/shard_map/ppermute | solution.py:21
  202.0 5.3 %collective-permute-start.26 = (f32[4,2,192,256]{3,2,1,0:T(8,128)S(1)}, f32[4,2,192,256]{3,2,1,0:T(8,128)S(1)}, u32[]{:S(2)}, u32[]{:S(2)}) collective-permute-start(f32[4,2,192,256]{3,2,1,0:T(8,128)S(1)} %dynamic-slice_bitcast_fusion), channel_id=1, source_target_pairs={{0,1},{1,0},{2,3},{3,2},{4,5},{5,4},{6,7},{7,6},{8,9},{9,8},{10,11... | collective-permute-start | bytes 4718600 | tf_op jit(solution)/shard_map/ppermute | solution.py:21
  208.4 16.8 %all-to-all-start = ((bf16[4,2,192,256]{3,2,1,0:T(8,128)(2,1)}), bf16[4,2,192,256]{3,2,1,0:T(8,128)(2,1)S(1)}, u32[]{:S(2)}, u32[]{:S(2)}) async-start(bf16[4,2,192,256]{3,2,1,0:T(8,128)(2,1)} %fusion.10), calls=%async_computation | async-start | bytes 1572864 | tf_op jit(solution)/shard_map/all_to_all | solution.py:109
  225.3 17.0 %collective-permute-start.27 = (bf16[192,256]{1,0:T(8,128)(2,1)S(1)}, bf16[192,256]{1,0:T(8,128)(2,1)S(1)}, u32[]{:S(2)}, u32[]{:S(2)}) collective-permute-start(bf16[192,256]{1,0:T(8,128)(2,1)S(1)} %fusion.47), channel_id=1, source_target_pairs={{0,8},{8,0},{1,9},{9,1},{2,10},{10,2},{3,11},{11,3},{4,12},{12,4},... | collective-permute-start | bytes 294920 | tf_op jit(solution)/shard_map/ppermute | solution.py:21

commit v5 on v4

--- a/solution.py
+++ b/solution.py
@@ -38,42 +38,57 @@
     return lax.dynamic_index_in_dim(v, i, axis, keepdims=False)
 
 
+def after(v, *done):
+    return lax.optimization_barrier((v, *done))[0]
+
+
 def body(tokens, tangent, cotangent, gates, slot_tokens, gate_weight, up_weight, down_weight):
     zl, x, zh, y, c = (lax.axis_index(a).astype(jnp.uint32) for a in ("zl", "x", "zh", "y", "c"))
     packed = take(jnp.asarray(SOURCES), zl)
 
     own = jnp.concatenate([gate_weight, up_weight, down_weight.T], axis=1)
     rows, width = own.shape
-    ups, downs = own, own
-    groups = [[own]]
-    for _ in range(3):
-        ups, downs = ring_up(ups), ring_down(downs)
-        groups.append([ups, downs])
-    groups.append([ring_up(ups)])
-
     fields = jnp.concatenate([tokens.T, tangent.T, cotangent.T], axis=1)
     feat = fields.shape[0]
 
-    def join(v, send, bit):
-        got = send(v)
+    def join(v, send, bit, *done):
+        got = after(send(v), *done)
         return jnp.concatenate([jnp.where(bit == 0, v, got), jnp.where(bit == 0, got, v)])
 
-    fields = join(fields, other_half, zh)
-    fields = join(fields, y_near, y & 1)
-    fields = join(fields, y_far, y >> 1)
+    g0 = own[None]
+    a1, b1 = ring_up(own), ring_down(own)
+    p0, m0 = x_up(g0), x_down(g0)
+    a2, b2 = ring_up(a1), ring_down(b1)
+    g1 = jnp.stack([a1, b1])
+    p1, m1 = x_up(after(g1, p0)), x_down(after(g1, m0))
+    a3, b3 = ring_up(a2), ring_down(b2)
+    f1 = x_far(after(g1, p1))
+    f0 = x_far(after(g0, m1))
+    g2 = jnp.stack([a2, b2])
+    p2 = x_up(after(g2, a3))
+    m2 = x_down(after(g2, b3))
+    f2 = x_far(after(g2, f0))
+    fields = join(fields, other_half, zh, b3)
+    fields = join(fields, y_near, y & 1, p2)
+    a4 = ring_up(after(a3, f1))
+    g3 = jnp.stack([a3, b3])
+    p3 = x_up(after(g3, p2))
+    m3 = x_down(after(g3, m2))
+    f3 = x_far(after(g3, f2))
+    fields = join(fields, y_far, y >> 1, p3)
+    g4 = a4[None]
+    p4 = x_up(g4)
+    m4 = x_down(after(g4, p3))
+    f4 = x_far(after(g4, m3))
     fields = join(fields, other_core, c)
 
-    zero = groups[2][0][0, 0] * 0
+    zero = a2[0, 0] * 0
     full = jnp.broadcast_to(zero, (NC, NY, NH, 2, rows, width))
     none = jnp.uint32(0)
     sources = iter((((packed >> 3 * j) & 3, (packed >> 3 * j + 2) & 1) for j in range(NZ)))
-    for blocks in groups:
-        sent = jnp.stack(blocks)
-        late = sent
-        if blocks[0] is own:
-            late, _ = lax.optimization_barrier((sent, groups[1][0]))
-        parts = (sent, x_down(sent), x_far(late), x_up(sent))
-        at = [next(sources) for _ in blocks]
+    groups = ((g0, m0, f0, p0), (g1, m1, f1, p1), (g2, m2, f2, p2), (g3, m3, f3, p3), (g4, m4, f4, p4))
+    for parts in groups:
+        at = [next(sources) for _ in parts[0]]
         for step, part in enumerate(parts):
             col = x + step
             for j, (row, far) in enumerate(at):

time: 244 us -> 214 us (0.88)
  the two profiles are of different devices: /device:TPU:96 before, /device:TPU:99 now
where the time goes in v5:
time: 214 us; the launch traced here: 213 us
  starting transfers between devices  116 us (54%)
  waiting for transfers between devices  67 us (31%)
  between operations  11.8 us (6%)
  other arithmetic  7.72 us (4%)
  matrix products  6.52 us (3%)
  local copies, waits for them, and re-layouts  3.91 us (2%)
    ppermute x26, starting transfers between devices, shift(): return lambda v: lax.ppermute(v, axis, pairs)  104 us
    ppermute x26, waiting for transfers between devices, shift(): return lambda v: lax.ppermute(v, axis, pairs)  54.1 us
    all_to_all x1, waiting for transfers between devices, body(): shares = lax.all_to_all(sums.astype(BF), 'y', 0, 0, tiled=True).astype(F32)  11.7 us
    ppermute x2, starting transfers between devices, flip(): return lambda v: lax.ppermute(v, axis, [(i, i ^ bit) for i in range(n)])  8.03 us
  transfers between devices with their start and end apart: 29, of which 11 were waited for; matrix products, arithmetic and copies ran while one was open for 3% of the time, Pallas kernels for 0%

profile of v5, /device:TPU:99, one launch (start us, length us, event | category | flops | bytes accessed | tf_op | source)
XLA Modules:
  0.0 212.9 jit_solution(15857195564400740862)
XLA Ops:
  0.0 1.1 fusion.52
  1.1 1.9 collective-permute-start
  3.1 6.1 %collective-permute-start.3 = (bf16[96,1536]{1,0:T(8,128)(2,1)S(1)}, bf16[96,1536]{1,0:T(8,128)(2,1)S(1)}, u32[]{:S(2)}, u32[]{:S(2)}) collective-permute-start(bf16[96,1536]{1,0:T(8,128)(2,1)S(1)} %get-tuple-element.48), channel_id=1, source_target_pairs={{0,64},{128,0},{256,128},{384,256},{448,384},{320,448},{192,320},{... | collective-permute-start | bytes 884744 | tf_op jit(solution)/shard_map/ppermute | solution.py:21
  9.2 2.2 %collective-permute-start.2 = (bf16[1,96,1536]{2,1,0:T(8,128)(2,1)S(1)}, bf16[1,96,1536]{2,1,0:T(8,128)(2,1)S(1)}, u32[]{:S(2)}, u32[]{:S(2)}) collective-permute-start(bf16[1,96,1536]{2,1,0:T(8,128)(2,1)S(1)} %get-tuple-element.22), channel_id=1, source_target_pairs={{0,48},{16,0},{32,16},{48,32},{1,49},{17,1},{33,17},{49,33},{2,50}... | collective-permute-start | bytes 884744 | tf_op jit(solution)/shard_map/ppermute | solution.py:21
  11.4 3.1 %collective-permute-start.6 = (bf16[1,96,1536]{2,1,0:T(8,128)(2,1)S(1)}, bf16[1,96,1536]{2,1,0:T(8,128)(2,1)S(1)}, u32[]{:S(2)}, u32[]{:S(2)}) collective-permute-start(bf16[1,96,1536]{2,1,0:T(8,128)(2,1)S(1)} %get-tuple-element.22), channel_id=1, source_target_pairs={{0,16},{16,32},{32,48},{48,0},{1,17},{17,33},{33,49},{49,1},{2,18}... | collective-permute-start | bytes 884744 | tf_op jit(solution)/shard_map/ppermute | solution.py:21
  14.5 1.0 pad_maximum_fusion.9
  15.5 12.1 %collective-permute-start.22 = (bf16[192,768]{1,0:T(8,128)(2,1)S(1)}, bf16[192,768]{1,0:T(8,128)(2,1)S(1)}, u32[]{:S(2)}, u32[]{:S(2)}) collective-permute-start(bf16[192,768]{1,0:T(8,128)(2,1)S(1)} %pad_maximum_fusion.9), channel_id=1, source_target_pairs={{0,8},{8,0},{1,9},{9,1},{2,10},{10,2},{3,11},{11,3},{4,12},{12,4},... | collective-permute-start | bytes 884744 | tf_op jit(solution)/shard_map/ppermute | solution.py:21
  27.6 0.8 fusion.45
  28.4 1.9 collective-permute-start.1
  31.0 1.2 dynamic_slice.18
  42.7 5.5 %collective-permute-start.9 = (bf16[96,1536]{1,0:T(8,128)(2,1)S(1)}, bf16[96,1536]{1,0:T(8,128)(2,1)S(1)}, u32[]{:S(2)}, u32[]{:S(2)}) collective-permute-start(bf16[96,1536]{1,0:T(8,128)(2,1)S(1)} %collective-permute-done.3), channel_id=1, source_target_pairs={{0,64},{128,0},{256,128},{384,256},{448,384},{320,448},{192,320},{... | collective-permute-start | bytes 884744 | tf_op jit(solution)/shard_map/ppermute | solution.py:21
  48.2 3.2 %collective-permute-start.4 = (bf16[2,96,1536]{2,1,0:T(8,128)(2,1)S(1)}, bf16[2,96,1536]{2,1,0:T(8,128)(2,1)S(1)}, u32[]{:S(2)}, u32[]{:S(2)}) collective-permute-start(bf16[2,96,1536]{2,1,0:T(8,128)(2,1)S(1)} %pad_maximum_fusion.4), channel_id=1, source_target_pairs={{0,48},{16,0},{32,16},{48,32},{1,49},{17,1},{33,17},{49,33},{2,50}... | collective-permute-start | bytes 1769480 | tf_op jit(solution)/shard_map/ppermute | solution.py:21
  51.4 2.1 collective-permute-start.7
  53.5 7.1 %collective-permute-done.1 = bf16[96,1536]{1,0:T(8,128)(2,1)S(1)} collective-permute-done((bf16[96,1536]{1,0:T(8,128)(2,1)S(1)}, bf16[96,1536]{1,0:T(8,128)(2,1)S(1)}, u32[]{:S(2)}, u32[]{:S(2)}) %collective-permute-start.1) | collective-permute-done | bytes 294944 | tf_op jit(solution)/shard_map/ppermute | solution.py:21
  61.8 3.8 %collective-permute-start.13 = (bf16[96,1536]{1,0:T(8,128)(2,1)S(1)}, bf16[96,1536]{1,0:T(8,128)(2,1)S(1)}, u32[]{:S(2)}, u32[]{:S(2)}) collective-permute-start(bf16[96,1536]{1,0:T(8,128)(2,1)S(1)} %collective-permute-done.1), channel_id=1, source_target_pairs={{0,128},{128,256},{256,384},{384,448},{448,320},{320,192},{192,64}... | collective-permute-start | bytes 884744 | tf_op jit(solution)/shard_map/ppermute | solution.py:21
  65.6 1.1 broadcast_in_dim.15
  66.7 4.7 %collective-permute-start.10 = (bf16[96,1536]{1,0:T(8,128)(2,1)S(1)}, bf16[96,1536]{1,0:T(8,128)(2,1)S(1)}, u32[]{:S(2)}, u32[]{:S(2)}) collective-permute-start(bf16[96,1536]{1,0:T(8,128)(2,1)S(1)} %collective-permute-done.9), channel_id=1, source_target_pairs={{0,64},{128,0},{256,128},{384,256},{448,384},{320,448},{192,320},{... | collective-permute-start | bytes 884744 | tf_op jit(solution)/shard_map/ppermute | solution.py:21
  71.6 5.0 %collective-permute-start.5 = (bf16[1,96,1536]{2,1,0:T(8,128)(2,1)S(1)}, bf16[1,96,1536]{2,1,0:T(8,128)(2,1)S(1)}, u32[]{:S(2)}, u32[]{:S(2)}) collective-permute-start(bf16[1,96,1536]{2,1,0:T(8,128)(2,1)S(1)} %get-tuple-element.22), channel_id=1, source_target_pairs={{0,32},{16,48},{32,0},{48,16},{1,33},{17,49},{33,1},{49,17},{2,34}... | collective-permute-start | bytes 884744 | tf_op jit(solution)/shard_map/ppermute | solution.py:21
  76.5 1.9 collective-permute-start.8
  78.5 3.3 %collective-permute-start.11 = (bf16[2,96,1536]{2,1,0:T(8,128)(2,1)S(1)}, bf16[2,96,1536]{2,1,0:T(8,128)(2,1)S(1)}, u32[]{:S(2)}, u32[]{:S(2)}) collective-permute-start(bf16[2,96,1536]{2,1,0:T(8,128)(2,1)S(1)} %pad_maximum_fusion.5), channel_id=1, source_target_pairs={{0,48},{16,0},{32,16},{48,32},{1,49},{17,1},{33,17},{49,33},{2,50}... | collective-permute-start | bytes 1769480 | tf_op jit(solution)/shard_map/ppermute | solution.py:21
  81.8 1.9 collective-permute-start.14
  84.0 3.2 %collective-permute-start.23 = (bf16[384,768]{1,0:T(8,128)(2,1)S(1)}, bf16[384,768]{1,0:T(8,128)(2,1)S(1)}, u32[]{:S(2)}, u32[]{:S(2)}) collective-permute-start(bf16[384,768]{1,0:T(8,128)(2,1)S(1)} %pad_maximum_fusion.7), channel_id=1, source_target_pairs={{0,2},{2,0},{4,6},{6,4},{1,3},{3,1},{5,7},{7,5},{8,10},{10,8},{12,... | collective-permute-start | bytes 1769480 | tf_op jit(solution)/shard_map/ppermute | solution.py:29
  87.3 6.4 %collective-permute-start.12 = (bf16[2,96,1536]{2,1,0:T(8,128)(2,1)S(1)}, bf16[2,96,1536]{2,1,0:T(8,128)(2,1)S(1)}, u32[]{:S(2)}, u32[]{:S(2)}) collective-permute-start(bf16[2,96,1536]{2,1,0:T(8,128)(2,1)S(1)} %pad_maximum_fusion.5), channel_id=1, source_target_pairs={{0,32},{16,48},{32,0},{48,16},{1,33},{17,49},{33,1},{49,17},{2,34}... | collective-permute-start | bytes 1769480 | tf_op jit(solution)/shard_map/ppermute | solution.py:21
  93.9 16.5 %collective-permute-done.11 = bf16[2,96,1536]{2,1,0:T(8,128)(2,1)S(1)} collective-permute-done((bf16[2,96,1536]{2,1,0:T(8,128)(2,1)S(1)}, bf16[2,96,1536]{2,1,0:T(8,128)(2,1)S(1)}, u32[]{:S(2)}, u32[]{:S(2)}) %collective-permute-start.11) | collective-permute-done | bytes 589856 | tf_op jit(solution)/shard_map/ppermute | solution.py:21
  110.4 1.9 collective-permute-start.15
  112.3 3.4 %collective-permute-start.17 = (bf16[2,96,1536]{2,1,0:T(8,128)(2,1)S(1)}, bf16[2,96,1536]{2,1,0:T(8,128)(2,1)S(1)}, u32[]{:S(2)}, u32[]{:S(2)}) collective-permute-start(bf16[2,96,1536]{2,1,0:T(8,128)(2,1)S(1)} %pad_maximum_fusion.6), channel_id=1, source_target_pairs={{0,16},{16,32},{32,48},{48,0},{1,17},{17,33},{33,49},{49,1},{2,18}... | collective-permute-start | bytes 1769480 | tf_op jit(solution)/shard_map/ppermute | solution.py:21
  115.7 1.9 collective-permute-start.18
  118.0 4.8 %collective-permute-start.24 = (bf16[768,768]{1,0:T(8,128)(2,1)S(1)}, bf16[768,768]{1,0:T(8,128)(2,1)S(1)}, u32[]{:S(2)}, u32[]{:S(2)}) collective-permute-start(bf16[768,768]{1,0:T(8,128)(2,1)S(1)} %pad_maximum_fusion.3), channel_id=1, source_target_pairs={{0,4},{2,6},{4,0},{6,2},{1,5},{3,7},{5,1},{7,3},{8,12},{10,14},{12... | collective-permute-start | bytes 3538952 | tf_op jit(solution)/shard_map/ppermute | solution.py:29
  123.1 6.1 %collective-permute-start.16 = (bf16[2,96,1536]{2,1,0:T(8,128)(2,1)S(1)}, bf16[2,96,1536]{2,1,0:T(8,128)(2,1)S(1)}, u32[]{:S(2)}, u32[]{:S(2)}) collective-permute-start(bf16[2,96,1536]{2,1,0:T(8,128)(2,1)S(1)} %pad_maximum_fusion.6), channel_id=1, source_target_pairs={{0,32},{16,48},{32,0},{48,16},{1,33},{17,49},{33,1},{49,17},{2,34}... | collective-permute-start | bytes 1769480 | tf_op jit(solution)/shard_map/ppermute | solution.py:21
  129.2 1.9 collective-permute-start.21
  131.4 2.9 %collective-permute-done.17 = bf16[2,96,1536]{2,1,0:T(8,128)(2,1)S(1)} collective-permute-done((bf16[2,96,1536]{2,1,0:T(8,128)(2,1)S(1)}, bf16[2,96,1536]{2,1,0:T(8,128)(2,1)S(1)}, u32[]{:S(2)}, u32[]{:S(2)}) %collective-permute-start.17) | collective-permute-done | bytes 589856 | tf_op jit(solution)/shard_map/ppermute | solution.py:21
  134.2 3.6 %collective-permute-start.19 = (bf16[1,96,1536]{2,1,0:T(8,128)(2,1)S(1)}, bf16[1,96,1536]{2,1,0:T(8,128)(2,1)S(1)}, u32[]{:S(2)}, u32[]{:S(2)}) collective-permute-start(bf16[1,96,1536]{2,1,0:T(8,128)(2,1)S(1)} %bitcast.168), channel_id=1, source_target_pairs={{0,48},{16,0},{32,16},{48,32},{1,49},{17,1},{33,17},{49,33},{2,50}... | collective-permute-start | bytes 884744 | tf_op jit(solution)/shard_map/ppermute | solution.py:21
  137.9 4.1 %collective-permute-start.20 = (bf16[1,96,1536]{2,1,0:T(8,128)(2,1)S(1)}, bf16[1,96,1536]{2,1,0:T(8,128)(2,1)S(1)}, u32[]{:S(2)}, u32[]{:S(2)}) collective-permute-start(bf16[1,96,1536]{2,1,0:T(8,128)(2,1)S(1)} %bitcast.169), channel_id=1, source_target_pairs={{0,32},{16,48},{32,0},{48,16},{1,33},{17,49},{33,1},{49,17},{2,34}... | collective-permute-start | bytes 884744 | tf_op jit(solution)/shard_map/ppermute | solution.py:21
  142.0 4.1 %collective-permute-done.16 = bf16[2,96,1536]{2,1,0:T(8,128)(2,1)S(1)} collective-permute-done((bf16[2,96,1536]{2,1,0:T(8,128)(2,1)S(1)}, bf16[2,96,1536]{2,1,0:T(8,128)(2,1)S(1)}, u32[]{:S(2)}, u32[]{:S(2)}) %collective-permute-start.16) | collective-permute-done | bytes 589856 | tf_op jit(solution)/shard_map/ppermute | solution.py:21
  146.2 1.2 collective-permute-done.24
  148.0 8.1 %collective-permute-start.25 = (bf16[1536,768]{1,0:T(8,128)(2,1)S(1)}, bf16[1536,768]{1,0:T(8,128)(2,1)S(1)}, u32[]{:S(2)}, u32[]{:S(2)}) collective-permute-start(bf16[1536,768]{1,0:T(8,128)(2,1)S(1)} %pad_maximum_fusion.2), channel_id=1, source_target_pairs={{0,1},{1,0},{2,3},{3,2},{4,5},{5,4},{6,7},{7,6},{8,9},{9,8},{10,11... | collective-permute-start | bytes 7077896 | tf_op jit(solution)/shard_map/ppermute | solution.py:21
  156.7 3.4 %collective-permute-done.25 = bf16[1536,768]{1,0:T(8,128)(2,1)S(1)} collective-permute-done((bf16[1536,768]{1,0:T(8,128)(2,1)S(1)}, bf16[1536,768]{1,0:T(8,128)(2,1)S(1)}, u32[]{:S(2)}, u32[]{:S(2)}) %collective-permute-start.25) | collective-permute-done | bytes 2359328 | tf_op jit(solution)/shard_map/ppermute | solution.py:21
  160.0 1.0 broadcast_select_fusion.1
  161.0 3.4 %fusion.2 = f32[512,1024]{1,0:T(8,128)S(1)} fusion(bf16[3072,1536]{1,0:T(8,128)(2,1)S(1)} %bitcast.148, bf16[1536,768]{1,0:T(8,128)(2,1)S(1)} %get-tuple-element.38, bf16[1536,768]{1,0:T(8,128)(2,1)S(1)} %get-tuple-element.37), kind=kOutput, calls=%fused_computation.2 | convolution fusion | flops 3227516928 | bytes 13107200 | tf_op jit(solution)/shard_map/dot_general | solution.py:102
  164.5 1.3 fusion.23
  165.7 1.8 fusion
  167.7 3.3 %collective-permute-start.26 = (f32[4,2,192,256]{3,2,1,0:T(8,128)S(1)}, f32[4,2,192,256]{3,2,1,0:T(8,128)S(1)}, u32[]{:S(2)}, u32[]{:S(2)}) collective-permute-start(f32[4,2,192,256]{3,2,1,0:T(8,128)S(1)} %dynamic-slice_bitcast_fusion), channel_id=1, source_target_pairs={{0,1},{1,0},{2,3},{3,2},{4,5},{5,4},{6,7},{7,6},{8,9},{9,8},{10,11... | collective-permute-start | bytes 4718600 | tf_op jit(solution)/shard_map/ppermute | solution.py:21
  171.1 3.0 %collective-permute-done.26 = f32[4,2,192,256]{3,2,1,0:T(8,128)S(1)} collective-permute-done((f32[4,2,192,256]{3,2,1,0:T(8,128)S(1)}, f32[4,2,192,256]{3,2,1,0:T(8,128)S(1)}, u32[]{:S(2)}, u32[]{:S(2)}) %collective-permute-start.26) | collective-permute-done | bytes 1572896 | tf_op jit(solution)/shard_map/ppermute | solution.py:21
  174.1 1.1 fusion.10
  175.2 4.2 %all-to-all-start = ((bf16[4,2,192,256]{3,2,1,0:T(8,128)(2,1)}), bf16[4,2,192,256]{3,2,1,0:T(8,128)(2,1)S(1)}, u32[]{:S(2)}, u32[]{:S(2)}) async-start(bf16[4,2,192,256]{3,2,1,0:T(8,128)(2,1)} %fusion.10), calls=%async_computation | async-start | bytes 1572864 | tf_op jit(solution)/shard_map/all_to_all | solution.py:124
  179.4 11.7 %all-to-all-done = bf16[4,2,192,256]{3,2,1,0:T(8,128)(2,1)S(1)} async-done(((bf16[4,2,192,256]{3,2,1,0:T(8,128)(2,1)}), bf16[4,2,192,256]{3,2,1,0:T(8,128)(2,1)S(1)}, u32[]{:S(2)}, u32[]{:S(2)}) %all-to-all-start) | async-done | bytes 786464 | tf_op jit(solution)/shard_map/all_to_all | solution.py:124
  191.2 4.2 %collective-permute-start.27 = (bf16[192,256]{1,0:T(8,128)(2,1)S(1)}, bf16[192,256]{1,0:T(8,128)(2,1)S(1)}, u32[]{:S(2)}, u32[]{:S(2)}) collective-permute-start(bf16[192,256]{1,0:T(8,128)(2,1)S(1)} %fusion.47), channel_id=1, source_target_pairs={{0,8},{8,0},{1,9},{9,1},{2,10},{10,2},{3,11},{11,3},{4,12},{12,4},... | collective-permute-start | bytes 294920 | tf_op jit(solution)/shard_map/ppermute | solution.py:21
  195.5 16.8 %collective-permute-done.27 = bf16[192,256]{1,0:T(8,128)(2,1)S(1)} collective-permute-done((bf16[192,256]{1,0:T(8,128)(2,1)S(1)}, bf16[192,256]{1,0:T(8,128)(2,1)S(1)}, u32[]{:S(2)}, u32[]{:S(2)}) %collective-permute-start.27) | collective-permute-done | bytes 98336 | tf_op jit(solution)/shard_map/ppermute | solution.py:21
  (79 shorter events, 4.8 us)
Async XLA Ops:
  0.0 66.6 %copy-start = (bf16[512,96]{0,1:T(8,128)(2,1)S(1)}, bf16[512,96]{0,1:T(8,128)(2,1)}, u32[]{:S(2)}) copy-start(bf16[512,96]{0,1:T(8,128)(2,1)} %param.16) | copy-start | bytes 294916
  0.0 66.6 %copy-start.1 = (bf16[96,512]{1,0:T(8,128)(2,1)S(1)}, bf16[96,512]{1,0:T(8,128)(2,1)}, u32[]{:S(2)}) copy-start(bf16[96,512]{1,0:T(8,128)(2,1)} %param.15) | copy-start | bytes 294916
  0.0 66.6 %copy-start.2 = (bf16[96,512]{1,0:T(8,128)(2,1)S(1)}, bf16[96,512]{1,0:T(8,128)(2,1)}, u32[]{:S(2)}) copy-start(bf16[96,512]{1,0:T(8,128)(2,1)} %param.14) | copy-start | bytes 294916
  0.0 83.8 %copy-start.3 = (bf16[256,192]{0,1:T(8,128)(2,1)S(1)}, bf16[256,192]{0,1:T(8,128)(2,1)}, u32[]{:S(2)}) copy-start(bf16[256,192]{0,1:T(8,128)(2,1)} %param.11) | copy-start | bytes 294916
  0.0 83.8 %copy-start.4 = (bf16[256,192]{0,1:T(8,128)(2,1)S(1)}, bf16[256,192]{0,1:T(8,128)(2,1)}, u32[]{:S(2)}) copy-start(bf16[256,192]{0,1:T(8,128)(2,1)} %param.10) | copy-start | bytes 294916
  0.0 83.8 %copy-start.5 = (bf16[256,192]{0,1:T(8,128)(2,1)S(1)}, bf16[256,192]{0,1:T(8,128)(2,1)}, u32[]{:S(2)}) copy-start(bf16[256,192]{0,1:T(8,128)(2,1)} %param.9) | copy-start | bytes 294916
  1.1 27.3 %collective-permute-start = (bf16[96,1536]{1,0:T(8,128)(2,1)S(1)}, bf16[96,1536]{1,0:T(8,128)(2,1)S(1)}, u32[]{:S(2)}, u32[]{:S(2)}) collective-permute-start(bf16[96,1536]{1,0:T(8,128)(2,1)S(1)} %get-tuple-element.48), channel_id=1, source_target_pairs={{0,128},{128,256},{256,384},{384,448},{448,320},{320,192},{192,64}... | collective-permute-start | bytes 884744 | tf_op jit(solution)/shard_map/ppermute | solution.py:21
  3.1 39.6 %collective-permute-start.3 = (bf16[96,1536]{1,0:T(8,128)(2,1)S(1)}, bf16[96,1536]{1,0:T(8,128)(2,1)S(1)}, u32[]{:S(2)}, u32[]{:S(2)}) collective-permute-start(bf16[96,1536]{1,0:T(8,128)(2,1)S(1)} %get-tuple-element.48), channel_id=1, source_target_pairs={{0,64},{128,0},{256,128},{384,256},{448,384},{320,448},{192,320},{... | collective-permute-start | bytes 884744 | tf_op jit(solution)/shard_map/ppermute | solution.py:21
  9.2 39.0 %collective-permute-start.2 = (bf16[1,96,1536]{2,1,0:T(8,128)(2,1)S(1)}, bf16[1,96,1536]{2,1,0:T(8,128)(2,1)S(1)}, u32[]{:S(2)}, u32[]{:S(2)}) collective-permute-start(bf16[1,96,1536]{2,1,0:T(8,128)(2,1)S(1)} %get-tuple-element.22), channel_id=1, source_target_pairs={{0,48},{16,0},{32,16},{48,32},{1,49},{17,1},{33,17},{49,33},{2,50}... | collective-permute-start | bytes 884744 | tf_op jit(solution)/shard_map/ppermute | solution.py:21
  11.4 40.1 %collective-permute-start.6 = (bf16[1,96,1536]{2,1,0:T(8,128)(2,1)S(1)}, bf16[1,96,1536]{2,1,0:T(8,128)(2,1)S(1)}, u32[]{:S(2)}, u32[]{:S(2)}) collective-permute-start(bf16[1,96,1536]{2,1,0:T(8,128)(2,1)S(1)} %get-tuple-element.22), channel_id=1, source_target_pairs={{0,16},{16,32},{32,48},{48,0},{1,17},{17,33},{33,49},{49,1},{2,18}... | collective-permute-start | bytes 884744 | tf_op jit(solution)/shard_map/ppermute | solution.py:21
  15.5 68.3 %collective-permute-start.22 = (bf16[192,768]{1,0:T(8,128)(2,1)S(1)}, bf16[192,768]{1,0:T(8,128)(2,1)S(1)}, u32[]{:S(2)}, u32[]{:S(2)}) collective-permute-start(bf16[192,768]{1,0:T(8,128)(2,1)S(1)} %pad_maximum_fusion.9), channel_id=1, source_target_pairs={{0,8},{8,0},{1,9},{9,1},{2,10},{10,2},{3,11},{11,3},{4,12},{12,4},... | collective-permute-start | bytes 884744 | tf_op jit(solution)/shard_map/ppermute | solution.py:21
  28.4 32.2 %collective-permute-start.1 = (bf16[96,1536]{1,0:T(8,128)(2,1)S(1)}, bf16[96,1536]{1,0:T(8,128)(2,1)S(1)}, u32[]{:S(2)}, u32[]{:S(2)}) collective-permute-start(bf16[96,1536]{1,0:T(8,128)(2,1)S(1)} %collective-permute-done), channel_id=1, source_target_pairs={{0,128},{128,256},{256,384},{384,448},{448,320},{320,192},{192,64}... | collective-permute-start | bytes 884744 | tf_op jit(solution)/shard_map/ppermute | solution.py:21
  42.7 24.0 %collective-permute-start.9 = (bf16[96,1536]{1,0:T(8,128)(2,1)S(1)}, bf16[96,1536]{1,0:T(8,128)(2,1)S(1)}, u32[]{:S(2)}, u32[]{:S(2)}) collective-permute-start(bf16[96,1536]{1,0:T(8,128)(2,1)S(1)} %collective-permute-done.3), channel_id=1, source_target_pairs={{0,64},{128,0},{256,128},{384,256},{448,384},{320,448},{192,320},{... | collective-permute-start | bytes 884744 | tf_op jit(solution)/shard_map/ppermute | solution.py:21
  48.2 23.3 %collective-permute-start.4 = (bf16[2,96,1536]{2,1,0:T(8,128)(2,1)S(1)}, bf16[2,96,1536]{2,1,0:T(8,128)(2,1)S(1)}, u32[]{:S(2)}, u32[]{:S(2)}) collective-permute-start(bf16[2,96,1536]{2,1,0:T(8,128)(2,1)S(1)} %pad_maximum_fusion.4), channel_id=1, source_target_pairs={{0,48},{16,0},{32,16},{48,32},{1,49},{17,1},{33,17},{49,33},{2,50}... | collective-permute-start | bytes 1769480 | tf_op jit(solution)/shard_map/ppermute | solution.py:21
  51.4 25.1 %collective-permute-start.7 = (bf16[2,96,1536]{2,1,0:T(8,128)(2,1)S(1)}, bf16[2,96,1536]{2,1,0:T(8,128)(2,1)S(1)}, u32[]{:S(2)}, u32[]{:S(2)}) collective-permute-start(bf16[2,96,1536]{2,1,0:T(8,128)(2,1)S(1)} %pad_maximum_fusion.4), channel_id=1, source_target_pairs={{0,16},{16,32},{32,48},{48,0},{1,17},{17,33},{33,49},{49,1},{2,18}... | collective-permute-start | bytes 1769480 | tf_op jit(solution)/shard_map/ppermute | solution.py:21
  61.8 20.1 %collective-permute-start.13 = (bf16[96,1536]{1,0:T(8,128)(2,1)S(1)}, bf16[96,1536]{1,0:T(8,128)(2,1)S(1)}, u32[]{:S(2)}, u32[]{:S(2)}) collective-permute-start(bf16[96,1536]{1,0:T(8,128)(2,1)S(1)} %collective-permute-done.1), channel_id=1, source_target_pairs={{0,128},{128,256},{256,384},{384,448},{448,320},{320,192},{192,64}... | collective-permute-start | bytes 884744 | tf_op jit(solution)/shard_map/ppermute | solution.py:21
  66.7 11.8 %collective-permute-start.10 = (bf16[96,1536]{1,0:T(8,128)(2,1)S(1)}, bf16[96,1536]{1,0:T(8,128)(2,1)S(1)}, u32[]{:S(2)}, u32[]{:S(2)}) collective-permute-start(bf16[96,1536]{1,0:T(8,128)(2,1)S(1)} %collective-permute-done.9), channel_id=1, source_target_pairs={{0,64},{128,0},{256,128},{384,256},{448,384},{320,448},{192,320},{... | collective-permute-start | bytes 884744 | tf_op jit(solution)/shard_map/ppermute | solution.py:21
  71.6 15.7 %collective-permute-start.5 = (bf16[1,96,1536]{2,1,0:T(8,128)(2,1)S(1)}, bf16[1,96,1536]{2,1,0:T(8,128)(2,1)S(1)}, u32[]{:S(2)}, u32[]{:S(2)}) collective-permute-start(bf16[1,96,1536]{2,1,0:T(8,128)(2,1)S(1)} %get-tuple-element.22), channel_id=1, source_target_pairs={{0,32},{16,48},{32,0},{48,16},{1,33},{17,49},{33,1},{49,17},{2,34}... | collective-permute-start | bytes 884744 | tf_op jit(solution)/shard_map/ppermute | solution.py:21
  76.5 39.1 %collective-permute-start.8 = (bf16[2,96,1536]{2,1,0:T(8,128)(2,1)S(1)}, bf16[2,96,1536]{2,1,0:T(8,128)(2,1)S(1)}, u32[]{:S(2)}, u32[]{:S(2)}) collective-permute-start(bf16[2,96,1536]{2,1,0:T(8,128)(2,1)S(1)} %pad_maximum_fusion.4), channel_id=1, source_target_pairs={{0,32},{16,48},{32,0},{48,16},{1,33},{17,49},{33,1},{49,17},{2,34}... | collective-permute-start | bytes 1769480 | tf_op jit(solution)/shard_map/ppermute | solution.py:21
  78.5 31.9 %collective-permute-start.11 = (bf16[2,96,1536]{2,1,0:T(8,128)(2,1)S(1)}, bf16[2,96,1536]{2,1,0:T(8,128)(2,1)S(1)}, u32[]{:S(2)}, u32[]{:S(2)}) collective-permute-start(bf16[2,96,1536]{2,1,0:T(8,128)(2,1)S(1)} %pad_maximum_fusion.5), channel_id=1, source_target_pairs={{0,48},{16,0},{32,16},{48,32},{1,49},{17,1},{33,17},{49,33},{2,50}... | collective-permute-start | bytes 1769480 | tf_op jit(solution)/shard_map/ppermute | solution.py:21
  81.8 30.5 %collective-permute-start.14 = (bf16[2,96,1536]{2,1,0:T(8,128)(2,1)S(1)}, bf16[2,96,1536]{2,1,0:T(8,128)(2,1)S(1)}, u32[]{:S(2)}, u32[]{:S(2)}) collective-permute-start(bf16[2,96,1536]{2,1,0:T(8,128)(2,1)S(1)} %pad_maximum_fusion.5), channel_id=1, source_target_pairs={{0,16},{16,32},{32,48},{48,0},{1,17},{17,33},{33,49},{49,1},{2,18}... | collective-permute-start | bytes 1769480 | tf_op jit(solution)/shard_map/ppermute | solution.py:21
  84.0 33.6 %collective-permute-start.23 = (bf16[384,768]{1,0:T(8,128)(2,1)S(1)}, bf16[384,768]{1,0:T(8,128)(2,1)S(1)}, u32[]{:S(2)}, u32[]{:S(2)}) collective-permute-start(bf16[384,768]{1,0:T(8,128)(2,1)S(1)} %pad_maximum_fusion.7), channel_id=1, source_target_pairs={{0,2},{2,0},{4,6},{6,4},{1,3},{3,1},{5,7},{7,5},{8,10},{10,8},{12,... | collective-permute-start | bytes 1769480 | tf_op jit(solution)/shard_map/ppermute | solution.py:29
  87.3 35.8 %collective-permute-start.12 = (bf16[2,96,1536]{2,1,0:T(8,128)(2,1)S(1)}, bf16[2,96,1536]{2,1,0:T(8,128)(2,1)S(1)}, u32[]{:S(2)}, u32[]{:S(2)}) collective-permute-start(bf16[2,96,1536]{2,1,0:T(8,128)(2,1)S(1)} %pad_maximum_fusion.5), channel_id=1, source_target_pairs={{0,32},{16,48},{32,0},{48,16},{1,33},{17,49},{33,1},{49,17},{2,34}... | collective-permute-start | bytes 1769480 | tf_op jit(solution)/shard_map/ppermute | solution.py:21
  110.4 27.5 %collective-permute-start.15 = (bf16[2,96,1536]{2,1,0:T(8,128)(2,1)S(1)}, bf16[2,96,1536]{2,1,0:T(8,128)(2,1)S(1)}, u32[]{:S(2)}, u32[]{:S(2)}) collective-permute-start(bf16[2,96,1536]{2,1,0:T(8,128)(2,1)S(1)} %pad_maximum_fusion.6), channel_id=1, source_target_pairs={{0,48},{16,0},{32,16},{48,32},{1,49},{17,1},{33,17},{49,33},{2,50}... | collective-permute-start | bytes 1769480 | tf_op jit(solution)/shard_map/ppermute | solution.py:21
  112.3 21.9 %collective-permute-start.17 = (bf16[2,96,1536]{2,1,0:T(8,128)(2,1)S(1)}, bf16[2,96,1536]{2,1,0:T(8,128)(2,1)S(1)}, u32[]{:S(2)}, u32[]{:S(2)}) collective-permute-start(bf16[2,96,1536]{2,1,0:T(8,128)(2,1)S(1)} %pad_maximum_fusion.6), channel_id=1, source_target_pairs={{0,16},{16,32},{32,48},{48,0},{1,17},{17,33},{33,49},{49,1},{2,18}... | collective-permute-start | bytes 1769480 | tf_op jit(solution)/shard_map/ppermute | solution.py:21
  115.7 13.5 %collective-permute-start.18 = (bf16[96,1536]{1,0:T(8,128)(2,1)S(1)}, bf16[96,1536]{1,0:T(8,128)(2,1)S(1)}, u32[]{:S(2)}, u32[]{:S(2)}) collective-permute-start(bf16[96,1536]{1,0:T(8,128)(2,1)S(1)} %collective-permute-done.13), channel_id=1, source_target_pairs={{0,128},{128,256},{256,384},{384,448},{448,320},{320,192},{192,64}... | collective-permute-start | bytes 884744 | tf_op jit(solution)/shard_map/ppermute | solution.py:21
  118.0 29.4 %collective-permute-start.24 = (bf16[768,768]{1,0:T(8,128)(2,1)S(1)}, bf16[768,768]{1,0:T(8,128)(2,1)S(1)}, u32[]{:S(2)}, u32[]{:S(2)}) collective-permute-start(bf16[768,768]{1,0:T(8,128)(2,1)S(1)} %pad_maximum_fusion.3), channel_id=1, source_target_pairs={{0,4},{2,6},{4,0},{6,2},{1,5},{3,7},{5,1},{7,3},{8,12},{10,14},{12... | collective-permute-start | bytes 3538952 | tf_op jit(solution)/shard_map/ppermute | solution.py:29
  123.1 23.1 %collective-permute-start.16 = (bf16[2,96,1536]{2,1,0:T(8,128)(2,1)S(1)}, bf16[2,96,1536]{2,1,0:T(8,128)(2,1)S(1)}, u32[]{:S(2)}, u32[]{:S(2)}) collective-permute-start(bf16[2,96,1536]{2,1,0:T(8,128)(2,1)S(1)} %pad_maximum_fusion.6), channel_id=1, source_target_pairs={{0,32},{16,48},{32,0},{48,16},{1,33},{17,49},{33,1},{49,17},{2,34}... | collective-permute-start | bytes 1769480 | tf_op jit(solution)/shard_map/ppermute | solution.py:21
  129.2 27.4 %collective-permute-start.21 = (bf16[1,96,1536]{2,1,0:T(8,128)(2,1)S(1)}, bf16[1,96,1536]{2,1,0:T(8,128)(2,1)S(1)}, u32[]{:S(2)}, u32[]{:S(2)}) collective-permute-start(bf16[1,96,1536]{2,1,0:T(8,128)(2,1)S(1)} %bitcast.167), channel_id=1, source_target_pairs={{0,16},{16,32},{32,48},{48,0},{1,17},{17,33},{33,49},{49,1},{2,18}... | collective-permute-start | bytes 884744 | tf_op jit(solution)/shard_map/ppermute | solution.py:21
  134.2 22.1 %collective-permute-start.19 = (bf16[1,96,1536]{2,1,0:T(8,128)(2,1)S(1)}, bf16[1,96,1536]{2,1,0:T(8,128)(2,1)S(1)}, u32[]{:S(2)}, u32[]{:S(2)}) collective-permute-start(bf16[1,96,1536]{2,1,0:T(8,128)(2,1)S(1)} %bitcast.168), channel_id=1, source_target_pairs={{0,48},{16,0},{32,16},{48,32},{1,49},{17,1},{33,17},{49,33},{2,50}... | collective-permute-start | bytes 884744 | tf_op jit(solution)/shard_map/ppermute | solution.py:21
  137.9 18.7 %collective-permute-start.20 = (bf16[1,96,1536]{2,1,0:T(8,128)(2,1)S(1)}, bf16[1,96,1536]{2,1,0:T(8,128)(2,1)S(1)}, u32[]{:S(2)}, u32[]{:S(2)}) collective-permute-start(bf16[1,96,1536]{2,1,0:T(8,128)(2,1)S(1)} %bitcast.169), channel_id=1, source_target_pairs={{0,32},{16,48},{32,0},{48,16},{1,33},{17,49},{33,1},{49,17},{2,34}... | collective-permute-start | bytes 884744 | tf_op jit(solution)/shard_map/ppermute | solution.py:21
  148.0 12.0 %collective-permute-start.25 = (bf16[1536,768]{1,0:T(8,128)(2,1)S(1)}, bf16[1536,768]{1,0:T(8,128)(2,1)S(1)}, u32[]{:S(2)}, u32[]{:S(2)}) collective-permute-start(bf16[1536,768]{1,0:T(8,128)(2,1)S(1)} %pad_maximum_fusion.2), channel_id=1, source_target_pairs={{0,1},{1,0},{2,3},{3,2},{4,5},{5,4},{6,7},{7,6},{8,9},{9,8},{10,11... | collective-permute-start | bytes 7077896 | tf_op jit(solution)/shard_map/ppermute | solution.py:21
  167.7 6.3 %collective-permute-start.26 = (f32[4,2,192,256]{3,2,1,0:T(8,128)S(1)}, f32[4,2,192,256]{3,2,1,0:T(8,128)S(1)}, u32[]{:S(2)}, u32[]{:S(2)}) collective-permute-start(f32[4,2,192,256]{3,2,1,0:T(8,128)S(1)} %dynamic-slice_bitcast_fusion), channel_id=1, source_target_pairs={{0,1},{1,0},{2,3},{3,2},{4,5},{5,4},{6,7},{7,6},{8,9},{9,8},{10,11... | collective-permute-start | bytes 4718600 | tf_op jit(solution)/shard_map/ppermute | solution.py:21
  175.2 15.9 %all-to-all-start = ((bf16[4,2,192,256]{3,2,1,0:T(8,128)(2,1)}), bf16[4,2,192,256]{3,2,1,0:T(8,128)(2,1)S(1)}, u32[]{:S(2)}, u32[]{:S(2)}) async-start(bf16[4,2,192,256]{3,2,1,0:T(8,128)(2,1)} %fusion.10), calls=%async_computation | async-start | bytes 1572864 | tf_op jit(solution)/shard_map/all_to_all | solution.py:124
  191.2 21.0 %collective-permute-start.27 = (bf16[192,256]{1,0:T(8,128)(2,1)S(1)}, bf16[192,256]{1,0:T(8,128)(2,1)S(1)}, u32[]{:S(2)}, u32[]{:S(2)}) collective-permute-start(bf16[192,256]{1,0:T(8,128)(2,1)S(1)} %fusion.47), channel_id=1, source_target_pairs={{0,8},{8,0},{1,9},{9,1},{2,10},{10,2},{3,11},{11,3},{4,12},{12,4},... | collective-permute-start | bytes 294920 | tf_op jit(solution)/shard_map/ppermute | solution.py:21

commit v6 on v5

--- a/solution.py
+++ b/solution.py
@@ -44,7 +44,6 @@
 
 def body(tokens, tangent, cotangent, gates, slot_tokens, gate_weight, up_weight, down_weight):
     zl, x, zh, y, c = (lax.axis_index(a).astype(jnp.uint32) for a in ("zl", "x", "zh", "y", "c"))
-    packed = take(jnp.asarray(SOURCES), zl)
 
     own = jnp.concatenate([gate_weight, up_weight, down_weight.T], axis=1)
     rows, width = own.shape
@@ -68,23 +67,25 @@
     p2 = x_up(after(g2, a3))
     m2 = x_down(after(g2, b3))
     f2 = x_far(after(g2, f0))
-    fields = join(fields, other_half, zh, b3)
-    fields = join(fields, y_near, y & 1, p2)
+    fields = join(fields, other_half, zh, m1, p1)
+    fields = join(fields, y_near, y & 1, b3)
     a4 = ring_up(after(a3, f1))
     g3 = jnp.stack([a3, b3])
     p3 = x_up(after(g3, p2))
     m3 = x_down(after(g3, m2))
     f3 = x_far(after(g3, f2))
-    fields = join(fields, y_far, y >> 1, p3)
+    fields = join(fields, y_far, y >> 1, m2)
     g4 = a4[None]
     p4 = x_up(g4)
     m4 = x_down(after(g4, p3))
     f4 = x_far(after(g4, m3))
     fields = join(fields, other_core, c)
 
-    zero = a2[0, 0] * 0
+    zero = f0[0, 0, 0] * 0
     full = jnp.broadcast_to(zero, (NC, NY, NH, 2, rows, width))
     none = jnp.uint32(0)
+    zl, x, _ = lax.optimization_barrier((zl, x, f0))
+    packed = take(jnp.asarray(SOURCES), zl)
     sources = iter((((packed >> 3 * j) & 3, (packed >> 3 * j + 2) & 1) for j in range(NZ)))
     groups = ((g0, m0, f0, p0), (g1, m1, f1, p1), (g2, m2, f2, p2), (g3, m3, f3, p3), (g4, m4, f4, p4))
     for parts in groups:

time: 214 us -> 216 us (level)
  the two profiles are of different devices: /device:TPU:99 before, /device:TPU:65 now
where the time goes in v6:
time: 216 us; the launch traced here: 215 us
  starting transfers between devices  108 us (50%)
  waiting for transfers between devices  64.6 us (30%)
  other arithmetic  12.7 us (6%)
  between operations  11.8 us (5%)
  local copies, waits for them, and re-layouts  11.4 us (5%)
  matrix products  6.51 us (3%)
    ppermute x26, starting transfers between devices, shift(): return lambda v: lax.ppermute(v, axis, pairs)  97.7 us
    ppermute x26, waiting for transfers between devices, shift(): return lambda v: lax.ppermute(v, axis, pairs)  48.5 us
    all_to_all x1, waiting for transfers between devices, body(): shares = lax.all_to_all(sums.astype(BF), 'y', 0, 0, tiled=True).astype(F32)  12 us
    dynamic_update_slice x31, local copies, waits for them, and re-layouts, body(): lax.dynamic_update_slice(full, part[j][None, None, None, None], where)  7.62 us
    ppermute x2, starting transfers between devices, flip(): return lambda v: lax.ppermute(v, axis, [(i, i ^ bit) for i in range(n)])  6.44 us
  transfers between devices with their start and end apart: 29, of which 9 were waited for; matrix products, arithmetic and copies ran while one was open for 9% of the time, Pallas kernels for 0%

profile of v6, /device:TPU:65, one launch (start us, length us, event | category | flops | bytes accessed | tf_op | source)
XLA Modules:
  0.0 214.6 jit_solution(7056639201471744717)
XLA Ops:
  0.0 1.8 pad_maximum_fusion.8
  1.8 6.1 %collective-permute-start = (bf16[96,1536]{1,0:T(8,128)(2,1)S(1)}, bf16[96,1536]{1,0:T(8,128)(2,1)S(1)}, u32[]{:S(2)}, u32[]{:S(2)}) collective-permute-start(bf16[96,1536]{1,0:T(8,128)(2,1)S(1)} %get-tuple-element.51), channel_id=1, source_target_pairs={{0,128},{128,256},{256,384},{384,448},{448,320},{320,192},{192,64}... | collective-permute-start | bytes 884744 | tf_op jit(solution)/shard_map/ppermute | solution.py:21
  7.9 1.9 collective-permute-start.1
  9.8 4.4 %collective-permute-start.2 = (bf16[1,96,1536]{2,1,0:T(8,128)(2,1)}, bf16[1,96,1536]{2,1,0:T(8,128)(2,1)S(1)}, u32[]{:S(2)}, u32[]{:S(2)}) collective-permute-start(bf16[1,96,1536]{2,1,0:T(8,128)(2,1)} %get-tuple-element.24), channel_id=1, source_target_pairs={{0,48},{16,0},{32,16},{48,32},{1,49},{17,1},{33,17},{49,33},{2,50}... | collective-permute-start | bytes 884744 | tf_op jit(solution)/shard_map/ppermute | solution.py:21
  14.2 1.9 collective-permute-start.5
  16.1 3.8 %collective-permute-done = bf16[96,1536]{1,0:T(8,128)(2,1)S(1)} collective-permute-done((bf16[96,1536]{1,0:T(8,128)(2,1)S(1)}, bf16[96,1536]{1,0:T(8,128)(2,1)S(1)}, u32[]{:S(2)}, u32[]{:S(2)}) %collective-permute-start) | collective-permute-done | bytes 294944 | tf_op jit(solution)/shard_map/ppermute | solution.py:21
  19.9 6.3 %collective-permute-start.8 = (bf16[96,1536]{1,0:T(8,128)(2,1)S(1)}, bf16[96,1536]{1,0:T(8,128)(2,1)S(1)}, u32[]{:S(2)}, u32[]{:S(2)}) collective-permute-start(bf16[96,1536]{1,0:T(8,128)(2,1)S(1)} %collective-permute-done), channel_id=1, source_target_pairs={{0,128},{128,256},{256,384},{384,448},{448,320},{320,192},{192,64}... | collective-permute-start | bytes 884744 | tf_op jit(solution)/shard_map/ppermute | solution.py:21
  26.2 1.9 collective-permute-start.9
  29.0 4.3 %collective-permute-start.3 = (bf16[2,96,1536]{2,1,0:T(8,128)(2,1)}, bf16[2,96,1536]{2,1,0:T(8,128)(2,1)S(1)}, u32[]{:S(2)}, u32[]{:S(2)}) collective-permute-start(bf16[2,96,1536]{2,1,0:T(8,128)(2,1)} %pad_maximum_fusion.4), channel_id=1, source_target_pairs={{0,48},{16,0},{32,16},{48,32},{1,49},{17,1},{33,17},{49,33},{2,50}... | collective-permute-start | bytes 1769480 | tf_op jit(solution)/shard_map/ppermute | solution.py:21
  33.4 1.9 collective-permute-start.6
  35.3 1.0 pad_maximum_fusion.9
  36.3 8.9 %collective-permute-start.22 = (bf16[192,768]{1,0:T(8,128)(2,1)S(1)}, bf16[192,768]{1,0:T(8,128)(2,1)S(1)}, u32[]{:S(2)}, u32[]{:S(2)}) collective-permute-start(bf16[192,768]{1,0:T(8,128)(2,1)S(1)} %pad_maximum_fusion.9), channel_id=1, source_target_pairs={{0,8},{8,0},{1,9},{9,1},{2,10},{10,2},{3,11},{11,3},{4,12},{12,4},... | collective-permute-start | bytes 884744 | tf_op jit(solution)/shard_map/ppermute | solution.py:21
  46.1 1.9 collective-permute-start.10
  48.0 5.5 %collective-permute-start.13 = (bf16[96,1536]{1,0:T(8,128)(2,1)S(1)}, bf16[96,1536]{1,0:T(8,128)(2,1)S(1)}, u32[]{:S(2)}, u32[]{:S(2)}) collective-permute-start(bf16[96,1536]{1,0:T(8,128)(2,1)S(1)} %collective-permute-done.8), channel_id=1, source_target_pairs={{0,128},{128,256},{256,384},{384,448},{448,320},{320,192},{192,64}... | collective-permute-start | bytes 884744 | tf_op jit(solution)/shard_map/ppermute | solution.py:21
  55.1 3.7 %collective-permute-start.4 = (bf16[1,96,1536]{2,1,0:T(8,128)(2,1)}, bf16[1,96,1536]{2,1,0:T(8,128)(2,1)}, u32[]{:S(2)}, u32[]{:S(2)}) collective-permute-start(bf16[1,96,1536]{2,1,0:T(8,128)(2,1)} %get-tuple-element.24), channel_id=1, source_target_pairs={{0,32},{16,48},{32,0},{48,16},{1,33},{17,49},{33,1},{49,17},{2,34}... | collective-permute-start | bytes 884744 | tf_op jit(solution)/shard_map/ppermute | solution.py:21
  58.8 3.1 %collective-permute-start.7 = (bf16[2,96,1536]{2,1,0:T(8,128)(2,1)}, bf16[2,96,1536]{2,1,0:T(8,128)(2,1)}, u32[]{:S(2)}, u32[]{:S(2)}) collective-permute-start(bf16[2,96,1536]{2,1,0:T(8,128)(2,1)} %pad_maximum_fusion.4), channel_id=1, source_target_pairs={{0,32},{16,48},{32,0},{48,16},{1,33},{17,49},{33,1},{49,17},{2,34}... | collective-permute-start | bytes 1769480 | tf_op jit(solution)/shard_map/ppermute | solution.py:21
  61.9 22.0 %collective-permute-done.10 = bf16[96,1536]{1,0:T(8,128)(2,1)S(1)} collective-permute-done((bf16[96,1536]{1,0:T(8,128)(2,1)S(1)}, bf16[96,1536]{1,0:T(8,128)(2,1)S(1)}, u32[]{:S(2)}, u32[]{:S(2)}) %collective-permute-start.10) | collective-permute-done | bytes 294944 | tf_op jit(solution)/shard_map/ppermute | solution.py:21
  83.9 1.9 collective-permute-start.11
  85.8 3.4 %collective-permute-start.14 = (bf16[2,96,1536]{2,1,0:T(8,128)(2,1)}, bf16[2,96,1536]{2,1,0:T(8,128)(2,1)}, u32[]{:S(2)}, u32[]{:S(2)}) collective-permute-start(bf16[2,96,1536]{2,1,0:T(8,128)(2,1)} %pad_maximum_fusion.5), channel_id=1, source_target_pairs={{0,16},{16,32},{32,48},{48,0},{1,17},{17,33},{33,49},{49,1},{2,18}... | collective-permute-start | bytes 1769480 | tf_op jit(solution)/shard_map/ppermute | solution.py:21
  89.2 1.1 broadcast_select_fusion.7
  91.2 1.9 collective-permute-start.23
  94.0 1.3 dynamic_slice.18
  99.3 2.9 %collective-permute-start.12 = (bf16[2,96,1536]{2,1,0:T(8,128)(2,1)}, bf16[2,96,1536]{2,1,0:T(8,128)(2,1)S(1)}, u32[]{:S(2)}, u32[]{:S(2)}) collective-permute-start(bf16[2,96,1536]{2,1,0:T(8,128)(2,1)} %pad_maximum_fusion.5), channel_id=1, source_target_pairs={{0,32},{16,48},{32,0},{48,16},{1,33},{17,49},{33,1},{49,17},{2,34}... | collective-permute-start | bytes 1769480 | tf_op jit(solution)/shard_map/ppermute | solution.py:21
  102.2 1.2 slice.108
  104.0 1.1 broadcast_in_dim.16
  112.8 3.4 %collective-permute-start.15 = (bf16[2,96,1536]{2,1,0:T(8,128)(2,1)S(1)}, bf16[2,96,1536]{2,1,0:T(8,128)(2,1)S(1)}, u32[]{:S(2)}, u32[]{:S(2)}) collective-permute-start(bf16[2,96,1536]{2,1,0:T(8,128)(2,1)S(1)} %copy-done.2), channel_id=1, source_target_pairs={{0,48},{16,0},{32,16},{48,32},{1,49},{17,1},{33,17},{49,33},{2,50}... | collective-permute-start | bytes 1769480 | tf_op jit(solution)/shard_map/ppermute | solution.py:21
  116.1 1.9 collective-permute-start.17
  118.1 6.2 %collective-permute-start.18 = (bf16[96,1536]{1,0:T(8,128)(2,1)S(1)}, bf16[96,1536]{1,0:T(8,128)(2,1)S(1)}, u32[]{:S(2)}, u32[]{:S(2)}) collective-permute-start(bf16[96,1536]{1,0:T(8,128)(2,1)S(1)} %collective-permute-done.13), channel_id=1, source_target_pairs={{0,128},{128,256},{256,384},{384,448},{448,320},{320,192},{192,64}... | collective-permute-start | bytes 884744 | tf_op jit(solution)/shard_map/ppermute | solution.py:21
  124.6 4.5 %collective-permute-start.24 = (bf16[768,768]{1,0:T(8,128)(2,1)S(1)}, bf16[768,768]{1,0:T(8,128)(2,1)S(1)}, u32[]{:S(2)}, u32[]{:S(2)}) collective-permute-start(bf16[768,768]{1,0:T(8,128)(2,1)S(1)} %pad_maximum_fusion.3), channel_id=1, source_target_pairs={{0,4},{2,6},{4,0},{6,2},{1,5},{3,7},{5,1},{7,3},{8,12},{10,14},{12... | collective-permute-start | bytes 3538952 | tf_op jit(solution)/shard_map/ppermute | solution.py:29
  133.3 1.9 collective-permute-start.16
  135.2 3.8 %collective-permute-start.21 = (bf16[1,96,1536]{2,1,0:T(8,128)(2,1)S(1)}, bf16[1,96,1536]{2,1,0:T(8,128)(2,1)S(1)}, u32[]{:S(2)}, u32[]{:S(2)}) collective-permute-start(bf16[1,96,1536]{2,1,0:T(8,128)(2,1)S(1)} %bitcast.167), channel_id=1, source_target_pairs={{0,16},{16,32},{32,48},{48,0},{1,17},{17,33},{33,49},{49,1},{2,18}... | collective-permute-start | bytes 884744 | tf_op jit(solution)/shard_map/ppermute | solution.py:21
  141.2 2.7 %collective-permute-start.19 = (bf16[1,96,1536]{2,1,0:T(8,128)(2,1)S(1)}, bf16[1,96,1536]{2,1,0:T(8,128)(2,1)S(1)}, u32[]{:S(2)}, u32[]{:S(2)}) collective-permute-start(bf16[1,96,1536]{2,1,0:T(8,128)(2,1)S(1)} %bitcast.168), channel_id=1, source_target_pairs={{0,48},{16,0},{32,16},{48,32},{1,49},{17,1},{33,17},{49,33},{2,50}... | collective-permute-start | bytes 884744 | tf_op jit(solution)/shard_map/ppermute | solution.py:21
  143.9 3.7 %collective-permute-start.20 = (bf16[1,96,1536]{2,1,0:T(8,128)(2,1)S(1)}, bf16[1,96,1536]{2,1,0:T(8,128)(2,1)S(1)}, u32[]{:S(2)}, u32[]{:S(2)}) collective-permute-start(bf16[1,96,1536]{2,1,0:T(8,128)(2,1)S(1)} %bitcast.169), channel_id=1, source_target_pairs={{0,32},{16,48},{32,0},{48,16},{1,33},{17,49},{33,1},{49,17},{2,34}... | collective-permute-start | bytes 884744 | tf_op jit(solution)/shard_map/ppermute | solution.py:21
  147.6 1.5 collective-permute-done.16
  149.2 4.1 %collective-permute-done.24 = bf16[768,768]{1,0:T(8,128)(2,1)S(1)} collective-permute-done((bf16[768,768]{1,0:T(8,128)(2,1)S(1)}, bf16[768,768]{1,0:T(8,128)(2,1)S(1)}, u32[]{:S(2)}, u32[]{:S(2)}) %collective-permute-start.24) | collective-permute-done | bytes 1179680 | tf_op jit(solution)/shard_map/ppermute | solution.py:29
  153.9 5.2 %collective-permute-start.25 = (bf16[1536,768]{1,0:T(8,128)(2,1)S(1)}, bf16[1536,768]{1,0:T(8,128)(2,1)S(1)}, u32[]{:S(2)}, u32[]{:S(2)}) collective-permute-start(bf16[1536,768]{1,0:T(8,128)(2,1)S(1)} %pad_maximum_fusion.2), channel_id=1, source_target_pairs={{0,1},{1,0},{2,3},{3,2},{4,5},{5,4},{6,7},{7,6},{8,9},{9,8},{10,11... | collective-permute-start | bytes 7077896 | tf_op jit(solution)/shard_map/ppermute | solution.py:21
  159.3 2.4 %collective-permute-done.20 = bf16[1,96,1536]{2,1,0:T(8,128)(2,1)S(1)} collective-permute-done((bf16[1,96,1536]{2,1,0:T(8,128)(2,1)S(1)}, bf16[1,96,1536]{2,1,0:T(8,128)(2,1)S(1)}, u32[]{:S(2)}, u32[]{:S(2)}) %collective-permute-start.20) | collective-permute-done | bytes 294944 | tf_op jit(solution)/shard_map/ppermute | solution.py:21
  161.8 1.3 collective-permute-done.25
  164.1 3.4 %fusion.2 = f32[512,1024]{1,0:T(8,128)S(1)} fusion(bf16[3072,1536]{1,0:T(8,128)(2,1)S(1)} %bitcast.148, bf16[1536,768]{1,0:T(8,128)(2,1)S(1)} %get-tuple-element.42, bf16[1536,768]{1,0:T(8,128)(2,1)S(1)} %get-tuple-element.41), kind=kOutput, calls=%fused_computation.2 | convolution fusion | flops 3227516928 | bytes 13107200 | tf_op jit(solution)/shard_map/dot_general | solution.py:103
  167.5 1.3 fusion.23
  168.8 1.8 fusion
  170.8 4.0 %collective-permute-start.26 = (f32[4,2,192,256]{3,2,1,0:T(8,128)S(1)}, f32[4,2,192,256]{3,2,1,0:T(8,128)S(1)}, u32[]{:S(2)}, u32[]{:S(2)}) collective-permute-start(f32[4,2,192,256]{3,2,1,0:T(8,128)S(1)} %dynamic-slice_bitcast_fusion), channel_id=1, source_target_pairs={{0,1},{1,0},{2,3},{3,2},{4,5},{5,4},{6,7},{7,6},{8,9},{9,8},{10,11... | collective-permute-start | bytes 4718600 | tf_op jit(solution)/shard_map/ppermute | solution.py:21
  174.8 3.0 %collective-permute-done.26 = f32[4,2,192,256]{3,2,1,0:T(8,128)S(1)} collective-permute-done((f32[4,2,192,256]{3,2,1,0:T(8,128)S(1)}, f32[4,2,192,256]{3,2,1,0:T(8,128)S(1)}, u32[]{:S(2)}, u32[]{:S(2)}) %collective-permute-start.26) | collective-permute-done | bytes 1572896 | tf_op jit(solution)/shard_map/ppermute | solution.py:21
  177.8 1.1 fusion.10
  178.9 3.5 %all-to-all-start = ((bf16[4,2,192,256]{3,2,1,0:T(8,128)(2,1)}), bf16[4,2,192,256]{3,2,1,0:T(8,128)(2,1)S(1)}, u32[]{:S(2)}, u32[]{:S(2)}) async-start(bf16[4,2,192,256]{3,2,1,0:T(8,128)(2,1)} %fusion.10), calls=%async_computation | async-start | bytes 1572864 | tf_op jit(solution)/shard_map/all_to_all | solution.py:125
  182.4 12.0 %all-to-all-done = bf16[4,2,192,256]{3,2,1,0:T(8,128)(2,1)S(1)} async-done(((bf16[4,2,192,256]{3,2,1,0:T(8,128)(2,1)}), bf16[4,2,192,256]{3,2,1,0:T(8,128)(2,1)S(1)}, u32[]{:S(2)}, u32[]{:S(2)}) %all-to-all-start) | async-done | bytes 786464 | tf_op jit(solution)/shard_map/all_to_all | solution.py:125
  194.6 5.0 %collective-permute-start.27 = (bf16[192,256]{1,0:T(8,128)(2,1)S(1)}, bf16[192,256]{1,0:T(8,128)(2,1)S(1)}, u32[]{:S(2)}, u32[]{:S(2)}) collective-permute-start(bf16[192,256]{1,0:T(8,128)(2,1)S(1)} %fusion.47), channel_id=1, source_target_pairs={{0,8},{8,0},{1,9},{9,1},{2,10},{10,2},{3,11},{11,3},{4,12},{12,4},... | collective-permute-start | bytes 294920 | tf_op jit(solution)/shard_map/ppermute | solution.py:21
  199.5 14.4 %collective-permute-done.27 = bf16[192,256]{1,0:T(8,128)(2,1)S(1)} collective-permute-done((bf16[192,256]{1,0:T(8,128)(2,1)S(1)}, bf16[192,256]{1,0:T(8,128)(2,1)S(1)}, u32[]{:S(2)}, u32[]{:S(2)}) %collective-permute-start.27) | collective-permute-done | bytes 98336 | tf_op jit(solution)/shard_map/ppermute | solution.py:21
  (87 shorter events, 15.6 us)
Async XLA Ops:
  1.8 18.2 %collective-permute-start = (bf16[96,1536]{1,0:T(8,128)(2,1)S(1)}, bf16[96,1536]{1,0:T(8,128)(2,1)S(1)}, u32[]{:S(2)}, u32[]{:S(2)}) collective-permute-start(bf16[96,1536]{1,0:T(8,128)(2,1)S(1)} %get-tuple-element.51), channel_id=1, source_target_pairs={{0,128},{128,256},{256,384},{384,448},{448,320},{320,192},{192,64}... | collective-permute-start | bytes 884744 | tf_op jit(solution)/shard_map/ppermute | solution.py:21
  7.9 18.3 %collective-permute-start.1 = (bf16[96,1536]{1,0:T(8,128)(2,1)S(1)}, bf16[96,1536]{1,0:T(8,128)(2,1)S(1)}, u32[]{:S(2)}, u32[]{:S(2)}) collective-permute-start(bf16[96,1536]{1,0:T(8,128)(2,1)S(1)} %get-tuple-element.51), channel_id=1, source_target_pairs={{0,64},{128,0},{256,128},{384,256},{448,384},{320,448},{192,320},{... | collective-permute-start | bytes 884744 | tf_op jit(solution)/shard_map/ppermute | solution.py:21
  9.8 19.2 %collective-permute-start.2 = (bf16[1,96,1536]{2,1,0:T(8,128)(2,1)}, bf16[1,96,1536]{2,1,0:T(8,128)(2,1)S(1)}, u32[]{:S(2)}, u32[]{:S(2)}) collective-permute-start(bf16[1,96,1536]{2,1,0:T(8,128)(2,1)} %get-tuple-element.24), channel_id=1, source_target_pairs={{0,48},{16,0},{32,16},{48,32},{1,49},{17,1},{33,17},{49,33},{2,50}... | collective-permute-start | bytes 884744 | tf_op jit(solution)/shard_map/ppermute | solution.py:21
  14.2 19.2 %collective-permute-start.5 = (bf16[1,96,1536]{2,1,0:T(8,128)(2,1)}, bf16[1,96,1536]{2,1,0:T(8,128)(2,1)S(1)}, u32[]{:S(2)}, u32[]{:S(2)}) collective-permute-start(bf16[1,96,1536]{2,1,0:T(8,128)(2,1)} %get-tuple-element.24), channel_id=1, source_target_pairs={{0,16},{16,32},{32,48},{48,0},{1,17},{17,33},{33,49},{49,1},{2,18}... | collective-permute-start | bytes 884744 | tf_op jit(solution)/shard_map/ppermute | solution.py:21
  19.9 28.1 %collective-permute-start.8 = (bf16[96,1536]{1,0:T(8,128)(2,1)S(1)}, bf16[96,1536]{1,0:T(8,128)(2,1)S(1)}, u32[]{:S(2)}, u32[]{:S(2)}) collective-permute-start(bf16[96,1536]{1,0:T(8,128)(2,1)S(1)} %collective-permute-done), channel_id=1, source_target_pairs={{0,128},{128,256},{256,384},{384,448},{448,320},{320,192},{192,64}... | collective-permute-start | bytes 884744 | tf_op jit(solution)/shard_map/ppermute | solution.py:21
  26.2 19.9 %collective-permute-start.9 = (bf16[96,1536]{1,0:T(8,128)(2,1)S(1)}, bf16[96,1536]{1,0:T(8,128)(2,1)S(1)}, u32[]{:S(2)}, u32[]{:S(2)}) collective-permute-start(bf16[96,1536]{1,0:T(8,128)(2,1)S(1)} %collective-permute-done.1), channel_id=1, source_target_pairs={{0,64},{128,0},{256,128},{384,256},{448,384},{320,448},{192,320},{... | collective-permute-start | bytes 884744 | tf_op jit(solution)/shard_map/ppermute | solution.py:21
  29.0 19.0 %copy-start.8 = (bf16[1,96,1536]{2,1,0:T(8,128)(2,1)}, bf16[1,96,1536]{2,1,0:T(8,128)(2,1)S(1)}, u32[]{:S(2)}) copy-start(bf16[1,96,1536]{2,1,0:T(8,128)(2,1)S(1)} %collective-permute-done.2) | copy-start | bytes 884740
  29.0 26.1 %collective-permute-start.3 = (bf16[2,96,1536]{2,1,0:T(8,128)(2,1)}, bf16[2,96,1536]{2,1,0:T(8,128)(2,1)S(1)}, u32[]{:S(2)}, u32[]{:S(2)}) collective-permute-start(bf16[2,96,1536]{2,1,0:T(8,128)(2,1)} %pad_maximum_fusion.4), channel_id=1, source_target_pairs={{0,48},{16,0},{32,16},{48,32},{1,49},{17,1},{33,17},{49,33},{2,50}... | collective-permute-start | bytes 1769480 | tf_op jit(solution)/shard_map/ppermute | solution.py:21
  33.4 12.7 %copy-start.6 = (bf16[1,96,1536]{2,1,0:T(8,128)(2,1)}, bf16[1,96,1536]{2,1,0:T(8,128)(2,1)S(1)}, u32[]{:S(2)}) copy-start(bf16[1,96,1536]{2,1,0:T(8,128)(2,1)S(1)} %collective-permute-done.5) | copy-start | bytes 884740
  33.4 25.4 %collective-permute-start.6 = (bf16[2,96,1536]{2,1,0:T(8,128)(2,1)}, bf16[2,96,1536]{2,1,0:T(8,128)(2,1)S(1)}, u32[]{:S(2)}, u32[]{:S(2)}) collective-permute-start(bf16[2,96,1536]{2,1,0:T(8,128)(2,1)} %pad_maximum_fusion.4), channel_id=1, source_target_pairs={{0,16},{16,32},{32,48},{48,0},{1,17},{17,33},{33,49},{49,1},{2,18}... | collective-permute-start | bytes 1769480 | tf_op jit(solution)/shard_map/ppermute | solution.py:21
  36.3 52.9 %collective-permute-start.22 = (bf16[192,768]{1,0:T(8,128)(2,1)S(1)}, bf16[192,768]{1,0:T(8,128)(2,1)S(1)}, u32[]{:S(2)}, u32[]{:S(2)}) collective-permute-start(bf16[192,768]{1,0:T(8,128)(2,1)S(1)} %pad_maximum_fusion.9), channel_id=1, source_target_pairs={{0,8},{8,0},{1,9},{9,1},{2,10},{10,2},{3,11},{11,3},{4,12},{12,4},... | collective-permute-start | bytes 884744 | tf_op jit(solution)/shard_map/ppermute | solution.py:21
  46.1 37.8 %collective-permute-start.10 = (bf16[96,1536]{1,0:T(8,128)(2,1)S(1)}, bf16[96,1536]{1,0:T(8,128)(2,1)S(1)}, u32[]{:S(2)}, u32[]{:S(2)}) collective-permute-start(bf16[96,1536]{1,0:T(8,128)(2,1)S(1)} %collective-permute-done.9), channel_id=1, source_target_pairs={{0,64},{128,0},{256,128},{384,256},{448,384},{320,448},{192,320},{... | collective-permute-start | bytes 884744 | tf_op jit(solution)/shard_map/ppermute | solution.py:21
  48.0 37.8 %collective-permute-start.13 = (bf16[96,1536]{1,0:T(8,128)(2,1)S(1)}, bf16[96,1536]{1,0:T(8,128)(2,1)S(1)}, u32[]{:S(2)}, u32[]{:S(2)}) collective-permute-start(bf16[96,1536]{1,0:T(8,128)(2,1)S(1)} %collective-permute-done.8), channel_id=1, source_target_pairs={{0,128},{128,256},{256,384},{384,448},{448,320},{320,192},{192,64}... | collective-permute-start | bytes 884744 | tf_op jit(solution)/shard_map/ppermute | solution.py:21
  55.1 34.1 %copy-start = (bf16[2,96,1536]{2,1,0:T(8,128)(2,1)}, bf16[2,96,1536]{2,1,0:T(8,128)(2,1)S(1)}, u32[]{:S(2)}) copy-start(bf16[2,96,1536]{2,1,0:T(8,128)(2,1)S(1)} %collective-permute-done.3) | copy-start | bytes 1769476
  55.1 38.9 %collective-permute-start.4 = (bf16[1,96,1536]{2,1,0:T(8,128)(2,1)}, bf16[1,96,1536]{2,1,0:T(8,128)(2,1)}, u32[]{:S(2)}, u32[]{:S(2)}) collective-permute-start(bf16[1,96,1536]{2,1,0:T(8,128)(2,1)} %get-tuple-element.24), channel_id=1, source_target_pairs={{0,32},{16,48},{32,0},{48,16},{1,33},{17,49},{33,1},{49,17},{2,34}... | collective-permute-start | bytes 884744 | tf_op jit(solution)/shard_map/ppermute | solution.py:21
  58.8 59.3 %collective-permute-start.7 = (bf16[2,96,1536]{2,1,0:T(8,128)(2,1)}, bf16[2,96,1536]{2,1,0:T(8,128)(2,1)}, u32[]{:S(2)}, u32[]{:S(2)}) collective-permute-start(bf16[2,96,1536]{2,1,0:T(8,128)(2,1)} %pad_maximum_fusion.4), channel_id=1, source_target_pairs={{0,32},{16,48},{32,0},{48,16},{1,33},{17,49},{33,1},{49,17},{2,34}... | collective-permute-start | bytes 1769480 | tf_op jit(solution)/shard_map/ppermute | solution.py:21
  83.9 28.8 %collective-permute-start.11 = (bf16[2,96,1536]{2,1,0:T(8,128)(2,1)}, bf16[2,96,1536]{2,1,0:T(8,128)(2,1)}, u32[]{:S(2)}, u32[]{:S(2)}) collective-permute-start(bf16[2,96,1536]{2,1,0:T(8,128)(2,1)} %pad_maximum_fusion.5), channel_id=1, source_target_pairs={{0,48},{16,0},{32,16},{48,32},{1,49},{17,1},{33,17},{49,33},{2,50}... | collective-permute-start | bytes 1769480 | tf_op jit(solution)/shard_map/ppermute | solution.py:21
  85.8 30.3 %collective-permute-start.14 = (bf16[2,96,1536]{2,1,0:T(8,128)(2,1)}, bf16[2,96,1536]{2,1,0:T(8,128)(2,1)}, u32[]{:S(2)}, u32[]{:S(2)}) collective-permute-start(bf16[2,96,1536]{2,1,0:T(8,128)(2,1)} %pad_maximum_fusion.5), channel_id=1, source_target_pairs={{0,16},{16,32},{32,48},{48,0},{1,17},{17,33},{33,49},{49,1},{2,18}... | collective-permute-start | bytes 1769480 | tf_op jit(solution)/shard_map/ppermute | solution.py:21
  91.2 33.1 %collective-permute-start.23 = (bf16[384,768]{1,0:T(8,128)(2,1)}, bf16[384,768]{1,0:T(8,128)(2,1)S(1)}, u32[]{:S(2)}, u32[]{:S(2)}) collective-permute-start(bf16[384,768]{1,0:T(8,128)(2,1)} %pad_maximum_fusion.7), channel_id=1, source_target_pairs={{0,2},{2,0},{4,6},{6,4},{1,3},{3,1},{5,7},{7,5},{8,10},{10,8},{12,... | collective-permute-start | bytes 1769480 | tf_op jit(solution)/shard_map/ppermute | solution.py:29
  97.2 7.9 %copy-start.3 = (bf16[512,96]{0,1:T(8,128)(2,1)S(1)}, bf16[512,96]{0,1:T(8,128)(2,1)}, u32[]{:S(2)}) copy-start(bf16[512,96]{0,1:T(8,128)(2,1)} %param.16) | copy-start | bytes 294916
  97.2 7.9 %copy-start.4 = (bf16[96,512]{1,0:T(8,128)(2,1)S(1)}, bf16[96,512]{1,0:T(8,128)(2,1)}, u32[]{:S(2)}) copy-start(bf16[96,512]{1,0:T(8,128)(2,1)} %param.15) | copy-start | bytes 294916
  97.2 7.9 %copy-start.5 = (bf16[96,512]{1,0:T(8,128)(2,1)S(1)}, bf16[96,512]{1,0:T(8,128)(2,1)}, u32[]{:S(2)}) copy-start(bf16[96,512]{1,0:T(8,128)(2,1)} %param.14) | copy-start | bytes 294916
  97.2 7.9 %copy-start.9 = (bf16[1,96,1536]{2,1,0:T(8,128)(2,1)S(1)}, bf16[1,96,1536]{2,1,0:T(8,128)(2,1)}, u32[]{:S(2)}) copy-start(bf16[1,96,1536]{2,1,0:T(8,128)(2,1)} %copy-done.8) | copy-start | bytes 884740
  97.2 9.0 %copy-start.7 = (bf16[1,96,1536]{2,1,0:T(8,128)(2,1)S(1)}, bf16[1,96,1536]{2,1,0:T(8,128)(2,1)}, u32[]{:S(2)}) copy-start(bf16[1,96,1536]{2,1,0:T(8,128)(2,1)} %copy-done.6) | copy-start | bytes 884740
  97.2 9.1 %copy-start.1 = (bf16[2,96,1536]{2,1,0:T(8,128)(2,1)S(1)}, bf16[2,96,1536]{2,1,0:T(8,128)(2,1)}, u32[]{:S(2)}) copy-start(bf16[2,96,1536]{2,1,0:T(8,128)(2,1)} %copy-done) | copy-start | bytes 1769476
  97.3 15.5 %copy-start.2 = (bf16[2,96,1536]{2,1,0:T(8,128)(2,1)S(1)}, bf16[2,96,1536]{2,1,0:T(8,128)(2,1)}, u32[]{:S(2)}) copy-start(bf16[2,96,1536]{2,1,0:T(8,128)(2,1)} %pad_maximum_fusion.6) | copy-start | bytes 1769476
  99.3 34.0 %collective-permute-start.12 = (bf16[2,96,1536]{2,1,0:T(8,128)(2,1)}, bf16[2,96,1536]{2,1,0:T(8,128)(2,1)S(1)}, u32[]{:S(2)}, u32[]{:S(2)}) collective-permute-start(bf16[2,96,1536]{2,1,0:T(8,128)(2,1)} %pad_maximum_fusion.5), channel_id=1, source_target_pairs={{0,32},{16,48},{32,0},{48,16},{1,33},{17,49},{33,1},{49,17},{2,34}... | collective-permute-start | bytes 1769480 | tf_op jit(solution)/shard_map/ppermute | solution.py:21
  112.8 31.1 %collective-permute-start.15 = (bf16[2,96,1536]{2,1,0:T(8,128)(2,1)S(1)}, bf16[2,96,1536]{2,1,0:T(8,128)(2,1)S(1)}, u32[]{:S(2)}, u32[]{:S(2)}) collective-permute-start(bf16[2,96,1536]{2,1,0:T(8,128)(2,1)S(1)} %copy-done.2), channel_id=1, source_target_pairs={{0,48},{16,0},{32,16},{48,32},{1,49},{17,1},{33,17},{49,33},{2,50}... | collective-permute-start | bytes 1769480 | tf_op jit(solution)/shard_map/ppermute | solution.py:21
  116.1 25.1 %collective-permute-start.17 = (bf16[2,96,1536]{2,1,0:T(8,128)(2,1)S(1)}, bf16[2,96,1536]{2,1,0:T(8,128)(2,1)S(1)}, u32[]{:S(2)}, u32[]{:S(2)}) collective-permute-start(bf16[2,96,1536]{2,1,0:T(8,128)(2,1)S(1)} %copy-done.2), channel_id=1, source_target_pairs={{0,16},{16,32},{32,48},{48,0},{1,17},{17,33},{33,49},{49,1},{2,18}... | collective-permute-start | bytes 1769480 | tf_op jit(solution)/shard_map/ppermute | solution.py:21
  118.1 17.1 %collective-permute-start.18 = (bf16[96,1536]{1,0:T(8,128)(2,1)S(1)}, bf16[96,1536]{1,0:T(8,128)(2,1)S(1)}, u32[]{:S(2)}, u32[]{:S(2)}) collective-permute-start(bf16[96,1536]{1,0:T(8,128)(2,1)S(1)} %collective-permute-done.13), channel_id=1, source_target_pairs={{0,128},{128,256},{256,384},{384,448},{448,320},{320,192},{192,64}... | collective-permute-start | bytes 884744 | tf_op jit(solution)/shard_map/ppermute | solution.py:21
  124.6 28.7 %collective-permute-start.24 = (bf16[768,768]{1,0:T(8,128)(2,1)S(1)}, bf16[768,768]{1,0:T(8,128)(2,1)S(1)}, u32[]{:S(2)}, u32[]{:S(2)}) collective-permute-start(bf16[768,768]{1,0:T(8,128)(2,1)S(1)} %pad_maximum_fusion.3), channel_id=1, source_target_pairs={{0,4},{2,6},{4,0},{6,2},{1,5},{3,7},{5,1},{7,3},{8,12},{10,14},{12... | collective-permute-start | bytes 3538952 | tf_op jit(solution)/shard_map/ppermute | solution.py:29
  133.3 15.8 %collective-permute-start.16 = (bf16[2,96,1536]{2,1,0:T(8,128)(2,1)S(1)}, bf16[2,96,1536]{2,1,0:T(8,128)(2,1)S(1)}, u32[]{:S(2)}, u32[]{:S(2)}) collective-permute-start(bf16[2,96,1536]{2,1,0:T(8,128)(2,1)S(1)} %copy-done.2), channel_id=1, source_target_pairs={{0,32},{16,48},{32,0},{48,16},{1,33},{17,49},{33,1},{49,17},{2,34}... | collective-permute-start | bytes 1769480 | tf_op jit(solution)/shard_map/ppermute | solution.py:21
  135.2 26.5 %collective-permute-start.21 = (bf16[1,96,1536]{2,1,0:T(8,128)(2,1)S(1)}, bf16[1,96,1536]{2,1,0:T(8,128)(2,1)S(1)}, u32[]{:S(2)}, u32[]{:S(2)}) collective-permute-start(bf16[1,96,1536]{2,1,0:T(8,128)(2,1)S(1)} %bitcast.167), channel_id=1, source_target_pairs={{0,16},{16,32},{32,48},{48,0},{1,17},{17,33},{33,49},{49,1},{2,18}... | collective-permute-start | bytes 884744 | tf_op jit(solution)/shard_map/ppermute | solution.py:21
  141.2 18.1 %collective-permute-start.19 = (bf16[1,96,1536]{2,1,0:T(8,128)(2,1)S(1)}, bf16[1,96,1536]{2,1,0:T(8,128)(2,1)S(1)}, u32[]{:S(2)}, u32[]{:S(2)}) collective-permute-start(bf16[1,96,1536]{2,1,0:T(8,128)(2,1)S(1)} %bitcast.168), channel_id=1, source_target_pairs={{0,48},{16,0},{32,16},{48,32},{1,49},{17,1},{33,17},{49,33},{2,50}... | collective-permute-start | bytes 884744 | tf_op jit(solution)/shard_map/ppermute | solution.py:21
  143.9 17.8 %collective-permute-start.20 = (bf16[1,96,1536]{2,1,0:T(8,128)(2,1)S(1)}, bf16[1,96,1536]{2,1,0:T(8,128)(2,1)S(1)}, u32[]{:S(2)}, u32[]{:S(2)}) collective-permute-start(bf16[1,96,1536]{2,1,0:T(8,128)(2,1)S(1)} %bitcast.169), channel_id=1, source_target_pairs={{0,32},{16,48},{32,0},{48,16},{1,33},{17,49},{33,1},{49,17},{2,34}... | collective-permute-start | bytes 884744 | tf_op jit(solution)/shard_map/ppermute | solution.py:21
  153.9 9.2 %collective-permute-start.25 = (bf16[1536,768]{1,0:T(8,128)(2,1)S(1)}, bf16[1536,768]{1,0:T(8,128)(2,1)S(1)}, u32[]{:S(2)}, u32[]{:S(2)}) collective-permute-start(bf16[1536,768]{1,0:T(8,128)(2,1)S(1)} %pad_maximum_fusion.2), channel_id=1, source_target_pairs={{0,1},{1,0},{2,3},{3,2},{4,5},{5,4},{6,7},{7,6},{8,9},{9,8},{10,11... | collective-permute-start | bytes 7077896 | tf_op jit(solution)/shard_map/ppermute | solution.py:21
  170.8 7.0 %collective-permute-start.26 = (f32[4,2,192,256]{3,2,1,0:T(8,128)S(1)}, f32[4,2,192,256]{3,2,1,0:T(8,128)S(1)}, u32[]{:S(2)}, u32[]{:S(2)}) collective-permute-start(f32[4,2,192,256]{3,2,1,0:T(8,128)S(1)} %dynamic-slice_bitcast_fusion), channel_id=1, source_target_pairs={{0,1},{1,0},{2,3},{3,2},{4,5},{5,4},{6,7},{7,6},{8,9},{9,8},{10,11... | collective-permute-start | bytes 4718600 | tf_op jit(solution)/shard_map/ppermute | solution.py:21
  178.9 15.5 %all-to-all-start = ((bf16[4,2,192,256]{3,2,1,0:T(8,128)(2,1)}), bf16[4,2,192,256]{3,2,1,0:T(8,128)(2,1)S(1)}, u32[]{:S(2)}, u32[]{:S(2)}) async-start(bf16[4,2,192,256]{3,2,1,0:T(8,128)(2,1)} %fusion.10), calls=%async_computation | async-start | bytes 1572864 | tf_op jit(solution)/shard_map/all_to_all | solution.py:125
  194.6 19.4 %collective-permute-start.27 = (bf16[192,256]{1,0:T(8,128)(2,1)S(1)}, bf16[192,256]{1,0:T(8,128)(2,1)S(1)}, u32[]{:S(2)}, u32[]{:S(2)}) collective-permute-start(bf16[192,256]{1,0:T(8,128)(2,1)S(1)} %fusion.47), channel_id=1, source_target_pairs={{0,8},{8,0},{1,9},{9,1},{2,10},{10,2},{3,11},{11,3},{4,12},{12,4},... | collective-permute-start | bytes 294920 | tf_op jit(solution)/shard_map/ppermute | solution.py:21

commit v7 on v5

--- a/solution.py
+++ b/solution.py
@@ -44,10 +44,10 @@
 
 def body(tokens, tangent, cotangent, gates, slot_tokens, gate_weight, up_weight, down_weight):
     zl, x, zh, y, c = (lax.axis_index(a).astype(jnp.uint32) for a in ("zl", "x", "zh", "y", "c"))
-    packed = take(jnp.asarray(SOURCES), zl)
 
     own = jnp.concatenate([gate_weight, up_weight, down_weight.T], axis=1)
     rows, width = own.shape
+    half = rows // 2
     fields = jnp.concatenate([tokens.T, tangent.T, cotangent.T], axis=1)
     feat = fields.shape[0]
 
@@ -55,45 +55,48 @@
         got = after(send(v), *done)
         return jnp.concatenate([jnp.where(bit == 0, v, got), jnp.where(bit == 0, got, v)])
 
-    g0 = own[None]
+    def pile(*blocks):
+        return jnp.concatenate(blocks, axis=0)
+
     a1, b1 = ring_up(own), ring_down(own)
-    p0, m0 = x_up(g0), x_down(g0)
+    p0, m0 = x_up(own), x_down(own)
     a2, b2 = ring_up(a1), ring_down(b1)
-    g1 = jnp.stack([a1, b1])
+    g1 = pile(a1, b1)
     p1, m1 = x_up(after(g1, p0)), x_down(after(g1, m0))
     a3, b3 = ring_up(a2), ring_down(b2)
-    f1 = x_far(after(g1, p1))
-    f0 = x_far(after(g0, m1))
-    g2 = jnp.stack([a2, b2])
-    p2 = x_up(after(g2, a3))
-    m2 = x_down(after(g2, b3))
-    f2 = x_far(after(g2, f0))
+    p2 = x_up(after(pile(a2, b2, p0[:half]), p1))
+    m2 = x_down(after(pile(a2, b2, m0[half:]), m1))
     fields = join(fields, other_half, zh, b3)
-    fields = join(fields, y_near, y & 1, p2)
-    a4 = ring_up(after(a3, f1))
-    g3 = jnp.stack([a3, b3])
-    p3 = x_up(after(g3, p2))
-    m3 = x_down(after(g3, m2))
-    f3 = x_far(after(g3, f2))
+    fields = join(fields, y_near, y & 1, m2)
+    a4 = ring_up(a3)
+    g3 = pile(a3, b3)
+    p3 = x_up(after(pile(a3, b3, p1[:rows]), p2))
+    m3 = x_down(after(pile(a3, b3, m1[rows:]), m2))
+    f3 = x_far(after(g3, a4))
     fields = join(fields, y_far, y >> 1, p3)
-    g4 = a4[None]
-    p4 = x_up(g4)
-    m4 = x_down(after(g4, p3))
-    f4 = x_far(after(g4, m3))
+    p4 = x_up(after(pile(a4, p2[:rows]), p3))
+    m4 = x_down(after(pile(a4, m2[rows : 2 * rows]), m3))
+    f4 = x_far(after(a4, m3))
     fields = join(fields, other_core, c)
 
-    zero = a2[0, 0] * 0
+    zero = p3[0, 0] * 0
     full = jnp.broadcast_to(zero, (NC, NY, NH, 2, rows, width))
     none = jnp.uint32(0)
-    sources = iter((((packed >> 3 * j) & 3, (packed >> 3 * j + 2) & 1) for j in range(NZ)))
-    groups = ((g0, m0, f0, p0), (g1, m1, f1, p1), (g2, m2, f2, p2), (g3, m3, f3, p3), (g4, m4, f4, p4))
-    for parts in groups:
-        at = [next(sources) for _ in parts[0]]
-        for step, part in enumerate(parts):
-            col = x + step
-            for j, (row, far) in enumerate(at):
-                where = ((col >> 1) & 1, row, far, col & 1, none, none)
-                full = lax.dynamic_update_slice(full, part[j][None, None, None, None], where)
+    none_yet = zero.astype(jnp.uint32)
+    zl, x = zl + none_yet, x + none_yet
+    packed = take(jnp.asarray(SOURCES), zl)
+    lines = [((packed >> 3 * j) & 3, (packed >> 3 * j + 2) & 1) for j in range(NZ)]
+    cols = [(((x + s) >> 1) & 1, (x + s) & 1) for s in range(NX)]
+    pieces = [(own, 0, 0, 0), (m0, 0, 1, 0), (p0, 0, 3, 0), (p2[2 * rows :], 0, 2, 0), (m2[2 * rows :], 0, 2, half)]
+    for k, parts in ((1, (g1, m1, p1)), (3, (pile(a2, b2), m2, p2)), (5, (g3, m3, p3))):
+        for part, step in zip(parts, (0, 1, 3)):
+            pieces += [(part[:rows], k, step, 0), (part[rows : 2 * rows], k + 1, step, 0)]
+    pieces += [(p3[2 * rows :], 1, 2, 0), (m3[2 * rows :], 2, 2, 0), (f3[:rows], 5, 2, 0), (f3[rows:], 6, 2, 0)]
+    pieces += [(p4[rows:], 3, 2, 0), (m4[rows:], 4, 2, 0)]
+    pieces += [(a4, 7, 0, 0), (m4[:rows], 7, 1, 0), (p4[:rows], 7, 3, 0), (f4, 7, 2, 0)]
+    for part, j, step, first in pieces:
+        where = (cols[step][0], *lines[j], cols[step][1], jnp.uint32(first), none)
+        full = lax.dynamic_update_slice(full, part[None, None, None, None], where)
     full = full.reshape(NZ * NX * rows, width)
 
     n_tok = tokens.shape[0]

time: 214 us -> 220 us (1.028)
  the two profiles are of different devices: /device:TPU:99 before, /device:TPU:68 now
where the time goes in v7:
time: 220 us; the launch traced here: 219 us
  starting transfers between devices  111 us (50%)
  waiting for transfers between devices  58.4 us (27%)
  other arithmetic  16.3 us (7%)
  local copies, waits for them, and re-layouts  15.3 us (7%)
  between operations  11.8 us (5%)
  matrix products  6.51 us (3%)
    ppermute x23, starting transfers between devices, shift(): return lambda v: lax.ppermute(v, axis, pairs)  98.9 us
    ppermute x23, waiting for transfers between devices, shift(): return lambda v: lax.ppermute(v, axis, pairs)  45.6 us
    all_to_all x1, waiting for transfers between devices, body(): shares = lax.all_to_all(sums.astype(BF), 'y', 0, 0, tiled=True).astype(F32)  12.8 us
    ppermute x2, starting transfers between devices, flip(): return lambda v: lax.ppermute(v, axis, [(i, i ^ bit) for i in range(n)])  8.27 us
    dynamic_update_slice x32, local copies, waits for them, and re-layouts, body(): full = lax.dynamic_update_slice(full, part[None, None, None, None], where)  5.76 us
    select_n x4, other arithmetic, join(): jnp.where(bit == 0, v, got)  5.15 us
  transfers between devices with their start and end apart: 26, of which 8 were waited for; matrix products, arithmetic and copies ran while one was open for 11% of the time, Pallas kernels for 0%

profile of v7, /device:TPU:68, one launch (start us, length us, event | category | flops | bytes accessed | tf_op | source)
XLA Modules:
  0.0 218.9 jit_solution(13826715617423837854)
XLA Ops:
  0.0 1.0 pad_maximum_fusion.14
  1.0 6.4 %collective-permute-start = (bf16[96,1536]{1,0:T(8,128)(2,1)S(1)}, bf16[96,1536]{1,0:T(8,128)(2,1)S(1)}, u32[]{:S(2)}, u32[]{:S(2)}) collective-permute-start(bf16[96,1536]{1,0:T(8,128)(2,1)S(1)} %pad_maximum_fusion.14), channel_id=1, source_target_pairs={{0,128},{128,256},{256,384},{384,448},{448,320},{320,192},{192,64}... | collective-permute-start | bytes 884744 | tf_op jit(solution)/shard_map/ppermute | solution.py:21
  7.4 1.9 collective-permute-start.3
  9.4 2.4 %collective-permute-start.10 = (bf16[96,1536]{1,0:T(8,128)(2,1)S(1)}, bf16[96,1536]{1,0:T(8,128)(2,1)S(1)}, u32[]{:S(2)}, u32[]{:S(2)}) collective-permute-start(bf16[96,1536]{1,0:T(8,128)(2,1)S(1)} %pad_maximum_fusion.14), channel_id=1, source_target_pairs={{0,48},{16,0},{32,16},{48,32},{1,49},{17,1},{33,17},{49,33},{2,50}... | collective-permute-start | bytes 884744 | tf_op jit(solution)/shard_map/ppermute | solution.py:21
  11.8 3.4 %collective-permute-start.6 = (bf16[96,1536]{1,0:T(8,128)(2,1)S(1)}, bf16[96,1536]{1,0:T(8,128)(2,1)S(1)}, u32[]{:S(2)}, u32[]{:S(2)}) collective-permute-start(bf16[96,1536]{1,0:T(8,128)(2,1)S(1)} %pad_maximum_fusion.14), channel_id=1, source_target_pairs={{0,16},{16,32},{32,48},{48,0},{1,17},{17,33},{33,49},{49,1},{2,18}... | collective-permute-start | bytes 884744 | tf_op jit(solution)/shard_map/ppermute | solution.py:21
  15.2 4.8 %collective-permute-done = bf16[96,1536]{1,0:T(8,128)(2,1)S(1)} collective-permute-done((bf16[96,1536]{1,0:T(8,128)(2,1)S(1)}, bf16[96,1536]{1,0:T(8,128)(2,1)S(1)}, u32[]{:S(2)}, u32[]{:S(2)}) %collective-permute-start) | collective-permute-done | bytes 294944 | tf_op jit(solution)/shard_map/ppermute | solution.py:21
  20.8 1.3 collective-permute-done.3
  22.1 1.9 collective-permute-start.4
  24.7 3.1 %collective-permute-start.7 = (bf16[192,1536]{1,0:T(8,128)(2,1)}, bf16[192,1536]{1,0:T(8,128)(2,1)S(1)}, u32[]{:S(2)}, u32[]{:S(2)}) collective-permute-start(bf16[192,1536]{1,0:T(8,128)(2,1)} %constant_dynamic-update-slice_fusion), channel_id=1, source_target_pairs={{0,16},{16,32},{32,48},{48,0},{1,17},{17,33},{33,49},{49,1},{2,18}... | collective-permute-start | bytes 1769480 | tf_op jit(solution)/shard_map/ppermute | solution.py:21
  27.9 2.7 %collective-permute-start.11 = (bf16[192,1536]{1,0:T(8,128)(2,1)}, bf16[192,1536]{1,0:T(8,128)(2,1)S(1)}, u32[]{:S(2)}, u32[]{:S(2)}) collective-permute-start(bf16[192,1536]{1,0:T(8,128)(2,1)} %constant_dynamic-update-slice_fusion), channel_id=1, source_target_pairs={{0,48},{16,0},{32,16},{48,32},{1,49},{17,1},{33,17},{49,33},{2,50}... | collective-permute-start | bytes 1769480 | tf_op jit(solution)/shard_map/ppermute | solution.py:21
  30.6 6.0 %collective-permute-start.1 = (bf16[96,1536]{1,0:T(8,128)(2,1)S(1)}, bf16[96,1536]{1,0:T(8,128)(2,1)S(1)}, u32[]{:S(2)}, u32[]{:S(2)}) collective-permute-start(bf16[96,1536]{1,0:T(8,128)(2,1)S(1)} %collective-permute-done), channel_id=1, source_target_pairs={{0,128},{128,256},{256,384},{384,448},{448,320},{320,192},{192,64}... | collective-permute-start | bytes 884744 | tf_op jit(solution)/shard_map/ppermute | solution.py:21
  37.7 12.2 %collective-permute-start.19 = (bf16[192,768]{1,0:T(8,128)(2,1)S(1)}, bf16[192,768]{1,0:T(8,128)(2,1)}, u32[]{:S(2)}, u32[]{:S(2)}) collective-permute-start(bf16[192,768]{1,0:T(8,128)(2,1)S(1)} %pad_maximum_fusion.15), channel_id=1, source_target_pairs={{0,8},{8,0},{1,9},{9,1},{2,10},{10,2},{3,11},{11,3},{4,12},{12,4},... | collective-permute-start | bytes 884744 | tf_op jit(solution)/shard_map/ppermute | solution.py:21
  49.9 1.9 collective-permute-start.5
  52.7 6.0 %collective-permute-start.2 = (bf16[96,1536]{1,0:T(8,128)(2,1)S(1)}, bf16[96,1536]{1,0:T(8,128)(2,1)S(1)}, u32[]{:S(2)}, u32[]{:S(2)}) collective-permute-start(bf16[96,1536]{1,0:T(8,128)(2,1)S(1)} %collective-permute-done.1), channel_id=1, source_target_pairs={{0,128},{128,256},{256,384},{384,448},{448,320},{320,192},{192,64}... | collective-permute-start | bytes 884744 | tf_op jit(solution)/shard_map/ppermute | solution.py:21
  58.8 1.2 pad_maximum_fusion.9
  60.8 3.1 %collective-permute-start.8 = (bf16[240,1536]{1,0:T(8,128)(2,1)}, bf16[240,1536]{1,0:T(8,128)(2,1)S(1)}, u32[]{:S(2)}, u32[]{:S(2)}) collective-permute-start(bf16[240,1536]{1,0:T(8,128)(2,1)} %get-tuple-element.19), channel_id=1, source_target_pairs={{0,16},{16,32},{32,48},{48,0},{1,17},{17,33},{33,49},{49,1},{2,18}... | collective-permute-start | bytes 2211848 | tf_op jit(solution)/shard_map/ppermute | solution.py:21
  64.8 2.7 %collective-permute-start.12 = (bf16[240,1536]{1,0:T(8,128)(2,1)}, bf16[240,1536]{1,0:T(8,128)(2,1)S(1)}, u32[]{:S(2)}, u32[]{:S(2)}) collective-permute-start(bf16[240,1536]{1,0:T(8,128)(2,1)} %get-tuple-element.22), channel_id=1, source_target_pairs={{0,48},{16,0},{32,16},{48,32},{1,49},{17,1},{33,17},{49,33},{2,50}... | collective-permute-start | bytes 2211848 | tf_op jit(solution)/shard_map/ppermute | solution.py:21
  67.6 18.8 %collective-permute-done.19 = bf16[192,768]{1,0:T(8,128)(2,1)} collective-permute-done((bf16[192,768]{1,0:T(8,128)(2,1)S(1)}, bf16[192,768]{1,0:T(8,128)(2,1)}, u32[]{:S(2)}, u32[]{:S(2)}) %collective-permute-start.19) | collective-permute-done | bytes 294944 | tf_op jit(solution)/shard_map/ppermute | solution.py:21
  86.4 1.2 broadcast_select_fusion.7
  88.4 3.5 %collective-permute-start.20 = (bf16[384,768]{1,0:T(8,128)(2,1)}, bf16[384,768]{1,0:T(8,128)(2,1)}, u32[]{:S(2)}, u32[]{:S(2)}) collective-permute-start(bf16[384,768]{1,0:T(8,128)(2,1)} %pad_maximum_fusion.13), channel_id=1, source_target_pairs={{0,2},{2,0},{4,6},{6,4},{1,3},{3,1},{5,7},{7,5},{8,10},{10,8},{12,... | collective-permute-start | bytes 1769480 | tf_op jit(solution)/shard_map/ppermute | solution.py:29
  93.9 1.9 collective-permute-start.14
  95.9 1.0 pad_maximum_fusion.6
  96.9 3.1 %collective-permute-start.9 = (bf16[288,1536]{1,0:T(8,128)(2,1)S(1)}, bf16[288,1536]{1,0:T(8,128)(2,1)S(1)}, u32[]{:S(2)}, u32[]{:S(2)}) collective-permute-start(bf16[288,1536]{1,0:T(8,128)(2,1)S(1)} %get-tuple-element.20), channel_id=1, source_target_pairs={{0,16},{16,32},{32,48},{48,0},{1,17},{17,33},{33,49},{49,1},{2,18}... | collective-permute-start | bytes 2654216 | tf_op jit(solution)/shard_map/ppermute | solution.py:21
  100.0 2.7 %collective-permute-start.13 = (bf16[288,1536]{1,0:T(8,128)(2,1)}, bf16[288,1536]{1,0:T(8,128)(2,1)}, u32[]{:S(2)}, u32[]{:S(2)}) collective-permute-start(bf16[288,1536]{1,0:T(8,128)(2,1)} %get-tuple-element.23), channel_id=1, source_target_pairs={{0,48},{16,0},{32,16},{48,32},{1,49},{17,1},{33,17},{49,33},{2,50}... | collective-permute-start | bytes 2654216 | tf_op jit(solution)/shard_map/ppermute | solution.py:21
  103.6 4.8 %collective-permute-start.15 = (bf16[192,1536]{1,0:T(8,128)(2,1)}, bf16[192,1536]{1,0:T(8,128)(2,1)}, u32[]{:S(2)}, u32[]{:S(2)}) collective-permute-start(bf16[192,1536]{1,0:T(8,128)(2,1)} %pad_maximum_fusion.12), channel_id=1, source_target_pairs={{0,32},{16,48},{32,0},{48,16},{1,33},{17,49},{33,1},{49,17},{2,34}... | collective-permute-start | bytes 1769480 | tf_op jit(solution)/shard_map/ppermute | solution.py:21
  108.5 1.3 broadcast_select_fusion.5
  109.8 1.2 pad_maximum_fusion.3
  110.9 4.8 %collective-permute-start.21 = (bf16[768,768]{1,0:T(8,128)(2,1)}, bf16[768,768]{1,0:T(8,128)(2,1)}, u32[]{:S(2)}, u32[]{:S(2)}) collective-permute-start(bf16[768,768]{1,0:T(8,128)(2,1)} %pad_maximum_fusion.3), channel_id=1, source_target_pairs={{0,4},{2,6},{4,0},{6,2},{1,5},{3,7},{5,1},{7,3},{8,12},{10,14},{12... | collective-permute-start | bytes 3538952 | tf_op jit(solution)/shard_map/ppermute | solution.py:29
  116.8 1.1 pad_maximum_fusion.10
  117.9 3.4 %collective-permute-done.9 = bf16[288,1536]{1,0:T(8,128)(2,1)S(1)} collective-permute-done((bf16[288,1536]{1,0:T(8,128)(2,1)S(1)}, bf16[288,1536]{1,0:T(8,128)(2,1)S(1)}, u32[]{:S(2)}, u32[]{:S(2)}) %collective-permute-start.9) | collective-permute-done | bytes 884768 | tf_op jit(solution)/shard_map/ppermute | solution.py:21
  133.0 3.1 %collective-permute-start.16 = (bf16[192,1536]{1,0:T(8,128)(2,1)}, bf16[192,1536]{1,0:T(8,128)(2,1)S(1)}, u32[]{:S(2)}, u32[]{:S(2)}) collective-permute-start(bf16[192,1536]{1,0:T(8,128)(2,1)} %get-tuple-element.25), channel_id=1, source_target_pairs={{0,16},{16,32},{32,48},{48,0},{1,17},{17,33},{33,49},{49,1},{2,18}... | collective-permute-start | bytes 1769480 | tf_op jit(solution)/shard_map/ppermute | solution.py:21
  136.2 2.7 %collective-permute-start.17 = (bf16[192,1536]{1,0:T(8,128)(2,1)}, bf16[192,1536]{1,0:T(8,128)(2,1)S(1)}, u32[]{:S(2)}, u32[]{:S(2)}) collective-permute-start(bf16[192,1536]{1,0:T(8,128)(2,1)} %get-tuple-element.26), channel_id=1, source_target_pairs={{0,48},{16,0},{32,16},{48,32},{1,49},{17,1},{33,17},{49,33},{2,50}... | collective-permute-start | bytes 1769480 | tf_op jit(solution)/shard_map/ppermute | solution.py:21
  140.2 12.7 %collective-permute-start.18 = (bf16[96,1536]{1,0:T(8,128)(2,1)}, bf16[96,1536]{1,0:T(8,128)(2,1)S(1)}, u32[]{:S(2)}, u32[]{:S(2)}) collective-permute-start(bf16[96,1536]{1,0:T(8,128)(2,1)} %copy-done.12), channel_id=1, source_target_pairs={{0,32},{16,48},{32,0},{48,16},{1,33},{17,49},{33,1},{49,17},{2,34}... | collective-permute-start | bytes 884744 | tf_op jit(solution)/shard_map/ppermute | solution.py:21
  152.9 1.1 broadcast_in_dim.108
  156.9 1.0 fusion.33
  159.9 1.7 broadcast_select_fusion.3
  161.8 2.1 collective-permute-start.22
  164.2 4.1 %collective-permute-done.22 = bf16[1536,768]{1,0:T(8,128)(2,1)S(1)} collective-permute-done((bf16[1536,768]{1,0:T(8,128)(2,1)S(1)}, bf16[1536,768]{1,0:T(8,128)(2,1)S(1)}, u32[]{:S(2)}, u32[]{:S(2)}) %collective-permute-start.22) | collective-permute-done | bytes 2359328 | tf_op jit(solution)/shard_map/ppermute | solution.py:21
  169.2 3.4 %fusion.2 = f32[512,1024]{1,0:T(8,128)S(1)} fusion(bf16[3072,1536]{1,0:T(8,128)(2,1)S(1)} %bitcast.141, bf16[1536,768]{1,0:T(8,128)(2,1)S(1)} %get-tuple-element.32, bf16[1536,768]{1,0:T(8,128)(2,1)S(1)} %get-tuple-element.31), kind=kOutput, calls=%fused_computation.2 | convolution fusion | flops 3227516928 | bytes 13107200 | tf_op jit(solution)/shard_map/dot_general | solution.py:105
  172.7 1.3 fusion.23
  173.9 1.8 fusion
  175.9 2.0 collective-permute-start.23
  178.0 3.3 %collective-permute-done.23 = f32[4,2,192,256]{3,2,1,0:T(8,128)S(1)} collective-permute-done((f32[4,2,192,256]{3,2,1,0:T(8,128)S(1)}, f32[4,2,192,256]{3,2,1,0:T(8,128)S(1)}, u32[]{:S(2)}, u32[]{:S(2)}) %collective-permute-start.23) | collective-permute-done | bytes 1572896 | tf_op jit(solution)/shard_map/ppermute | solution.py:21
  181.2 1.1 fusion.10
  182.3 3.5 %all-to-all-start = ((bf16[4,2,192,256]{3,2,1,0:T(8,128)(2,1)}), bf16[4,2,192,256]{3,2,1,0:T(8,128)(2,1)S(1)}, u32[]{:S(2)}, u32[]{:S(2)}) async-start(bf16[4,2,192,256]{3,2,1,0:T(8,128)(2,1)} %fusion.10), calls=%async_computation | async-start | bytes 1572864 | tf_op jit(solution)/shard_map/all_to_all | solution.py:127
  185.8 12.8 %all-to-all-done = bf16[4,2,192,256]{3,2,1,0:T(8,128)(2,1)S(1)} async-done(((bf16[4,2,192,256]{3,2,1,0:T(8,128)(2,1)}), bf16[4,2,192,256]{3,2,1,0:T(8,128)(2,1)S(1)}, u32[]{:S(2)}, u32[]{:S(2)}) %all-to-all-start) | async-done | bytes 786464 | tf_op jit(solution)/shard_map/all_to_all | solution.py:127
  198.8 9.6 %collective-permute-start.24 = (bf16[192,256]{1,0:T(8,128)(2,1)S(1)}, bf16[192,256]{1,0:T(8,128)(2,1)S(1)}, u32[]{:S(2)}, u32[]{:S(2)}) collective-permute-start(bf16[192,256]{1,0:T(8,128)(2,1)S(1)} %fusion.47), channel_id=1, source_target_pairs={{0,8},{8,0},{1,9},{9,1},{2,10},{10,2},{3,11},{11,3},{4,12},{12,4},... | collective-permute-start | bytes 294920 | tf_op jit(solution)/shard_map/ppermute | solution.py:21
  208.4 9.9 %collective-permute-done.24 = bf16[192,256]{1,0:T(8,128)(2,1)S(1)} collective-permute-done((bf16[192,256]{1,0:T(8,128)(2,1)S(1)}, bf16[192,256]{1,0:T(8,128)(2,1)S(1)}, u32[]{:S(2)}, u32[]{:S(2)}) %collective-permute-start.24) | collective-permute-done | bytes 98336 | tf_op jit(solution)/shard_map/ppermute | solution.py:21
  (121 shorter events, 18.7 us)
Async XLA Ops:
  0.0 91.9 %copy-start.23 = (f32[256]{0:T(256)S(1)}, f32[256]{0:T(256)}, u32[]{:S(2)}) copy-start(f32[256]{0:T(256)} %param.12) | copy-start | bytes 3076
  1.0 19.0 %collective-permute-start = (bf16[96,1536]{1,0:T(8,128)(2,1)S(1)}, bf16[96,1536]{1,0:T(8,128)(2,1)S(1)}, u32[]{:S(2)}, u32[]{:S(2)}) collective-permute-start(bf16[96,1536]{1,0:T(8,128)(2,1)S(1)} %pad_maximum_fusion.14), channel_id=1, source_target_pairs={{0,128},{128,256},{256,384},{384,448},{448,320},{320,192},{192,64}... | collective-permute-start | bytes 884744 | tf_op jit(solution)/shard_map/ppermute | solution.py:21
  7.4 14.7 %collective-permute-start.3 = (bf16[96,1536]{1,0:T(8,128)(2,1)S(1)}, bf16[96,1536]{1,0:T(8,128)(2,1)S(1)}, u32[]{:S(2)}, u32[]{:S(2)}) collective-permute-start(bf16[96,1536]{1,0:T(8,128)(2,1)S(1)} %pad_maximum_fusion.14), channel_id=1, source_target_pairs={{0,64},{128,0},{256,128},{384,256},{448,384},{320,448},{192,320},{... | collective-permute-start | bytes 884744 | tf_op jit(solution)/shard_map/ppermute | solution.py:21
  9.4 18.5 %collective-permute-start.10 = (bf16[96,1536]{1,0:T(8,128)(2,1)S(1)}, bf16[96,1536]{1,0:T(8,128)(2,1)S(1)}, u32[]{:S(2)}, u32[]{:S(2)}) collective-permute-start(bf16[96,1536]{1,0:T(8,128)(2,1)S(1)} %pad_maximum_fusion.14), channel_id=1, source_target_pairs={{0,48},{16,0},{32,16},{48,32},{1,49},{17,1},{33,17},{49,33},{2,50}... | collective-permute-start | bytes 884744 | tf_op jit(solution)/shard_map/ppermute | solution.py:21
  11.8 12.9 %collective-permute-start.6 = (bf16[96,1536]{1,0:T(8,128)(2,1)S(1)}, bf16[96,1536]{1,0:T(8,128)(2,1)S(1)}, u32[]{:S(2)}, u32[]{:S(2)}) collective-permute-start(bf16[96,1536]{1,0:T(8,128)(2,1)S(1)} %pad_maximum_fusion.14), channel_id=1, source_target_pairs={{0,16},{16,32},{32,48},{48,0},{1,17},{17,33},{33,49},{49,1},{2,18}... | collective-permute-start | bytes 884744 | tf_op jit(solution)/shard_map/ppermute | solution.py:21
  20.0 32.7 %copy-start.8 = (bf16[96,1536]{1,0:T(8,128)(2,1)}, bf16[96,1536]{1,0:T(8,128)(2,1)S(1)}, u32[]{:S(2)}) copy-start(bf16[96,1536]{1,0:T(8,128)(2,1)S(1)} %collective-permute-done) | copy-start | bytes 884740
  22.1 27.8 %copy-start.10 = (bf16[96,1536]{1,0:T(8,128)(2,1)}, bf16[96,1536]{1,0:T(8,128)(2,1)S(1)}, u32[]{:S(2)}) copy-start(bf16[96,1536]{1,0:T(8,128)(2,1)S(1)} %collective-permute-done.3) | copy-start | bytes 884740
  22.1 27.8 %collective-permute-start.4 = (bf16[96,1536]{1,0:T(8,128)(2,1)S(1)}, bf16[96,1536]{1,0:T(8,128)(2,1)S(1)}, u32[]{:S(2)}, u32[]{:S(2)}) collective-permute-start(bf16[96,1536]{1,0:T(8,128)(2,1)S(1)} %collective-permute-done.3), channel_id=1, source_target_pairs={{0,64},{128,0},{256,128},{384,256},{448,384},{320,448},{192,320},{... | collective-permute-start | bytes 884744 | tf_op jit(solution)/shard_map/ppermute | solution.py:21
  24.7 61.6 %copy-start.18 = (bf16[96,1536]{1,0:T(8,128)(2,1)}, bf16[96,1536]{1,0:T(8,128)(2,1)S(1)}, u32[]{:S(2)}) copy-start(bf16[96,1536]{1,0:T(8,128)(2,1)S(1)} %collective-permute-done.6) | copy-start | bytes 884740
  24.7 35.3 %collective-permute-start.7 = (bf16[192,1536]{1,0:T(8,128)(2,1)}, bf16[192,1536]{1,0:T(8,128)(2,1)S(1)}, u32[]{:S(2)}, u32[]{:S(2)}) collective-permute-start(bf16[192,1536]{1,0:T(8,128)(2,1)} %constant_dynamic-update-slice_fusion), channel_id=1, source_target_pairs={{0,16},{16,32},{32,48},{48,0},{1,17},{17,33},{33,49},{49,1},{2,18}... | collective-permute-start | bytes 1769480 | tf_op jit(solution)/shard_map/ppermute | solution.py:21
  27.9 36.1 %copy-start.16 = (bf16[96,1536]{1,0:T(8,128)(2,1)}, bf16[96,1536]{1,0:T(8,128)(2,1)S(1)}, u32[]{:S(2)}) copy-start(bf16[96,1536]{1,0:T(8,128)(2,1)S(1)} %collective-permute-done.10) | copy-start | bytes 884740
  27.9 36.1 %collective-permute-start.11 = (bf16[192,1536]{1,0:T(8,128)(2,1)}, bf16[192,1536]{1,0:T(8,128)(2,1)S(1)}, u32[]{:S(2)}, u32[]{:S(2)}) collective-permute-start(bf16[192,1536]{1,0:T(8,128)(2,1)} %constant_dynamic-update-slice_fusion), channel_id=1, source_target_pairs={{0,48},{16,0},{32,16},{48,32},{1,49},{17,1},{33,17},{49,33},{2,50}... | collective-permute-start | bytes 1769480 | tf_op jit(solution)/shard_map/ppermute | solution.py:21
  30.6 22.1 %collective-permute-start.1 = (bf16[96,1536]{1,0:T(8,128)(2,1)S(1)}, bf16[96,1536]{1,0:T(8,128)(2,1)S(1)}, u32[]{:S(2)}, u32[]{:S(2)}) collective-permute-start(bf16[96,1536]{1,0:T(8,128)(2,1)S(1)} %collective-permute-done), channel_id=1, source_target_pairs={{0,128},{128,256},{256,384},{384,448},{448,320},{320,192},{192,64}... | collective-permute-start | bytes 884744 | tf_op jit(solution)/shard_map/ppermute | solution.py:21
  37.7 48.7 %collective-permute-start.19 = (bf16[192,768]{1,0:T(8,128)(2,1)S(1)}, bf16[192,768]{1,0:T(8,128)(2,1)}, u32[]{:S(2)}, u32[]{:S(2)}) collective-permute-start(bf16[192,768]{1,0:T(8,128)(2,1)S(1)} %pad_maximum_fusion.15), channel_id=1, source_target_pairs={{0,8},{8,0},{1,9},{9,1},{2,10},{10,2},{3,11},{11,3},{4,12},{12,4},... | collective-permute-start | bytes 884744 | tf_op jit(solution)/shard_map/ppermute | solution.py:21
  49.9 36.5 %collective-permute-start.5 = (bf16[96,1536]{1,0:T(8,128)(2,1)S(1)}, bf16[96,1536]{1,0:T(8,128)(2,1)S(1)}, u32[]{:S(2)}, u32[]{:S(2)}) collective-permute-start(bf16[96,1536]{1,0:T(8,128)(2,1)S(1)} %collective-permute-done.4), channel_id=1, source_target_pairs={{0,64},{128,0},{256,128},{384,256},{448,384},{320,448},{192,320},{... | collective-permute-start | bytes 884744 | tf_op jit(solution)/shard_map/ppermute | solution.py:21
  52.7 55.8 %copy-start.6 = (bf16[96,1536]{1,0:T(8,128)(2,1)}, bf16[96,1536]{1,0:T(8,128)(2,1)S(1)}, u32[]{:S(2)}) copy-start(bf16[96,1536]{1,0:T(8,128)(2,1)S(1)} %collective-permute-done.1) | copy-start | bytes 884740
  52.7 41.2 %collective-permute-start.2 = (bf16[96,1536]{1,0:T(8,128)(2,1)S(1)}, bf16[96,1536]{1,0:T(8,128)(2,1)S(1)}, u32[]{:S(2)}, u32[]{:S(2)}) collective-permute-start(bf16[96,1536]{1,0:T(8,128)(2,1)S(1)} %collective-permute-done.1), channel_id=1, source_target_pairs={{0,128},{128,256},{256,384},{384,448},{448,320},{320,192},{192,64}... | collective-permute-start | bytes 884744 | tf_op jit(solution)/shard_map/ppermute | solution.py:21
  60.8 36.1 %collective-permute-start.8 = (bf16[240,1536]{1,0:T(8,128)(2,1)}, bf16[240,1536]{1,0:T(8,128)(2,1)S(1)}, u32[]{:S(2)}, u32[]{:S(2)}) collective-permute-start(bf16[240,1536]{1,0:T(8,128)(2,1)} %get-tuple-element.19), channel_id=1, source_target_pairs={{0,16},{16,32},{32,48},{48,0},{1,17},{17,33},{33,49},{49,1},{2,18}... | collective-permute-start | bytes 2211848 | tf_op jit(solution)/shard_map/ppermute | solution.py:21
  64.8 35.2 %collective-permute-start.12 = (bf16[240,1536]{1,0:T(8,128)(2,1)}, bf16[240,1536]{1,0:T(8,128)(2,1)S(1)}, u32[]{:S(2)}, u32[]{:S(2)}) collective-permute-start(bf16[240,1536]{1,0:T(8,128)(2,1)} %get-tuple-element.22), channel_id=1, source_target_pairs={{0,48},{16,0},{32,16},{48,32},{1,49},{17,1},{33,17},{49,33},{2,50}... | collective-permute-start | bytes 2211848 | tf_op jit(solution)/shard_map/ppermute | solution.py:21
  88.4 20.1 %collective-permute-start.20 = (bf16[384,768]{1,0:T(8,128)(2,1)}, bf16[384,768]{1,0:T(8,128)(2,1)}, u32[]{:S(2)}, u32[]{:S(2)}) collective-permute-start(bf16[384,768]{1,0:T(8,128)(2,1)} %pad_maximum_fusion.13), channel_id=1, source_target_pairs={{0,2},{2,0},{4,6},{6,4},{1,3},{3,1},{5,7},{7,5},{8,10},{10,8},{12,... | collective-permute-start | bytes 1769480 | tf_op jit(solution)/shard_map/ppermute | solution.py:29
  92.9 30.6 %copy-start.24 = (u32[8]{0:T(128)S(1)}, u32[8]{0:T(128)}, u32[]{:S(2)}) copy-start(u32[8]{0:T(128)} %constant.106.clone) | copy-start | bytes 100
  93.9 9.7 %collective-permute-start.14 = (bf16[96,1536]{1,0:T(8,128)(2,1)S(1)}, bf16[96,1536]{1,0:T(8,128)(2,1)S(1)}, u32[]{:S(2)}, u32[]{:S(2)}) collective-permute-start(bf16[96,1536]{1,0:T(8,128)(2,1)S(1)} %collective-permute-done.2), channel_id=1, source_target_pairs={{0,128},{128,256},{256,384},{384,448},{448,320},{320,192},{192,64}... | collective-permute-start | bytes 884744 | tf_op jit(solution)/shard_map/ppermute | solution.py:21
  96.9 24.5 %collective-permute-start.9 = (bf16[288,1536]{1,0:T(8,128)(2,1)S(1)}, bf16[288,1536]{1,0:T(8,128)(2,1)S(1)}, u32[]{:S(2)}, u32[]{:S(2)}) collective-permute-start(bf16[288,1536]{1,0:T(8,128)(2,1)S(1)} %get-tuple-element.20), channel_id=1, source_target_pairs={{0,16},{16,32},{32,48},{48,0},{1,17},{17,33},{33,49},{49,1},{2,18}... | collective-permute-start | bytes 2654216 | tf_op jit(solution)/shard_map/ppermute | solution.py:21
  100.0 8.5 %copy-start = (bf16[240,1536]{1,0:T(8,128)(2,1)}, bf16[240,1536]{1,0:T(8,128)(2,1)S(1)}, u32[]{:S(2)}) copy-start(bf16[240,1536]{1,0:T(8,128)(2,1)S(1)} %collective-permute-done.12) | copy-start | bytes 2211844
  100.0 36.1 %collective-permute-start.13 = (bf16[288,1536]{1,0:T(8,128)(2,1)}, bf16[288,1536]{1,0:T(8,128)(2,1)}, u32[]{:S(2)}, u32[]{:S(2)}) collective-permute-start(bf16[288,1536]{1,0:T(8,128)(2,1)} %get-tuple-element.23), channel_id=1, source_target_pairs={{0,48},{16,0},{32,16},{48,32},{1,49},{17,1},{33,17},{49,33},{2,50}... | collective-permute-start | bytes 2654216 | tf_op jit(solution)/shard_map/ppermute | solution.py:21
  103.6 13.1 %copy-start.12 = (bf16[96,1536]{1,0:T(8,128)(2,1)}, bf16[96,1536]{1,0:T(8,128)(2,1)S(1)}, u32[]{:S(2)}) copy-start(bf16[96,1536]{1,0:T(8,128)(2,1)S(1)} %collective-permute-done.14) | copy-start | bytes 884740
  103.6 54.3 %collective-permute-start.15 = (bf16[192,1536]{1,0:T(8,128)(2,1)}, bf16[192,1536]{1,0:T(8,128)(2,1)}, u32[]{:S(2)}, u32[]{:S(2)}) collective-permute-start(bf16[192,1536]{1,0:T(8,128)(2,1)} %pad_maximum_fusion.12), channel_id=1, source_target_pairs={{0,32},{16,48},{32,0},{48,16},{1,33},{17,49},{33,1},{49,17},{2,34}... | collective-permute-start | bytes 1769480 | tf_op jit(solution)/shard_map/ppermute | solution.py:21
  110.9 49.0 %collective-permute-start.21 = (bf16[768,768]{1,0:T(8,128)(2,1)}, bf16[768,768]{1,0:T(8,128)(2,1)}, u32[]{:S(2)}, u32[]{:S(2)}) collective-permute-start(bf16[768,768]{1,0:T(8,128)(2,1)} %pad_maximum_fusion.3), channel_id=1, source_target_pairs={{0,4},{2,6},{4,0},{6,2},{1,5},{3,7},{5,1},{7,3},{8,12},{10,14},{12... | collective-permute-start | bytes 3538952 | tf_op jit(solution)/shard_map/ppermute | solution.py:29
  117.9 36.3 %copy-start.1 = (bf16[240,1536]{1,0:T(8,128)(2,1)S(1)}, bf16[240,1536]{1,0:T(8,128)(2,1)}, u32[]{:S(2)}) copy-start(bf16[240,1536]{1,0:T(8,128)(2,1)} %copy-done) | copy-start | bytes 2211844
  126.0 28.0 %copy-start.20 = (bf16[512,96]{0,1:T(8,128)(2,1)S(1)}, bf16[512,96]{0,1:T(8,128)(2,1)}, u32[]{:S(2)}) copy-start(bf16[512,96]{0,1:T(8,128)(2,1)} %param.16) | copy-start | bytes 294916
  126.0 28.0 %copy-start.21 = (bf16[96,512]{1,0:T(8,128)(2,1)S(1)}, bf16[96,512]{1,0:T(8,128)(2,1)}, u32[]{:S(2)}) copy-start(bf16[96,512]{1,0:T(8,128)(2,1)} %param.15) | copy-start | bytes 294916
  126.0 28.0 %copy-start.22 = (bf16[96,512]{1,0:T(8,128)(2,1)S(1)}, bf16[96,512]{1,0:T(8,128)(2,1)}, u32[]{:S(2)}) copy-start(bf16[96,512]{1,0:T(8,128)(2,1)} %param.14) | copy-start | bytes 294916
  126.0 28.0 %copy-start.17 = (bf16[96,1536]{1,0:T(8,128)(2,1)S(1)}, bf16[96,1536]{1,0:T(8,128)(2,1)}, u32[]{:S(2)}) copy-start(bf16[96,1536]{1,0:T(8,128)(2,1)} %copy-done.16) | copy-start | bytes 884740
  126.0 28.1 %copy-start.19 = (bf16[96,1536]{1,0:T(8,128)(2,1)S(1)}, bf16[96,1536]{1,0:T(8,128)(2,1)}, u32[]{:S(2)}) copy-start(bf16[96,1536]{1,0:T(8,128)(2,1)} %copy-done.18) | copy-start | bytes 884740
  126.0 28.2 %copy-start.9 = (bf16[96,1536]{1,0:T(8,128)(2,1)S(1)}, bf16[96,1536]{1,0:T(8,128)(2,1)}, u32[]{:S(2)}) copy-start(bf16[96,1536]{1,0:T(8,128)(2,1)} %copy-done.8) | copy-start | bytes 884740
  126.1 28.2 %copy-start.11 = (bf16[96,1536]{1,0:T(8,128)(2,1)S(1)}, bf16[96,1536]{1,0:T(8,128)(2,1)}, u32[]{:S(2)}) copy-start(bf16[96,1536]{1,0:T(8,128)(2,1)} %copy-done.10) | copy-start | bytes 884740
  133.0 30.9 %collective-permute-start.16 = (bf16[192,1536]{1,0:T(8,128)(2,1)}, bf16[192,1536]{1,0:T(8,128)(2,1)S(1)}, u32[]{:S(2)}, u32[]{:S(2)}) collective-permute-start(bf16[192,1536]{1,0:T(8,128)(2,1)} %get-tuple-element.25), channel_id=1, source_target_pairs={{0,16},{16,32},{32,48},{48,0},{1,17},{17,33},{33,49},{49,1},{2,18}... | collective-permute-start | bytes 1769480 | tf_op jit(solution)/shard_map/ppermute | solution.py:21
  136.2 27.8 %collective-permute-start.17 = (bf16[192,1536]{1,0:T(8,128)(2,1)}, bf16[192,1536]{1,0:T(8,128)(2,1)S(1)}, u32[]{:S(2)}, u32[]{:S(2)}) collective-permute-start(bf16[192,1536]{1,0:T(8,128)(2,1)} %get-tuple-element.26), channel_id=1, source_target_pairs={{0,48},{16,0},{32,16},{48,32},{1,49},{17,1},{33,17},{49,33},{2,50}... | collective-permute-start | bytes 1769480 | tf_op jit(solution)/shard_map/ppermute | solution.py:21
  140.1 14.2 %copy-start.5 = (bf16[192,1536]{1,0:T(8,128)(2,1)S(1)}, bf16[192,1536]{1,0:T(8,128)(2,1)}, u32[]{:S(2)}) copy-start(bf16[192,1536]{1,0:T(8,128)(2,1)} %copy-done.4) | copy-start | bytes 1769476
  140.2 14.2 %copy-start.3 = (bf16[192,1536]{1,0:T(8,128)(2,1)S(1)}, bf16[192,1536]{1,0:T(8,128)(2,1)}, u32[]{:S(2)}) copy-start(bf16[192,1536]{1,0:T(8,128)(2,1)} %copy-done.2) | copy-start | bytes 1769476
  140.2 14.3 %copy-start.7 = (bf16[96,1536]{1,0:T(8,128)(2,1)S(1)}, bf16[96,1536]{1,0:T(8,128)(2,1)}, u32[]{:S(2)}) copy-start(bf16[96,1536]{1,0:T(8,128)(2,1)} %copy-done.6) | copy-start | bytes 884740
  140.2 24.0 %collective-permute-start.18 = (bf16[96,1536]{1,0:T(8,128)(2,1)}, bf16[96,1536]{1,0:T(8,128)(2,1)S(1)}, u32[]{:S(2)}, u32[]{:S(2)}) collective-permute-start(bf16[96,1536]{1,0:T(8,128)(2,1)} %copy-done.12), channel_id=1, source_target_pairs={{0,32},{16,48},{32,0},{48,16},{1,33},{17,49},{33,1},{49,17},{2,34}... | collective-permute-start | bytes 884744 | tf_op jit(solution)/shard_map/ppermute | solution.py:21
  154.0 2.8 %copy-start.15 = (bf16[288,1536]{1,0:T(8,128)(2,1)S(1)}, bf16[288,1536]{1,0:T(8,128)(2,1)}, u32[]{:S(2)}) copy-start(bf16[288,1536]{1,0:T(8,128)(2,1)} %copy-done.14) | copy-start | bytes 2654212
  156.9 7.1 %copy-start.13 = (bf16[96,1536]{1,0:T(8,128)(2,1)S(1)}, bf16[96,1536]{1,0:T(8,128)(2,1)}, u32[]{:S(2)}) copy-start(bf16[96,1536]{1,0:T(8,128)(2,1)} %copy-done.12) | copy-start | bytes 884740
  161.8 6.4 %collective-permute-start.22 = (bf16[1536,768]{1,0:T(8,128)(2,1)S(1)}, bf16[1536,768]{1,0:T(8,128)(2,1)S(1)}, u32[]{:S(2)}, u32[]{:S(2)}) collective-permute-start(bf16[1536,768]{1,0:T(8,128)(2,1)S(1)} %pad_maximum_fusion.2), channel_id=1, source_target_pairs={{0,1},{1,0},{2,3},{3,2},{4,5},{5,4},{6,7},{7,6},{8,9},{9,8},{10,11... | collective-permute-start | bytes 7077896 | tf_op jit(solution)/shard_map/ppermute | solution.py:21
  175.9 5.3 %collective-permute-start.23 = (f32[4,2,192,256]{3,2,1,0:T(8,128)S(1)}, f32[4,2,192,256]{3,2,1,0:T(8,128)S(1)}, u32[]{:S(2)}, u32[]{:S(2)}) collective-permute-start(f32[4,2,192,256]{3,2,1,0:T(8,128)S(1)} %dynamic-slice_bitcast_fusion), channel_id=1, source_target_pairs={{0,1},{1,0},{2,3},{3,2},{4,5},{5,4},{6,7},{7,6},{8,9},{9,8},{10,11... | collective-permute-start | bytes 4718600 | tf_op jit(solution)/shard_map/ppermute | solution.py:21
  182.3 16.3 %all-to-all-start = ((bf16[4,2,192,256]{3,2,1,0:T(8,128)(2,1)}), bf16[4,2,192,256]{3,2,1,0:T(8,128)(2,1)S(1)}, u32[]{:S(2)}, u32[]{:S(2)}) async-start(bf16[4,2,192,256]{3,2,1,0:T(8,128)(2,1)} %fusion.10), calls=%async_computation | async-start | bytes 1572864 | tf_op jit(solution)/shard_map/all_to_all | solution.py:127
  198.8 19.5 %collective-permute-start.24 = (bf16[192,256]{1,0:T(8,128)(2,1)S(1)}, bf16[192,256]{1,0:T(8,128)(2,1)S(1)}, u32[]{:S(2)}, u32[]{:S(2)}) collective-permute-start(bf16[192,256]{1,0:T(8,128)(2,1)S(1)} %fusion.47), channel_id=1, source_target_pairs={{0,8},{8,0},{1,9},{9,1},{2,10},{10,2},{3,11},{11,3},{4,12},{12,4},... | collective-permute-start | bytes 294920 | tf_op jit(solution)/shard_map/ppermute | solution.py:21
  (3 other events, 2.6 us)

commit v8 on v7

--- a/solution.py
+++ b/solution.py
@@ -10,9 +10,14 @@
 NZ, NX, NH, NY, NC = 8, 4, 2, 4, 2
 RING = (0, 2, 4, 6, 7, 5, 3, 1)
 STEPS = (0, -1, 1, -2, 2, -3, 3, -4)
-SOURCES = np.array(
-    [sum(RING[(RING.index(z) + s) % NZ] << 3 * j for j, s in enumerate(STEPS)) for z in range(NZ)], np.uint32
-)
+
+
+def offset_table(rows):
+    table = np.zeros((NZ, NX, NZ * NX), np.uint32)
+    for zl, x, j, s in np.ndindex(NZ, NX, NZ, NX):
+        z, col = RING[(RING.index(zl) + STEPS[j]) % NZ], (x + s) % NX
+        table[zl, x, j * NX + s] = ((((col // 2) * NY + z % NY) * NH + z // NY) * 2 + col % 2) * rows
+    return table
 
 
 def shift(axis, order, step):
@@ -47,7 +52,6 @@
 
     own = jnp.concatenate([gate_weight, up_weight, down_weight.T], axis=1)
     rows, width = own.shape
-    half = rows // 2
     fields = jnp.concatenate([tokens.T, tangent.T, cotangent.T], axis=1)
     feat = fields.shape[0]
 
@@ -60,44 +64,40 @@
 
     a1, b1 = ring_up(own), ring_down(own)
     p0, m0 = x_up(own), x_down(own)
-    a2, b2 = ring_up(a1), ring_down(b1)
+    a2, b2 = ring_up(after(a1, p0)), ring_down(after(b1, m0))
     g1 = pile(a1, b1)
     p1, m1 = x_up(after(g1, p0)), x_down(after(g1, m0))
     a3, b3 = ring_up(a2), ring_down(b2)
-    p2 = x_up(after(pile(a2, b2, p0[:half]), p1))
-    m2 = x_down(after(pile(a2, b2, m0[half:]), m1))
+    f0 = x_far(after(own, m1))
+    m2 = x_down(after(pile(a2, b2, m1[rows:]), p1))
+    p2 = x_up(after(pile(a2, b2, p1[:rows]), a3))
     fields = join(fields, other_half, zh, b3)
     fields = join(fields, y_near, y & 1, m2)
-    a4 = ring_up(a3)
     g3 = pile(a3, b3)
-    p3 = x_up(after(pile(a3, b3, p1[:rows]), p2))
-    m3 = x_down(after(pile(a3, b3, m1[rows:]), m2))
-    f3 = x_far(after(g3, a4))
+    m3 = x_down(after(g3, b3))
+    p3 = x_up(after(g3, f0))
+    a4 = ring_up(after(a3, m2))
+    f3 = x_far(after(g3, p2))
     fields = join(fields, y_far, y >> 1, p3)
-    p4 = x_up(after(pile(a4, p2[:rows]), p3))
-    m4 = x_down(after(pile(a4, m2[rows : 2 * rows]), m3))
-    f4 = x_far(after(a4, m3))
+    m4 = x_down(pile(a4, m2[rows : 2 * rows]))
+    p4 = x_up(after(pile(a4, p2[:rows]), m3))
+    f4 = x_far(after(a4, p3))
     fields = join(fields, other_core, c)
 
-    zero = p3[0, 0] * 0
-    full = jnp.broadcast_to(zero, (NC, NY, NH, 2, rows, width))
-    none = jnp.uint32(0)
-    none_yet = zero.astype(jnp.uint32)
-    zl, x = zl + none_yet, x + none_yet
-    packed = take(jnp.asarray(SOURCES), zl)
-    lines = [((packed >> 3 * j) & 3, (packed >> 3 * j + 2) & 1) for j in range(NZ)]
-    cols = [(((x + s) >> 1) & 1, (x + s) & 1) for s in range(NX)]
-    pieces = [(own, 0, 0, 0), (m0, 0, 1, 0), (p0, 0, 3, 0), (p2[2 * rows :], 0, 2, 0), (m2[2 * rows :], 0, 2, half)]
+    zl, x, _ = lax.optimization_barrier((zl, x, m2))
+    offsets = lax.dynamic_slice(jnp.asarray(offset_table(rows)), (zl, x, jnp.uint32(0)), (1, 1, NZ * NX)).reshape(-1)
+    full = jnp.broadcast_to(m2[0, 0] * 0, (NZ * NX * rows, width))
+    pieces = [(own, 0, 0), (m0, 0, 1), (f0, 0, 2), (p0, 0, 3)]
     for k, parts in ((1, (g1, m1, p1)), (3, (pile(a2, b2), m2, p2)), (5, (g3, m3, p3))):
         for part, step in zip(parts, (0, 1, 3)):
-            pieces += [(part[:rows], k, step, 0), (part[rows : 2 * rows], k + 1, step, 0)]
-    pieces += [(p3[2 * rows :], 1, 2, 0), (m3[2 * rows :], 2, 2, 0), (f3[:rows], 5, 2, 0), (f3[rows:], 6, 2, 0)]
-    pieces += [(p4[rows:], 3, 2, 0), (m4[rows:], 4, 2, 0)]
-    pieces += [(a4, 7, 0, 0), (m4[:rows], 7, 1, 0), (p4[:rows], 7, 3, 0), (f4, 7, 2, 0)]
-    for part, j, step, first in pieces:
-        where = (cols[step][0], *lines[j], cols[step][1], jnp.uint32(first), none)
-        full = lax.dynamic_update_slice(full, part[None, None, None, None], where)
-    full = full.reshape(NZ * NX * rows, width)
+            pieces += [(part[:rows], k, step), (part[rows : 2 * rows], k + 1, step)]
+    pieces += [(p2[2 * rows :], 1, 2), (m2[2 * rows :], 2, 2), (f3[:rows], 5, 2), (f3[rows:], 6, 2)]
+    pieces += [(p4[rows:], 3, 2), (m4[rows:], 4, 2)]
+    pieces += [(a4, 7, 0), (m4[:rows], 7, 1), (p4[:rows], 7, 3), (f4, 7, 2)]
+    for part, j, step in pieces:
+        at = j * NX + step
+        first = lax.squeeze(lax.slice(offsets, (at,), (at + 1,)), (0,))
+        full = lax.dynamic_update_slice(full, part, (first, jnp.uint32(0)))
 
     n_tok = tokens.shape[0]
     ff = gate_weight.shape[1]

time: 220 us -> 346 us (1.57)
  the two profiles are of different devices: /device:TPU:68 before, /device:TPU:102 now
where the time goes in v8:
time: 346 us; the launch traced here: 343 us
  local copies, waits for them, and re-layouts  131 us (38%)
  starting transfers between devices  118 us (34%)
  waiting for transfers between devices  74.8 us (22%)
  other arithmetic  11.4 us (3%)
  matrix products  6.57 us (2%)
    dynamic_update_slice x32, local copies, waits for them, and re-layouts, body(): full = lax.dynamic_update_slice(full, part, (first, jnp.uint32(0)))  110 us
    ppermute x24, starting transfers between devices, shift(): return lambda v: lax.ppermute(v, axis, pairs)  105 us
    ppermute x24, waiting for transfers between devices, shift(): return lambda v: lax.ppermute(v, axis, pairs)  58.9 us
    all_to_all x1, waiting for transfers between devices, body(): shares = lax.all_to_all(sums.astype(BF), 'y', 0, 0, tiled=True).astype(F32)  12.6 us
    ppermute x2, starting transfers between devices, flip(): return lambda v: lax.ppermute(v, axis, [(i, i ^ bit) for i in range(n)])  8.59 us
  transfers between devices with their start and end apart: 27, of which 14 were waited for; matrix products, arithmetic and copies ran while one was open for 39% of the time, Pallas kernels for 0%

profile of v8, /device:TPU:102, one launch (start us, length us, event | category | flops | bytes accessed | tf_op | source)
XLA Modules:
  0.0 343.1 jit_solution(15223870481363734125)
XLA Ops:
  3.0 6.4 %collective-permute-start.3 = (bf16[96,1536]{1,0:T(8,128)(2,1)S(1)}, bf16[96,1536]{1,0:T(8,128)(2,1)S(1)}, u32[]{:S(2)}, u32[]{:S(2)}) collective-permute-start(bf16[96,1536]{1,0:T(8,128)(2,1)S(1)} %pad_maximum_fusion.10), channel_id=1, source_target_pairs={{0,64},{128,0},{256,128},{384,256},{448,384},{320,448},{192,320},{... | collective-permute-start | bytes 884744 | tf_op jit(solution)/shard_map/ppermute | solution.py:26
  11.8 3.5 %collective-permute-start.4 = (bf16[96,1536]{1,0:T(8,128)(2,1)S(1)}, bf16[96,1536]{1,0:T(8,128)(2,1)S(1)}, u32[]{:S(2)}, u32[]{:S(2)}) collective-permute-start(bf16[96,1536]{1,0:T(8,128)(2,1)S(1)} %pad_maximum_fusion.10), channel_id=1, source_target_pairs={{0,48},{16,0},{32,16},{48,32},{1,49},{17,1},{33,17},{49,33},{2,50}... | collective-permute-start | bytes 884744 | tf_op jit(solution)/shard_map/ppermute | solution.py:26
  19.7 3.8 %collective-permute-start.7 = (bf16[192,1536]{1,0:T(8,128)(2,1)}, bf16[192,1536]{1,0:T(8,128)(2,1)S(1)}, u32[]{:S(2)}, u32[]{:S(2)}) collective-permute-start(bf16[192,1536]{1,0:T(8,128)(2,1)} %constant_dynamic-update-slice_fusion), channel_id=1, source_target_pairs={{0,16},{16,32},{32,48},{48,0},{1,17},{17,33},{33,49},{49,1},{2,18}... | collective-permute-start | bytes 1769480 | tf_op jit(solution)/shard_map/ppermute | solution.py:26
  25.5 6.5 %collective-permute-start.5 = (bf16[96,1536]{1,0:T(8,128)(2,1)S(1)}, bf16[96,1536]{1,0:T(8,128)(2,1)S(1)}, u32[]{:S(2)}, u32[]{:S(2)}) collective-permute-start(bf16[96,1536]{1,0:T(8,128)(2,1)S(1)} %collective-permute-done.3), channel_id=1, source_target_pairs={{0,64},{128,0},{256,128},{384,256},{448,384},{320,448},{192,320},{... | collective-permute-start | bytes 884744 | tf_op jit(solution)/shard_map/ppermute | solution.py:26
  33.0 13.2 %collective-permute-start.20 = (bf16[192,768]{1,0:T(8,128)(2,1)S(1)}, bf16[192,768]{1,0:T(8,128)(2,1)S(1)}, u32[]{:S(2)}, u32[]{:S(2)}) collective-permute-start(bf16[192,768]{1,0:T(8,128)(2,1)S(1)} %pad_maximum_fusion.11), channel_id=1, source_target_pairs={{0,8},{8,0},{1,9},{9,1},{2,10},{10,2},{3,11},{11,3},{4,12},{12,4},... | collective-permute-start | bytes 884744 | tf_op jit(solution)/shard_map/ppermute | solution.py:26
  46.2 3.5 %collective-permute-start.6 = (bf16[192,1536]{1,0:T(8,128)(2,1)}, bf16[192,1536]{1,0:T(8,128)(2,1)S(1)}, u32[]{:S(2)}, u32[]{:S(2)}) collective-permute-start(bf16[192,1536]{1,0:T(8,128)(2,1)} %constant_dynamic-update-slice_fusion), channel_id=1, source_target_pairs={{0,48},{16,0},{32,16},{48,32},{1,49},{17,1},{33,17},{49,33},{2,50}... | collective-permute-start | bytes 1769480 | tf_op jit(solution)/shard_map/ppermute | solution.py:26
  51.7 6.0 %collective-permute-start.12 = (bf16[96,1536]{1,0:T(8,128)(2,1)S(1)}, bf16[96,1536]{1,0:T(8,128)(2,1)S(1)}, u32[]{:S(2)}, u32[]{:S(2)}) collective-permute-start(bf16[96,1536]{1,0:T(8,128)(2,1)S(1)} %collective-permute-done.5), channel_id=1, source_target_pairs={{0,64},{128,0},{256,128},{384,256},{448,384},{320,448},{192,320},{... | collective-permute-start | bytes 884744 | tf_op jit(solution)/shard_map/ppermute | solution.py:26
  58.5 3.5 %collective-permute-done.6 = bf16[192,1536]{1,0:T(8,128)(2,1)S(1)} collective-permute-done((bf16[192,1536]{1,0:T(8,128)(2,1)}, bf16[192,1536]{1,0:T(8,128)(2,1)S(1)}, u32[]{:S(2)}, u32[]{:S(2)}) %collective-permute-start.6) | collective-permute-done | bytes 589856 | tf_op jit(solution)/shard_map/ppermute | solution.py:26
  68.6 9.1 %collective-permute-done.20 = bf16[192,768]{1,0:T(8,128)(2,1)S(1)} collective-permute-done((bf16[192,768]{1,0:T(8,128)(2,1)S(1)}, bf16[192,768]{1,0:T(8,128)(2,1)S(1)}, u32[]{:S(2)}, u32[]{:S(2)}) %collective-permute-start.20) | collective-permute-done | bytes 294944 | tf_op jit(solution)/shard_map/ppermute | solution.py:26
  77.6 5.1 %collective-permute-done.12 = bf16[96,1536]{1,0:T(8,128)(2,1)S(1)} collective-permute-done((bf16[96,1536]{1,0:T(8,128)(2,1)S(1)}, bf16[96,1536]{1,0:T(8,128)(2,1)S(1)}, u32[]{:S(2)}, u32[]{:S(2)}) %collective-permute-start.12) | collective-permute-done | bytes 294944 | tf_op jit(solution)/shard_map/ppermute | solution.py:26
  82.9 3.5 %collective-permute-start.21 = (bf16[384,768]{1,0:T(8,128)(2,1)S(1)}, bf16[384,768]{1,0:T(8,128)(2,1)S(1)}, u32[]{:S(2)}, u32[]{:S(2)}) collective-permute-start(bf16[384,768]{1,0:T(8,128)(2,1)S(1)} %pad_maximum_fusion.9), channel_id=1, source_target_pairs={{0,2},{2,0},{4,6},{6,4},{1,3},{3,1},{5,7},{7,5},{8,10},{10,8},{12,... | collective-permute-start | bytes 1769480 | tf_op jit(solution)/shard_map/ppermute | solution.py:34
  88.8 3.4 %collective-permute-start.13 = (bf16[192,1536]{1,0:T(8,128)(2,1)}, bf16[192,1536]{1,0:T(8,128)(2,1)S(1)}, u32[]{:S(2)}, u32[]{:S(2)}) collective-permute-start(bf16[192,1536]{1,0:T(8,128)(2,1)} %constant_dynamic-update-slice_fusion.2), channel_id=1, source_target_pairs={{0,48},{16,0},{32,16},{48,32},{1,49},{17,1},{33,17},{49,33},{2,50}... | collective-permute-start | bytes 1769480 | tf_op jit(solution)/shard_map/ppermute | solution.py:26
  92.3 3.6 %collective-permute-start.11 = (bf16[288,1536]{1,0:T(8,128)(2,1)S(1)}, bf16[288,1536]{1,0:T(8,128)(2,1)S(1)}, u32[]{:S(2)}, u32[]{:S(2)}) collective-permute-start(bf16[288,1536]{1,0:T(8,128)(2,1)S(1)} %get-tuple-element.31), channel_id=1, source_target_pairs={{0,16},{16,32},{32,48},{48,0},{1,17},{17,33},{33,49},{49,1},{2,18}... | collective-permute-start | bytes 2654216 | tf_op jit(solution)/shard_map/ppermute | solution.py:26
  100.3 5.1 %collective-permute-start.22 = (bf16[768,768]{1,0:T(8,128)(2,1)S(1)}, bf16[768,768]{1,0:T(8,128)(2,1)S(1)}, u32[]{:S(2)}, u32[]{:S(2)}) collective-permute-start(bf16[768,768]{1,0:T(8,128)(2,1)S(1)} %pad_maximum_fusion.3), channel_id=1, source_target_pairs={{0,4},{2,6},{4,0},{6,2},{1,5},{3,7},{5,1},{7,3},{8,12},{10,14},{12... | collective-permute-start | bytes 3538952 | tf_op jit(solution)/shard_map/ppermute | solution.py:34
  108.0 8.8 %collective-permute-done.11 = bf16[288,1536]{1,0:T(8,128)(2,1)S(1)} collective-permute-done((bf16[288,1536]{1,0:T(8,128)(2,1)S(1)}, bf16[288,1536]{1,0:T(8,128)(2,1)S(1)}, u32[]{:S(2)}, u32[]{:S(2)}) %collective-permute-start.11) | collective-permute-done | bytes 884768 | tf_op jit(solution)/shard_map/ppermute | solution.py:26
  124.4 5.0 %collective-permute-done.14 = bf16[192,1536]{1,0:T(8,128)(2,1)S(1)} collective-permute-done((bf16[192,1536]{1,0:T(8,128)(2,1)}, bf16[192,1536]{1,0:T(8,128)(2,1)S(1)}, u32[]{:S(2)}, u32[]{:S(2)}) %collective-permute-start.14) | collective-permute-done | bytes 589856 | tf_op jit(solution)/shard_map/ppermute | solution.py:26
  138.1 4.3 %broadcast_in_dim.9 = bf16[3072,1536]{1,0:T(8,128)(2,1)} broadcast(bf16[]{:T(256)} %bitcast.1), dimensions={} | broadcast | bytes 9437186 | tf_op jit(solution)/shard_map/broadcast_in_dim | solution.py:89
  142.4 3.5 %dynamic_update_slice.96 = bf16[3072,1536]{1,0:T(8,128)(2,1)} dynamic-update-slice(bf16[3072,1536]{1,0:T(8,128)(2,1)} %broadcast_in_dim.9, bf16[96,1536]{1,0:T(8,128)(2,1)} %copy-done.8, u32[]{:T(128)} %bitcast.2, u32[]{:T(128)} %constant.35.clone.1) | dynamic-update-slice | bytes 589828 | tf_op jit(solution)/shard_map/dynamic_update_slice | solution.py:100
  145.9 3.6 %dynamic_update_slice.97 = bf16[3072,1536]{1,0:T(8,128)(2,1)} dynamic-update-slice(bf16[3072,1536]{1,0:T(8,128)(2,1)} %dynamic_update_slice.96, bf16[96,1536]{1,0:T(8,128)(2,1)} %copy-done.15, u32[]{:T(128)} %bitcast.3, u32[]{:T(128)} %constant.35.clone.1) | dynamic-update-slice | bytes 589828 | tf_op jit(solution)/shard_map/dynamic_update_slice | solution.py:100
  149.5 3.4 %dynamic_update_slice.98 = bf16[3072,1536]{1,0:T(8,128)(2,1)} dynamic-update-slice(bf16[3072,1536]{1,0:T(8,128)(2,1)} %dynamic_update_slice.97, bf16[96,1536]{1,0:T(8,128)(2,1)} %copy-done.16, u32[]{:T(128)} %bitcast.4, u32[]{:T(128)} %constant.35.clone.1) | dynamic-update-slice | bytes 589828 | tf_op jit(solution)/shard_map/dynamic_update_slice | solution.py:100
  152.9 3.6 %dynamic_update_slice.99 = bf16[3072,1536]{1,0:T(8,128)(2,1)} dynamic-update-slice(bf16[3072,1536]{1,0:T(8,128)(2,1)} %dynamic_update_slice.98, bf16[96,1536]{1,0:T(8,128)(2,1)} %copy-done.14, u32[]{:T(128)} %bitcast.5, u32[]{:T(128)} %constant.35.clone.1) | dynamic-update-slice | bytes 589828 | tf_op jit(solution)/shard_map/dynamic_update_slice | solution.py:100
  156.5 3.4 dynamic_update_slice.100
  159.9 3.5 %dynamic_update_slice.101 = bf16[3072,1536]{1,0:T(8,128)(2,1)} dynamic-update-slice(bf16[3072,1536]{1,0:T(8,128)(2,1)} %dynamic_update_slice.100, bf16[96,1536]{1,0:T(8,128)(2,1)} %copy-done.7, u32[]{:T(128)} %bitcast.7, u32[]{:T(128)} %constant.35.clone.1) | dynamic-update-slice | bytes 589828 | tf_op jit(solution)/shard_map/dynamic_update_slice | solution.py:100
  163.4 3.5 %dynamic_update_slice.102 = bf16[3072,1536]{1,0:T(8,128)(2,1)} dynamic-update-slice(bf16[3072,1536]{1,0:T(8,128)(2,1)} %dynamic_update_slice.101, bf16[96,1536]{1,0:T(8,128)(2,1)} %get-tuple-element.71, u32[]{:T(128)} %bitcast.8, u32[]{:T(128)} %constant.35.clone.1) | dynamic-update-slice | bytes 589828 | tf_op jit(solution)/shard_map/dynamic_update_slice | solution.py:100
  166.9 3.4 dynamic_update_slice.103
  173.7 3.6 %dynamic_update_slice.105 = bf16[3072,1536]{1,0:T(8,128)(2,1)} dynamic-update-slice(bf16[3072,1536]{1,0:T(8,128)(2,1)} %dynamic_update_slice.104, bf16[96,1536]{1,0:T(8,128)(2,1)} %get-tuple-element.69, u32[]{:T(128)} %bitcast.11, u32[]{:T(128)} %constant.35.clone.1) | dynamic-update-slice | bytes 589828 | tf_op jit(solution)/shard_map/dynamic_update_slice | solution.py:100
  179.9 3.5 %dynamic_update_slice.107 = bf16[3072,1536]{1,0:T(8,128)(2,1)} dynamic-update-slice(bf16[3072,1536]{1,0:T(8,128)(2,1)} %dynamic_update_slice.106, bf16[96,1536]{1,0:T(8,128)(2,1)} %copy-done.2, u32[]{:T(128)} %bitcast.13, u32[]{:T(128)} %constant.35.clone.1) | dynamic-update-slice | bytes 589828 | tf_op jit(solution)/shard_map/dynamic_update_slice | solution.py:100
  188.8 15.3 %collective-permute-start.17 = (bf16[192,1536]{1,0:T(8,128)(2,1)}, bf16[192,1536]{1,0:T(8,128)(2,1)}, u32[]{:S(2)}, u32[]{:S(2)}) collective-permute-start(bf16[192,1536]{1,0:T(8,128)(2,1)} %get-tuple-element.36), channel_id=1, source_target_pairs={{0,16},{16,32},{32,48},{48,0},{1,17},{17,33},{33,49},{49,1},{2,18}... | collective-permute-start | bytes 1769480 | tf_op jit(solution)/shard_map/ppermute | solution.py:26
  204.8 3.4 dynamic_update_slice.109
  208.3 3.5 %dynamic_update_slice.110 = bf16[3072,1536]{1,0:T(8,128)(2,1)} dynamic-update-slice(bf16[3072,1536]{1,0:T(8,128)(2,1)} %dynamic_update_slice.109, bf16[96,1536]{1,0:T(8,128)(2,1)S(1)} %get-tuple-element.54, u32[]{:T(128)} %bitcast.16, u32[]{:T(128)} %constant.35.clone.1) | dynamic-update-slice | bytes 589828 | tf_op jit(solution)/shard_map/dynamic_update_slice | solution.py:100
  211.8 3.5 %dynamic_update_slice.111 = bf16[3072,1536]{1,0:T(8,128)(2,1)} dynamic-update-slice(bf16[3072,1536]{1,0:T(8,128)(2,1)} %dynamic_update_slice.110, bf16[96,1536]{1,0:T(8,128)(2,1)} %get-tuple-element.53, u32[]{:T(128)} %bitcast.17, u32[]{:T(128)} %constant.35.clone.1) | dynamic-update-slice | bytes 589828 | tf_op jit(solution)/shard_map/dynamic_update_slice | solution.py:100
  215.3 3.5 %dynamic_update_slice.112 = bf16[3072,1536]{1,0:T(8,128)(2,1)} dynamic-update-slice(bf16[3072,1536]{1,0:T(8,128)(2,1)} %dynamic_update_slice.111, bf16[96,1536]{1,0:T(8,128)(2,1)} %collective-permute-done.10, u32[]{:T(128)} %bitcast.18, u32[]{:T(128)} %constant.35.clone.1) | dynamic-update-slice | bytes 589828 | tf_op jit(solution)/shard_map/dynamic_update_slice | solution.py:100
  218.8 3.4 %dynamic_update_slice.113 = bf16[3072,1536]{1,0:T(8,128)(2,1)} dynamic-update-slice(bf16[3072,1536]{1,0:T(8,128)(2,1)} %dynamic_update_slice.112, bf16[96,1536]{1,0:T(8,128)(2,1)} %copy-done.9, u32[]{:T(128)} %bitcast.19, u32[]{:T(128)} %constant.35.clone.1) | dynamic-update-slice | bytes 589828 | tf_op jit(solution)/shard_map/dynamic_update_slice | solution.py:100
  222.2 3.5 %dynamic_update_slice.114 = bf16[3072,1536]{1,0:T(8,128)(2,1)} dynamic-update-slice(bf16[3072,1536]{1,0:T(8,128)(2,1)} %dynamic_update_slice.113, bf16[96,1536]{1,0:T(8,128)(2,1)} %get-tuple-element.66, u32[]{:T(128)} %bitcast.20, u32[]{:T(128)} %constant.35.clone.1) | dynamic-update-slice | bytes 589828 | tf_op jit(solution)/shard_map/dynamic_update_slice | solution.py:100
  225.8 3.5 %dynamic_update_slice.115 = bf16[3072,1536]{1,0:T(8,128)(2,1)} dynamic-update-slice(bf16[3072,1536]{1,0:T(8,128)(2,1)} %dynamic_update_slice.114, bf16[96,1536]{1,0:T(8,128)(2,1)} %get-tuple-element.65, u32[]{:T(128)} %bitcast.21, u32[]{:T(128)} %constant.35.clone.1) | dynamic-update-slice | bytes 589828 | tf_op jit(solution)/shard_map/dynamic_update_slice | solution.py:100
  232.7 3.5 %dynamic_update_slice.117 = bf16[3072,1536]{1,0:T(8,128)(2,1)} dynamic-update-slice(bf16[3072,1536]{1,0:T(8,128)(2,1)} %dynamic_update_slice.116, bf16[96,1536]{1,0:T(8,128)(2,1)S(1)} %copy-done.10, u32[]{:T(128)} %bitcast.23, u32[]{:T(128)} %constant.35.clone.1) | dynamic-update-slice | bytes 589828 | tf_op jit(solution)/shard_map/dynamic_update_slice | solution.py:100
  236.2 3.5 %dynamic_update_slice.118 = bf16[3072,1536]{1,0:T(8,128)(2,1)} dynamic-update-slice(bf16[3072,1536]{1,0:T(8,128)(2,1)} %dynamic_update_slice.117, bf16[96,1536]{1,0:T(8,128)(2,1)S(1)} %copy-done.4, u32[]{:T(128)} %bitcast.24, u32[]{:T(128)} %constant.35.clone.1) | dynamic-update-slice | bytes 589828 | tf_op jit(solution)/shard_map/dynamic_update_slice | solution.py:100
  248.6 3.5 %dynamic_update_slice.120 = bf16[3072,1536]{1,0:T(8,128)(2,1)} dynamic-update-slice(bf16[3072,1536]{1,0:T(8,128)(2,1)} %dynamic_update_slice.119, bf16[96,1536]{1,0:T(8,128)(2,1)S(1)} %get-tuple-element.62, u32[]{:T(128)} %bitcast.26, u32[]{:T(128)} %constant.35.clone.1) | dynamic-update-slice | bytes 589828 | tf_op jit(solution)/shard_map/dynamic_update_slice | solution.py:100
  252.1 3.4 dynamic_update_slice.121
  260.0 8.2 %collective-permute-done.18 = bf16[192,1536]{1,0:T(8,128)(2,1)} collective-permute-done((bf16[192,1536]{1,0:T(8,128)(2,1)}, bf16[192,1536]{1,0:T(8,128)(2,1)}, u32[]{:S(2)}, u32[]{:S(2)}) %collective-permute-start.18) | collective-permute-done | bytes 589856 | tf_op jit(solution)/shard_map/ppermute | solution.py:26
  272.7 3.5 %dynamic_update_slice.124 = bf16[3072,1536]{1,0:T(8,128)(2,1)} dynamic-update-slice(bf16[3072,1536]{1,0:T(8,128)(2,1)} %dynamic_update_slice.123, bf16[96,1536]{1,0:T(8,128)(2,1)} %collective-permute-done.16, u32[]{:T(128)} %bitcast.30, u32[]{:T(128)} %constant.35.clone.1) | dynamic-update-slice | bytes 589828 | tf_op jit(solution)/shard_map/dynamic_update_slice | solution.py:100
  279.5 3.5 %dynamic_update_slice.126 = bf16[3072,1536]{1,0:T(8,128)(2,1)} dynamic-update-slice(bf16[3072,1536]{1,0:T(8,128)(2,1)} %dynamic_update_slice.125, bf16[96,1536]{1,0:T(8,128)(2,1)S(1)} %get-tuple-element.57, u32[]{:T(128)} %bitcast.32, u32[]{:T(128)} %constant.35.clone.1) | dynamic-update-slice | bytes 589828 | tf_op jit(solution)/shard_map/dynamic_update_slice | solution.py:100
  283.0 3.4 %dynamic_update_slice.127 = bf16[3072,1536]{1,0:T(8,128)(2,1)} dynamic-update-slice(bf16[3072,1536]{1,0:T(8,128)(2,1)} %dynamic_update_slice.126, bf16[96,1536]{1,0:T(8,128)(2,1)S(1)} %collective-permute-done.19, u32[]{:T(128)} %bitcast.33, u32[]{:T(128)} %constant.35.clone.1) | dynamic-update-slice | bytes 589828 | tf_op jit(solution)/shard_map/dynamic_update_slice | solution.py:100
  290.8 3.4 fusion.2
  304.0 4.2 %all-to-all-start = ((bf16[4,2,192,256]{3,2,1,0:T(8,128)(2,1)}), bf16[4,2,192,256]{3,2,1,0:T(8,128)(2,1)S(1)}, u32[]{:S(2)}, u32[]{:S(2)}) async-start(bf16[4,2,192,256]{3,2,1,0:T(8,128)(2,1)} %fusion.10), calls=%async_computation | async-start | bytes 1572864 | tf_op jit(solution)/shard_map/all_to_all | solution.py:127
  308.2 12.6 %all-to-all-done = bf16[4,2,192,256]{3,2,1,0:T(8,128)(2,1)S(1)} async-done(((bf16[4,2,192,256]{3,2,1,0:T(8,128)(2,1)}), bf16[4,2,192,256]{3,2,1,0:T(8,128)(2,1)S(1)}, u32[]{:S(2)}, u32[]{:S(2)}) %all-to-all-start) | async-done | bytes 786464 | tf_op jit(solution)/shard_map/all_to_all | solution.py:127
  320.9 10.2 %collective-permute-start.25 = (bf16[192,256]{1,0:T(8,128)(2,1)S(1)}, bf16[192,256]{1,0:T(8,128)(2,1)S(1)}, u32[]{:S(2)}, u32[]{:S(2)}) collective-permute-start(bf16[192,256]{1,0:T(8,128)(2,1)S(1)} %fusion.29), channel_id=1, source_target_pairs={{0,8},{8,0},{1,9},{9,1},{2,10},{10,2},{3,11},{11,3},{4,12},{12,4},... | collective-permute-start | bytes 294920 | tf_op jit(solution)/shard_map/ppermute | solution.py:26
  331.2 11.3 %collective-permute-done.25 = bf16[192,256]{1,0:T(8,128)(2,1)S(1)} collective-permute-done((bf16[192,256]{1,0:T(8,128)(2,1)S(1)}, bf16[192,256]{1,0:T(8,128)(2,1)S(1)}, u32[]{:S(2)}, u32[]{:S(2)}) %collective-permute-start.25) | collective-permute-done | bytes 98336 | tf_op jit(solution)/shard_map/ppermute | solution.py:26
  (115 shorter events, 99.0 us)
Async XLA Ops:
  0.0 49.6 %copy-start.18 = (s32[256]{0:T(256)S(1)}, s32[256]{0:T(256)}, u32[]{:S(2)}) copy-start(s32[256]{0:T(256)} %param.13) | copy-start | bytes 3076
  1.0 64.2 %copy-start.8 = (bf16[96,1536]{1,0:T(8,128)(2,1)}, bf16[96,1536]{1,0:T(8,128)(2,1)S(1)}, u32[]{:S(2)}) copy-start(bf16[96,1536]{1,0:T(8,128)(2,1)S(1)} %pad_maximum_fusion.10) | copy-start | bytes 884740
  1.0 14.2 %collective-permute-start = (bf16[96,1536]{1,0:T(8,128)(2,1)S(1)}, bf16[96,1536]{1,0:T(8,128)(2,1)S(1)}, u32[]{:S(2)}, u32[]{:S(2)}) collective-permute-start(bf16[96,1536]{1,0:T(8,128)(2,1)S(1)} %pad_maximum_fusion.10), channel_id=1, source_target_pairs={{0,128},{128,256},{256,384},{384,448},{448,320},{320,192},{192,64}... | collective-permute-start | bytes 884744 | tf_op jit(solution)/shard_map/ppermute | solution.py:26
  3.0 15.6 %collective-permute-start.3 = (bf16[96,1536]{1,0:T(8,128)(2,1)S(1)}, bf16[96,1536]{1,0:T(8,128)(2,1)S(1)}, u32[]{:S(2)}, u32[]{:S(2)}) collective-permute-start(bf16[96,1536]{1,0:T(8,128)(2,1)S(1)} %pad_maximum_fusion.10), channel_id=1, source_target_pairs={{0,64},{128,0},{256,128},{384,256},{448,384},{320,448},{192,320},{... | collective-permute-start | bytes 884744 | tf_op jit(solution)/shard_map/ppermute | solution.py:26
  9.4 10.4 %collective-permute-start.1 = (bf16[96,1536]{1,0:T(8,128)(2,1)S(1)}, bf16[96,1536]{1,0:T(8,128)(2,1)S(1)}, u32[]{:S(2)}, u32[]{:S(2)}) collective-permute-start(bf16[96,1536]{1,0:T(8,128)(2,1)S(1)} %pad_maximum_fusion.10), channel_id=1, source_target_pairs={{0,16},{16,32},{32,48},{48,0},{1,17},{17,33},{33,49},{49,1},{2,18}... | collective-permute-start | bytes 884744 | tf_op jit(solution)/shard_map/ppermute | solution.py:26
  11.8 11.8 %collective-permute-start.4 = (bf16[96,1536]{1,0:T(8,128)(2,1)S(1)}, bf16[96,1536]{1,0:T(8,128)(2,1)S(1)}, u32[]{:S(2)}, u32[]{:S(2)}) collective-permute-start(bf16[96,1536]{1,0:T(8,128)(2,1)S(1)} %pad_maximum_fusion.10), channel_id=1, source_target_pairs={{0,48},{16,0},{32,16},{48,32},{1,49},{17,1},{33,17},{49,33},{2,50}... | collective-permute-start | bytes 884744 | tf_op jit(solution)/shard_map/ppermute | solution.py:26
  15.2 47.7 %copy-start.6 = (bf16[96,1536]{1,0:T(8,128)(2,1)}, bf16[96,1536]{1,0:T(8,128)(2,1)S(1)}, u32[]{:S(2)}) copy-start(bf16[96,1536]{1,0:T(8,128)(2,1)S(1)} %collective-permute-done) | copy-start | bytes 884740
  18.5 44.4 %copy-start.7 = (bf16[96,1536]{1,0:T(8,128)(2,1)}, bf16[96,1536]{1,0:T(8,128)(2,1)S(1)}, u32[]{:S(2)}) copy-start(bf16[96,1536]{1,0:T(8,128)(2,1)S(1)} %collective-permute-done.3) | copy-start | bytes 884740
  19.7 3.8 %copy-start.14 = (bf16[96,1536]{1,0:T(8,128)(2,1)}, bf16[96,1536]{1,0:T(8,128)(2,1)S(1)}, u32[]{:S(2)}) copy-start(bf16[96,1536]{1,0:T(8,128)(2,1)S(1)} %collective-permute-done.1) | copy-start | bytes 884740
  19.7 38.1 %collective-permute-start.7 = (bf16[192,1536]{1,0:T(8,128)(2,1)}, bf16[192,1536]{1,0:T(8,128)(2,1)S(1)}, u32[]{:S(2)}, u32[]{:S(2)}) collective-permute-start(bf16[192,1536]{1,0:T(8,128)(2,1)} %constant_dynamic-update-slice_fusion), channel_id=1, source_target_pairs={{0,16},{16,32},{32,48},{48,0},{1,17},{17,33},{33,49},{49,1},{2,18}... | collective-permute-start | bytes 1769480 | tf_op jit(solution)/shard_map/ppermute | solution.py:26
  23.5 28.2 %copy-start.15 = (bf16[96,1536]{1,0:T(8,128)(2,1)}, bf16[96,1536]{1,0:T(8,128)(2,1)S(1)}, u32[]{:S(2)}) copy-start(bf16[96,1536]{1,0:T(8,128)(2,1)S(1)} %collective-permute-done.4) | copy-start | bytes 884740
  23.5 26.2 %collective-permute-start.2 = (bf16[96,1536]{1,0:T(8,128)(2,1)S(1)}, bf16[96,1536]{1,0:T(8,128)(2,1)S(1)}, u32[]{:S(2)}, u32[]{:S(2)}) collective-permute-start(bf16[96,1536]{1,0:T(8,128)(2,1)S(1)} %collective-permute-done), channel_id=1, source_target_pairs={{0,128},{128,256},{256,384},{384,448},{448,320},{320,192},{192,64}... | collective-permute-start | bytes 884744 | tf_op jit(solution)/shard_map/ppermute | solution.py:26
  25.5 26.3 %collective-permute-start.5 = (bf16[96,1536]{1,0:T(8,128)(2,1)S(1)}, bf16[96,1536]{1,0:T(8,128)(2,1)S(1)}, u32[]{:S(2)}, u32[]{:S(2)}) collective-permute-start(bf16[96,1536]{1,0:T(8,128)(2,1)S(1)} %collective-permute-done.3), channel_id=1, source_target_pairs={{0,64},{128,0},{256,128},{384,256},{448,384},{320,448},{192,320},{... | collective-permute-start | bytes 884744 | tf_op jit(solution)/shard_map/ppermute | solution.py:26
  33.0 44.7 %collective-permute-start.20 = (bf16[192,768]{1,0:T(8,128)(2,1)S(1)}, bf16[192,768]{1,0:T(8,128)(2,1)S(1)}, u32[]{:S(2)}, u32[]{:S(2)}) collective-permute-start(bf16[192,768]{1,0:T(8,128)(2,1)S(1)} %pad_maximum_fusion.11), channel_id=1, source_target_pairs={{0,8},{8,0},{1,9},{9,1},{2,10},{10,2},{3,11},{11,3},{4,12},{12,4},... | collective-permute-start | bytes 884744 | tf_op jit(solution)/shard_map/ppermute | solution.py:26
  46.2 15.9 %collective-permute-start.6 = (bf16[192,1536]{1,0:T(8,128)(2,1)}, bf16[192,1536]{1,0:T(8,128)(2,1)S(1)}, u32[]{:S(2)}, u32[]{:S(2)}) collective-permute-start(bf16[192,1536]{1,0:T(8,128)(2,1)} %constant_dynamic-update-slice_fusion), channel_id=1, source_target_pairs={{0,48},{16,0},{32,16},{48,32},{1,49},{17,1},{33,17},{49,33},{2,50}... | collective-permute-start | bytes 1769480 | tf_op jit(solution)/shard_map/ppermute | solution.py:26
  49.8 13.2 %copy-start.1 = (bf16[96,1536]{1,0:T(8,128)(2,1)}, bf16[96,1536]{1,0:T(8,128)(2,1)S(1)}, u32[]{:S(2)}) copy-start(bf16[96,1536]{1,0:T(8,128)(2,1)S(1)} %collective-permute-done.2) | copy-start | bytes 884740
  49.8 36.6 %collective-permute-start.10 = (bf16[96,1536]{1,0:T(8,128)(2,1)S(1)}, bf16[96,1536]{1,0:T(8,128)(2,1)}, u32[]{:S(2)}, u32[]{:S(2)}) collective-permute-start(bf16[96,1536]{1,0:T(8,128)(2,1)S(1)} %collective-permute-done.2), channel_id=1, source_target_pairs={{0,128},{128,256},{256,384},{384,448},{448,320},{320,192},{192,64}... | collective-permute-start | bytes 884744 | tf_op jit(solution)/shard_map/ppermute | solution.py:26
  51.7 11.2 %copy-start.2 = (bf16[96,1536]{1,0:T(8,128)(2,1)}, bf16[96,1536]{1,0:T(8,128)(2,1)S(1)}, u32[]{:S(2)}) copy-start(bf16[96,1536]{1,0:T(8,128)(2,1)S(1)} %collective-permute-done.5) | copy-start | bytes 884740
  51.7 30.9 %collective-permute-start.12 = (bf16[96,1536]{1,0:T(8,128)(2,1)S(1)}, bf16[96,1536]{1,0:T(8,128)(2,1)S(1)}, u32[]{:S(2)}, u32[]{:S(2)}) collective-permute-start(bf16[96,1536]{1,0:T(8,128)(2,1)S(1)} %collective-permute-done.5), channel_id=1, source_target_pairs={{0,64},{128,0},{256,128},{384,256},{448,384},{320,448},{192,320},{... | collective-permute-start | bytes 884744 | tf_op jit(solution)/shard_map/ppermute | solution.py:26
  58.5 24.2 %copy-start.11 = (bf16[256,192]{0,1:T(8,128)(2,1)S(1)}, bf16[256,192]{0,1:T(8,128)(2,1)}, u32[]{:S(2)}) copy-start(bf16[256,192]{0,1:T(8,128)(2,1)} %param.11) | copy-start | bytes 294916
  58.5 24.2 %copy-start.12 = (bf16[256,192]{0,1:T(8,128)(2,1)S(1)}, bf16[256,192]{0,1:T(8,128)(2,1)}, u32[]{:S(2)}) copy-start(bf16[256,192]{0,1:T(8,128)(2,1)} %param.10) | copy-start | bytes 294916
  58.5 24.2 %copy-start.13 = (bf16[256,192]{0,1:T(8,128)(2,1)S(1)}, bf16[256,192]{0,1:T(8,128)(2,1)}, u32[]{:S(2)}) copy-start(bf16[256,192]{0,1:T(8,128)(2,1)} %param.9) | copy-start | bytes 294916
  63.0 29.3 %copy-start.17 = (f32[256]{0:T(256)S(1)}, f32[256]{0:T(256)}, u32[]{:S(2)}) copy-start(f32[256]{0:T(256)} %param.12) | copy-start | bytes 3076
  63.0 37.1 %collective-permute-start.8 = (bf16[288,1536]{1,0:T(8,128)(2,1)S(1)}, bf16[288,1536]{1,0:T(8,128)(2,1)S(1)}, u32[]{:S(2)}, u32[]{:S(2)}) collective-permute-start(bf16[288,1536]{1,0:T(8,128)(2,1)S(1)} %get-tuple-element.27), channel_id=1, source_target_pairs={{0,48},{16,0},{32,16},{48,32},{1,49},{17,1},{33,17},{49,33},{2,50}... | collective-permute-start | bytes 2654216 | tf_op jit(solution)/shard_map/ppermute | solution.py:26
  65.2 30.7 %collective-permute-start.9 = (bf16[96,1536]{1,0:T(8,128)(2,1)S(1)}, bf16[96,1536]{1,0:T(8,128)(2,1)S(1)}, u32[]{:S(2)}, u32[]{:S(2)}) collective-permute-start(bf16[96,1536]{1,0:T(8,128)(2,1)S(1)} %pad_maximum_fusion.10), channel_id=1, source_target_pairs={{0,32},{16,48},{32,0},{48,16},{1,33},{17,49},{33,1},{49,17},{2,34}... | collective-permute-start | bytes 884744 | tf_op jit(solution)/shard_map/ppermute | solution.py:26
  82.7 17.5 %copy-start.9 = (bf16[96,1536]{1,0:T(8,128)(2,1)}, bf16[96,1536]{1,0:T(8,128)(2,1)S(1)}, u32[]{:S(2)}) copy-start(bf16[96,1536]{1,0:T(8,128)(2,1)S(1)} %collective-permute-done.12) | copy-start | bytes 884740
  82.9 17.1 %collective-permute-start.21 = (bf16[384,768]{1,0:T(8,128)(2,1)S(1)}, bf16[384,768]{1,0:T(8,128)(2,1)S(1)}, u32[]{:S(2)}, u32[]{:S(2)}) collective-permute-start(bf16[384,768]{1,0:T(8,128)(2,1)S(1)} %pad_maximum_fusion.9), channel_id=1, source_target_pairs={{0,2},{2,0},{4,6},{6,4},{1,3},{3,1},{5,7},{7,5},{8,10},{10,8},{12,... | collective-permute-start | bytes 1769480 | tf_op jit(solution)/shard_map/ppermute | solution.py:34
  88.8 18.3 %collective-permute-start.13 = (bf16[192,1536]{1,0:T(8,128)(2,1)}, bf16[192,1536]{1,0:T(8,128)(2,1)S(1)}, u32[]{:S(2)}, u32[]{:S(2)}) collective-permute-start(bf16[192,1536]{1,0:T(8,128)(2,1)} %constant_dynamic-update-slice_fusion.2), channel_id=1, source_target_pairs={{0,48},{16,0},{32,16},{48,32},{1,49},{17,1},{33,17},{49,33},{2,50}... | collective-permute-start | bytes 1769480 | tf_op jit(solution)/shard_map/ppermute | solution.py:26
  92.3 24.5 %collective-permute-start.11 = (bf16[288,1536]{1,0:T(8,128)(2,1)S(1)}, bf16[288,1536]{1,0:T(8,128)(2,1)S(1)}, u32[]{:S(2)}, u32[]{:S(2)}) collective-permute-start(bf16[288,1536]{1,0:T(8,128)(2,1)S(1)} %get-tuple-element.31), channel_id=1, source_target_pairs={{0,16},{16,32},{32,48},{48,0},{1,17},{17,33},{33,49},{49,1},{2,18}... | collective-permute-start | bytes 2654216 | tf_op jit(solution)/shard_map/ppermute | solution.py:26
  95.9 4.4 %copy-start.16 = (bf16[96,1536]{1,0:T(8,128)(2,1)}, bf16[96,1536]{1,0:T(8,128)(2,1)S(1)}, u32[]{:S(2)}) copy-start(bf16[96,1536]{1,0:T(8,128)(2,1)S(1)} %collective-permute-done.9) | copy-start | bytes 884740
  95.9 33.5 %collective-permute-start.14 = (bf16[192,1536]{1,0:T(8,128)(2,1)}, bf16[192,1536]{1,0:T(8,128)(2,1)S(1)}, u32[]{:S(2)}, u32[]{:S(2)}) collective-permute-start(bf16[192,1536]{1,0:T(8,128)(2,1)} %constant_dynamic-update-slice_fusion.2), channel_id=1, source_target_pairs={{0,16},{16,32},{32,48},{48,0},{1,17},{17,33},{33,49},{49,1},{2,18}... | collective-permute-start | bytes 1769480 | tf_op jit(solution)/shard_map/ppermute | solution.py:26
  100.3 30.4 %collective-permute-start.22 = (bf16[768,768]{1,0:T(8,128)(2,1)S(1)}, bf16[768,768]{1,0:T(8,128)(2,1)S(1)}, u32[]{:S(2)}, u32[]{:S(2)}) collective-permute-start(bf16[768,768]{1,0:T(8,128)(2,1)S(1)} %pad_maximum_fusion.3), channel_id=1, source_target_pairs={{0,4},{2,6},{4,0},{6,2},{1,5},{3,7},{5,1},{7,3},{8,12},{10,14},{12... | collective-permute-start | bytes 3538952 | tf_op jit(solution)/shard_map/ppermute | solution.py:34
  116.8 130.8 %collective-permute-start.15 = (bf16[192,1536]{1,0:T(8,128)(2,1)}, bf16[192,1536]{1,0:T(8,128)(2,1)}, u32[]{:S(2)}, u32[]{:S(2)}) collective-permute-start(bf16[192,1536]{1,0:T(8,128)(2,1)} %constant_dynamic-update-slice_fusion.2), channel_id=1, source_target_pairs={{0,32},{16,48},{32,0},{48,16},{1,33},{17,49},{33,1},{49,17},{2,34}... | collective-permute-start | bytes 1769480 | tf_op jit(solution)/shard_map/ppermute | solution.py:26
  120.1 66.7 %collective-permute-start.16 = (bf16[96,1536]{1,0:T(8,128)(2,1)}, bf16[96,1536]{1,0:T(8,128)(2,1)}, u32[]{:S(2)}, u32[]{:S(2)}) collective-permute-start(bf16[96,1536]{1,0:T(8,128)(2,1)} %collective-permute-done.10), channel_id=1, source_target_pairs={{0,128},{128,256},{256,384},{384,448},{448,320},{320,192},{192,64}... | collective-permute-start | bytes 884744 | tf_op jit(solution)/shard_map/ppermute | solution.py:26
  132.8 153.6 %collective-permute-start.23 = (bf16[1536,768]{1,0:T(8,128)(2,1)}, bf16[1536,768]{1,0:T(8,128)(2,1)}, u32[]{:S(2)}, u32[]{:S(2)}) collective-permute-start(bf16[1536,768]{1,0:T(8,128)(2,1)} %pad_maximum_fusion.2), channel_id=1, source_target_pairs={{0,1},{1,0},{2,3},{3,2},{4,5},{5,4},{6,7},{7,6},{8,9},{9,8},{10,11... | collective-permute-start | bytes 7077896 | tf_op jit(solution)/shard_map/ppermute | solution.py:26
  170.3 13.1 %copy-start.5 = (bf16[96,1536]{1,0:T(8,128)(2,1)S(1)}, bf16[96,1536]{1,0:T(8,128)(2,1)}, u32[]{:S(2)}) copy-start(bf16[96,1536]{1,0:T(8,128)(2,1)} %get-tuple-element.51) | copy-start | bytes 884740
  188.8 66.7 %collective-permute-start.17 = (bf16[192,1536]{1,0:T(8,128)(2,1)}, bf16[192,1536]{1,0:T(8,128)(2,1)}, u32[]{:S(2)}, u32[]{:S(2)}) collective-permute-start(bf16[192,1536]{1,0:T(8,128)(2,1)} %get-tuple-element.36), channel_id=1, source_target_pairs={{0,16},{16,32},{32,48},{48,0},{1,17},{17,33},{33,49},{49,1},{2,18}... | collective-permute-start | bytes 1769480 | tf_op jit(solution)/shard_map/ppermute | solution.py:26
  208.3 24.4 %copy-start.10 = (bf16[96,1536]{1,0:T(8,128)(2,1)S(1)}, bf16[96,1536]{1,0:T(8,128)(2,1)}, u32[]{:S(2)}) copy-start(bf16[96,1536]{1,0:T(8,128)(2,1)} %get-tuple-element.63) | copy-start | bytes 884740
  208.3 27.9 %copy-start.4 = (bf16[96,1536]{1,0:T(8,128)(2,1)S(1)}, bf16[96,1536]{1,0:T(8,128)(2,1)}, u32[]{:S(2)}) copy-start(bf16[96,1536]{1,0:T(8,128)(2,1)} %get-tuple-element.52) | copy-start | bytes 884740
  211.7 27.9 %copy-start.3 = (bf16[96,1536]{1,0:T(8,128)(2,1)S(1)}, bf16[96,1536]{1,0:T(8,128)(2,1)}, u32[]{:S(2)}) copy-start(bf16[96,1536]{1,0:T(8,128)(2,1)} %get-tuple-element.49) | copy-start | bytes 884740
  243.0 25.2 %collective-permute-start.18 = (bf16[192,1536]{1,0:T(8,128)(2,1)}, bf16[192,1536]{1,0:T(8,128)(2,1)}, u32[]{:S(2)}, u32[]{:S(2)}) collective-permute-start(bf16[192,1536]{1,0:T(8,128)(2,1)} %get-tuple-element.73), channel_id=1, source_target_pairs={{0,48},{16,0},{32,16},{48,32},{1,49},{17,1},{33,17},{49,33},{2,50}... | collective-permute-start | bytes 1769480 | tf_op jit(solution)/shard_map/ppermute | solution.py:26
  244.9 38.1 %collective-permute-start.19 = (bf16[96,1536]{1,0:T(8,128)(2,1)}, bf16[96,1536]{1,0:T(8,128)(2,1)S(1)}, u32[]{:S(2)}, u32[]{:S(2)}) collective-permute-start(bf16[96,1536]{1,0:T(8,128)(2,1)} %collective-permute-done.16), channel_id=1, source_target_pairs={{0,32},{16,48},{32,0},{48,16},{1,33},{17,49},{33,1},{49,17},{2,34}... | collective-permute-start | bytes 884744 | tf_op jit(solution)/shard_map/ppermute | solution.py:26
  286.4 4.4 %copy-start = (bf16[3072,1536]{1,0:T(8,128)(2,1)S(1)}, bf16[3072,1536]{1,0:T(8,128)(2,1)}, u32[]{:S(2)}) copy-start(bf16[3072,1536]{1,0:T(8,128)(2,1)} %dynamic_update_slice.127) | copy-start | bytes 28311556
  297.6 5.3 %collective-permute-start.24 = (f32[4,2,192,256]{3,2,1,0:T(8,128)S(1)}, f32[4,2,192,256]{3,2,1,0:T(8,128)S(1)}, u32[]{:S(2)}, u32[]{:S(2)}) collective-permute-start(f32[4,2,192,256]{3,2,1,0:T(8,128)S(1)} %dynamic-slice_bitcast_fusion), channel_id=1, source_target_pairs={{0,1},{1,0},{2,3},{3,2},{4,5},{5,4},{6,7},{7,6},{8,9},{9,8},{10,11... | collective-permute-start | bytes 4718600 | tf_op jit(solution)/shard_map/ppermute | solution.py:26
  304.0 16.8 %all-to-all-start = ((bf16[4,2,192,256]{3,2,1,0:T(8,128)(2,1)}), bf16[4,2,192,256]{3,2,1,0:T(8,128)(2,1)S(1)}, u32[]{:S(2)}, u32[]{:S(2)}) async-start(bf16[4,2,192,256]{3,2,1,0:T(8,128)(2,1)} %fusion.10), calls=%async_computation | async-start | bytes 1572864 | tf_op jit(solution)/shard_map/all_to_all | solution.py:127
  320.9 21.5 %collective-permute-start.25 = (bf16[192,256]{1,0:T(8,128)(2,1)S(1)}, bf16[192,256]{1,0:T(8,128)(2,1)S(1)}, u32[]{:S(2)}, u32[]{:S(2)}) collective-permute-start(bf16[192,256]{1,0:T(8,128)(2,1)S(1)} %fusion.29), channel_id=1, source_target_pairs={{0,8},{8,0},{1,9},{9,1},{2,10},{10,2},{3,11},{11,3},{4,12},{12,4},... | collective-permute-start | bytes 294920 | tf_op jit(solution)/shard_map/ppermute | solution.py:26

commit v9 on v8

--- a/solution.py
+++ b/solution.py
@@ -12,11 +12,11 @@
 STEPS = (0, -1, 1, -2, 2, -3, 3, -4)
 
 
-def offset_table(rows):
+def block_table():
     table = np.zeros((NZ, NX, NZ * NX), np.uint32)
     for zl, x, j, s in np.ndindex(NZ, NX, NZ, NX):
         z, col = RING[(RING.index(zl) + STEPS[j]) % NZ], (x + s) % NX
-        table[zl, x, j * NX + s] = ((((col // 2) * NY + z % NY) * NH + z // NY) * 2 + col % 2) * rows
+        table[zl, x, j * NX + s] = (((col // 2) * NY + z % NY) * NH + z // NY) * 2 + col % 2
     return table
 
 
@@ -68,16 +68,16 @@
     g1 = pile(a1, b1)
     p1, m1 = x_up(after(g1, p0)), x_down(after(g1, m0))
     a3, b3 = ring_up(a2), ring_down(b2)
-    f0 = x_far(after(own, m1))
-    m2 = x_down(after(pile(a2, b2, m1[rows:]), p1))
-    p2 = x_up(after(pile(a2, b2, p1[:rows]), a3))
+    f0 = x_far(after(own, a3))
+    m2 = x_down(pile(a2, b2, m1[rows:]))
+    p2 = x_up(pile(a2, b2, p1[:rows]))
     fields = join(fields, other_half, zh, b3)
     fields = join(fields, y_near, y & 1, m2)
     g3 = pile(a3, b3)
-    m3 = x_down(after(g3, b3))
-    p3 = x_up(after(g3, f0))
-    a4 = ring_up(after(a3, m2))
-    f3 = x_far(after(g3, p2))
+    m3 = x_down(after(g3, m2))
+    p3 = x_up(after(g3, p2))
+    a4 = ring_up(a3)
+    f3 = x_far(after(g3, f0))
     fields = join(fields, y_far, y >> 1, p3)
     m4 = x_down(pile(a4, m2[rows : 2 * rows]))
     p4 = x_up(after(pile(a4, p2[:rows]), m3))
@@ -85,8 +85,8 @@
     fields = join(fields, other_core, c)
 
     zl, x, _ = lax.optimization_barrier((zl, x, m2))
-    offsets = lax.dynamic_slice(jnp.asarray(offset_table(rows)), (zl, x, jnp.uint32(0)), (1, 1, NZ * NX)).reshape(-1)
-    full = jnp.broadcast_to(m2[0, 0] * 0, (NZ * NX * rows, width))
+    offsets = lax.dynamic_slice(jnp.asarray(block_table()), (zl, x, jnp.uint32(0)), (1, 1, NZ * NX)).reshape(-1)
+    full = jnp.broadcast_to(m2[0, 0] * 0, (NZ * NX, rows, width))
     pieces = [(own, 0, 0), (m0, 0, 1), (f0, 0, 2), (p0, 0, 3)]
     for k, parts in ((1, (g1, m1, p1)), (3, (pile(a2, b2), m2, p2)), (5, (g3, m3, p3))):
         for part, step in zip(parts, (0, 1, 3)):
@@ -94,10 +94,12 @@
     pieces += [(p2[2 * rows :], 1, 2), (m2[2 * rows :], 2, 2), (f3[:rows], 5, 2), (f3[rows:], 6, 2)]
     pieces += [(p4[rows:], 3, 2), (m4[rows:], 4, 2)]
     pieces += [(a4, 7, 0), (m4[:rows], 7, 1), (p4[:rows], 7, 3), (f4, 7, 2)]
+    none = jnp.uint32(0)
     for part, j, step in pieces:
         at = j * NX + step
         first = lax.squeeze(lax.slice(offsets, (at,), (at + 1,)), (0,))
-        full = lax.dynamic_update_slice(full, part, (first, jnp.uint32(0)))
+        full = lax.dynamic_update_slice(full, part[None], (first, none, none))
+    full = full.reshape(NZ * NX * rows, width)
 
     n_tok = tokens.shape[0]
     ff = gate_weight.shape[1]

time: 346 us -> 232 us (0.67)
  the two profiles are of different devices: /device:TPU:102 before, /device:TPU:384 now
where the time goes in v9:
time: 232 us; the launch traced here: 230 us
  starting transfers between devices  101 us (44%)
  waiting for transfers between devices  70.3 us (30%)
  local copies, waits for them, and re-layouts  37.2 us (16%)
  other arithmetic  13.2 us (6%)
  matrix products  6.51 us (3%)
    ppermute x24, starting transfers between devices, shift(): return lambda v: lax.ppermute(v, axis, pairs)  87.9 us
    ppermute x24, waiting for transfers between devices, shift(): return lambda v: lax.ppermute(v, axis, pairs)  57.5 us
    dynamic_update_slice x31, local copies, waits for them, and re-layouts, body(): full = lax.dynamic_update_slice(full, part[None], (first, none, none))  29.8 us
    all_to_all x1, waiting for transfers between devices, body(): shares = lax.all_to_all(sums.astype(BF), 'y', 0, 0, tiled=True).astype(F32)  12.8 us
    ppermute x2, starting transfers between devices, flip(): return lambda v: lax.ppermute(v, axis, [(i, i ^ bit) for i in range(n)])  9.58 us
  transfers between devices with their start and end apart: 27, of which 9 were waited for; matrix products, arithmetic and copies ran while one was open for 20% of the time, Pallas kernels for 0%

profile of v9, /device:TPU:384, one launch (start us, length us, event | category | flops | bytes accessed | tf_op | source)
XLA Modules:
  0.0 229.8 jit_solution(17359815532620071232)
XLA Ops:
  1.0 3.4 %collective-permute-start = (bf16[96,1536]{1,0:T(8,128)(2,1)S(1)}, bf16[96,1536]{1,0:T(8,128)(2,1)S(1)}, u32[]{:S(2)}, u32[]{:S(2)}) collective-permute-start(bf16[96,1536]{1,0:T(8,128)(2,1)S(1)} %pad_maximum_fusion.10), channel_id=1, source_target_pairs={{0,128},{128,256},{256,384},{384,448},{448,320},{320,192},{192,64}... | collective-permute-start | bytes 884744 | tf_op jit(solution)/shard_map/ppermute | solution.py:26
  4.4 4.6 %collective-permute-start.3 = (bf16[96,1536]{1,0:T(8,128)(2,1)S(1)}, bf16[96,1536]{1,0:T(8,128)(2,1)S(1)}, u32[]{:S(2)}, u32[]{:S(2)}) collective-permute-start(bf16[96,1536]{1,0:T(8,128)(2,1)S(1)} %pad_maximum_fusion.10), channel_id=1, source_target_pairs={{0,64},{128,0},{256,128},{384,256},{448,384},{320,448},{192,320},{... | collective-permute-start | bytes 884744 | tf_op jit(solution)/shard_map/ppermute | solution.py:26
  9.0 3.4 %collective-permute-start.1 = (bf16[96,1536]{1,0:T(8,128)(2,1)S(1)}, bf16[96,1536]{1,0:T(8,128)(2,1)S(1)}, u32[]{:S(2)}, u32[]{:S(2)}) collective-permute-start(bf16[96,1536]{1,0:T(8,128)(2,1)S(1)} %pad_maximum_fusion.10), channel_id=1, source_target_pairs={{0,16},{16,32},{32,48},{48,0},{1,17},{17,33},{33,49},{49,1},{2,18}... | collective-permute-start | bytes 884744 | tf_op jit(solution)/shard_map/ppermute | solution.py:26
  12.4 3.7 %collective-permute-start.4 = (bf16[96,1536]{1,0:T(8,128)(2,1)S(1)}, bf16[96,1536]{1,0:T(8,128)(2,1)S(1)}, u32[]{:S(2)}, u32[]{:S(2)}) collective-permute-start(bf16[96,1536]{1,0:T(8,128)(2,1)S(1)} %pad_maximum_fusion.10), channel_id=1, source_target_pairs={{0,48},{16,0},{32,16},{48,32},{1,49},{17,1},{33,17},{49,33},{2,50}... | collective-permute-start | bytes 884744 | tf_op jit(solution)/shard_map/ppermute | solution.py:26
  16.1 3.3 %collective-permute-done.3 = bf16[96,1536]{1,0:T(8,128)(2,1)S(1)} collective-permute-done((bf16[96,1536]{1,0:T(8,128)(2,1)S(1)}, bf16[96,1536]{1,0:T(8,128)(2,1)S(1)}, u32[]{:S(2)}, u32[]{:S(2)}) %collective-permute-start.3) | collective-permute-done | bytes 294944 | tf_op jit(solution)/shard_map/ppermute | solution.py:26
  20.3 2.6 %collective-permute-start.10 = (bf16[192,1536]{1,0:T(8,128)(2,1)S(1)}, bf16[192,1536]{1,0:T(8,128)(2,1)S(1)}, u32[]{:S(2)}, u32[]{:S(2)}) collective-permute-start(bf16[192,1536]{1,0:T(8,128)(2,1)S(1)} %constant_dynamic-update-slice_fusion), channel_id=1, source_target_pairs={{0,16},{16,32},{32,48},{48,0},{1,17},{17,33},{33,49},{49,1},{2,18}... | collective-permute-start | bytes 1769480 | tf_op jit(solution)/shard_map/ppermute | solution.py:26
  22.9 4.4 %collective-permute-start.6 = (bf16[192,1536]{1,0:T(8,128)(2,1)S(1)}, bf16[192,1536]{1,0:T(8,128)(2,1)S(1)}, u32[]{:S(2)}, u32[]{:S(2)}) collective-permute-start(bf16[192,1536]{1,0:T(8,128)(2,1)S(1)} %constant_dynamic-update-slice_fusion), channel_id=1, source_target_pairs={{0,48},{16,0},{32,16},{48,32},{1,49},{17,1},{33,17},{49,33},{2,50}... | collective-permute-start | bytes 1769480 | tf_op jit(solution)/shard_map/ppermute | solution.py:26
  27.4 2.2 collective-permute-start.2
  29.5 5.8 %collective-permute-start.5 = (bf16[96,1536]{1,0:T(8,128)(2,1)S(1)}, bf16[96,1536]{1,0:T(8,128)(2,1)S(1)}, u32[]{:S(2)}, u32[]{:S(2)}) collective-permute-start(bf16[96,1536]{1,0:T(8,128)(2,1)S(1)} %collective-permute-done.3), channel_id=1, source_target_pairs={{0,64},{128,0},{256,128},{384,256},{448,384},{320,448},{192,320},{... | collective-permute-start | bytes 884744 | tf_op jit(solution)/shard_map/ppermute | solution.py:26
  35.3 1.7 pad_maximum_fusion.11
  37.1 4.3 %collective-permute-start.20 = (bf16[192,768]{1,0:T(8,128)(2,1)}, bf16[192,768]{1,0:T(8,128)(2,1)}, u32[]{:S(2)}, u32[]{:S(2)}) collective-permute-start(bf16[192,768]{1,0:T(8,128)(2,1)} %pad_maximum_fusion.11), channel_id=1, source_target_pairs={{0,8},{8,0},{1,9},{9,1},{2,10},{10,2},{3,11},{11,3},{4,12},{12,4},... | collective-permute-start | bytes 884744 | tf_op jit(solution)/shard_map/ppermute | solution.py:26
  42.2 2.1 collective-permute-start.8
  44.3 7.4 %collective-permute-done.5 = bf16[96,1536]{1,0:T(8,128)(2,1)S(1)} collective-permute-done((bf16[96,1536]{1,0:T(8,128)(2,1)S(1)}, bf16[96,1536]{1,0:T(8,128)(2,1)S(1)}, u32[]{:S(2)}, u32[]{:S(2)}) %collective-permute-start.5) | collective-permute-done | bytes 294944 | tf_op jit(solution)/shard_map/ppermute | solution.py:26
  51.7 4.1 %collective-permute-start.12 = (bf16[96,1536]{1,0:T(8,128)(2,1)S(1)}, bf16[96,1536]{1,0:T(8,128)(2,1)}, u32[]{:S(2)}, u32[]{:S(2)}) collective-permute-start(bf16[96,1536]{1,0:T(8,128)(2,1)S(1)} %collective-permute-done.5), channel_id=1, source_target_pairs={{0,64},{128,0},{256,128},{384,256},{448,384},{320,448},{192,320},{... | collective-permute-start | bytes 884744 | tf_op jit(solution)/shard_map/ppermute | solution.py:26
  57.3 5.5 %collective-permute-start.7 = (bf16[288,1536]{1,0:T(8,128)(2,1)}, bf16[288,1536]{1,0:T(8,128)(2,1)S(1)}, u32[]{:S(2)}, u32[]{:S(2)}) collective-permute-start(bf16[288,1536]{1,0:T(8,128)(2,1)} %get-tuple-element.46), channel_id=1, source_target_pairs={{0,48},{16,0},{32,16},{48,32},{1,49},{17,1},{33,17},{49,33},{2,50}... | collective-permute-start | bytes 2654216 | tf_op jit(solution)/shard_map/ppermute | solution.py:26
  62.7 1.9 collective-permute-start.11
  65.4 13.9 %collective-permute-done.8 = bf16[96,1536]{1,0:T(8,128)(2,1)} collective-permute-done((bf16[96,1536]{1,0:T(8,128)(2,1)S(1)}, bf16[96,1536]{1,0:T(8,128)(2,1)}, u32[]{:S(2)}, u32[]{:S(2)}) %collective-permute-start.8) | collective-permute-done | bytes 294944 | tf_op jit(solution)/shard_map/ppermute | solution.py:26
  79.2 13.9 %collective-permute-start.9 = (bf16[96,1536]{1,0:T(8,128)(2,1)}, bf16[96,1536]{1,0:T(8,128)(2,1)S(1)}, u32[]{:S(2)}, u32[]{:S(2)}) collective-permute-start(bf16[96,1536]{1,0:T(8,128)(2,1)} %copy-done.7), channel_id=1, source_target_pairs={{0,32},{16,48},{32,0},{48,16},{1,33},{17,49},{33,1},{49,17},{2,34}... | collective-permute-start | bytes 884744 | tf_op jit(solution)/shard_map/ppermute | solution.py:26
  94.5 3.6 %collective-permute-start.21 = (bf16[384,768]{1,0:T(8,128)(2,1)S(1)}, bf16[384,768]{1,0:T(8,128)(2,1)S(1)}, u32[]{:S(2)}, u32[]{:S(2)}) collective-permute-start(bf16[384,768]{1,0:T(8,128)(2,1)S(1)} %pad_maximum_fusion.9), channel_id=1, source_target_pairs={{0,2},{2,0},{4,6},{6,4},{1,3},{3,1},{5,7},{7,5},{8,10},{10,8},{12,... | collective-permute-start | bytes 1769480 | tf_op jit(solution)/shard_map/ppermute | solution.py:34
  98.1 1.9 collective-permute-start.16
  100.0 1.7 constant_dynamic-update-slice_fusion.3
  101.7 1.7 constant_dynamic-update-slice_fusion.2
  103.4 12.6 %collective-permute-done.9 = bf16[96,1536]{1,0:T(8,128)(2,1)S(1)} collective-permute-done((bf16[96,1536]{1,0:T(8,128)(2,1)}, bf16[96,1536]{1,0:T(8,128)(2,1)S(1)}, u32[]{:S(2)}, u32[]{:S(2)}) %collective-permute-start.9) | collective-permute-done | bytes 294944 | tf_op jit(solution)/shard_map/ppermute | solution.py:26
  116.0 1.9 collective-permute-start.15
  117.9 2.3 %collective-permute-start.13 = (bf16[192,1536]{1,0:T(8,128)(2,1)}, bf16[192,1536]{1,0:T(8,128)(2,1)}, u32[]{:S(2)}, u32[]{:S(2)}) collective-permute-start(bf16[192,1536]{1,0:T(8,128)(2,1)} %constant_dynamic-update-slice_fusion.2), channel_id=1, source_target_pairs={{0,48},{16,0},{32,16},{48,32},{1,49},{17,1},{33,17},{49,33},{2,50}... | collective-permute-start | bytes 1769480 | tf_op jit(solution)/shard_map/ppermute | solution.py:26
  120.3 3.5 %collective-permute-start.14 = (bf16[192,1536]{1,0:T(8,128)(2,1)}, bf16[192,1536]{1,0:T(8,128)(2,1)}, u32[]{:S(2)}, u32[]{:S(2)}) collective-permute-start(bf16[192,1536]{1,0:T(8,128)(2,1)} %constant_dynamic-update-slice_fusion.2), channel_id=1, source_target_pairs={{0,16},{16,32},{32,48},{48,0},{1,17},{17,33},{33,49},{49,1},{2,18}... | collective-permute-start | bytes 1769480 | tf_op jit(solution)/shard_map/ppermute | solution.py:26
  125.0 4.0 %collective-permute-start.18 = (bf16[192,1536]{1,0:T(8,128)(2,1)}, bf16[192,1536]{1,0:T(8,128)(2,1)S(1)}, u32[]{:S(2)}, u32[]{:S(2)}) collective-permute-start(bf16[192,1536]{1,0:T(8,128)(2,1)} %get-tuple-element.47), channel_id=1, source_target_pairs={{0,48},{16,0},{32,16},{48,32},{1,49},{17,1},{33,17},{49,33},{2,50}... | collective-permute-start | bytes 1769480 | tf_op jit(solution)/shard_map/ppermute | solution.py:26
  131.4 6.0 %collective-permute-start.22 = (bf16[768,768]{1,0:T(8,128)(2,1)S(1)}, bf16[768,768]{1,0:T(8,128)(2,1)S(1)}, u32[]{:S(2)}, u32[]{:S(2)}) collective-permute-start(bf16[768,768]{1,0:T(8,128)(2,1)S(1)} %pad_maximum_fusion.3), channel_id=1, source_target_pairs={{0,4},{2,6},{4,0},{6,2},{1,5},{3,7},{5,1},{7,3},{8,12},{10,14},{12... | collective-permute-start | bytes 3538952 | tf_op jit(solution)/shard_map/ppermute | solution.py:34
  141.1 1.7 bitcast_dynamic-update-slice_fusion.14
  143.5 1.6 bitcast_dynamic-update-slice_fusion.12
  153.0 1.6 bitcast_dynamic-update-slice_fusion.3
  154.6 1.6 bitcast_dynamic-update-slice_fusion.2
  156.3 2.7 %collective-permute-start.17 = (bf16[192,1536]{1,0:T(8,128)(2,1)S(1)}, bf16[192,1536]{1,0:T(8,128)(2,1)S(1)}, u32[]{:S(2)}, u32[]{:S(2)}) collective-permute-start(bf16[192,1536]{1,0:T(8,128)(2,1)S(1)} %copy-done.4), channel_id=1, source_target_pairs={{0,16},{16,32},{32,48},{48,0},{1,17},{17,33},{33,49},{49,1},{2,18}... | collective-permute-start | bytes 1769480 | tf_op jit(solution)/shard_map/ppermute | solution.py:26
  159.0 3.8 %collective-permute-start.19 = (bf16[96,1536]{1,0:T(8,128)(2,1)S(1)}, bf16[96,1536]{1,0:T(8,128)(2,1)S(1)}, u32[]{:S(2)}, u32[]{:S(2)}) collective-permute-start(bf16[96,1536]{1,0:T(8,128)(2,1)S(1)} %collective-permute-done.16), channel_id=1, source_target_pairs={{0,32},{16,48},{32,0},{48,16},{1,33},{17,49},{33,1},{49,17},{2,34}... | collective-permute-start | bytes 884744 | tf_op jit(solution)/shard_map/ppermute | solution.py:26
  164.4 1.7 fusion.37
  166.1 1.6 fusion.36
  167.7 1.6 fusion.35
  170.6 1.6 fusion.32
  174.5 2.1 collective-permute-start.23
  176.6 1.7 collective-permute-done.17
  183.2 3.4 %fusion.2 = f32[512,1024]{1,0:T(8,128)S(1)} fusion(bf16[3072,1536]{1,0:T(8,128)(2,1)S(1)} %bitcast.151, bf16[1536,768]{1,0:T(8,128)(2,1)S(1)} %get-tuple-element.36, bf16[1536,768]{1,0:T(8,128)(2,1)S(1)} %get-tuple-element.35), kind=kOutput, calls=%fused_computation.2 | convolution fusion | flops 3227516928 | bytes 13107200 | tf_op jit(solution)/shard_map/dot_general | solution.py:107
  187.9 1.8 fusion
  189.9 1.9 collective-permute-start.24
  191.9 3.4 %collective-permute-done.24 = f32[4,2,192,256]{3,2,1,0:T(8,128)S(1)} collective-permute-done((f32[4,2,192,256]{3,2,1,0:T(8,128)S(1)}, f32[4,2,192,256]{3,2,1,0:T(8,128)S(1)}, u32[]{:S(2)}, u32[]{:S(2)}) %collective-permute-start.24) | collective-permute-done | bytes 1572896 | tf_op jit(solution)/shard_map/ppermute | solution.py:26
  196.4 3.5 %all-to-all-start = ((bf16[4,2,192,256]{3,2,1,0:T(8,128)(2,1)}), bf16[4,2,192,256]{3,2,1,0:T(8,128)(2,1)S(1)}, u32[]{:S(2)}, u32[]{:S(2)}) async-start(bf16[4,2,192,256]{3,2,1,0:T(8,128)(2,1)} %fusion.10), calls=%async_computation | async-start | bytes 1572864 | tf_op jit(solution)/shard_map/all_to_all | solution.py:129
  199.9 12.8 %all-to-all-done = bf16[4,2,192,256]{3,2,1,0:T(8,128)(2,1)S(1)} async-done(((bf16[4,2,192,256]{3,2,1,0:T(8,128)(2,1)}), bf16[4,2,192,256]{3,2,1,0:T(8,128)(2,1)S(1)}, u32[]{:S(2)}, u32[]{:S(2)}) %all-to-all-start) | async-done | bytes 786464 | tf_op jit(solution)/shard_map/all_to_all | solution.py:129
  212.9 1.9 collective-permute-start.25
  214.8 14.3 %collective-permute-done.25 = bf16[192,256]{1,0:T(8,128)(2,1)S(1)} collective-permute-done((bf16[192,256]{1,0:T(8,128)(2,1)S(1)}, bf16[192,256]{1,0:T(8,128)(2,1)S(1)}, u32[]{:S(2)}, u32[]{:S(2)}) %collective-permute-start.25) | collective-permute-done | bytes 98336 | tf_op jit(solution)/shard_map/ppermute | solution.py:26
  (96 shorter events, 34.5 us)
Async XLA Ops:
  1.0 54.8 %copy-start.7 = (bf16[96,1536]{1,0:T(8,128)(2,1)}, bf16[96,1536]{1,0:T(8,128)(2,1)S(1)}, u32[]{:S(2)}) copy-start(bf16[96,1536]{1,0:T(8,128)(2,1)S(1)} %pad_maximum_fusion.10) | copy-start | bytes 884740
  1.0 15.0 %collective-permute-start = (bf16[96,1536]{1,0:T(8,128)(2,1)S(1)}, bf16[96,1536]{1,0:T(8,128)(2,1)S(1)}, u32[]{:S(2)}, u32[]{:S(2)}) collective-permute-start(bf16[96,1536]{1,0:T(8,128)(2,1)S(1)} %pad_maximum_fusion.10), channel_id=1, source_target_pairs={{0,128},{128,256},{256,384},{384,448},{448,320},{320,192},{192,64}... | collective-permute-start | bytes 884744 | tf_op jit(solution)/shard_map/ppermute | solution.py:26
  4.4 15.0 %collective-permute-start.3 = (bf16[96,1536]{1,0:T(8,128)(2,1)S(1)}, bf16[96,1536]{1,0:T(8,128)(2,1)S(1)}, u32[]{:S(2)}, u32[]{:S(2)}) collective-permute-start(bf16[96,1536]{1,0:T(8,128)(2,1)S(1)} %pad_maximum_fusion.10), channel_id=1, source_target_pairs={{0,64},{128,0},{256,128},{384,256},{448,384},{320,448},{192,320},{... | collective-permute-start | bytes 884744 | tf_op jit(solution)/shard_map/ppermute | solution.py:26
  9.0 11.3 %collective-permute-start.1 = (bf16[96,1536]{1,0:T(8,128)(2,1)S(1)}, bf16[96,1536]{1,0:T(8,128)(2,1)S(1)}, u32[]{:S(2)}, u32[]{:S(2)}) collective-permute-start(bf16[96,1536]{1,0:T(8,128)(2,1)S(1)} %pad_maximum_fusion.10), channel_id=1, source_target_pairs={{0,16},{16,32},{32,48},{48,0},{1,17},{17,33},{33,49},{49,1},{2,18}... | collective-permute-start | bytes 884744 | tf_op jit(solution)/shard_map/ppermute | solution.py:26
  12.4 10.5 %collective-permute-start.4 = (bf16[96,1536]{1,0:T(8,128)(2,1)S(1)}, bf16[96,1536]{1,0:T(8,128)(2,1)S(1)}, u32[]{:S(2)}, u32[]{:S(2)}) collective-permute-start(bf16[96,1536]{1,0:T(8,128)(2,1)S(1)} %pad_maximum_fusion.10), channel_id=1, source_target_pairs={{0,48},{16,0},{32,16},{48,32},{1,49},{17,1},{33,17},{49,33},{2,50}... | collective-permute-start | bytes 884744 | tf_op jit(solution)/shard_map/ppermute | solution.py:26
  16.1 39.8 %copy-start = (bf16[96,1536]{1,0:T(8,128)(2,1)}, bf16[96,1536]{1,0:T(8,128)(2,1)S(1)}, u32[]{:S(2)}) copy-start(bf16[96,1536]{1,0:T(8,128)(2,1)S(1)} %collective-permute-done) | copy-start | bytes 884740
  19.4 36.4 %copy-start.2 = (bf16[96,1536]{1,0:T(8,128)(2,1)}, bf16[96,1536]{1,0:T(8,128)(2,1)S(1)}, u32[]{:S(2)}) copy-start(bf16[96,1536]{1,0:T(8,128)(2,1)S(1)} %collective-permute-done.3) | copy-start | bytes 884740
  20.3 35.6 %copy-start.8 = (bf16[96,1536]{1,0:T(8,128)(2,1)}, bf16[96,1536]{1,0:T(8,128)(2,1)S(1)}, u32[]{:S(2)}) copy-start(bf16[96,1536]{1,0:T(8,128)(2,1)S(1)} %collective-permute-done.1) | copy-start | bytes 884740
  20.3 35.5 %collective-permute-start.10 = (bf16[192,1536]{1,0:T(8,128)(2,1)S(1)}, bf16[192,1536]{1,0:T(8,128)(2,1)S(1)}, u32[]{:S(2)}, u32[]{:S(2)}) collective-permute-start(bf16[192,1536]{1,0:T(8,128)(2,1)S(1)} %constant_dynamic-update-slice_fusion), channel_id=1, source_target_pairs={{0,16},{16,32},{32,48},{48,0},{1,17},{17,33},{33,49},{49,1},{2,18}... | collective-permute-start | bytes 1769480 | tf_op jit(solution)/shard_map/ppermute | solution.py:26
  22.9 33.0 %copy-start.9 = (bf16[96,1536]{1,0:T(8,128)(2,1)}, bf16[96,1536]{1,0:T(8,128)(2,1)S(1)}, u32[]{:S(2)}) copy-start(bf16[96,1536]{1,0:T(8,128)(2,1)S(1)} %collective-permute-done.4) | copy-start | bytes 884740
  22.9 32.9 %collective-permute-start.6 = (bf16[192,1536]{1,0:T(8,128)(2,1)S(1)}, bf16[192,1536]{1,0:T(8,128)(2,1)S(1)}, u32[]{:S(2)}, u32[]{:S(2)}) collective-permute-start(bf16[192,1536]{1,0:T(8,128)(2,1)S(1)} %constant_dynamic-update-slice_fusion), channel_id=1, source_target_pairs={{0,48},{16,0},{32,16},{48,32},{1,49},{17,1},{33,17},{49,33},{2,50}... | collective-permute-start | bytes 1769480 | tf_op jit(solution)/shard_map/ppermute | solution.py:26
  27.4 14.8 %collective-permute-start.2 = (bf16[96,1536]{1,0:T(8,128)(2,1)S(1)}, bf16[96,1536]{1,0:T(8,128)(2,1)S(1)}, u32[]{:S(2)}, u32[]{:S(2)}) collective-permute-start(bf16[96,1536]{1,0:T(8,128)(2,1)S(1)} %collective-permute-done), channel_id=1, source_target_pairs={{0,128},{128,256},{256,384},{384,448},{448,320},{320,192},{192,64}... | collective-permute-start | bytes 884744 | tf_op jit(solution)/shard_map/ppermute | solution.py:26
  29.5 22.2 %collective-permute-start.5 = (bf16[96,1536]{1,0:T(8,128)(2,1)S(1)}, bf16[96,1536]{1,0:T(8,128)(2,1)S(1)}, u32[]{:S(2)}, u32[]{:S(2)}) collective-permute-start(bf16[96,1536]{1,0:T(8,128)(2,1)S(1)} %collective-permute-done.3), channel_id=1, source_target_pairs={{0,64},{128,0},{256,128},{384,256},{448,384},{320,448},{192,320},{... | collective-permute-start | bytes 884744 | tf_op jit(solution)/shard_map/ppermute | solution.py:26
  37.1 56.1 %collective-permute-start.20 = (bf16[192,768]{1,0:T(8,128)(2,1)}, bf16[192,768]{1,0:T(8,128)(2,1)}, u32[]{:S(2)}, u32[]{:S(2)}) collective-permute-start(bf16[192,768]{1,0:T(8,128)(2,1)} %pad_maximum_fusion.11), channel_id=1, source_target_pairs={{0,8},{8,0},{1,9},{9,1},{2,10},{10,2},{3,11},{11,3},{4,12},{12,4},... | collective-permute-start | bytes 884744 | tf_op jit(solution)/shard_map/ppermute | solution.py:26
  42.2 37.1 %collective-permute-start.8 = (bf16[96,1536]{1,0:T(8,128)(2,1)S(1)}, bf16[96,1536]{1,0:T(8,128)(2,1)}, u32[]{:S(2)}, u32[]{:S(2)}) collective-permute-start(bf16[96,1536]{1,0:T(8,128)(2,1)S(1)} %collective-permute-done.2), channel_id=1, source_target_pairs={{0,128},{128,256},{256,384},{384,448},{448,320},{320,192},{192,64}... | collective-permute-start | bytes 884744 | tf_op jit(solution)/shard_map/ppermute | solution.py:26
  51.7 41.5 %collective-permute-start.12 = (bf16[96,1536]{1,0:T(8,128)(2,1)S(1)}, bf16[96,1536]{1,0:T(8,128)(2,1)}, u32[]{:S(2)}, u32[]{:S(2)}) collective-permute-start(bf16[96,1536]{1,0:T(8,128)(2,1)S(1)} %collective-permute-done.5), channel_id=1, source_target_pairs={{0,64},{128,0},{256,128},{384,256},{448,384},{320,448},{192,320},{... | collective-permute-start | bytes 884744 | tf_op jit(solution)/shard_map/ppermute | solution.py:26
  57.3 60.6 %collective-permute-start.7 = (bf16[288,1536]{1,0:T(8,128)(2,1)}, bf16[288,1536]{1,0:T(8,128)(2,1)S(1)}, u32[]{:S(2)}, u32[]{:S(2)}) collective-permute-start(bf16[288,1536]{1,0:T(8,128)(2,1)} %get-tuple-element.46), channel_id=1, source_target_pairs={{0,48},{16,0},{32,16},{48,32},{1,49},{17,1},{33,17},{49,33},{2,50}... | collective-permute-start | bytes 2654216 | tf_op jit(solution)/shard_map/ppermute | solution.py:26
  62.7 57.5 %collective-permute-start.11 = (bf16[288,1536]{1,0:T(8,128)(2,1)}, bf16[288,1536]{1,0:T(8,128)(2,1)S(1)}, u32[]{:S(2)}, u32[]{:S(2)}) collective-permute-start(bf16[288,1536]{1,0:T(8,128)(2,1)} %get-tuple-element.45), channel_id=1, source_target_pairs={{0,16},{16,32},{32,48},{48,0},{1,17},{17,33},{33,49},{49,1},{2,18}... | collective-permute-start | bytes 2654216 | tf_op jit(solution)/shard_map/ppermute | solution.py:26
  79.2 36.7 %collective-permute-start.9 = (bf16[96,1536]{1,0:T(8,128)(2,1)}, bf16[96,1536]{1,0:T(8,128)(2,1)S(1)}, u32[]{:S(2)}, u32[]{:S(2)}) collective-permute-start(bf16[96,1536]{1,0:T(8,128)(2,1)} %copy-done.7), channel_id=1, source_target_pairs={{0,32},{16,48},{32,0},{48,16},{1,33},{17,49},{33,1},{49,17},{2,34}... | collective-permute-start | bytes 884744 | tf_op jit(solution)/shard_map/ppermute | solution.py:26
  94.4 45.2 %copy-start.5 = (bf16[512,96]{0,1:T(8,128)(2,1)S(1)}, bf16[512,96]{0,1:T(8,128)(2,1)}, u32[]{:S(2)}) copy-start(bf16[512,96]{0,1:T(8,128)(2,1)} %param.16) | copy-start | bytes 294916
  94.4 45.2 %copy-start.6 = (bf16[96,512]{1,0:T(8,128)(2,1)S(1)}, bf16[96,512]{1,0:T(8,128)(2,1)}, u32[]{:S(2)}) copy-start(bf16[96,512]{1,0:T(8,128)(2,1)} %param.15) | copy-start | bytes 294916
  94.5 36.6 %collective-permute-start.21 = (bf16[384,768]{1,0:T(8,128)(2,1)S(1)}, bf16[384,768]{1,0:T(8,128)(2,1)S(1)}, u32[]{:S(2)}, u32[]{:S(2)}) collective-permute-start(bf16[384,768]{1,0:T(8,128)(2,1)S(1)} %pad_maximum_fusion.9), channel_id=1, source_target_pairs={{0,2},{2,0},{4,6},{6,4},{1,3},{3,1},{5,7},{7,5},{8,10},{10,8},{12,... | collective-permute-start | bytes 1769480 | tf_op jit(solution)/shard_map/ppermute | solution.py:34
  98.1 25.8 %collective-permute-start.16 = (bf16[96,1536]{1,0:T(8,128)(2,1)}, bf16[96,1536]{1,0:T(8,128)(2,1)S(1)}, u32[]{:S(2)}, u32[]{:S(2)}) collective-permute-start(bf16[96,1536]{1,0:T(8,128)(2,1)} %collective-permute-done.8), channel_id=1, source_target_pairs={{0,128},{128,256},{256,384},{384,448},{448,320},{320,192},{192,64}... | collective-permute-start | bytes 884744 | tf_op jit(solution)/shard_map/ppermute | solution.py:26
  116.0 4.3 %copy-start.10 = (bf16[96,1536]{1,0:T(8,128)(2,1)}, bf16[96,1536]{1,0:T(8,128)(2,1)S(1)}, u32[]{:S(2)}) copy-start(bf16[96,1536]{1,0:T(8,128)(2,1)S(1)} %collective-permute-done.9) | copy-start | bytes 884740
  116.0 54.7 %collective-permute-start.15 = (bf16[192,1536]{1,0:T(8,128)(2,1)}, bf16[192,1536]{1,0:T(8,128)(2,1)}, u32[]{:S(2)}, u32[]{:S(2)}) collective-permute-start(bf16[192,1536]{1,0:T(8,128)(2,1)} %constant_dynamic-update-slice_fusion.2), channel_id=1, source_target_pairs={{0,32},{16,48},{32,0},{48,16},{1,33},{17,49},{33,1},{49,17},{2,34}... | collective-permute-start | bytes 1769480 | tf_op jit(solution)/shard_map/ppermute | solution.py:26
  117.9 38.4 %collective-permute-start.13 = (bf16[192,1536]{1,0:T(8,128)(2,1)}, bf16[192,1536]{1,0:T(8,128)(2,1)}, u32[]{:S(2)}, u32[]{:S(2)}) collective-permute-start(bf16[192,1536]{1,0:T(8,128)(2,1)} %constant_dynamic-update-slice_fusion.2), channel_id=1, source_target_pairs={{0,48},{16,0},{32,16},{48,32},{1,49},{17,1},{33,17},{49,33},{2,50}... | collective-permute-start | bytes 1769480 | tf_op jit(solution)/shard_map/ppermute | solution.py:26
  120.3 38.7 %collective-permute-start.14 = (bf16[192,1536]{1,0:T(8,128)(2,1)}, bf16[192,1536]{1,0:T(8,128)(2,1)}, u32[]{:S(2)}, u32[]{:S(2)}) collective-permute-start(bf16[192,1536]{1,0:T(8,128)(2,1)} %constant_dynamic-update-slice_fusion.2), channel_id=1, source_target_pairs={{0,16},{16,32},{32,48},{48,0},{1,17},{17,33},{33,49},{49,1},{2,18}... | collective-permute-start | bytes 1769480 | tf_op jit(solution)/shard_map/ppermute | solution.py:26
  123.8 21.2 %copy-start.1 = (bf16[96,1536]{1,0:T(8,128)(2,1)S(1)}, bf16[96,1536]{1,0:T(8,128)(2,1)}, u32[]{:S(2)}) copy-start(bf16[96,1536]{1,0:T(8,128)(2,1)} %copy-done) | copy-start | bytes 884740
  123.9 21.9 %copy-start.3 = (bf16[96,1536]{1,0:T(8,128)(2,1)S(1)}, bf16[96,1536]{1,0:T(8,128)(2,1)}, u32[]{:S(2)}) copy-start(bf16[96,1536]{1,0:T(8,128)(2,1)} %copy-done.2) | copy-start | bytes 884740
  125.0 53.9 %collective-permute-start.18 = (bf16[192,1536]{1,0:T(8,128)(2,1)}, bf16[192,1536]{1,0:T(8,128)(2,1)S(1)}, u32[]{:S(2)}, u32[]{:S(2)}) collective-permute-start(bf16[192,1536]{1,0:T(8,128)(2,1)} %get-tuple-element.47), channel_id=1, source_target_pairs={{0,48},{16,0},{32,16},{48,32},{1,49},{17,1},{33,17},{49,33},{2,50}... | collective-permute-start | bytes 1769480 | tf_op jit(solution)/shard_map/ppermute | solution.py:26
  131.3 11.5 %copy-start.11 = (bf16[96,1536]{1,0:T(8,128)(2,1)S(1)}, bf16[96,1536]{1,0:T(8,128)(2,1)}, u32[]{:S(2)}) copy-start(bf16[96,1536]{1,0:T(8,128)(2,1)} %copy-done.10) | copy-start | bytes 884740
  131.4 42.4 %collective-permute-start.22 = (bf16[768,768]{1,0:T(8,128)(2,1)S(1)}, bf16[768,768]{1,0:T(8,128)(2,1)S(1)}, u32[]{:S(2)}, u32[]{:S(2)}) collective-permute-start(bf16[768,768]{1,0:T(8,128)(2,1)S(1)} %pad_maximum_fusion.3), channel_id=1, source_target_pairs={{0,4},{2,6},{4,0},{6,2},{1,5},{3,7},{5,1},{7,3},{8,12},{10,14},{12... | collective-permute-start | bytes 3538952 | tf_op jit(solution)/shard_map/ppermute | solution.py:34
  138.6 17.7 %copy-start.4 = (bf16[192,1536]{1,0:T(8,128)(2,1)S(1)}, bf16[192,1536]{1,0:T(8,128)(2,1)}, u32[]{:S(2)}) copy-start(bf16[192,1536]{1,0:T(8,128)(2,1)} %get-tuple-element.30) | copy-start | bytes 1769476
  156.3 22.0 %collective-permute-start.17 = (bf16[192,1536]{1,0:T(8,128)(2,1)S(1)}, bf16[192,1536]{1,0:T(8,128)(2,1)S(1)}, u32[]{:S(2)}, u32[]{:S(2)}) collective-permute-start(bf16[192,1536]{1,0:T(8,128)(2,1)S(1)} %copy-done.4), channel_id=1, source_target_pairs={{0,16},{16,32},{32,48},{48,0},{1,17},{17,33},{33,49},{49,1},{2,18}... | collective-permute-start | bytes 1769480 | tf_op jit(solution)/shard_map/ppermute | solution.py:26
  159.0 22.5 %collective-permute-start.19 = (bf16[96,1536]{1,0:T(8,128)(2,1)S(1)}, bf16[96,1536]{1,0:T(8,128)(2,1)S(1)}, u32[]{:S(2)}, u32[]{:S(2)}) collective-permute-start(bf16[96,1536]{1,0:T(8,128)(2,1)S(1)} %collective-permute-done.16), channel_id=1, source_target_pairs={{0,32},{16,48},{32,0},{48,16},{1,33},{17,49},{33,1},{49,17},{2,34}... | collective-permute-start | bytes 884744 | tf_op jit(solution)/shard_map/ppermute | solution.py:26
  174.5 7.8 %collective-permute-start.23 = (bf16[1536,768]{1,0:T(8,128)(2,1)S(1)}, bf16[1536,768]{1,0:T(8,128)(2,1)S(1)}, u32[]{:S(2)}, u32[]{:S(2)}) collective-permute-start(bf16[1536,768]{1,0:T(8,128)(2,1)S(1)} %pad_maximum_fusion.2), channel_id=1, source_target_pairs={{0,1},{1,0},{2,3},{3,2},{4,5},{5,4},{6,7},{7,6},{8,9},{9,8},{10,11... | collective-permute-start | bytes 7077896 | tf_op jit(solution)/shard_map/ppermute | solution.py:26
  189.9 5.3 %collective-permute-start.24 = (f32[4,2,192,256]{3,2,1,0:T(8,128)S(1)}, f32[4,2,192,256]{3,2,1,0:T(8,128)S(1)}, u32[]{:S(2)}, u32[]{:S(2)}) collective-permute-start(f32[4,2,192,256]{3,2,1,0:T(8,128)S(1)} %dynamic-slice_bitcast_fusion), channel_id=1, source_target_pairs={{0,1},{1,0},{2,3},{3,2},{4,5},{5,4},{6,7},{7,6},{8,9},{9,8},{10,11... | collective-permute-start | bytes 4718600 | tf_op jit(solution)/shard_map/ppermute | solution.py:26
  196.4 16.3 %all-to-all-start = ((bf16[4,2,192,256]{3,2,1,0:T(8,128)(2,1)}), bf16[4,2,192,256]{3,2,1,0:T(8,128)(2,1)S(1)}, u32[]{:S(2)}, u32[]{:S(2)}) async-start(bf16[4,2,192,256]{3,2,1,0:T(8,128)(2,1)} %fusion.10), calls=%async_computation | async-start | bytes 1572864 | tf_op jit(solution)/shard_map/all_to_all | solution.py:129
  212.9 16.3 %collective-permute-start.25 = (bf16[192,256]{1,0:T(8,128)(2,1)S(1)}, bf16[192,256]{1,0:T(8,128)(2,1)S(1)}, u32[]{:S(2)}, u32[]{:S(2)}) collective-permute-start(bf16[192,256]{1,0:T(8,128)(2,1)S(1)} %fusion.45), channel_id=1, source_target_pairs={{0,8},{8,0},{1,9},{9,1},{2,10},{10,2},{3,11},{11,3},{4,12},{12,4},... | collective-permute-start | bytes 294920 | tf_op jit(solution)/shard_map/ppermute | solution.py:26

commit v10 on v9

--- a/solution.py
+++ b/solution.py
@@ -12,12 +12,11 @@
 STEPS = (0, -1, 1, -2, 2, -3, 3, -4)
 
 
-def block_table():
-    table = np.zeros((NZ, NX, NZ * NX), np.uint32)
-    for zl, x, j, s in np.ndindex(NZ, NX, NZ, NX):
-        z, col = RING[(RING.index(zl) + STEPS[j]) % NZ], (x + s) % NX
-        table[zl, x, j * NX + s] = (((col // 2) * NY + z % NY) * NH + z // NY) * 2 + col % 2
-    return table
+PLACES = np.zeros((NZ, NX, 2 * NZ + 2 * NX), np.uint32)
+for zl_, x_ in np.ndindex(NZ, NX):
+    rings = [RING[(RING.index(zl_) + step) % NZ] for step in STEPS]
+    at = [v for z in rings for v in (z % NY, z // NY)]
+    PLACES[zl_, x_] = at + [v for step in range(NX) for v in ((x_ + step) % NX // 2, (x_ + step) % 2)]
 
 
 def shift(axis, order, step):
@@ -59,46 +58,50 @@
         got = after(send(v), *done)
         return jnp.concatenate([jnp.where(bit == 0, v, got), jnp.where(bit == 0, got, v)])
 
-    def pile(*blocks):
-        return jnp.concatenate(blocks, axis=0)
-
     a1, b1 = ring_up(own), ring_down(own)
-    p0, m0 = x_up(own), x_down(own)
+    p0, m0 = x_up(own[None]), x_down(own[None])
     a2, b2 = ring_up(after(a1, p0)), ring_down(after(b1, m0))
-    g1 = pile(a1, b1)
+    g1 = jnp.stack([a1, b1])
     p1, m1 = x_up(after(g1, p0)), x_down(after(g1, m0))
     a3, b3 = ring_up(a2), ring_down(b2)
-    f0 = x_far(after(own, a3))
-    m2 = x_down(pile(a2, b2, m1[rows:]))
-    p2 = x_up(pile(a2, b2, p1[:rows]))
+    f0 = x_far(after(own[None], a3))
+    m2 = x_down(jnp.stack([a2, b2, m1[1]]))
+    p2 = x_up(jnp.stack([a2, b2, p1[0]]))
     fields = join(fields, other_half, zh, b3)
     fields = join(fields, y_near, y & 1, m2)
-    g3 = pile(a3, b3)
+    g3 = jnp.stack([a3, b3])
     m3 = x_down(after(g3, m2))
     p3 = x_up(after(g3, p2))
     a4 = ring_up(a3)
     f3 = x_far(after(g3, f0))
     fields = join(fields, y_far, y >> 1, p3)
-    m4 = x_down(pile(a4, m2[rows : 2 * rows]))
-    p4 = x_up(after(pile(a4, p2[:rows]), m3))
-    f4 = x_far(after(a4, p3))
+    m4 = x_down(jnp.stack([a4, m2[1]]))
+    p4 = x_up(after(jnp.stack([a4, p2[0]]), m3))
+    f4 = x_far(after(a4[None], p3))
     fields = join(fields, other_core, c)
 
     zl, x, _ = lax.optimization_barrier((zl, x, m2))
-    offsets = lax.dynamic_slice(jnp.asarray(block_table()), (zl, x, jnp.uint32(0)), (1, 1, NZ * NX)).reshape(-1)
-    full = jnp.broadcast_to(m2[0, 0] * 0, (NZ * NX, rows, width))
-    pieces = [(own, 0, 0), (m0, 0, 1), (f0, 0, 2), (p0, 0, 3)]
-    for k, parts in ((1, (g1, m1, p1)), (3, (pile(a2, b2), m2, p2)), (5, (g3, m3, p3))):
+    places = lax.dynamic_slice(jnp.asarray(PLACES), (zl, x, jnp.uint32(0)), (1, 1, PLACES.shape[2])).reshape(-1)
+
+    def place(i):
+        return lax.squeeze(lax.slice(places, (i,), (i + 1,)), (0,))
+
+    lines = [(place(2 * j), place(2 * j + 1)) for j in range(NZ)]
+    cols = [(place(2 * NZ + 2 * step), place(2 * NZ + 2 * step + 1)) for step in range(NX)]
+    none = jnp.uint32(0)
+    full = jnp.broadcast_to(p3[0, 0, 0] * 0, (NC, NY, NH, 2, rows, width))
+    pieces = [(own, 0, 0), (m0[0], 0, 1), (p0[0], 0, 3)]
+    for k, parts in ((1, (g1, m1, p1)), (3, (jnp.stack([a2, b2]), m2, p2))):
         for part, step in zip(parts, (0, 1, 3)):
-            pieces += [(part[:rows], k, step), (part[rows : 2 * rows], k + 1, step)]
-    pieces += [(p2[2 * rows :], 1, 2), (m2[2 * rows :], 2, 2), (f3[:rows], 5, 2), (f3[rows:], 6, 2)]
-    pieces += [(p4[rows:], 3, 2), (m4[rows:], 4, 2)]
-    pieces += [(a4, 7, 0), (m4[:rows], 7, 1), (p4[:rows], 7, 3), (f4, 7, 2)]
-    none = jnp.uint32(0)
+            pieces += [(part[0], k, step), (part[1], k + 1, step)]
+    pieces += [(p2[2], 1, 2), (m2[2], 2, 2), (f0[0], 0, 2)]
+    for part, step in ((g3, 0), (m3, 1), (p3, 3), (f3, 2)):
+        pieces += [(part[0], 5, step), (part[1], 6, step)]
+    pieces += [(p4[1], 3, 2), (m4[1], 4, 2)]
+    pieces += [(a4, 7, 0), (m4[0], 7, 1), (p4[0], 7, 3), (f4[0], 7, 2)]
     for part, j, step in pieces:
-        at = j * NX + step
-        first = lax.squeeze(lax.slice(offsets, (at,), (at + 1,)), (0,))
-        full = lax.dynamic_update_slice(full, part[None], (first, none, none))
+        where = (cols[step][0], *lines[j], cols[step][1], none, none)
+        full = lax.dynamic_update_slice(full, part[None, None, None, None], where)
     full = full.reshape(NZ * NX * rows, width)
 
     n_tok = tokens.shape[0]

time: 232 us -> 293 us (1.26)
  the two profiles are of different devices: /device:TPU:384 before, /device:TPU:65 now
where the time goes in v10:
time: 293 us; the launch traced here: 290 us
  starting transfers between devices  112 us (38%)
  local copies, waits for them, and re-layouts  91.1 us (31%)
  waiting for transfers between devices  59.4 us (20%)
  other arithmetic  19.3 us (7%)
  matrix products  6.51 us (2%)
    ppermute x24, starting transfers between devices, shift(): return lambda v: lax.ppermute(v, axis, pairs)  101 us
    dynamic_update_slice x31, local copies, waits for them, and re-layouts, body(): full = lax.dynamic_update_slice(full, part[None, None, None, None], where)  87.1 us
    ppermute x24, waiting for transfers between devices, shift(): return lambda v: lax.ppermute(v, axis, pairs)  47.4 us
    all_to_all x1, waiting for transfers between devices, body(): shares = lax.all_to_all(sums.astype(BF), 'y', 0, 0, tiled=True).astype(F32)  12 us
    ppermute x2, starting transfers between devices, flip(): return lambda v: lax.ppermute(v, axis, [(i, i ^ bit) for i in range(n)])  7.85 us
  transfers between devices with their start and end apart: 27, of which 6 were waited for; matrix products, arithmetic and copies ran while one was open for 37% of the time, Pallas kernels for 0%

profile of v10, /device:TPU:65, one launch (start us, length us, event | category | flops | bytes accessed | tf_op | source)
XLA Modules:
  0.0 290.4 jit_solution(1105147974897041362)
XLA Ops:
  3.0 6.1 %collective-permute-start = (bf16[96,1536]{1,0:T(8,128)(2,1)S(1)}, bf16[96,1536]{1,0:T(8,128)(2,1)S(1)}, u32[]{:S(2)}, u32[]{:S(2)}) collective-permute-start(bf16[96,1536]{1,0:T(8,128)(2,1)S(1)} %get-tuple-element.50), channel_id=1, source_target_pairs={{0,128},{128,256},{256,384},{384,448},{448,320},{320,192},{192,64}... | collective-permute-start | bytes 884744 | tf_op jit(solution)/shard_map/ppermute | solution.py:25
  9.1 4.4 %collective-permute-start.5 = (bf16[1,96,1536]{2,1,0:T(8,128)(2,1)S(1)}, bf16[1,96,1536]{2,1,0:T(8,128)(2,1)S(1)}, u32[]{:S(2)}, u32[]{:S(2)}) collective-permute-start(bf16[1,96,1536]{2,1,0:T(8,128)(2,1)S(1)} %get-tuple-element.27), channel_id=1, source_target_pairs={{0,48},{16,0},{32,16},{48,32},{1,49},{17,1},{33,17},{49,33},{2,50}... | collective-permute-start | bytes 884744 | tf_op jit(solution)/shard_map/ppermute | solution.py:25
  15.4 3.9 %collective-permute-done = bf16[96,1536]{1,0:T(8,128)(2,1)S(1)} collective-permute-done((bf16[96,1536]{1,0:T(8,128)(2,1)S(1)}, bf16[96,1536]{1,0:T(8,128)(2,1)S(1)}, u32[]{:S(2)}, u32[]{:S(2)}) %collective-permute-start) | collective-permute-done | bytes 294944 | tf_op jit(solution)/shard_map/ppermute | solution.py:25
  19.4 4.7 %collective-permute-start.11 = (bf16[2,96,1536]{2,1,0:T(8,128)(2,1)S(1)}, bf16[2,96,1536]{2,1,0:T(8,128)(2,1)S(1)}, u32[]{:S(2)}, u32[]{:S(2)}) collective-permute-start(bf16[2,96,1536]{2,1,0:T(8,128)(2,1)S(1)} %pad_maximum_fusion.10), channel_id=1, source_target_pairs={{0,48},{16,0},{32,16},{48,32},{1,49},{17,1},{33,17},{49,33},{2,50}... | collective-permute-start | bytes 1769480 | tf_op jit(solution)/shard_map/ppermute | solution.py:25
  28.0 5.5 %collective-permute-start.2 = (bf16[96,1536]{1,0:T(8,128)(2,1)S(1)}, bf16[96,1536]{1,0:T(8,128)(2,1)S(1)}, u32[]{:S(2)}, u32[]{:S(2)}) collective-permute-start(bf16[96,1536]{1,0:T(8,128)(2,1)S(1)} %collective-permute-done), channel_id=1, source_target_pairs={{0,128},{128,256},{256,384},{384,448},{448,320},{320,192},{192,64}... | collective-permute-start | bytes 884744 | tf_op jit(solution)/shard_map/ppermute | solution.py:25
  35.2 12.7 %collective-permute-start.20 = (bf16[192,768]{1,0:T(8,128)(2,1)}, bf16[192,768]{1,0:T(8,128)(2,1)}, u32[]{:S(2)}, u32[]{:S(2)}) collective-permute-start(bf16[192,768]{1,0:T(8,128)(2,1)} %pad_maximum_fusion.13), channel_id=1, source_target_pairs={{0,8},{8,0},{1,9},{9,1},{2,10},{10,2},{3,11},{11,3},{4,12},{12,4},... | collective-permute-start | bytes 884744 | tf_op jit(solution)/shard_map/ppermute | solution.py:25
  50.2 5.2 %collective-permute-start.3 = (bf16[96,1536]{1,0:T(8,128)(2,1)S(1)}, bf16[96,1536]{1,0:T(8,128)(2,1)}, u32[]{:S(2)}, u32[]{:S(2)}) collective-permute-start(bf16[96,1536]{1,0:T(8,128)(2,1)S(1)} %collective-permute-done.2), channel_id=1, source_target_pairs={{0,128},{128,256},{256,384},{384,448},{448,320},{320,192},{192,64}... | collective-permute-start | bytes 884744 | tf_op jit(solution)/shard_map/ppermute | solution.py:25
  58.8 4.6 %collective-permute-start.12 = (bf16[3,96,1536]{2,1,0:T(8,128)(2,1)}, bf16[3,96,1536]{2,1,0:T(8,128)(2,1)S(1)}, u32[]{:S(2)}, u32[]{:S(2)}) collective-permute-start(bf16[3,96,1536]{2,1,0:T(8,128)(2,1)} %get-tuple-element.45), channel_id=1, source_target_pairs={{0,48},{16,0},{32,16},{48,32},{1,49},{17,1},{33,17},{49,33},{2,50}... | collective-permute-start | bytes 2654216 | tf_op jit(solution)/shard_map/ppermute | solution.py:25
  64.2 22.3 %collective-permute-done.3 = bf16[96,1536]{1,0:T(8,128)(2,1)} collective-permute-done((bf16[96,1536]{1,0:T(8,128)(2,1)S(1)}, bf16[96,1536]{1,0:T(8,128)(2,1)}, u32[]{:S(2)}, u32[]{:S(2)}) %collective-permute-start.3) | collective-permute-done | bytes 294944 | tf_op jit(solution)/shard_map/ppermute | solution.py:25
  86.5 2.8 collective-permute-start.13
  91.4 3.2 %collective-permute-start.21 = (bf16[384,768]{1,0:T(8,128)(2,1)}, bf16[384,768]{1,0:T(8,128)(2,1)}, u32[]{:S(2)}, u32[]{:S(2)}) collective-permute-start(bf16[384,768]{1,0:T(8,128)(2,1)} %pad_maximum_fusion.11), channel_id=1, source_target_pairs={{0,2},{2,0},{4,6},{6,4},{1,3},{3,1},{5,7},{7,5},{8,10},{10,8},{12,... | collective-permute-start | bytes 1769480 | tf_op jit(solution)/shard_map/ppermute | solution.py:33
  94.6 6.3 %collective-permute-start.16 = (bf16[96,1536]{1,0:T(8,128)(2,1)}, bf16[96,1536]{1,0:T(8,128)(2,1)}, u32[]{:S(2)}, u32[]{:S(2)}) collective-permute-start(bf16[96,1536]{1,0:T(8,128)(2,1)} %collective-permute-done.3), channel_id=1, source_target_pairs={{0,128},{128,256},{256,384},{384,448},{448,320},{320,192},{192,64}... | collective-permute-start | bytes 884744 | tf_op jit(solution)/shard_map/ppermute | solution.py:25
  103.6 3.9 %collective-permute-start.15 = (bf16[2,96,1536]{2,1,0:T(8,128)(2,1)}, bf16[2,96,1536]{2,1,0:T(8,128)(2,1)S(1)}, u32[]{:S(2)}, u32[]{:S(2)}) collective-permute-start(bf16[2,96,1536]{2,1,0:T(8,128)(2,1)} %pad_maximum_fusion.9), channel_id=1, source_target_pairs={{0,32},{16,48},{32,0},{48,16},{1,33},{17,49},{33,1},{49,17},{2,34}... | collective-permute-start | bytes 1769480 | tf_op jit(solution)/shard_map/ppermute | solution.py:25
  109.7 4.3 %collective-permute-start.14 = (bf16[2,96,1536]{2,1,0:T(8,128)(2,1)}, bf16[2,96,1536]{2,1,0:T(8,128)(2,1)S(1)}, u32[]{:S(2)}, u32[]{:S(2)}) collective-permute-start(bf16[2,96,1536]{2,1,0:T(8,128)(2,1)} %pad_maximum_fusion.9), channel_id=1, source_target_pairs={{0,48},{16,0},{32,16},{48,32},{1,49},{17,1},{33,17},{49,33},{2,50}... | collective-permute-start | bytes 1769480 | tf_op jit(solution)/shard_map/ppermute | solution.py:25
  116.3 3.5 %collective-permute-start.18 = (bf16[2,96,1536]{2,1,0:T(8,128)(2,1)}, bf16[2,96,1536]{2,1,0:T(8,128)(2,1)S(1)}, u32[]{:S(2)}, u32[]{:S(2)}) collective-permute-start(bf16[2,96,1536]{2,1,0:T(8,128)(2,1)} %get-tuple-element.47), channel_id=1, source_target_pairs={{0,48},{16,0},{32,16},{48,32},{1,49},{17,1},{33,17},{49,33},{2,50}... | collective-permute-start | bytes 1769480 | tf_op jit(solution)/shard_map/ppermute | solution.py:25
  121.2 4.7 %collective-permute-start.22 = (bf16[768,768]{1,0:T(8,128)(2,1)S(1)}, bf16[768,768]{1,0:T(8,128)(2,1)S(1)}, u32[]{:S(2)}, u32[]{:S(2)}) collective-permute-start(bf16[768,768]{1,0:T(8,128)(2,1)S(1)} %pad_maximum_fusion.3), channel_id=1, source_target_pairs={{0,4},{2,6},{4,0},{6,2},{1,5},{3,7},{5,1},{7,3},{8,12},{10,14},{12... | collective-permute-start | bytes 3538952 | tf_op jit(solution)/shard_map/ppermute | solution.py:33
  127.9 5.5 %collective-permute-done.14 = bf16[2,96,1536]{2,1,0:T(8,128)(2,1)S(1)} collective-permute-done((bf16[2,96,1536]{2,1,0:T(8,128)(2,1)}, bf16[2,96,1536]{2,1,0:T(8,128)(2,1)S(1)}, u32[]{:S(2)}, u32[]{:S(2)}) %collective-permute-start.14) | collective-permute-done | bytes 589856 | tf_op jit(solution)/shard_map/ppermute | solution.py:25
  133.5 5.8 %collective-permute-start.17 = (bf16[2,96,1536]{2,1,0:T(8,128)(2,1)}, bf16[2,96,1536]{2,1,0:T(8,128)(2,1)}, u32[]{:S(2)}, u32[]{:S(2)}) collective-permute-start(bf16[2,96,1536]{2,1,0:T(8,128)(2,1)} %get-tuple-element.30), channel_id=1, source_target_pairs={{0,16},{16,32},{32,48},{48,0},{1,17},{17,33},{33,49},{49,1},{2,18}... | collective-permute-start | bytes 1769480 | tf_op jit(solution)/shard_map/ppermute | solution.py:25
  139.3 2.5 collective-permute-start.19
  144.1 2.6 bitcast_dynamic-update-slice_fusion.15
  146.8 3.5 %bitcast_dynamic-update-slice_fusion.14 = bf16[2,4,2,2,96,1536]{5,4,3,2,1,0:T(8,128)(2,1)S(1)} fusion(bf16[2,4,2,2,96,1536]{5,4,3,2,1,0:T(8,128)(2,1)S(1)} %bitcast_dynamic-update-slice_fusion.15, u32[]{:T(128)} %bitcast.15, u32[]{:T(128)} %bitcast.11, u32[]{:T(128)} %bitcast.12, u32[]{:T(128)} %bitcast.16, bf16[1,96,1536]{2,1,0:T(8,128)(2,1)} %copy-done.16), kind=kLoop, calls=%fused_computation.96 | loop fusion | bytes 589840 | tf_op jit(solution)/shard_map/dynamic_update_slice | solution.py:104
  150.3 3.6 %bitcast_dynamic-update-slice_fusion.13 = bf16[2,4,2,2,96,1536]{5,4,3,2,1,0:T(8,128)(2,1)S(1)} fusion(bf16[2,4,2,2,96,1536]{5,4,3,2,1,0:T(8,128)(2,1)S(1)} %bitcast_dynamic-update-slice_fusion.14, u32[]{:T(128)} %bitcast.18, u32[]{:T(128)} %bitcast.11, u32[]{:T(128)} %bitcast.12, u32[]{:T(128)} %bitcast.19, bf16[1,96,1536]{2,1,0:T(8,128)(2,1)} %copy-done.17), kind=kLoop, calls=%fused_computation.95 | loop fusion | bytes 589840 | tf_op jit(solution)/shard_map/dynamic_update_slice | solution.py:104
  156.3 2.6 bitcast_dynamic-update-slice_fusion.11
  161.4 2.6 bitcast_dynamic-update-slice_fusion.10
  166.5 2.6 fusion.41
  169.1 2.5 bitcast_dynamic-update-slice_fusion.8
  174.1 2.5 fusion.40
  179.1 2.6 bitcast_dynamic-update-slice_fusion.5
  186.7 2.6 fusion.37
  189.2 3.5 %bitcast_dynamic-update-slice_fusion.4 = bf16[2,4,2,2,96,1536]{5,4,3,2,1,0:T(8,128)(2,1)S(1)} fusion(bf16[2,4,2,2,96,1536]{5,4,3,2,1,0:T(8,128)(2,1)S(1)} %fusion.37, u32[]{:T(128)} %bitcast.41, u32[]{:T(128)} %bitcast.11, u32[]{:T(128)} %bitcast.12, u32[]{:T(128)} %bitcast.42, bf16[1,96,1536]{2,1,0:T(8,128)(2,1)} %collective-permute-done.13), kind=kLoop, calls=%fused_computation.86 | loop fusion | bytes 589840 | tf_op jit(solution)/shard_map/dynamic_update_slice | solution.py:104
  192.8 3.6 %bitcast_dynamic-update-slice_fusion.3 = bf16[2,4,2,2,96,1536]{5,4,3,2,1,0:T(8,128)(2,1)S(1)} fusion(bf16[2,4,2,2,96,1536]{5,4,3,2,1,0:T(8,128)(2,1)S(1)} %bitcast_dynamic-update-slice_fusion.4, u32[]{:T(128)} %bitcast.10, u32[]{:T(128)} %bitcast.46, u32[]{:T(128)} %bitcast.47, u32[]{:T(128)} %bitcast.13, bf16[96,1536]{1,0:T(8,128)(2,1)} %collective-permute-done.3), kind=kLoop, calls=%fused_computation.85 | loop fusion | bytes 589840 | tf_op jit(solution)/shard_map/dynamic_update_slice | solution.py:104
  196.4 3.4 %bitcast_dynamic-update-slice_fusion.2 = bf16[2,4,2,2,96,1536]{5,4,3,2,1,0:T(8,128)(2,1)S(1)} fusion(bf16[2,4,2,2,96,1536]{5,4,3,2,1,0:T(8,128)(2,1)S(1)} %bitcast_dynamic-update-slice_fusion.3, u32[]{:T(128)} %bitcast.10, u32[]{:T(128)} %bitcast.49, u32[]{:T(128)} %bitcast.50, u32[]{:T(128)} %bitcast.13, bf16[96,1536]{1,0:T(8,128)(2,1)} %collective-permute-done.7), kind=kLoop, calls=%fused_computation.84 | loop fusion | bytes 589840 | tf_op jit(solution)/shard_map/dynamic_update_slice | solution.py:104
  199.8 2.6 fusion.36
  204.9 2.7 fusion.34
  207.6 2.5 fusion.33
  210.1 2.6 fusion.32
  215.9 4.8 %collective-permute-start.23 = (bf16[1536,768]{1,0:T(8,128)(2,1)S(1)}, bf16[1536,768]{1,0:T(8,128)(2,1)S(1)}, u32[]{:S(2)}, u32[]{:S(2)}) collective-permute-start(bf16[1536,768]{1,0:T(8,128)(2,1)S(1)} %pad_maximum_fusion.2), channel_id=1, source_target_pairs={{0,1},{1,0},{2,3},{3,2},{4,5},{5,4},{6,7},{7,6},{8,9},{9,8},{10,11... | collective-permute-start | bytes 7077896 | tf_op jit(solution)/shard_map/ppermute | solution.py:25
  220.7 3.5 %fusion.30 = bf16[2,4,2,2,96,1536]{5,4,3,2,1,0:T(8,128)(2,1)S(1)} fusion(bf16[2,4,2,2,96,1536]{5,4,3,2,1,0:T(8,128)(2,1)S(1)} %fusion.31, u32[]{:T(128)} %bitcast.41, u32[]{:T(128)} %bitcast.31, u32[]{:T(128)} %bitcast.32, u32[]{:T(128)} %bitcast.42, bf16[2,96,1536]{2,1,0:T(8,128)(2,1)} %collective-permute-done.17), kind=kLoop, calls=%fused_computation.55 | loop fusion | bytes 589840 | tf_op jit(solution)/shard_map/dynamic_update_slice | solution.py:104
  226.6 3.5 %bitcast_dynamic-update-slice_fusion.1 = bf16[2,4,2,2,96,1536]{5,4,3,2,1,0:T(8,128)(2,1)S(1)} fusion(bf16[2,4,2,2,96,1536]{5,4,3,2,1,0:T(8,128)(2,1)S(1)} %fusion.29, u32[]{:T(128)} %bitcast.10, u32[]{:T(128)} %bitcast.61, u32[]{:T(128)} %bitcast.62, u32[]{:T(128)} %bitcast.13, bf16[96,1536]{1,0:T(8,128)(2,1)} %collective-permute-done.16), kind=kLoop, calls=%fused_computation.83 | loop fusion | bytes 589840 | tf_op jit(solution)/shard_map/dynamic_update_slice | solution.py:104
  230.1 2.5 fusion.28
  232.6 3.5 %fusion.27 = bf16[2,4,2,2,96,1536]{5,4,3,2,1,0:T(8,128)(2,1)S(1)} fusion(bf16[2,4,2,2,96,1536]{5,4,3,2,1,0:T(8,128)(2,1)S(1)} %fusion.28, u32[]{:T(128)} %bitcast.18, u32[]{:T(128)} %bitcast.61, u32[]{:T(128)} %bitcast.62, u32[]{:T(128)} %bitcast.19, bf16[2,96,1536]{2,1,0:T(8,128)(2,1)} %collective-permute-done.17), kind=kLoop, calls=%fused_computation.49 | loop fusion | bytes 589840 | tf_op jit(solution)/shard_map/dynamic_update_slice | solution.py:104
  236.2 3.5 %bitcast_dynamic-update-slice_fusion = bf16[2,4,2,2,96,1536]{5,4,3,2,1,0:T(8,128)(2,1)S(1)} fusion(bf16[2,4,2,2,96,1536]{5,4,3,2,1,0:T(8,128)(2,1)S(1)} %fusion.27, u32[]{:T(128)} %bitcast.41, u32[]{:T(128)} %bitcast.61, u32[]{:T(128)} %bitcast.62, u32[]{:T(128)} %bitcast.42, bf16[1,96,1536]{2,1,0:T(8,128)(2,1)} %collective-permute-done.19), kind=kLoop, calls=%fused_computation.82 | loop fusion | bytes 589840 | tf_op jit(solution)/shard_map/dynamic_update_slice | solution.py:104
  240.6 3.4 %fusion.2 = f32[512,1024]{1,0:T(8,128)S(1)} fusion(bf16[3072,1536]{1,0:T(8,128)(2,1)S(1)} %bitcast.152, bf16[1536,768]{1,0:T(8,128)(2,1)S(1)} %get-tuple-element.36, bf16[1536,768]{1,0:T(8,128)(2,1)S(1)} %get-tuple-element.35), kind=kOutput, calls=%fused_computation.2 | convolution fusion | flops 3227516928 | bytes 13107200 | tf_op jit(solution)/shard_map/dot_general | solution.py:110
  249.3 3.4 %collective-permute-done.24 = f32[4,2,192,256]{3,2,1,0:T(8,128)S(1)} collective-permute-done((f32[4,2,192,256]{3,2,1,0:T(8,128)S(1)}, f32[4,2,192,256]{3,2,1,0:T(8,128)S(1)}, u32[]{:S(2)}, u32[]{:S(2)}) %collective-permute-start.24) | collective-permute-done | bytes 1572896 | tf_op jit(solution)/shard_map/ppermute | solution.py:25
  253.8 3.9 %all-to-all-start = ((bf16[4,2,192,256]{3,2,1,0:T(8,128)(2,1)}), bf16[4,2,192,256]{3,2,1,0:T(8,128)(2,1)S(1)}, u32[]{:S(2)}, u32[]{:S(2)}) async-start(bf16[4,2,192,256]{3,2,1,0:T(8,128)(2,1)} %fusion.10), calls=%async_computation | async-start | bytes 1572864 | tf_op jit(solution)/shard_map/all_to_all | solution.py:132
  257.7 12.0 %all-to-all-done = bf16[4,2,192,256]{3,2,1,0:T(8,128)(2,1)S(1)} async-done(((bf16[4,2,192,256]{3,2,1,0:T(8,128)(2,1)}), bf16[4,2,192,256]{3,2,1,0:T(8,128)(2,1)S(1)}, u32[]{:S(2)}, u32[]{:S(2)}) %all-to-all-start) | async-done | bytes 786464 | tf_op jit(solution)/shard_map/all_to_all | solution.py:132
  269.8 7.6 %collective-permute-start.25 = (bf16[192,256]{1,0:T(8,128)(2,1)S(1)}, bf16[192,256]{1,0:T(8,128)(2,1)S(1)}, u32[]{:S(2)}, u32[]{:S(2)}) collective-permute-start(bf16[192,256]{1,0:T(8,128)(2,1)S(1)} %fusion.45), channel_id=1, source_target_pairs={{0,8},{8,0},{1,9},{9,1},{2,10},{10,2},{3,11},{11,3},{4,12},{12,4},... | collective-permute-start | bytes 294920 | tf_op jit(solution)/shard_map/ppermute | solution.py:25
  277.4 12.3 %collective-permute-done.25 = bf16[192,256]{1,0:T(8,128)(2,1)S(1)} collective-permute-done((bf16[192,256]{1,0:T(8,128)(2,1)S(1)}, bf16[192,256]{1,0:T(8,128)(2,1)S(1)}, u32[]{:S(2)}, u32[]{:S(2)}) %collective-permute-start.25) | collective-permute-done | bytes 98336 | tf_op jit(solution)/shard_map/ppermute | solution.py:25
  (106 shorter events, 64.3 us)
Async XLA Ops:
  1.0 57.8 %copy-start.15 = (bf16[1,96,1536]{2,1,0:T(8,128)(2,1)}, bf16[1,96,1536]{2,1,0:T(8,128)(2,1)S(1)}, u32[]{:S(2)}) copy-start(bf16[1,96,1536]{2,1,0:T(8,128)(2,1)S(1)} %get-tuple-element.27) | copy-start | bytes 884740
  1.0 14.4 %collective-permute-start.4 = (bf16[96,1536]{1,0:T(8,128)(2,1)S(1)}, bf16[96,1536]{1,0:T(8,128)(2,1)S(1)}, u32[]{:S(2)}, u32[]{:S(2)}) collective-permute-start(bf16[96,1536]{1,0:T(8,128)(2,1)S(1)} %get-tuple-element.50), channel_id=1, source_target_pairs={{0,64},{128,0},{256,128},{384,256},{448,384},{320,448},{192,320},{... | collective-permute-start | bytes 884744 | tf_op jit(solution)/shard_map/ppermute | solution.py:25
  3.0 16.3 %collective-permute-start = (bf16[96,1536]{1,0:T(8,128)(2,1)S(1)}, bf16[96,1536]{1,0:T(8,128)(2,1)S(1)}, u32[]{:S(2)}, u32[]{:S(2)}) collective-permute-start(bf16[96,1536]{1,0:T(8,128)(2,1)S(1)} %get-tuple-element.50), channel_id=1, source_target_pairs={{0,128},{128,256},{256,384},{384,448},{448,320},{320,192},{192,64}... | collective-permute-start | bytes 884744 | tf_op jit(solution)/shard_map/ppermute | solution.py:25
  9.1 10.3 %collective-permute-start.5 = (bf16[1,96,1536]{2,1,0:T(8,128)(2,1)S(1)}, bf16[1,96,1536]{2,1,0:T(8,128)(2,1)S(1)}, u32[]{:S(2)}, u32[]{:S(2)}) collective-permute-start(bf16[1,96,1536]{2,1,0:T(8,128)(2,1)S(1)} %get-tuple-element.27), channel_id=1, source_target_pairs={{0,48},{16,0},{32,16},{48,32},{1,49},{17,1},{33,17},{49,33},{2,50}... | collective-permute-start | bytes 884744 | tf_op jit(solution)/shard_map/ppermute | solution.py:25
  13.5 10.7 %collective-permute-start.1 = (bf16[1,96,1536]{2,1,0:T(8,128)(2,1)S(1)}, bf16[1,96,1536]{2,1,0:T(8,128)(2,1)S(1)}, u32[]{:S(2)}, u32[]{:S(2)}) collective-permute-start(bf16[1,96,1536]{2,1,0:T(8,128)(2,1)S(1)} %get-tuple-element.27), channel_id=1, source_target_pairs={{0,16},{16,32},{32,48},{48,0},{1,17},{17,33},{33,49},{49,1},{2,18}... | collective-permute-start | bytes 884744 | tf_op jit(solution)/shard_map/ppermute | solution.py:25
  15.4 40.0 %copy-start.4 = (bf16[96,1536]{1,0:T(8,128)(2,1)}, bf16[96,1536]{1,0:T(8,128)(2,1)S(1)}, u32[]{:S(2)}) copy-start(bf16[96,1536]{1,0:T(8,128)(2,1)S(1)} %collective-permute-done.4) | copy-start | bytes 884740
  19.3 36.1 %copy-start.6 = (bf16[96,1536]{1,0:T(8,128)(2,1)}, bf16[96,1536]{1,0:T(8,128)(2,1)S(1)}, u32[]{:S(2)}) copy-start(bf16[96,1536]{1,0:T(8,128)(2,1)S(1)} %collective-permute-done) | copy-start | bytes 884740
  19.4 36.1 %copy-start.16 = (bf16[1,96,1536]{2,1,0:T(8,128)(2,1)}, bf16[1,96,1536]{2,1,0:T(8,128)(2,1)S(1)}, u32[]{:S(2)}) copy-start(bf16[1,96,1536]{2,1,0:T(8,128)(2,1)S(1)} %collective-permute-done.5) | copy-start | bytes 884740
  19.4 36.0 %collective-permute-start.11 = (bf16[2,96,1536]{2,1,0:T(8,128)(2,1)S(1)}, bf16[2,96,1536]{2,1,0:T(8,128)(2,1)S(1)}, u32[]{:S(2)}, u32[]{:S(2)}) collective-permute-start(bf16[2,96,1536]{2,1,0:T(8,128)(2,1)S(1)} %pad_maximum_fusion.10), channel_id=1, source_target_pairs={{0,48},{16,0},{32,16},{48,32},{1,49},{17,1},{33,17},{49,33},{2,50}... | collective-permute-start | bytes 1769480 | tf_op jit(solution)/shard_map/ppermute | solution.py:25
  24.1 34.7 %copy-start.17 = (bf16[1,96,1536]{2,1,0:T(8,128)(2,1)}, bf16[1,96,1536]{2,1,0:T(8,128)(2,1)S(1)}, u32[]{:S(2)}) copy-start(bf16[1,96,1536]{2,1,0:T(8,128)(2,1)S(1)} %collective-permute-done.1) | copy-start | bytes 884740
  24.2 31.3 %collective-permute-start.8 = (bf16[2,96,1536]{2,1,0:T(8,128)(2,1)S(1)}, bf16[2,96,1536]{2,1,0:T(8,128)(2,1)S(1)}, u32[]{:S(2)}, u32[]{:S(2)}) collective-permute-start(bf16[2,96,1536]{2,1,0:T(8,128)(2,1)S(1)} %pad_maximum_fusion.10), channel_id=1, source_target_pairs={{0,16},{16,32},{32,48},{48,0},{1,17},{17,33},{33,49},{49,1},{2,18}... | collective-permute-start | bytes 1769480 | tf_op jit(solution)/shard_map/ppermute | solution.py:25
  26.1 21.9 %collective-permute-start.6 = (bf16[96,1536]{1,0:T(8,128)(2,1)S(1)}, bf16[96,1536]{1,0:T(8,128)(2,1)S(1)}, u32[]{:S(2)}, u32[]{:S(2)}) collective-permute-start(bf16[96,1536]{1,0:T(8,128)(2,1)S(1)} %collective-permute-done.4), channel_id=1, source_target_pairs={{0,64},{128,0},{256,128},{384,256},{448,384},{320,448},{192,320},{... | collective-permute-start | bytes 884744 | tf_op jit(solution)/shard_map/ppermute | solution.py:25
  28.0 22.2 %collective-permute-start.2 = (bf16[96,1536]{1,0:T(8,128)(2,1)S(1)}, bf16[96,1536]{1,0:T(8,128)(2,1)S(1)}, u32[]{:S(2)}, u32[]{:S(2)}) collective-permute-start(bf16[96,1536]{1,0:T(8,128)(2,1)S(1)} %collective-permute-done), channel_id=1, source_target_pairs={{0,128},{128,256},{256,384},{384,448},{448,320},{320,192},{192,64}... | collective-permute-start | bytes 884744 | tf_op jit(solution)/shard_map/ppermute | solution.py:25
  35.2 54.1 %collective-permute-start.20 = (bf16[192,768]{1,0:T(8,128)(2,1)}, bf16[192,768]{1,0:T(8,128)(2,1)}, u32[]{:S(2)}, u32[]{:S(2)}) collective-permute-start(bf16[192,768]{1,0:T(8,128)(2,1)} %pad_maximum_fusion.13), channel_id=1, source_target_pairs={{0,8},{8,0},{1,9},{9,1},{2,10},{10,2},{3,11},{11,3},{4,12},{12,4},... | collective-permute-start | bytes 884744 | tf_op jit(solution)/shard_map/ppermute | solution.py:25
  47.9 41.4 %copy-start = (bf16[96,1536]{1,0:T(8,128)(2,1)}, bf16[96,1536]{1,0:T(8,128)(2,1)S(1)}, u32[]{:S(2)}) copy-start(bf16[96,1536]{1,0:T(8,128)(2,1)S(1)} %collective-permute-done.6) | copy-start | bytes 884740
  48.0 41.4 %collective-permute-start.7 = (bf16[96,1536]{1,0:T(8,128)(2,1)S(1)}, bf16[96,1536]{1,0:T(8,128)(2,1)}, u32[]{:S(2)}, u32[]{:S(2)}) collective-permute-start(bf16[96,1536]{1,0:T(8,128)(2,1)S(1)} %collective-permute-done.6), channel_id=1, source_target_pairs={{0,64},{128,0},{256,128},{384,256},{448,384},{320,448},{192,320},{... | collective-permute-start | bytes 884744 | tf_op jit(solution)/shard_map/ppermute | solution.py:25
  50.2 39.2 %copy-start.2 = (bf16[96,1536]{1,0:T(8,128)(2,1)}, bf16[96,1536]{1,0:T(8,128)(2,1)S(1)}, u32[]{:S(2)}) copy-start(bf16[96,1536]{1,0:T(8,128)(2,1)S(1)} %collective-permute-done.2) | copy-start | bytes 884740
  50.2 36.3 %collective-permute-start.3 = (bf16[96,1536]{1,0:T(8,128)(2,1)S(1)}, bf16[96,1536]{1,0:T(8,128)(2,1)}, u32[]{:S(2)}, u32[]{:S(2)}) collective-permute-start(bf16[96,1536]{1,0:T(8,128)(2,1)S(1)} %collective-permute-done.2), channel_id=1, source_target_pairs={{0,128},{128,256},{256,384},{384,448},{448,320},{320,192},{192,64}... | collective-permute-start | bytes 884744 | tf_op jit(solution)/shard_map/ppermute | solution.py:25
  56.9 50.6 %collective-permute-start.9 = (bf16[3,96,1536]{2,1,0:T(8,128)(2,1)}, bf16[3,96,1536]{2,1,0:T(8,128)(2,1)S(1)}, u32[]{:S(2)}, u32[]{:S(2)}) collective-permute-start(bf16[3,96,1536]{2,1,0:T(8,128)(2,1)} %get-tuple-element.46), channel_id=1, source_target_pairs={{0,16},{16,32},{32,48},{48,0},{1,17},{17,33},{33,49},{49,1},{2,18}... | collective-permute-start | bytes 2654216 | tf_op jit(solution)/shard_map/ppermute | solution.py:25
  58.8 50.9 %collective-permute-start.12 = (bf16[3,96,1536]{2,1,0:T(8,128)(2,1)}, bf16[3,96,1536]{2,1,0:T(8,128)(2,1)S(1)}, u32[]{:S(2)}, u32[]{:S(2)}) collective-permute-start(bf16[3,96,1536]{2,1,0:T(8,128)(2,1)} %get-tuple-element.45), channel_id=1, source_target_pairs={{0,48},{16,0},{32,16},{48,32},{1,49},{17,1},{33,17},{49,33},{2,50}... | collective-permute-start | bytes 2654216 | tf_op jit(solution)/shard_map/ppermute | solution.py:25
  86.5 17.1 %collective-permute-start.13 = (bf16[1,96,1536]{2,1,0:T(8,128)(2,1)}, bf16[1,96,1536]{2,1,0:T(8,128)(2,1)}, u32[]{:S(2)}, u32[]{:S(2)}) collective-permute-start(bf16[1,96,1536]{2,1,0:T(8,128)(2,1)} %copy-done.15), channel_id=1, source_target_pairs={{0,32},{16,48},{32,0},{48,16},{1,33},{17,49},{33,1},{49,17},{2,34}... | collective-permute-start | bytes 884744 | tf_op jit(solution)/shard_map/ppermute | solution.py:25
  91.4 28.4 %collective-permute-start.21 = (bf16[384,768]{1,0:T(8,128)(2,1)}, bf16[384,768]{1,0:T(8,128)(2,1)}, u32[]{:S(2)}, u32[]{:S(2)}) collective-permute-start(bf16[384,768]{1,0:T(8,128)(2,1)} %pad_maximum_fusion.11), channel_id=1, source_target_pairs={{0,2},{2,0},{4,6},{6,4},{1,3},{3,1},{5,7},{7,5},{8,10},{10,8},{12,... | collective-permute-start | bytes 1769480 | tf_op jit(solution)/shard_map/ppermute | solution.py:33
  94.6 19.5 %collective-permute-start.16 = (bf16[96,1536]{1,0:T(8,128)(2,1)}, bf16[96,1536]{1,0:T(8,128)(2,1)}, u32[]{:S(2)}, u32[]{:S(2)}) collective-permute-start(bf16[96,1536]{1,0:T(8,128)(2,1)} %collective-permute-done.3), channel_id=1, source_target_pairs={{0,128},{128,256},{256,384},{384,448},{448,320},{320,192},{192,64}... | collective-permute-start | bytes 884744 | tf_op jit(solution)/shard_map/ppermute | solution.py:25
  103.6 106.5 %collective-permute-start.15 = (bf16[2,96,1536]{2,1,0:T(8,128)(2,1)}, bf16[2,96,1536]{2,1,0:T(8,128)(2,1)S(1)}, u32[]{:S(2)}, u32[]{:S(2)}) collective-permute-start(bf16[2,96,1536]{2,1,0:T(8,128)(2,1)} %pad_maximum_fusion.9), channel_id=1, source_target_pairs={{0,32},{16,48},{32,0},{48,16},{1,33},{17,49},{33,1},{49,17},{2,34}... | collective-permute-start | bytes 1769480 | tf_op jit(solution)/shard_map/ppermute | solution.py:25
  107.5 31.8 %collective-permute-start.10 = (bf16[2,96,1536]{2,1,0:T(8,128)(2,1)}, bf16[2,96,1536]{2,1,0:T(8,128)(2,1)S(1)}, u32[]{:S(2)}, u32[]{:S(2)}) collective-permute-start(bf16[2,96,1536]{2,1,0:T(8,128)(2,1)} %pad_maximum_fusion.9), channel_id=1, source_target_pairs={{0,16},{16,32},{32,48},{48,0},{1,17},{17,33},{33,49},{49,1},{2,18}... | collective-permute-start | bytes 1769480 | tf_op jit(solution)/shard_map/ppermute | solution.py:25
  109.7 23.8 %collective-permute-start.14 = (bf16[2,96,1536]{2,1,0:T(8,128)(2,1)}, bf16[2,96,1536]{2,1,0:T(8,128)(2,1)S(1)}, u32[]{:S(2)}, u32[]{:S(2)}) collective-permute-start(bf16[2,96,1536]{2,1,0:T(8,128)(2,1)} %pad_maximum_fusion.9), channel_id=1, source_target_pairs={{0,48},{16,0},{32,16},{48,32},{1,49},{17,1},{33,17},{49,33},{2,50}... | collective-permute-start | bytes 1769480 | tf_op jit(solution)/shard_map/ppermute | solution.py:25
  114.0 39.8 %copy-start.7 = (bf16[96,1536]{1,0:T(8,128)(2,1)S(1)}, bf16[96,1536]{1,0:T(8,128)(2,1)}, u32[]{:S(2)}) copy-start(bf16[96,1536]{1,0:T(8,128)(2,1)} %copy-done.6) | copy-start | bytes 884740
  114.1 42.3 %copy-start.5 = (bf16[96,1536]{1,0:T(8,128)(2,1)S(1)}, bf16[96,1536]{1,0:T(8,128)(2,1)}, u32[]{:S(2)}) copy-start(bf16[96,1536]{1,0:T(8,128)(2,1)} %copy-done.4) | copy-start | bytes 884740
  116.3 52.9 %copy-start.3 = (bf16[96,1536]{1,0:T(8,128)(2,1)S(1)}, bf16[96,1536]{1,0:T(8,128)(2,1)}, u32[]{:S(2)}) copy-start(bf16[96,1536]{1,0:T(8,128)(2,1)} %copy-done.2) | copy-start | bytes 884740
  116.3 107.9 %collective-permute-start.18 = (bf16[2,96,1536]{2,1,0:T(8,128)(2,1)}, bf16[2,96,1536]{2,1,0:T(8,128)(2,1)S(1)}, u32[]{:S(2)}, u32[]{:S(2)}) collective-permute-start(bf16[2,96,1536]{2,1,0:T(8,128)(2,1)} %get-tuple-element.47), channel_id=1, source_target_pairs={{0,48},{16,0},{32,16},{48,32},{1,49},{17,1},{33,17},{49,33},{2,50}... | collective-permute-start | bytes 1769480 | tf_op jit(solution)/shard_map/ppermute | solution.py:25
  121.1 23.0 %copy-start.12 = (bf16[512,96]{0,1:T(8,128)(2,1)S(1)}, bf16[512,96]{0,1:T(8,128)(2,1)}, u32[]{:S(2)}) copy-start(bf16[512,96]{0,1:T(8,128)(2,1)} %param.16) | copy-start | bytes 294916
  121.1 23.0 %copy-start.13 = (bf16[96,512]{1,0:T(8,128)(2,1)S(1)}, bf16[96,512]{1,0:T(8,128)(2,1)}, u32[]{:S(2)}) copy-start(bf16[96,512]{1,0:T(8,128)(2,1)} %param.15) | copy-start | bytes 294916
  121.1 23.0 %copy-start.14 = (bf16[96,512]{1,0:T(8,128)(2,1)S(1)}, bf16[96,512]{1,0:T(8,128)(2,1)}, u32[]{:S(2)}) copy-start(bf16[96,512]{1,0:T(8,128)(2,1)} %param.14) | copy-start | bytes 294916
  121.1 50.6 %copy-start.1 = (bf16[96,1536]{1,0:T(8,128)(2,1)S(1)}, bf16[96,1536]{1,0:T(8,128)(2,1)}, u32[]{:S(2)}) copy-start(bf16[96,1536]{1,0:T(8,128)(2,1)} %copy-done) | copy-start | bytes 884740
  121.2 94.0 %collective-permute-start.22 = (bf16[768,768]{1,0:T(8,128)(2,1)S(1)}, bf16[768,768]{1,0:T(8,128)(2,1)S(1)}, u32[]{:S(2)}, u32[]{:S(2)}) collective-permute-start(bf16[768,768]{1,0:T(8,128)(2,1)S(1)} %pad_maximum_fusion.3), channel_id=1, source_target_pairs={{0,4},{2,6},{4,0},{6,2},{1,5},{3,7},{5,1},{7,3},{8,12},{10,14},{12... | collective-permute-start | bytes 3538952 | tf_op jit(solution)/shard_map/ppermute | solution.py:33
  133.5 9.5 %copy-start.10 = (bf16[2,96,1536]{2,1,0:T(8,128)(2,1)}, bf16[2,96,1536]{2,1,0:T(8,128)(2,1)S(1)}, u32[]{:S(2)}) copy-start(bf16[2,96,1536]{2,1,0:T(8,128)(2,1)S(1)} %collective-permute-done.14) | copy-start | bytes 1769476
  133.5 87.2 %collective-permute-start.17 = (bf16[2,96,1536]{2,1,0:T(8,128)(2,1)}, bf16[2,96,1536]{2,1,0:T(8,128)(2,1)}, u32[]{:S(2)}, u32[]{:S(2)}) collective-permute-start(bf16[2,96,1536]{2,1,0:T(8,128)(2,1)} %get-tuple-element.30), channel_id=1, source_target_pairs={{0,16},{16,32},{32,48},{48,0},{1,17},{17,33},{33,49},{49,1},{2,18}... | collective-permute-start | bytes 1769480 | tf_op jit(solution)/shard_map/ppermute | solution.py:25
  139.3 3.7 %copy-start.8 = (bf16[2,96,1536]{2,1,0:T(8,128)(2,1)}, bf16[2,96,1536]{2,1,0:T(8,128)(2,1)S(1)}, u32[]{:S(2)}) copy-start(bf16[2,96,1536]{2,1,0:T(8,128)(2,1)S(1)} %collective-permute-done.10) | copy-start | bytes 1769476
  139.3 96.9 %collective-permute-start.19 = (bf16[1,96,1536]{2,1,0:T(8,128)(2,1)}, bf16[1,96,1536]{2,1,0:T(8,128)(2,1)}, u32[]{:S(2)}, u32[]{:S(2)}) collective-permute-start(bf16[1,96,1536]{2,1,0:T(8,128)(2,1)} %bitcast.57), channel_id=1, source_target_pairs={{0,32},{16,48},{32,0},{48,16},{1,33},{17,49},{33,1},{49,17},{2,34}... | collective-permute-start | bytes 884744 | tf_op jit(solution)/shard_map/ppermute | solution.py:25
  143.0 61.9 %copy-start.9 = (bf16[2,96,1536]{2,1,0:T(8,128)(2,1)S(1)}, bf16[2,96,1536]{2,1,0:T(8,128)(2,1)}, u32[]{:S(2)}) copy-start(bf16[2,96,1536]{2,1,0:T(8,128)(2,1)} %copy-done.8) | copy-start | bytes 1769476
  144.1 55.7 %copy-start.11 = (bf16[2,96,1536]{2,1,0:T(8,128)(2,1)S(1)}, bf16[2,96,1536]{2,1,0:T(8,128)(2,1)}, u32[]{:S(2)}) copy-start(bf16[2,96,1536]{2,1,0:T(8,128)(2,1)} %copy-done.10) | copy-start | bytes 1769476
  215.9 23.8 %collective-permute-start.23 = (bf16[1536,768]{1,0:T(8,128)(2,1)S(1)}, bf16[1536,768]{1,0:T(8,128)(2,1)S(1)}, u32[]{:S(2)}, u32[]{:S(2)}) collective-permute-start(bf16[1536,768]{1,0:T(8,128)(2,1)S(1)} %pad_maximum_fusion.2), channel_id=1, source_target_pairs={{0,1},{1,0},{2,3},{3,2},{4,5},{5,4},{6,7},{7,6},{8,9},{9,8},{10,11... | collective-permute-start | bytes 7077896 | tf_op jit(solution)/shard_map/ppermute | solution.py:25
  247.3 5.3 %collective-permute-start.24 = (f32[4,2,192,256]{3,2,1,0:T(8,128)S(1)}, f32[4,2,192,256]{3,2,1,0:T(8,128)S(1)}, u32[]{:S(2)}, u32[]{:S(2)}) collective-permute-start(f32[4,2,192,256]{3,2,1,0:T(8,128)S(1)} %dynamic-slice_bitcast_fusion), channel_id=1, source_target_pairs={{0,1},{1,0},{2,3},{3,2},{4,5},{5,4},{6,7},{7,6},{8,9},{9,8},{10,11... | collective-permute-start | bytes 4718600 | tf_op jit(solution)/shard_map/ppermute | solution.py:25
  253.8 15.9 %all-to-all-start = ((bf16[4,2,192,256]{3,2,1,0:T(8,128)(2,1)}), bf16[4,2,192,256]{3,2,1,0:T(8,128)(2,1)S(1)}, u32[]{:S(2)}, u32[]{:S(2)}) async-start(bf16[4,2,192,256]{3,2,1,0:T(8,128)(2,1)} %fusion.10), calls=%async_computation | async-start | bytes 1572864 | tf_op jit(solution)/shard_map/all_to_all | solution.py:132
  269.8 19.9 %collective-permute-start.25 = (bf16[192,256]{1,0:T(8,128)(2,1)S(1)}, bf16[192,256]{1,0:T(8,128)(2,1)S(1)}, u32[]{:S(2)}, u32[]{:S(2)}) collective-permute-start(bf16[192,256]{1,0:T(8,128)(2,1)S(1)} %fusion.45), channel_id=1, source_target_pairs={{0,8},{8,0},{1,9},{9,1},{2,10},{10,2},{3,11},{11,3},{4,12},{12,4},... | collective-permute-start | bytes 294920 | tf_op jit(solution)/shard_map/ppermute | solution.py:25

commit v11 on v5

--- a/solution.py
+++ b/solution.py
@@ -10,8 +10,16 @@
 NZ, NX, NH, NY, NC = 8, 4, 2, 4, 2
 RING = (0, 2, 4, 6, 7, 5, 3, 1)
 STEPS = (0, -1, 1, -2, 2, -3, 3, -4)
-SOURCES = np.array(
-    [sum(RING[(RING.index(z) + s) % NZ] << 3 * j for j, s in enumerate(STEPS)) for z in range(NZ)], np.uint32
+PLACES = np.array(
+    [
+        [
+            [v for s in STEPS for z in [RING[(RING.index(zl) + s) % NZ]] for v in (z % NY, z // NY)]
+            + [v for s in range(NX) for v in ((x + s) % NX // 2, (x + s) % 2)]
+            for x in range(NX)
+        ]
+        for zl in range(NZ)
+    ],
+    np.uint32,
 )
 
 
@@ -44,7 +52,11 @@
 
 def body(tokens, tangent, cotangent, gates, slot_tokens, gate_weight, up_weight, down_weight):
     zl, x, zh, y, c = (lax.axis_index(a).astype(jnp.uint32) for a in ("zl", "x", "zh", "y", "c"))
-    packed = take(jnp.asarray(SOURCES), zl)
+    places = lax.dynamic_slice(jnp.asarray(PLACES), (zl, x, jnp.uint32(0)), (1, 1, PLACES.shape[2])).reshape(-1)
+
+    def place(i):
+        return lax.squeeze(lax.slice(places, (i,), (i + 1,)), (0,))
+
 
     own = jnp.concatenate([gate_weight, up_weight, down_weight.T], axis=1)
     rows, width = own.shape
@@ -85,14 +97,14 @@
     zero = a2[0, 0] * 0
     full = jnp.broadcast_to(zero, (NC, NY, NH, 2, rows, width))
     none = jnp.uint32(0)
-    sources = iter((((packed >> 3 * j) & 3, (packed >> 3 * j + 2) & 1) for j in range(NZ)))
+    sources = iter([(place(2 * j), place(2 * j + 1)) for j in range(NZ)])
+    cols = [(place(2 * NZ + 2 * s), place(2 * NZ + 2 * s + 1)) for s in range(NX)]
     groups = ((g0, m0, f0, p0), (g1, m1, f1, p1), (g2, m2, f2, p2), (g3, m3, f3, p3), (g4, m4, f4, p4))
     for parts in groups:
         at = [next(sources) for _ in parts[0]]
         for step, part in enumerate(parts):
-            col = x + step
             for j, (row, far) in enumerate(at):
-                where = ((col >> 1) & 1, row, far, col & 1, none, none)
+                where = (cols[step][0], row, far, cols[step][1], none, none)
                 full = lax.dynamic_update_slice(full, part[j][None, None, None, None], where)
     full = full.reshape(NZ * NX * rows, width)
 

time: 214 us -> 261 us (1.22)
  the two profiles are of different devices: /device:TPU:99 before, /device:TPU:68 now
where the time goes in v11:
time: 261 us; the launch traced here: 259 us
  starting transfers between devices  112 us (43%)
  local copies, waits for them, and re-layouts  81 us (31%)
  waiting for transfers between devices  48 us (18%)
  other arithmetic  10.1 us (4%)
  matrix products  6.51 us (2%)
    ppermute x26, starting transfers between devices, shift(): return lambda v: lax.ppermute(v, axis, pairs)  99.6 us
    dynamic_update_slice x31, local copies, waits for them, and re-layouts, body(): lax.dynamic_update_slice(full, part[j][None, None, None, None], where)  77.1 us
    ppermute x26, waiting for transfers between devices, shift(): return lambda v: lax.ppermute(v, axis, pairs)  35 us
    all_to_all x1, waiting for transfers between devices, body(): shares = lax.all_to_all(sums.astype(BF), 'y', 0, 0, tiled=True).astype(F32)  13.1 us
    ppermute x2, starting transfers between devices, flip(): return lambda v: lax.ppermute(v, axis, [(i, i ^ bit) for i in range(n)])  8.59 us
  transfers between devices with their start and end apart: 29, of which 6 were waited for; matrix products, arithmetic and copies ran while one was open for 34% of the time, Pallas kernels for 0%

profile of v11, /device:TPU:68, one launch (start us, length us, event | category | flops | bytes accessed | tf_op | source)
XLA Modules:
  0.0 258.8 jit_solution(12899292795276746765)
XLA Ops:
  1.1 6.4 %collective-permute-start = (bf16[96,1536]{1,0:T(8,128)(2,1)S(1)}, bf16[96,1536]{1,0:T(8,128)(2,1)S(1)}, u32[]{:S(2)}, u32[]{:S(2)}) collective-permute-start(bf16[96,1536]{1,0:T(8,128)(2,1)S(1)} %get-tuple-element.48), channel_id=1, source_target_pairs={{0,128},{128,256},{256,384},{384,448},{448,320},{320,192},{192,64}... | collective-permute-start | bytes 884744 | tf_op jit(solution)/shard_map/ppermute | solution.py:29
  11.9 3.4 %collective-permute-start.6 = (bf16[1,96,1536]{2,1,0:T(8,128)(2,1)S(1)}, bf16[1,96,1536]{2,1,0:T(8,128)(2,1)S(1)}, u32[]{:S(2)}, u32[]{:S(2)}) collective-permute-start(bf16[1,96,1536]{2,1,0:T(8,128)(2,1)S(1)} %get-tuple-element.22), channel_id=1, source_target_pairs={{0,16},{16,32},{32,48},{48,0},{1,17},{17,33},{33,49},{49,1},{2,18}... | collective-permute-start | bytes 884744 | tf_op jit(solution)/shard_map/ppermute | solution.py:29
  16.3 12.4 %collective-permute-start.22 = (bf16[192,768]{1,0:T(8,128)(2,1)S(1)}, bf16[192,768]{1,0:T(8,128)(2,1)S(1)}, u32[]{:S(2)}, u32[]{:S(2)}) collective-permute-start(bf16[192,768]{1,0:T(8,128)(2,1)S(1)} %pad_maximum_fusion.9), channel_id=1, source_target_pairs={{0,8},{8,0},{1,9},{9,1},{2,10},{10,2},{3,11},{11,3},{4,12},{12,4},... | collective-permute-start | bytes 884744 | tf_op jit(solution)/shard_map/ppermute | solution.py:29
  31.6 4.6 %collective-permute-start.1 = (bf16[96,1536]{1,0:T(8,128)(2,1)S(1)}, bf16[96,1536]{1,0:T(8,128)(2,1)S(1)}, u32[]{:S(2)}, u32[]{:S(2)}) collective-permute-start(bf16[96,1536]{1,0:T(8,128)(2,1)S(1)} %collective-permute-done), channel_id=1, source_target_pairs={{0,128},{128,256},{256,384},{384,448},{448,320},{320,192},{192,64}... | collective-permute-start | bytes 884744 | tf_op jit(solution)/shard_map/ppermute | solution.py:29
  41.5 3.8 %collective-permute-start.7 = (bf16[2,96,1536]{2,1,0:T(8,128)(2,1)S(1)}, bf16[2,96,1536]{2,1,0:T(8,128)(2,1)S(1)}, u32[]{:S(2)}, u32[]{:S(2)}) collective-permute-start(bf16[2,96,1536]{2,1,0:T(8,128)(2,1)S(1)} %pad_maximum_fusion.4), channel_id=1, source_target_pairs={{0,16},{16,32},{32,48},{48,0},{1,17},{17,33},{33,49},{49,1},{2,18}... | collective-permute-start | bytes 1769480 | tf_op jit(solution)/shard_map/ppermute | solution.py:29
  45.3 15.6 %collective-permute-done.1 = bf16[96,1536]{1,0:T(8,128)(2,1)S(1)} collective-permute-done((bf16[96,1536]{1,0:T(8,128)(2,1)S(1)}, bf16[96,1536]{1,0:T(8,128)(2,1)S(1)}, u32[]{:S(2)}, u32[]{:S(2)}) %collective-permute-start.1) | collective-permute-done | bytes 294944 | tf_op jit(solution)/shard_map/ppermute | solution.py:29
  62.1 5.5 %collective-permute-start.13 = (bf16[96,1536]{1,0:T(8,128)(2,1)S(1)}, bf16[96,1536]{1,0:T(8,128)(2,1)S(1)}, u32[]{:S(2)}, u32[]{:S(2)}) collective-permute-start(bf16[96,1536]{1,0:T(8,128)(2,1)S(1)} %collective-permute-done.1), channel_id=1, source_target_pairs={{0,128},{128,256},{256,384},{384,448},{448,320},{320,192},{192,64}... | collective-permute-start | bytes 884744 | tf_op jit(solution)/shard_map/ppermute | solution.py:29
  75.5 3.2 %collective-permute-start.5 = (bf16[1,96,1536]{2,1,0:T(8,128)(2,1)S(1)}, bf16[1,96,1536]{2,1,0:T(8,128)(2,1)S(1)}, u32[]{:S(2)}, u32[]{:S(2)}) collective-permute-start(bf16[1,96,1536]{2,1,0:T(8,128)(2,1)S(1)} %get-tuple-element.22), channel_id=1, source_target_pairs={{0,32},{16,48},{32,0},{48,16},{1,33},{17,49},{33,1},{49,17},{2,34}... | collective-permute-start | bytes 884744 | tf_op jit(solution)/shard_map/ppermute | solution.py:29
  78.8 4.1 %collective-permute-start.8 = (bf16[2,96,1536]{2,1,0:T(8,128)(2,1)S(1)}, bf16[2,96,1536]{2,1,0:T(8,128)(2,1)S(1)}, u32[]{:S(2)}, u32[]{:S(2)}) collective-permute-start(bf16[2,96,1536]{2,1,0:T(8,128)(2,1)S(1)} %pad_maximum_fusion.4), channel_id=1, source_target_pairs={{0,32},{16,48},{32,0},{48,16},{1,33},{17,49},{33,1},{49,17},{2,34}... | collective-permute-start | bytes 1769480 | tf_op jit(solution)/shard_map/ppermute | solution.py:29
  86.2 3.4 %collective-permute-start.14 = (bf16[2,96,1536]{2,1,0:T(8,128)(2,1)S(1)}, bf16[2,96,1536]{2,1,0:T(8,128)(2,1)S(1)}, u32[]{:S(2)}, u32[]{:S(2)}) collective-permute-start(bf16[2,96,1536]{2,1,0:T(8,128)(2,1)S(1)} %pad_maximum_fusion.5), channel_id=1, source_target_pairs={{0,16},{16,32},{32,48},{48,0},{1,17},{17,33},{33,49},{49,1},{2,18}... | collective-permute-start | bytes 1769480 | tf_op jit(solution)/shard_map/ppermute | solution.py:29
  89.8 3.5 %collective-permute-start.23 = (bf16[384,768]{1,0:T(8,128)(2,1)S(1)}, bf16[384,768]{1,0:T(8,128)(2,1)S(1)}, u32[]{:S(2)}, u32[]{:S(2)}) collective-permute-start(bf16[384,768]{1,0:T(8,128)(2,1)S(1)} %pad_maximum_fusion.7), channel_id=1, source_target_pairs={{0,2},{2,0},{4,6},{6,4},{1,3},{3,1},{5,7},{7,5},{8,10},{10,8},{12,... | collective-permute-start | bytes 1769480 | tf_op jit(solution)/shard_map/ppermute | solution.py:37
  93.4 4.0 %collective-permute-start.12 = (bf16[2,96,1536]{2,1,0:T(8,128)(2,1)S(1)}, bf16[2,96,1536]{2,1,0:T(8,128)(2,1)S(1)}, u32[]{:S(2)}, u32[]{:S(2)}) collective-permute-start(bf16[2,96,1536]{2,1,0:T(8,128)(2,1)S(1)} %pad_maximum_fusion.5), channel_id=1, source_target_pairs={{0,32},{16,48},{32,0},{48,16},{1,33},{17,49},{33,1},{49,17},{2,34}... | collective-permute-start | bytes 1769480 | tf_op jit(solution)/shard_map/ppermute | solution.py:29
  102.1 2.6 %bitcast_dynamic-update-slice_fusion.9 = bf16[2,4,2,2,96,1536]{5,4,3,2,1,0:T(8,128)(2,1)S(1)} fusion(bf16[2,4,2,2,96,1536]{5,4,3,2,1,0:T(8,128)(2,1)S(1)} %bitcast_dynamic-update-slice_fusion.10, u32[]{:T(128)} %bitcast.3, u32[]{:T(128)} %bitcast.20, u32[]{:T(128)} %bitcast.21, u32[]{:T(128)} %bitcast.6, bf16[96,1536]{1,0:T(8,128)(2,1)S(1)} %collective-permute-done), kind=kLoop, calls=%fused_computation.91 | loop fusion | bytes 589840 | tf_op jit(solution)/shard_map/dynamic_update_slice | solution.py:108
  104.7 2.6 bitcast_dynamic-update-slice_fusion.8
  107.3 2.5 fusion.44
  109.9 2.5 fusion.43
  113.3 3.6 %collective-permute-start.15 = (bf16[2,96,1536]{2,1,0:T(8,128)(2,1)S(1)}, bf16[2,96,1536]{2,1,0:T(8,128)(2,1)S(1)}, u32[]{:S(2)}, u32[]{:S(2)}) collective-permute-start(bf16[2,96,1536]{2,1,0:T(8,128)(2,1)S(1)} %pad_maximum_fusion.6), channel_id=1, source_target_pairs={{0,48},{16,0},{32,16},{48,32},{1,49},{17,1},{33,17},{49,33},{2,50}... | collective-permute-start | bytes 1769480 | tf_op jit(solution)/shard_map/ppermute | solution.py:29
  116.9 3.1 %collective-permute-start.17 = (bf16[2,96,1536]{2,1,0:T(8,128)(2,1)S(1)}, bf16[2,96,1536]{2,1,0:T(8,128)(2,1)S(1)}, u32[]{:S(2)}, u32[]{:S(2)}) collective-permute-start(bf16[2,96,1536]{2,1,0:T(8,128)(2,1)S(1)} %pad_maximum_fusion.6), channel_id=1, source_target_pairs={{0,16},{16,32},{32,48},{48,0},{1,17},{17,33},{33,49},{49,1},{2,18}... | collective-permute-start | bytes 1769480 | tf_op jit(solution)/shard_map/ppermute | solution.py:29
  120.0 6.1 %collective-permute-start.18 = (bf16[96,1536]{1,0:T(8,128)(2,1)S(1)}, bf16[96,1536]{1,0:T(8,128)(2,1)S(1)}, u32[]{:S(2)}, u32[]{:S(2)}) collective-permute-start(bf16[96,1536]{1,0:T(8,128)(2,1)S(1)} %collective-permute-done.13), channel_id=1, source_target_pairs={{0,128},{128,256},{256,384},{384,448},{448,320},{320,192},{192,64}... | collective-permute-start | bytes 884744 | tf_op jit(solution)/shard_map/ppermute | solution.py:29
  126.4 5.1 %collective-permute-start.24 = (bf16[768,768]{1,0:T(8,128)(2,1)S(1)}, bf16[768,768]{1,0:T(8,128)(2,1)S(1)}, u32[]{:S(2)}, u32[]{:S(2)}) collective-permute-start(bf16[768,768]{1,0:T(8,128)(2,1)S(1)} %pad_maximum_fusion.3), channel_id=1, source_target_pairs={{0,4},{2,6},{4,0},{6,2},{1,5},{3,7},{5,1},{7,3},{8,12},{10,14},{12... | collective-permute-start | bytes 3538952 | tf_op jit(solution)/shard_map/ppermute | solution.py:37
  131.5 2.5 fusion.42
  134.0 2.5 fusion.41
  136.5 2.6 fusion.40
  139.0 2.5 fusion.39
  141.6 2.6 bitcast_dynamic-update-slice_fusion.7
  144.1 2.6 %bitcast_dynamic-update-slice_fusion.6 = bf16[2,4,2,2,96,1536]{5,4,3,2,1,0:T(8,128)(2,1)S(1)} fusion(bf16[2,4,2,2,96,1536]{5,4,3,2,1,0:T(8,128)(2,1)S(1)} %bitcast_dynamic-update-slice_fusion.7, u32[]{:T(128)} %bitcast.3, u32[]{:T(128)} %bitcast.35, u32[]{:T(128)} %bitcast.36, u32[]{:T(128)} %bitcast.6, bf16[96,1536]{1,0:T(8,128)(2,1)S(1)} %collective-permute-done.9), kind=kLoop, calls=%fused_computation.88 | loop fusion | bytes 589840 | tf_op jit(solution)/shard_map/dynamic_update_slice | solution.py:108
  146.7 2.5 fusion.38
  149.3 2.5 fusion.37
  151.8 4.0 %collective-permute-start.16 = (bf16[2,96,1536]{2,1,0:T(8,128)(2,1)S(1)}, bf16[2,96,1536]{2,1,0:T(8,128)(2,1)S(1)}, u32[]{:S(2)}, u32[]{:S(2)}) collective-permute-start(bf16[2,96,1536]{2,1,0:T(8,128)(2,1)S(1)} %pad_maximum_fusion.6), channel_id=1, source_target_pairs={{0,32},{16,48},{32,0},{48,16},{1,33},{17,49},{33,1},{49,17},{2,34}... | collective-permute-start | bytes 1769480 | tf_op jit(solution)/shard_map/ppermute | solution.py:29
  155.8 3.1 %collective-permute-start.21 = (bf16[1,96,1536]{2,1,0:T(8,128)(2,1)S(1)}, bf16[1,96,1536]{2,1,0:T(8,128)(2,1)S(1)}, u32[]{:S(2)}, u32[]{:S(2)}) collective-permute-start(bf16[1,96,1536]{2,1,0:T(8,128)(2,1)S(1)} %bitcast.175), channel_id=1, source_target_pairs={{0,16},{16,32},{32,48},{48,0},{1,17},{17,33},{33,49},{49,1},{2,18}... | collective-permute-start | bytes 884744 | tf_op jit(solution)/shard_map/ppermute | solution.py:29
  158.9 2.5 fusion.36
  161.4 2.5 fusion.35
  163.9 2.5 fusion.34
  166.4 2.5 fusion.33
  168.9 2.5 bitcast_dynamic-update-slice_fusion.5
  171.5 2.6 bitcast_dynamic-update-slice_fusion.4
  174.0 3.4 %collective-permute-start.19 = (bf16[1,96,1536]{2,1,0:T(8,128)(2,1)S(1)}, bf16[1,96,1536]{2,1,0:T(8,128)(2,1)S(1)}, u32[]{:S(2)}, u32[]{:S(2)}) collective-permute-start(bf16[1,96,1536]{2,1,0:T(8,128)(2,1)S(1)} %bitcast.176), channel_id=1, source_target_pairs={{0,48},{16,0},{32,16},{48,32},{1,49},{17,1},{33,17},{49,33},{2,50}... | collective-permute-start | bytes 884744 | tf_op jit(solution)/shard_map/ppermute | solution.py:29
  177.4 4.0 %collective-permute-start.20 = (bf16[1,96,1536]{2,1,0:T(8,128)(2,1)S(1)}, bf16[1,96,1536]{2,1,0:T(8,128)(2,1)S(1)}, u32[]{:S(2)}, u32[]{:S(2)}) collective-permute-start(bf16[1,96,1536]{2,1,0:T(8,128)(2,1)S(1)} %bitcast.177), channel_id=1, source_target_pairs={{0,32},{16,48},{32,0},{48,16},{1,33},{17,49},{33,1},{49,17},{2,34}... | collective-permute-start | bytes 884744 | tf_op jit(solution)/shard_map/ppermute | solution.py:29
  183.8 2.5 fusion.31
  196.4 2.5 fusion.27
  198.9 2.5 bitcast_dynamic-update-slice_fusion.3
  206.4 2.5 bitcast_dynamic-update-slice_fusion
  209.8 3.4 %fusion.2 = f32[512,1024]{1,0:T(8,128)S(1)} fusion(bf16[3072,1536]{1,0:T(8,128)(2,1)S(1)} %bitcast.156, bf16[1536,768]{1,0:T(8,128)(2,1)S(1)} %get-tuple-element.38, bf16[1536,768]{1,0:T(8,128)(2,1)S(1)} %get-tuple-element.37), kind=kOutput, calls=%fused_computation.2 | convolution fusion | flops 3227516928 | bytes 13107200 | tf_op jit(solution)/shard_map/dot_general | solution.py:114
  219.0 3.0 %collective-permute-done.26 = f32[4,2,192,256]{3,2,1,0:T(8,128)S(1)} collective-permute-done((f32[4,2,192,256]{3,2,1,0:T(8,128)S(1)}, f32[4,2,192,256]{3,2,1,0:T(8,128)S(1)}, u32[]{:S(2)}, u32[]{:S(2)}) %collective-permute-start.26) | collective-permute-done | bytes 1572896 | tf_op jit(solution)/shard_map/ppermute | solution.py:29
  223.1 3.5 %all-to-all-start = ((bf16[4,2,192,256]{3,2,1,0:T(8,128)(2,1)}), bf16[4,2,192,256]{3,2,1,0:T(8,128)(2,1)S(1)}, u32[]{:S(2)}, u32[]{:S(2)}) async-start(bf16[4,2,192,256]{3,2,1,0:T(8,128)(2,1)} %fusion.10), calls=%async_computation | async-start | bytes 1572864 | tf_op jit(solution)/shard_map/all_to_all | solution.py:136
  226.6 13.1 %all-to-all-done = bf16[4,2,192,256]{3,2,1,0:T(8,128)(2,1)S(1)} async-done(((bf16[4,2,192,256]{3,2,1,0:T(8,128)(2,1)}), bf16[4,2,192,256]{3,2,1,0:T(8,128)(2,1)S(1)}, u32[]{:S(2)}, u32[]{:S(2)}) %all-to-all-start) | async-done | bytes 786464 | tf_op jit(solution)/shard_map/all_to_all | solution.py:136
  239.8 3.8 %collective-permute-start.27 = (bf16[192,256]{1,0:T(8,128)(2,1)S(1)}, bf16[192,256]{1,0:T(8,128)(2,1)S(1)}, u32[]{:S(2)}, u32[]{:S(2)}) collective-permute-start(bf16[192,256]{1,0:T(8,128)(2,1)S(1)} %fusion.47), channel_id=1, source_target_pairs={{0,8},{8,0},{1,9},{9,1},{2,10},{10,2},{3,11},{11,3},{4,12},{12,4},... | collective-permute-start | bytes 294920 | tf_op jit(solution)/shard_map/ppermute | solution.py:29
  243.6 14.6 %collective-permute-done.27 = bf16[192,256]{1,0:T(8,128)(2,1)S(1)} collective-permute-done((bf16[192,256]{1,0:T(8,128)(2,1)S(1)}, bf16[192,256]{1,0:T(8,128)(2,1)S(1)}, u32[]{:S(2)}, u32[]{:S(2)}) %collective-permute-start.27) | collective-permute-done | bytes 98336 | tf_op jit(solution)/shard_map/ppermute | solution.py:29
  (81 shorter events, 58.4 us)
Async XLA Ops:
  0.0 68.7 %copy-start = (bf16[512,96]{0,1:T(8,128)(2,1)S(1)}, bf16[512,96]{0,1:T(8,128)(2,1)}, u32[]{:S(2)}) copy-start(bf16[512,96]{0,1:T(8,128)(2,1)} %param.16) | copy-start | bytes 294916
  0.0 68.7 %copy-start.1 = (bf16[96,512]{1,0:T(8,128)(2,1)S(1)}, bf16[96,512]{1,0:T(8,128)(2,1)}, u32[]{:S(2)}) copy-start(bf16[96,512]{1,0:T(8,128)(2,1)} %param.15) | copy-start | bytes 294916
  0.0 68.7 %copy-start.2 = (bf16[96,512]{1,0:T(8,128)(2,1)S(1)}, bf16[96,512]{1,0:T(8,128)(2,1)}, u32[]{:S(2)}) copy-start(bf16[96,512]{1,0:T(8,128)(2,1)} %param.14) | copy-start | bytes 294916
  0.0 89.7 %copy-start.3 = (bf16[256,192]{0,1:T(8,128)(2,1)S(1)}, bf16[256,192]{0,1:T(8,128)(2,1)}, u32[]{:S(2)}) copy-start(bf16[256,192]{0,1:T(8,128)(2,1)} %param.11) | copy-start | bytes 294916
  0.0 89.7 %copy-start.4 = (bf16[256,192]{0,1:T(8,128)(2,1)S(1)}, bf16[256,192]{0,1:T(8,128)(2,1)}, u32[]{:S(2)}) copy-start(bf16[256,192]{0,1:T(8,128)(2,1)} %param.10) | copy-start | bytes 294916
  0.0 89.6 %copy-start.5 = (bf16[256,192]{0,1:T(8,128)(2,1)S(1)}, bf16[256,192]{0,1:T(8,128)(2,1)}, u32[]{:S(2)}) copy-start(bf16[256,192]{0,1:T(8,128)(2,1)} %param.9) | copy-start | bytes 294916
  1.1 30.5 %collective-permute-start = (bf16[96,1536]{1,0:T(8,128)(2,1)S(1)}, bf16[96,1536]{1,0:T(8,128)(2,1)S(1)}, u32[]{:S(2)}, u32[]{:S(2)}) collective-permute-start(bf16[96,1536]{1,0:T(8,128)(2,1)S(1)} %get-tuple-element.48), channel_id=1, source_target_pairs={{0,128},{128,256},{256,384},{384,448},{448,320},{320,192},{192,64}... | collective-permute-start | bytes 884744 | tf_op jit(solution)/shard_map/ppermute | solution.py:29
  7.5 29.3 %collective-permute-start.3 = (bf16[96,1536]{1,0:T(8,128)(2,1)S(1)}, bf16[96,1536]{1,0:T(8,128)(2,1)S(1)}, u32[]{:S(2)}, u32[]{:S(2)}) collective-permute-start(bf16[96,1536]{1,0:T(8,128)(2,1)S(1)} %get-tuple-element.48), channel_id=1, source_target_pairs={{0,64},{128,0},{256,128},{384,256},{448,384},{320,448},{192,320},{... | collective-permute-start | bytes 884744 | tf_op jit(solution)/shard_map/ppermute | solution.py:29
  9.5 29.6 %collective-permute-start.2 = (bf16[1,96,1536]{2,1,0:T(8,128)(2,1)S(1)}, bf16[1,96,1536]{2,1,0:T(8,128)(2,1)S(1)}, u32[]{:S(2)}, u32[]{:S(2)}) collective-permute-start(bf16[1,96,1536]{2,1,0:T(8,128)(2,1)S(1)} %get-tuple-element.22), channel_id=1, source_target_pairs={{0,48},{16,0},{32,16},{48,32},{1,49},{17,1},{33,17},{49,33},{2,50}... | collective-permute-start | bytes 884744 | tf_op jit(solution)/shard_map/ppermute | solution.py:29
  11.9 29.6 %collective-permute-start.6 = (bf16[1,96,1536]{2,1,0:T(8,128)(2,1)S(1)}, bf16[1,96,1536]{2,1,0:T(8,128)(2,1)S(1)}, u32[]{:S(2)}, u32[]{:S(2)}) collective-permute-start(bf16[1,96,1536]{2,1,0:T(8,128)(2,1)S(1)} %get-tuple-element.22), channel_id=1, source_target_pairs={{0,16},{16,32},{32,48},{48,0},{1,17},{17,33},{33,49},{49,1},{2,18}... | collective-permute-start | bytes 884744 | tf_op jit(solution)/shard_map/ppermute | solution.py:29
  16.3 73.3 %collective-permute-start.22 = (bf16[192,768]{1,0:T(8,128)(2,1)S(1)}, bf16[192,768]{1,0:T(8,128)(2,1)S(1)}, u32[]{:S(2)}, u32[]{:S(2)}) collective-permute-start(bf16[192,768]{1,0:T(8,128)(2,1)S(1)} %pad_maximum_fusion.9), channel_id=1, source_target_pairs={{0,8},{8,0},{1,9},{9,1},{2,10},{10,2},{3,11},{11,3},{4,12},{12,4},... | collective-permute-start | bytes 884744 | tf_op jit(solution)/shard_map/ppermute | solution.py:29
  31.6 29.3 %collective-permute-start.1 = (bf16[96,1536]{1,0:T(8,128)(2,1)S(1)}, bf16[96,1536]{1,0:T(8,128)(2,1)S(1)}, u32[]{:S(2)}, u32[]{:S(2)}) collective-permute-start(bf16[96,1536]{1,0:T(8,128)(2,1)S(1)} %collective-permute-done), channel_id=1, source_target_pairs={{0,128},{128,256},{256,384},{384,448},{448,320},{320,192},{192,64}... | collective-permute-start | bytes 884744 | tf_op jit(solution)/shard_map/ppermute | solution.py:29
  36.9 34.3 %collective-permute-start.9 = (bf16[96,1536]{1,0:T(8,128)(2,1)S(1)}, bf16[96,1536]{1,0:T(8,128)(2,1)S(1)}, u32[]{:S(2)}, u32[]{:S(2)}) collective-permute-start(bf16[96,1536]{1,0:T(8,128)(2,1)S(1)} %collective-permute-done.3), channel_id=1, source_target_pairs={{0,64},{128,0},{256,128},{384,256},{448,384},{320,448},{192,320},{... | collective-permute-start | bytes 884744 | tf_op jit(solution)/shard_map/ppermute | solution.py:29
  39.1 36.5 %collective-permute-start.4 = (bf16[2,96,1536]{2,1,0:T(8,128)(2,1)S(1)}, bf16[2,96,1536]{2,1,0:T(8,128)(2,1)S(1)}, u32[]{:S(2)}, u32[]{:S(2)}) collective-permute-start(bf16[2,96,1536]{2,1,0:T(8,128)(2,1)S(1)} %pad_maximum_fusion.4), channel_id=1, source_target_pairs={{0,48},{16,0},{32,16},{48,32},{1,49},{17,1},{33,17},{49,33},{2,50}... | collective-permute-start | bytes 1769480 | tf_op jit(solution)/shard_map/ppermute | solution.py:29
  41.5 37.3 %collective-permute-start.7 = (bf16[2,96,1536]{2,1,0:T(8,128)(2,1)S(1)}, bf16[2,96,1536]{2,1,0:T(8,128)(2,1)S(1)}, u32[]{:S(2)}, u32[]{:S(2)}) collective-permute-start(bf16[2,96,1536]{2,1,0:T(8,128)(2,1)S(1)} %pad_maximum_fusion.4), channel_id=1, source_target_pairs={{0,16},{16,32},{32,48},{48,0},{1,17},{17,33},{33,49},{49,1},{2,18}... | collective-permute-start | bytes 1769480 | tf_op jit(solution)/shard_map/ppermute | solution.py:29
  62.1 24.1 %collective-permute-start.13 = (bf16[96,1536]{1,0:T(8,128)(2,1)S(1)}, bf16[96,1536]{1,0:T(8,128)(2,1)S(1)}, u32[]{:S(2)}, u32[]{:S(2)}) collective-permute-start(bf16[96,1536]{1,0:T(8,128)(2,1)S(1)} %collective-permute-done.1), channel_id=1, source_target_pairs={{0,128},{128,256},{256,384},{384,448},{448,320},{320,192},{192,64}... | collective-permute-start | bytes 884744 | tf_op jit(solution)/shard_map/ppermute | solution.py:29
  71.2 12.6 %collective-permute-start.10 = (bf16[96,1536]{1,0:T(8,128)(2,1)S(1)}, bf16[96,1536]{1,0:T(8,128)(2,1)S(1)}, u32[]{:S(2)}, u32[]{:S(2)}) collective-permute-start(bf16[96,1536]{1,0:T(8,128)(2,1)S(1)} %collective-permute-done.9), channel_id=1, source_target_pairs={{0,64},{128,0},{256,128},{384,256},{448,384},{320,448},{192,320},{... | collective-permute-start | bytes 884744 | tf_op jit(solution)/shard_map/ppermute | solution.py:29
  75.5 17.9 %collective-permute-start.5 = (bf16[1,96,1536]{2,1,0:T(8,128)(2,1)S(1)}, bf16[1,96,1536]{2,1,0:T(8,128)(2,1)S(1)}, u32[]{:S(2)}, u32[]{:S(2)}) collective-permute-start(bf16[1,96,1536]{2,1,0:T(8,128)(2,1)S(1)} %get-tuple-element.22), channel_id=1, source_target_pairs={{0,32},{16,48},{32,0},{48,16},{1,33},{17,49},{33,1},{49,17},{2,34}... | collective-permute-start | bytes 884744 | tf_op jit(solution)/shard_map/ppermute | solution.py:29
  78.8 41.2 %collective-permute-start.8 = (bf16[2,96,1536]{2,1,0:T(8,128)(2,1)S(1)}, bf16[2,96,1536]{2,1,0:T(8,128)(2,1)S(1)}, u32[]{:S(2)}, u32[]{:S(2)}) collective-permute-start(bf16[2,96,1536]{2,1,0:T(8,128)(2,1)S(1)} %pad_maximum_fusion.4), channel_id=1, source_target_pairs={{0,32},{16,48},{32,0},{48,16},{1,33},{17,49},{33,1},{49,17},{2,34}... | collective-permute-start | bytes 1769480 | tf_op jit(solution)/shard_map/ppermute | solution.py:29
  83.7 29.5 %collective-permute-start.11 = (bf16[2,96,1536]{2,1,0:T(8,128)(2,1)S(1)}, bf16[2,96,1536]{2,1,0:T(8,128)(2,1)S(1)}, u32[]{:S(2)}, u32[]{:S(2)}) collective-permute-start(bf16[2,96,1536]{2,1,0:T(8,128)(2,1)S(1)} %pad_maximum_fusion.5), channel_id=1, source_target_pairs={{0,48},{16,0},{32,16},{48,32},{1,49},{17,1},{33,17},{49,33},{2,50}... | collective-permute-start | bytes 1769480 | tf_op jit(solution)/shard_map/ppermute | solution.py:29
  86.2 30.7 %collective-permute-start.14 = (bf16[2,96,1536]{2,1,0:T(8,128)(2,1)S(1)}, bf16[2,96,1536]{2,1,0:T(8,128)(2,1)S(1)}, u32[]{:S(2)}, u32[]{:S(2)}) collective-permute-start(bf16[2,96,1536]{2,1,0:T(8,128)(2,1)S(1)} %pad_maximum_fusion.5), channel_id=1, source_target_pairs={{0,16},{16,32},{32,48},{48,0},{1,17},{17,33},{33,49},{49,1},{2,18}... | collective-permute-start | bytes 1769480 | tf_op jit(solution)/shard_map/ppermute | solution.py:29
  89.8 36.2 %collective-permute-start.23 = (bf16[384,768]{1,0:T(8,128)(2,1)S(1)}, bf16[384,768]{1,0:T(8,128)(2,1)S(1)}, u32[]{:S(2)}, u32[]{:S(2)}) collective-permute-start(bf16[384,768]{1,0:T(8,128)(2,1)S(1)} %pad_maximum_fusion.7), channel_id=1, source_target_pairs={{0,2},{2,0},{4,6},{6,4},{1,3},{3,1},{5,7},{7,5},{8,10},{10,8},{12,... | collective-permute-start | bytes 1769480 | tf_op jit(solution)/shard_map/ppermute | solution.py:37
  93.4 58.4 %collective-permute-start.12 = (bf16[2,96,1536]{2,1,0:T(8,128)(2,1)S(1)}, bf16[2,96,1536]{2,1,0:T(8,128)(2,1)S(1)}, u32[]{:S(2)}, u32[]{:S(2)}) collective-permute-start(bf16[2,96,1536]{2,1,0:T(8,128)(2,1)S(1)} %pad_maximum_fusion.5), channel_id=1, source_target_pairs={{0,32},{16,48},{32,0},{48,16},{1,33},{17,49},{33,1},{49,17},{2,34}... | collective-permute-start | bytes 1769480 | tf_op jit(solution)/shard_map/ppermute | solution.py:29
  113.3 64.2 %collective-permute-start.15 = (bf16[2,96,1536]{2,1,0:T(8,128)(2,1)S(1)}, bf16[2,96,1536]{2,1,0:T(8,128)(2,1)S(1)}, u32[]{:S(2)}, u32[]{:S(2)}) collective-permute-start(bf16[2,96,1536]{2,1,0:T(8,128)(2,1)S(1)} %pad_maximum_fusion.6), channel_id=1, source_target_pairs={{0,48},{16,0},{32,16},{48,32},{1,49},{17,1},{33,17},{49,33},{2,50}... | collective-permute-start | bytes 1769480 | tf_op jit(solution)/shard_map/ppermute | solution.py:29
  116.9 57.1 %collective-permute-start.17 = (bf16[2,96,1536]{2,1,0:T(8,128)(2,1)S(1)}, bf16[2,96,1536]{2,1,0:T(8,128)(2,1)S(1)}, u32[]{:S(2)}, u32[]{:S(2)}) collective-permute-start(bf16[2,96,1536]{2,1,0:T(8,128)(2,1)S(1)} %pad_maximum_fusion.6), channel_id=1, source_target_pairs={{0,16},{16,32},{32,48},{48,0},{1,17},{17,33},{33,49},{49,1},{2,18}... | collective-permute-start | bytes 1769480 | tf_op jit(solution)/shard_map/ppermute | solution.py:29
  120.0 35.8 %collective-permute-start.18 = (bf16[96,1536]{1,0:T(8,128)(2,1)S(1)}, bf16[96,1536]{1,0:T(8,128)(2,1)S(1)}, u32[]{:S(2)}, u32[]{:S(2)}) collective-permute-start(bf16[96,1536]{1,0:T(8,128)(2,1)S(1)} %collective-permute-done.13), channel_id=1, source_target_pairs={{0,128},{128,256},{256,384},{384,448},{448,320},{320,192},{192,64}... | collective-permute-start | bytes 884744 | tf_op jit(solution)/shard_map/ppermute | solution.py:29
  126.4 64.8 %collective-permute-start.24 = (bf16[768,768]{1,0:T(8,128)(2,1)S(1)}, bf16[768,768]{1,0:T(8,128)(2,1)S(1)}, u32[]{:S(2)}, u32[]{:S(2)}) collective-permute-start(bf16[768,768]{1,0:T(8,128)(2,1)S(1)} %pad_maximum_fusion.3), channel_id=1, source_target_pairs={{0,4},{2,6},{4,0},{6,2},{1,5},{3,7},{5,1},{7,3},{8,12},{10,14},{12... | collective-permute-start | bytes 3538952 | tf_op jit(solution)/shard_map/ppermute | solution.py:37
  151.8 34.5 %collective-permute-start.16 = (bf16[2,96,1536]{2,1,0:T(8,128)(2,1)S(1)}, bf16[2,96,1536]{2,1,0:T(8,128)(2,1)S(1)}, u32[]{:S(2)}, u32[]{:S(2)}) collective-permute-start(bf16[2,96,1536]{2,1,0:T(8,128)(2,1)S(1)} %pad_maximum_fusion.6), channel_id=1, source_target_pairs={{0,32},{16,48},{32,0},{48,16},{1,33},{17,49},{33,1},{49,17},{2,34}... | collective-permute-start | bytes 1769480 | tf_op jit(solution)/shard_map/ppermute | solution.py:29
  155.8 50.6 %collective-permute-start.21 = (bf16[1,96,1536]{2,1,0:T(8,128)(2,1)S(1)}, bf16[1,96,1536]{2,1,0:T(8,128)(2,1)S(1)}, u32[]{:S(2)}, u32[]{:S(2)}) collective-permute-start(bf16[1,96,1536]{2,1,0:T(8,128)(2,1)S(1)} %bitcast.175), channel_id=1, source_target_pairs={{0,16},{16,32},{32,48},{48,0},{1,17},{17,33},{33,49},{49,1},{2,18}... | collective-permute-start | bytes 884744 | tf_op jit(solution)/shard_map/ppermute | solution.py:29
  174.0 27.4 %collective-permute-start.19 = (bf16[1,96,1536]{2,1,0:T(8,128)(2,1)S(1)}, bf16[1,96,1536]{2,1,0:T(8,128)(2,1)S(1)}, u32[]{:S(2)}, u32[]{:S(2)}) collective-permute-start(bf16[1,96,1536]{2,1,0:T(8,128)(2,1)S(1)} %bitcast.176), channel_id=1, source_target_pairs={{0,48},{16,0},{32,16},{48,32},{1,49},{17,1},{33,17},{49,33},{2,50}... | collective-permute-start | bytes 884744 | tf_op jit(solution)/shard_map/ppermute | solution.py:29
  177.4 26.5 %collective-permute-start.20 = (bf16[1,96,1536]{2,1,0:T(8,128)(2,1)S(1)}, bf16[1,96,1536]{2,1,0:T(8,128)(2,1)S(1)}, u32[]{:S(2)}, u32[]{:S(2)}) collective-permute-start(bf16[1,96,1536]{2,1,0:T(8,128)(2,1)S(1)} %bitcast.177), channel_id=1, source_target_pairs={{0,32},{16,48},{32,0},{48,16},{1,33},{17,49},{33,1},{49,17},{2,34}... | collective-permute-start | bytes 884744 | tf_op jit(solution)/shard_map/ppermute | solution.py:29
  191.9 17.0 %collective-permute-start.25 = (bf16[1536,768]{1,0:T(8,128)(2,1)S(1)}, bf16[1536,768]{1,0:T(8,128)(2,1)S(1)}, u32[]{:S(2)}, u32[]{:S(2)}) collective-permute-start(bf16[1536,768]{1,0:T(8,128)(2,1)S(1)} %pad_maximum_fusion.2), channel_id=1, source_target_pairs={{0,1},{1,0},{2,3},{3,2},{4,5},{5,4},{6,7},{7,6},{8,9},{9,8},{10,11... | collective-permute-start | bytes 7077896 | tf_op jit(solution)/shard_map/ppermute | solution.py:29
  216.5 5.4 %collective-permute-start.26 = (f32[4,2,192,256]{3,2,1,0:T(8,128)S(1)}, f32[4,2,192,256]{3,2,1,0:T(8,128)S(1)}, u32[]{:S(2)}, u32[]{:S(2)}) collective-permute-start(f32[4,2,192,256]{3,2,1,0:T(8,128)S(1)} %dynamic-slice_bitcast_fusion), channel_id=1, source_target_pairs={{0,1},{1,0},{2,3},{3,2},{4,5},{5,4},{6,7},{7,6},{8,9},{9,8},{10,11... | collective-permute-start | bytes 4718600 | tf_op jit(solution)/shard_map/ppermute | solution.py:29
  223.1 16.6 %all-to-all-start = ((bf16[4,2,192,256]{3,2,1,0:T(8,128)(2,1)}), bf16[4,2,192,256]{3,2,1,0:T(8,128)(2,1)S(1)}, u32[]{:S(2)}, u32[]{:S(2)}) async-start(bf16[4,2,192,256]{3,2,1,0:T(8,128)(2,1)} %fusion.10), calls=%async_computation | async-start | bytes 1572864 | tf_op jit(solution)/shard_map/all_to_all | solution.py:136
  239.8 18.4 %collective-permute-start.27 = (bf16[192,256]{1,0:T(8,128)(2,1)S(1)}, bf16[192,256]{1,0:T(8,128)(2,1)S(1)}, u32[]{:S(2)}, u32[]{:S(2)}) collective-permute-start(bf16[192,256]{1,0:T(8,128)(2,1)S(1)} %fusion.47), channel_id=1, source_target_pairs={{0,8},{8,0},{1,9},{9,1},{2,10},{10,2},{3,11},{11,3},{4,12},{12,4},... | collective-permute-start | bytes 294920 | tf_op jit(solution)/shard_map/ppermute | solution.py:29
